TPU v7x, 32 devices: a whole 2x2x4 slice. The times are simulated.
32 devices in a mesh: groups: 2 (over y), dp: 2 (over x), seq: 4 (over z), mp: 2 (over core).
Axes of the slice: x: 2, y: 2, z: 4, core: 2. Of those that a mesh axis runs over, the one named last changes fastest.
Arguments:
- queries: bfloat16 [4, 512, 1024], P(('groups', 'dp'), 'seq', 'mp'), parts along dimension 0, may hold values from -6 to 6
- keys: bfloat16 [4, 512, 1024], P(('groups', 'dp'), 'seq', 'mp'), parts along dimension 0, may hold values from -6 to 6
- values: bfloat16 [4, 512, 1024], P(('groups', 'dp'), 'seq', 'mp'), parts along dimension 0, may hold values from -6 to 6
- cotangent: bfloat16 [4, 512, 1024], P(('groups', 'dp'), 'seq', 'mp'), parts along dimension 0, may hold values from -6 to 6
- conv_weight: float32 [31, 1024], P(None, 'mp'), may hold values from -2 to 2
- rec_lengths: int32 [4, 16], P(('groups', 'dp')), parts along dimension 0, may hold values from 1 to 320, 512 in all within a row
Outputs:
- mixed: bfloat16 [4, 512, 1024], P(('groups', 'dp'), 'seq', 'mp'), parts along dimension 0
- grad_queries: bfloat16 [4, 512, 1024], P(('groups', 'dp'), 'seq', 'mp'), parts along dimension 0
- grad_keys: bfloat16 [4, 512, 1024], P(('groups', 'dp'), 'seq', 'mp'), parts along dimension 0
- grad_values: bfloat16 [4, 512, 1024], P(('groups', 'dp'), 'seq', 'mp'), parts along dimension 0
- grad_kernel: float32 [62, 1024], P('groups', 'mp'), parts along dimension 0
There are 2 independent parts, one for each index of `groups`. A program takes and returns all parts, laid end to end along the dimension named above; an argument that names none is the same for every part. Nothing has to cross between parts.
Inputs may be any that keep to these rules, and one draw needn't show every extreme that they name: `rec_lengths`: each row holds the lengths of 16 recordings in the order they are packed; they sum to 512 and the longest is 320.
All inputs are finite; a program needn't handle non-finite values.
Results may differ from a plain program's by a relative error of at most 0.012.
The roundings to bfloat16 on the way count: a program that leaves them out, or rounds other values in their place, can miss the bound.
Values may be sent and summed in bfloat16 or wider, within the bound.
No kernel may reach another device: no remote copies, remote signals or barrier semaphores. Data moves between devices by JAX's collectives and lax.ppermute only.
A program may use at most 64 MiB of HBM per device.

v0:
```python
import math

import jax
import jax.numpy as jnp
from jax import lax
from jax.sharding import PartitionSpec as P

HDIM = 64
KERNEL = 31
HALF = 15


NEGATIVE_FILL = -1e30


def extended(block, sides, width):
    for axis, dim in sides:
        count = lax.axis_size(axis)
        forward = [(i, i + 1) for i in range(count - 1)]
        backward = [(target, source) for source, target in forward]
        low = lax.ppermute(
            lax.slice_in_dim(block, block.shape[dim] - width, None, axis=dim), axis, forward
        )
        high = lax.ppermute(lax.slice_in_dim(block, 0, width, axis=dim), axis, backward)
        block = jnp.concatenate([low, block, high], axis=dim)
    return block


def pick_block(total_rows):
    for candidate in (512, 256, 128):
        return candidate
    return total_rows


def over_blocks(total_rows, advance, initial):
    block_rows = pick_block(total_rows)
    block_count = total_rows // block_rows
    if block_count == 1:
        return advance(initial, 0, block_rows)
    return lax.fori_loop(
        0,
        block_count,
        lambda number, running: advance(running, number * block_rows, block_rows),
        initial,
    )


def when_shared(compute, running):
    result = compute(running)
    return result


def on_device(queries, keys, values, cotangent, conv_weight, rec_lengths):
    frames = queries.shape[1]
    channels = queries.shape[2]
    local_heads = channels // HDIM
    score_scale = 1.0 / math.sqrt(HDIM)
    length_all = frames * lax.axis_size("seq")
    offset = lax.axis_index("seq") * frames
    record_ends = jnp.cumsum(rec_lengths[0], dtype=jnp.int32)

    def segment_of(positions):
        return jnp.sum((record_ends[None, :] <= positions[:, None]).astype(jnp.int32), axis=1)

    own_seg = segment_of(offset + jnp.arange(frames, dtype=jnp.int32))

    def to_heads(array):
        return array.reshape(array.shape[0], local_heads, HDIM).transpose(1, 0, 2)

    def from_heads(array):
        return array.transpose(1, 0, 2).reshape(array.shape[1], channels)

    q_heads = to_heads(queries[0])
    k_heads = to_heads(keys[0])
    v_heads = to_heads(values[0])

    def over_rows(advance, initial, members, first_row):
        total_rows = members[0].shape[1]

        def one_block(running, block_start, block_rows):
            sliced = tuple(
                (lax.dynamic_slice_in_dim(member, block_start, block_rows, 1) for member in members)
            )
            other_seg = segment_of(
                first_row + block_start + jnp.arange(block_rows, dtype=jnp.int32)
            )
            return when_shared(lambda current: advance(current, sliced, other_seg), running)

        return over_blocks(total_rows, one_block, initial)

    def query_scores(key_block, key_seg):
        raw_scores = (
            jnp.einsum("hqd,hkd->hqk", q_heads, key_block, preferred_element_type=jnp.float32)
            * score_scale
        )
        return jnp.where((own_seg[:, None] == key_seg[None, :])[None], raw_scores, NEGATIVE_FILL)

    def stats_step(running, sliced, key_seg):
        top_now, total_now = running
        scores = query_scores(sliced[0], key_seg)
        top_new = jnp.maximum(top_now, jnp.max(scores, axis=2))
        total_new = total_now * jnp.exp(top_now - top_new) + jnp.sum(
            jnp.exp(scores - top_new[:, :, None]), axis=2
        )
        return (top_new, total_new)

    stats_init = (
        jnp.full((local_heads, frames), NEGATIVE_FILL, jnp.float32),
        jnp.zeros((local_heads, frames), jnp.float32),
    )
    gathered = (
        lax.all_gather(keys, "seq", axis=1, tiled=True),
        lax.all_gather(values, "seq", axis=1, tiled=True),
    )
    key_whole = to_heads(gathered[0][0])
    value_whole = to_heads(gathered[1][0])
    row_stats = over_rows(stats_step, stats_init, (key_whole,), 0)
    log_total = row_stats[0] + jnp.log(row_stats[1])

    def output_step(running, sliced, key_seg):
        scores = query_scores(sliced[0], key_seg)
        soft_rounded = jnp.exp(scores - log_total[:, :, None]).astype(jnp.bfloat16)
        return running + jnp.einsum(
            "hqk,hkd->hqd", soft_rounded, sliced[1], preferred_element_type=jnp.float32
        )

    frame_zeros = jnp.zeros((local_heads, frames, HDIM), jnp.float32)
    attended_sum = over_rows(output_step, frame_zeros, (key_whole, value_whole), 0)
    attended_heads = attended_sum.astype(jnp.bfloat16)
    attended = from_heads(attended_heads)
    padded = extended(attended[None], (("seq", 1),), HALF)
    padded_wide = padded[0].astype(jnp.float32)
    pad_positions = offset - HALF + jnp.arange(frames + 2 * HALF, dtype=jnp.int32)
    inside = jnp.logical_and(pad_positions >= 0, pad_positions < length_all)
    pad_seg = jnp.where(inside, segment_of(pad_positions), -1)
    conv_pre = jnp.zeros((frames, channels), jnp.float32)
    for tap_index in range(KERNEL):
        tap_mask = (pad_seg[tap_index : tap_index + frames] == own_seg)[:, None]
        conv_pre = conv_pre + jnp.where(
            tap_mask, conv_weight[tap_index] * padded_wide[tap_index : tap_index + frames], 0.0
        )
    gate_value = jax.nn.sigmoid(conv_pre)
    mixed = (conv_pre * gate_value).astype(jnp.bfloat16)
    conv_grad = (
        cotangent[0].astype(jnp.float32) * gate_value * (1.0 + conv_pre * (1.0 - gate_value))
    ).astype(jnp.bfloat16)
    padded_grad = extended(conv_grad[None], (("seq", 1),), HALF)
    grad_wide = padded_grad[0].astype(jnp.float32)
    conv_grad_wide = conv_grad.astype(jnp.float32)
    grad_attended = jnp.zeros((frames, channels), jnp.float32)
    kernel_rows = []
    for tap_index in range(KERNEL):
        back_start = 2 * HALF - tap_index
        back_mask = (pad_seg[back_start : back_start + frames] == own_seg)[:, None]
        grad_attended = grad_attended + jnp.where(
            back_mask, conv_weight[tap_index] * grad_wide[back_start : back_start + frames], 0.0
        )
        tap_mask = (pad_seg[tap_index : tap_index + frames] == own_seg)[:, None]
        product = conv_grad_wide * padded_wide[tap_index : tap_index + frames]
        kernel_rows.append(jnp.sum(jnp.where(tap_mask, product, 0.0), axis=0))
    grad_kernel = lax.psum(jnp.stack(kernel_rows), ("dp", "seq"))
    grad_attended = grad_attended.astype(jnp.bfloat16)
    g_heads = to_heads(grad_attended)
    row_delta = jnp.sum(g_heads.astype(jnp.float32) * attended_heads.astype(jnp.float32), axis=2)

    def query_grad_step(running, sliced, key_seg):
        key_block = sliced[0]
        value_block = sliced[1]
        soft_weights = jnp.exp(query_scores(key_block, key_seg) - log_total[:, :, None])
        slopes = jnp.einsum(
            "hqd,hkd->hqk", g_heads, value_block, preferred_element_type=jnp.float32
        )
        mixed_grad = (soft_weights * (slopes - row_delta[:, :, None])).astype(jnp.bfloat16)
        return running + jnp.einsum(
            "hqk,hkd->hqd", mixed_grad, key_block, preferred_element_type=jnp.float32
        )

    grad_query = over_rows(query_grad_step, frame_zeros, (key_whole, value_whole), 0)

    def key_grad_step(running, sliced, query_seg):
        grad_key_now, grad_value_now = running
        query_block = sliced[0]
        grad_block = sliced[1]
        total_block = sliced[2]
        delta_block = sliced[3]
        raw_scores = (
            jnp.einsum("hqd,hkd->hqk", query_block, k_heads, preferred_element_type=jnp.float32)
            * score_scale
        )
        scores = jnp.where(
            (query_seg[:, None] == own_seg[None, :])[None], raw_scores, NEGATIVE_FILL
        )
        soft_weights = jnp.exp(scores - total_block[:, :, None])
        grad_value_new = grad_value_now + jnp.einsum(
            "hqk,hqd->hkd",
            soft_weights.astype(jnp.bfloat16),
            grad_block,
            preferred_element_type=jnp.float32,
        )
        slopes = jnp.einsum("hqd,hkd->hqk", grad_block, v_heads, preferred_element_type=jnp.float32)
        mixed_grad = (soft_weights * (slopes - delta_block[:, :, None])).astype(jnp.bfloat16)
        grad_key_new = grad_key_now + jnp.einsum(
            "hqk,hqd->hkd", mixed_grad, query_block, preferred_element_type=jnp.float32
        )
        return (grad_key_new, grad_value_new)

    all_totals, all_deltas = (
        lax.all_gather(log_total[None], "seq", axis=2, tiled=True),
        lax.all_gather(row_delta[None], "seq", axis=2, tiled=True),
    )
    member = (
        lax.all_gather(queries, "seq", axis=1, tiled=True),
        lax.all_gather(grad_attended[None], "seq", axis=1, tiled=True),
    )
    totals_piece = all_totals[0]
    deltas_piece = all_deltas[0]
    grad_key, grad_value = over_rows(
        key_grad_step,
        (frame_zeros, frame_zeros),
        (to_heads(member[0][0]), to_heads(member[1][0]), totals_piece, deltas_piece),
        jnp.int32(0),
    )
    grad_queries = from_heads(grad_query * score_scale).astype(jnp.bfloat16)[None]
    grad_keys = from_heads(grad_key * score_scale).astype(jnp.bfloat16)[None]
    grad_values = from_heads(grad_value).astype(jnp.bfloat16)[None]
    return (mixed[None], grad_queries, grad_keys, grad_values, grad_kernel)


def solution(mesh):
    placed = (
        P(("groups", "dp"), "seq", "mp"),
        P(("groups", "dp"), "seq", "mp"),
        P(("groups", "dp"), "seq", "mp"),
        P(("groups", "dp"), "seq", "mp"),
        P(None, "mp"),
        P(("groups", "dp"), None),
    )
    return jax.shard_map(
        on_device,
        mesh=mesh,
        in_specs=placed,
        out_specs=(
            P(("groups", "dp"), "seq", "mp"),
            P(("groups", "dp"), "seq", "mp"),
            P(("groups", "dp"), "seq", "mp"),
            P(("groups", "dp"), "seq", "mp"),
            P("groups", "mp"),
        ),
        check_vma=False,
    )
```

profile of v0, /device:TPU:0, one launch (start us, length us, event | category | flops | bytes accessed | tf_op | source)
XLA Modules:
  0.0 171.9 jit_solution(4685257258361283763)
XLA Ops:
  0.6 17.6 %all_gather.19 = bf16[1,512,512]{2,1,0:T(8,128)(2,1)S(1)} all-gather(bf16[1,128,512]{2,1,0:T(8,128)(2,1)} %param.8), channel_id=1, replica_groups=mesh['groups'=2,'dp'=2,'seq'=4,'mp'=2] {'seq'}, dimensions={1}, use_global_device_ids=true | all-gather | bytes 655360 | tf_op jit(solution)/shard_map/all_gather | solution.py:113
  18.2 0.2 copy.43
  18.4 1.2 copy.41
  19.6 16.6 %all_gather.18 = bf16[1,512,512]{2,1,0:T(8,128)(2,1)S(1)} all-gather(bf16[1,128,512]{2,1,0:T(8,128)(2,1)} %param.7), channel_id=1, replica_groups=mesh['groups'=2,'dp'=2,'seq'=4,'mp'=2] {'seq'}, dimensions={1}, use_global_device_ids=true | all-gather | bytes 655360 | tf_op jit(solution)/shard_map/all_gather | solution.py:112
  36.2 0.2 copy.42
  36.6 0.1 reduce
  36.8 0.1 convert_reduce_fusion.2
  36.9 0.1 broadcast_compare_fusion.1
  37.0 0.6 fusion.180
  37.6 0.6 exponential_reduce_fusion
  38.3 0.6 convolution_convert_fusion.1
  39.0 0.1 copy.44
  39.1 0.6 fusion.177
  39.7 1.3 collective-permute-start.1
  41.0 5.1 %collective-permute-start = (bf16[1,15,512]{2,1,0:T(8,128)(2,1)}, bf16[1,15,512]{2,1,0:T(8,128)(2,1)}, u32[]{:S(2)}, u32[]{:S(2)}) collective-permute-start(bf16[1,15,512]{2,1,0:T(8,128)(2,1)} %get-tuple-element.55), channel_id=1, source_target_pairs={{0,2},{2,4},{4,6},{1,3},{3,5},{5,7},{8,10},{10,12},{12,14},{9,11},... | collective-permute-start | bytes 46088 | tf_op jit(solution)/shard_map/ppermute | solution.py:21
  46.1 1.6 fusion.179
  47.8 0.7 fusion.178
  48.4 14.8 %all_gather.20 = bf16[1,512,512]{2,1,0:T(8,128)(2,1)S(1)} all-gather(bf16[1,128,512]{2,1,0:T(8,128)(2,1)S(1)} %copy-done.6), channel_id=1, replica_groups=mesh['groups'=2,'dp'=2,'seq'=4,'mp'=2] {'seq'}, dimensions={1}, use_global_device_ids=true | all-gather | bytes 655360 | tf_op jit(solution)/shard_map/all_gather | solution.py:212
  63.2 0.8 copy.49
  64.0 0.6 fusion.172
  64.6 0.8 broadcast_compare_fusion
  65.5 0.7 slice_compare_fusion.30
  66.2 0.2 copy.48
  66.5 13.4 %all_gather.21 = f32[1,8,512]{2,1,0:T(8,128)S(1)} all-gather(f32[1,8,128]{2,1,0:T(8,128)} %fusion.172), channel_id=1, replica_groups=mesh['groups'=2,'dp'=2,'seq'=4,'mp'=2] {'seq'}, dimensions={2}, use_global_device_ids=true | all-gather | bytes 20480 | tf_op jit(solution)/shard_map/all_gather | solution.py:208
  79.9 3.0 %subtract_exponential_fusion = f32[8,512,128]{2,1,0:T(8,128)} fusion(bf16[8,512,64]{1,2,0:T(8,128)(2,1)S(1)} %bitcast.668, bf16[8,128,64]{1,2,0:T(8,128)(2,1)} %bitcast.676, f32[8,512]{1,0:T(8,128)S(1)} %bitcast.740, pred[512,128]{1,0:T(8,128)(4,1)} %broadcast_compare_fusion), kind=kOutput, calls=%fused_computation.32 | convolution fusion | flops 68681728 | bytes 2834432 | tf_op jit(solution)/shard_map/hqd,hkd->hqk/dot_general | solution.py:187
  82.9 0.7 slice_compare_fusion.29
  83.6 0.8 copy.51
  84.4 0.8 maximum_convert_fusion
  85.3 3.8 %fusion.70 = (f32[512]{0:T(512)S(1)}, f32[512]{0:T(512)S(1)}, f32[512]{0:T(512)S(1)}, f32[512]{0:T(512)S(1)}, f32[512]{0:T(512)S(1)}, /*index=5*/f32[512]{0:T(51...) fusion(f32[1,158,512]{2,1,0:T(8,128)S(1)} %maximum_convert_fusi, ...), kind=kLoop, calls=%fused_computation.108 | loop fusion | flops 8515072 | bytes 8736640 | tf_op jit(solution)/shard_map/reduce_sum | solution.py:160
  89.2 0.2 fusion.68
  89.5 0.5 fusion.74
  90.3 1.2 fusion.72
  91.5 0.7 fusion.170
  92.2 1.3 collective-permute-start.3
  93.5 4.5 %collective-permute-start.2 = (bf16[1,15,512]{2,1,0:T(8,128)(2,1)S(1)}, bf16[1,15,512]{2,1,0:T(8,128)(2,1)S(1)}, u32[]{:S(2)}, u32[]{:S(2)}) collective-permute-start(bf16[1,15,512]{2,1,0:T(8,128)(2,1)S(1)} %get-tuple-element.53), channel_id=1, source_target_pairs={{0,2},{2,4},{4,6},{1,3},{3,5},{5,7},{8,10},{10,12},{12,14},{9,11},... | collective-permute-start | bytes 46088 | tf_op jit(solution)/shard_map/ppermute | solution.py:21
  98.1 0.1 stack.127
  98.2 34.8 %psum.7 = f32[31,512]{1,0:T(8,128)} all-reduce(f32[31,512]{1,0:T(8,128)S(1)} %stack.127), channel_id=1, replica_groups=mesh['groups'=2,'dp'=2,'seq'=4,'mp'=2] {'dp','seq'}, use_global_device_ids=true, to_apply=%region_38.39 | all-reduce | flops 15872 | bytes 126976 | tf_op jit(solution)/shard_map/psum | solution.py:161
  133.4 2.7 %fusion.78 = bf16[128,512]{1,0:T(8,128)(2,1)S(1)} fusion(f32[1,158,512]{2,1,0:T(8,128)S(1)} %maximum_convert_fusion.1, f32[512]{0:T(512)S(1)} %bitcast.699, f32[512]{0:T(512)S(1)} %bitcast.701, f32[512]{0:T(512)S(1)} %bitcast.705, f32[512]{0:T(512)S(1)} %bitcast.707, f32[512]{0:T(512)S(1)} %bitcast.709, f32[512]{0:T(512)S(1)} %bitcast.711, ...), kind=kLoop, calls=%fused_computation.117 | loop fusion | flops 6094848 | bytes 8324992 | tf_op jit(solution)/shard_map/convert_element_type | solution.py:162
  136.1 0.1 copy.47
  136.2 14.7 %all-gather = bf16[512,512]{1,0:T(8,128)(2,1)S(1)} all-gather(bf16[128,512]{1,0:T(8,128)(2,1)S(1)} %fusion.78), channel_id=2, replica_groups=mesh['groups'=2,'dp'=2,'seq'=4,'mp'=2] {'seq'}, dimensions={0}, use_global_device_ids=true | all-gather | bytes 655360 | tf_op jit(solution)/shard_map/all_gather | solution.py:213
  150.9 13.3 %all-gather.1 = f32[8,512]{1,0:T(8,128)S(1)} all-gather(f32[8,128]{1,0:T(8,128)S(1)} %multiply_reduce_fusion), channel_id=3, replica_groups=mesh['groups'=2,'dp'=2,'seq'=4,'mp'=2] {'seq'}, dimensions={1}, use_global_device_ids=true | all-gather | bytes 20480 | tf_op jit(solution)/shard_map/all_gather | solution.py:209
  164.2 2.0 %fusion.5 = bf16[8,128,64]{1,2,0:T(8,128)(2,1)S(1)} fusion(bf16[8,512,64]{1,2,0:T(8,128)(2,1)} %bitcast.667, f32[8,128,512]{2,1,0:T(8,128)S(1)} %get-tuple-element.120, bf16[8,128,64]{1,2,0:T(8,128)(2,1)S(1)} %bitcast.672, bf16[8,512,64]{1,2,0:T(8,128)(2,1)S(1)} %bitcast.665, f32[8,128]{1,0:T(8,128)S(1)} %multiply_reduce_fusion, f32[8,128]{1,0:T(8,128)} %copy-done.42), kind=kOutput, calls=%fused_computation.42 | convolution fusion | flops 136445952 | bytes 3416064 | tf_op jit(solution)/shard_map/hqk,hkd->hqd/dot_general | solution.py:174
  166.3 0.8 copy.52
  167.0 0.2 copy.50
  167.3 1.9 %convolution_convert_fusion = bf16[8,128,64]{1,2,0:T(8,128)(2,1)S(1)} fusion(bf16[8,512,64]{1,2,0:T(8,128)(2,1)S(1)} %bitcast.660, f32[8,512,128]{2,1,0:T(8,128)} %subtract_exponential_fusion), kind=kOutput, calls=%fused_computation.44 | convolution fusion | flops 67698688 | bytes 2752512 | tf_op jit(solution)/shard_map/hqk,hqd->hkd/dot_general | solution.py:194
  169.2 1.1 fusion.6
  170.4 0.8 copy.53
  171.1 0.8 copy.54
  (150 shorter events, 0.7 us)
Async XLA Ops:
  0.6 35.8 %copy-start.66 = (s32[1,16]{1,0:T(1,128)S(1)}, s32[1,16]{1,0:T(1,128)}, u32[]{:S(2)}) copy-start(s32[1,16]{1,0:T(1,128)} %param.11) | copy-start | bytes 196
  18.4 19.9 %copy-start.1 = (bf16[1,512,512]{1,2,0:T(8,128)(2,1)}, bf16[1,512,512]{1,2,0:T(8,128)(2,1)S(1)}, u32[]{:S(2)}) copy-start(bf16[1,512,512]{1,2,0:T(8,128)(2,1)S(1)} %copy.43) | copy-start | bytes 1572868
  38.3 10.2 %copy-start.6 = (bf16[1,128,512]{2,1,0:T(8,128)(2,1)S(1)}, bf16[1,128,512]{2,1,0:T(8,128)(2,1)}, u32[]{:S(2)}) copy-start(bf16[1,128,512]{2,1,0:T(8,128)(2,1)} %param.6) | copy-start | bytes 393220
  38.3 9.5 %copy-start.11 = (f32[31,512]{1,0:T(8,128)S(1)}, f32[31,512]{1,0:T(8,128)}, u32[]{:S(2)}) copy-start(f32[31,512]{1,0:T(8,128)} %param.10) | copy-start | bytes 190468
  38.3 24.9 %copy-start.7 = (bf16[1,128,512]{2,1,0:T(8,128)(2,1)S(1)}, bf16[1,128,512]{2,1,0:T(8,128)(2,1)}, u32[]{:S(2)}) copy-start(bf16[1,128,512]{2,1,0:T(8,128)(2,1)} %param.7) | copy-start | bytes 393220
  38.3 26.3 %copy-start.62 = (s32[128]{0:T(128)S(1)}, s32[128]{0:T(128)}, u32[]{:S(2)}) copy-start(s32[128]{0:T(128)} %copy-done.61) | copy-start | bytes 1540
  38.3 27.0 %copy-start.65 = (s32[16]{0:T(128)S(1)}, s32[16]{0:T(128)}, u32[]{:S(2)}) copy-start(s32[16]{0:T(128)} %copy-done.64) | copy-start | bytes 196
  39.7 44.7 %collective-permute-start.1 = (bf16[1,15,512]{2,1,0:T(8,128)(2,1)}, bf16[1,15,512]{2,1,0:T(8,128)(2,1)}, u32[]{:S(2)}, u32[]{:S(2)}) collective-permute-start(bf16[1,15,512]{2,1,0:T(8,128)(2,1)} %get-tuple-element.56), channel_id=1, source_target_pairs={{2,0},{4,2},{6,4},{3,1},{5,3},{7,5},{10,8},{12,10},{14,12},{11,9},... | collective-permute-start | bytes 46088 | tf_op jit(solution)/shard_map/ppermute | solution.py:24
  41.0 43.4 %collective-permute-start = (bf16[1,15,512]{2,1,0:T(8,128)(2,1)}, bf16[1,15,512]{2,1,0:T(8,128)(2,1)}, u32[]{:S(2)}, u32[]{:S(2)}) collective-permute-start(bf16[1,15,512]{2,1,0:T(8,128)(2,1)} %get-tuple-element.55), channel_id=1, source_target_pairs={{0,2},{2,4},{4,6},{1,3},{3,5},{5,7},{8,10},{10,12},{12,14},{9,11},... | collective-permute-start | bytes 46088 | tf_op jit(solution)/shard_map/ppermute | solution.py:21
  66.2 17.4 %copy-start.8 = (bf16[1,128,512]{2,1,0:T(8,128)(2,1)S(1)}, bf16[1,128,512]{2,1,0:T(8,128)(2,1)}, u32[]{:S(2)}) copy-start(bf16[1,128,512]{2,1,0:T(8,128)(2,1)} %param.8) | copy-start | bytes 393220
  66.4 22.7 %copy-start.4 = (bf16[1,512,512]{1,2,0:T(8,128)(2,1)}, bf16[1,512,512]{1,2,0:T(8,128)(2,1)S(1)}, u32[]{:S(2)}) copy-start(bf16[1,512,512]{1,2,0:T(8,128)(2,1)S(1)} %copy.48) | copy-start | bytes 1572868
  66.4 16.5 %copy-start.63 = (s32[128]{0:T(128)S(1)}, s32[128]{0:T(128)}, u32[]{:S(2)}) copy-start(s32[128]{0:T(128)} %copy-done.61) | copy-start | bytes 1540
  66.4 18.7 %copy-start.10 = (bf16[1,128,512]{2,1,0:T(8,128)(2,1)S(1)}, bf16[1,128,512]{2,1,0:T(8,128)(2,1)}, u32[]{:S(2)}) copy-start(bf16[1,128,512]{2,1,0:T(8,128)(2,1)} %param.9) | copy-start | bytes 393220
  66.5 18.7 %copy-start.12 = (f32[1,512]{1,0:T(1,128)S(1)}, f32[1,512]{1,0:T(1,128)}, u32[]{:S(2)}) copy-start(f32[1,512]{1,0:T(1,128)} %get-tuple-element.77) | copy-start | bytes 6148
  66.5 18.7 %copy-start.13 = (f32[1,512]{1,0:T(1,128)S(1)}, f32[1,512]{1,0:T(1,128)}, u32[]{:S(2)}) copy-start(f32[1,512]{1,0:T(1,128)} %get-tuple-element.78) | copy-start | bytes 6148
  85.2 4.2 %copy-start.43 = (pred[128]{0:T(512)(128)(4,1)S(1)}, pred[128]{0:T(512)(128)(4,1)}, u32[]{:S(2)}) copy-start(pred[128]{0:T(512)(128)(4,1)} %get-tuple-element.106) | copy-start | bytes 388
  85.3 4.2 %copy-start.49 = (pred[128]{0:T(512)(128)(4,1)S(1)}, pred[128]{0:T(512)(128)(4,1)}, u32[]{:S(2)}) copy-start(pred[128]{0:T(512)(128)(4,1)} %get-tuple-element.112) | copy-start | bytes 388
  90.0 43.1 %copy-start.14 = (f32[1,512]{1,0:T(1,128)S(1)}, f32[1,512]{1,0:T(1,128)}, u32[]{:S(2)}) copy-start(f32[1,512]{1,0:T(1,128)} %get-tuple-element.79) | copy-start | bytes 6148
  90.0 43.1 %copy-start.15 = (f32[1,512]{1,0:T(1,128)S(1)}, f32[1,512]{1,0:T(1,128)}, u32[]{:S(2)}) copy-start(f32[1,512]{1,0:T(1,128)} %get-tuple-element.80) | copy-start | bytes 6148
  90.1 43.1 %copy-start.16 = (f32[1,512]{1,0:T(1,128)S(1)}, f32[1,512]{1,0:T(1,128)}, u32[]{:S(2)}) copy-start(f32[1,512]{1,0:T(1,128)} %get-tuple-element.81) | copy-start | bytes 6148
  90.1 43.1 %copy-start.17 = (f32[1,512]{1,0:T(1,128)S(1)}, f32[1,512]{1,0:T(1,128)}, u32[]{:S(2)}) copy-start(f32[1,512]{1,0:T(1,128)} %get-tuple-element.82) | copy-start | bytes 6148
  90.1 43.1 %copy-start.18 = (f32[1,512]{1,0:T(1,128)S(1)}, f32[1,512]{1,0:T(1,128)}, u32[]{:S(2)}) copy-start(f32[1,512]{1,0:T(1,128)} %get-tuple-element.83) | copy-start | bytes 6148
  90.1 43.1 %copy-start.19 = (f32[1,512]{1,0:T(1,128)S(1)}, f32[1,512]{1,0:T(1,128)}, u32[]{:S(2)}) copy-start(f32[1,512]{1,0:T(1,128)} %get-tuple-element.84) | copy-start | bytes 6148
  90.1 43.1 %copy-start.20 = (f32[1,512]{1,0:T(1,128)S(1)}, f32[1,512]{1,0:T(1,128)}, u32[]{:S(2)}) copy-start(f32[1,512]{1,0:T(1,128)} %get-tuple-element.85) | copy-start | bytes 6148
  90.1 43.1 %copy-start.21 = (f32[1,512]{1,0:T(1,128)S(1)}, f32[1,512]{1,0:T(1,128)}, u32[]{:S(2)}) copy-start(f32[1,512]{1,0:T(1,128)} %get-tuple-element.86) | copy-start | bytes 6148
  90.1 43.1 %copy-start.22 = (f32[1,512]{1,0:T(1,128)S(1)}, f32[1,512]{1,0:T(1,128)}, u32[]{:S(2)}) copy-start(f32[1,512]{1,0:T(1,128)} %get-tuple-element.87) | copy-start | bytes 6148
  90.1 43.1 %copy-start.23 = (f32[1,512]{1,0:T(1,128)S(1)}, f32[1,512]{1,0:T(1,128)}, u32[]{:S(2)}) copy-start(f32[1,512]{1,0:T(1,128)} %get-tuple-element.57) | copy-start | bytes 6148
  90.1 43.1 %copy-start.24 = (f32[1,512]{1,0:T(1,128)S(1)}, f32[1,512]{1,0:T(1,128)}, u32[]{:S(2)}) copy-start(f32[1,512]{1,0:T(1,128)} %get-tuple-element.58) | copy-start | bytes 6148
  90.1 43.1 %copy-start.25 = (f32[1,512]{1,0:T(1,128)S(1)}, f32[1,512]{1,0:T(1,128)}, u32[]{:S(2)}) copy-start(f32[1,512]{1,0:T(1,128)} %get-tuple-element.59) | copy-start | bytes 6148
  90.2 43.1 %copy-start.26 = (f32[1,512]{1,0:T(1,128)S(1)}, f32[1,512]{1,0:T(1,128)}, u32[]{:S(2)}) copy-start(f32[1,512]{1,0:T(1,128)} %get-tuple-element.60) | copy-start | bytes 6148
  90.2 43.1 %copy-start.27 = (f32[1,512]{1,0:T(1,128)S(1)}, f32[1,512]{1,0:T(1,128)}, u32[]{:S(2)}) copy-start(f32[1,512]{1,0:T(1,128)} %get-tuple-element.61) | copy-start | bytes 6148
  90.2 43.1 %copy-start.28 = (f32[1,512]{1,0:T(1,128)S(1)}, f32[1,512]{1,0:T(1,128)}, u32[]{:S(2)}) copy-start(f32[1,512]{1,0:T(1,128)} %get-tuple-element.62) | copy-start | bytes 6148
  90.2 43.1 %copy-start.29 = (f32[1,512]{1,0:T(1,128)S(1)}, f32[1,512]{1,0:T(1,128)}, u32[]{:S(2)}) copy-start(f32[1,512]{1,0:T(1,128)} %get-tuple-element.63) | copy-start | bytes 6148
  90.2 43.1 %copy-start.30 = (f32[1,512]{1,0:T(1,128)S(1)}, f32[1,512]{1,0:T(1,128)}, u32[]{:S(2)}) copy-start(f32[1,512]{1,0:T(1,128)} %get-tuple-element.64) | copy-start | bytes 6148
  90.2 43.1 %copy-start.31 = (f32[1,512]{1,0:T(1,128)S(1)}, f32[1,512]{1,0:T(1,128)}, u32[]{:S(2)}) copy-start(f32[1,512]{1,0:T(1,128)} %get-tuple-element.65) | copy-start | bytes 6148
  90.2 43.1 %copy-start.32 = (f32[1,512]{1,0:T(1,128)S(1)}, f32[1,512]{1,0:T(1,128)}, u32[]{:S(2)}) copy-start(f32[1,512]{1,0:T(1,128)} %get-tuple-element.66) | copy-start | bytes 6148
  90.2 43.1 %copy-start.33 = (f32[1,512]{1,0:T(1,128)S(1)}, f32[1,512]{1,0:T(1,128)}, u32[]{:S(2)}) copy-start(f32[1,512]{1,0:T(1,128)} %get-tuple-element.67) | copy-start | bytes 6148
  90.2 43.1 %copy-start.34 = (f32[1,512]{1,0:T(1,128)S(1)}, f32[1,512]{1,0:T(1,128)}, u32[]{:S(2)}) copy-start(f32[1,512]{1,0:T(1,128)} %get-tuple-element.68) | copy-start | bytes 6148
  90.2 43.1 %copy-start.35 = (f32[1,512]{1,0:T(1,128)S(1)}, f32[1,512]{1,0:T(1,128)}, u32[]{:S(2)}) copy-start(f32[1,512]{1,0:T(1,128)} %get-tuple-element.69) | copy-start | bytes 6148
  90.3 43.1 %copy-start.36 = (f32[1,512]{1,0:T(1,128)S(1)}, f32[1,512]{1,0:T(1,128)}, u32[]{:S(2)}) copy-start(f32[1,512]{1,0:T(1,128)} %get-tuple-element.70) | copy-start | bytes 6148
  90.3 43.1 %copy-start.37 = (f32[1,512]{1,0:T(1,128)S(1)}, f32[1,512]{1,0:T(1,128)}, u32[]{:S(2)}) copy-start(f32[1,512]{1,0:T(1,128)} %get-tuple-element.71) | copy-start | bytes 6148
  90.3 43.1 %copy-start.38 = (f32[1,512]{1,0:T(1,128)S(1)}, f32[1,512]{1,0:T(1,128)}, u32[]{:S(2)}) copy-start(f32[1,512]{1,0:T(1,128)} %get-tuple-element.72) | copy-start | bytes 6148
  90.3 43.1 %copy-start.39 = (f32[1,512]{1,0:T(1,128)S(1)}, f32[1,512]{1,0:T(1,128)}, u32[]{:S(2)}) copy-start(f32[1,512]{1,0:T(1,128)} %get-tuple-element.73) | copy-start | bytes 6148
  90.3 43.1 %copy-start.40 = (f32[1,512]{1,0:T(1,128)S(1)}, f32[1,512]{1,0:T(1,128)}, u32[]{:S(2)}) copy-start(f32[1,512]{1,0:T(1,128)} %get-tuple-element.74) | copy-start | bytes 6148
  90.3 43.1 %copy-start.41 = (f32[1,512]{1,0:T(1,128)S(1)}, f32[1,512]{1,0:T(1,128)}, u32[]{:S(2)}) copy-start(f32[1,512]{1,0:T(1,128)} %get-tuple-element.75) | copy-start | bytes 6148
  92.2 40.8 %collective-permute-start.3 = (bf16[1,15,512]{2,1,0:T(8,128)(2,1)S(1)}, bf16[1,15,512]{2,1,0:T(8,128)(2,1)S(1)}, u32[]{:S(2)}, u32[]{:S(2)}) collective-permute-start(bf16[1,15,512]{2,1,0:T(8,128)(2,1)S(1)} %get-tuple-element.54), channel_id=1, source_target_pairs={{2,0},{4,2},{6,4},{3,1},{5,3},{7,5},{10,8},{12,10},{14,12},{11,9},... | collective-permute-start | bytes 46088 | tf_op jit(solution)/shard_map/ppermute | solution.py:24
  93.5 39.5 %collective-permute-start.2 = (bf16[1,15,512]{2,1,0:T(8,128)(2,1)S(1)}, bf16[1,15,512]{2,1,0:T(8,128)(2,1)S(1)}, u32[]{:S(2)}, u32[]{:S(2)}) collective-permute-start(bf16[1,15,512]{2,1,0:T(8,128)(2,1)S(1)} %get-tuple-element.53), channel_id=1, source_target_pairs={{0,2},{2,4},{4,6},{1,3},{3,5},{5,7},{8,10},{10,12},{12,14},{9,11},... | collective-permute-start | bytes 46088 | tf_op jit(solution)/shard_map/ppermute | solution.py:21
  133.4 30.8 %copy-start.2 = (bf16[1,512,512]{1,2,0:T(8,128)(2,1)S(1)}, bf16[1,512,512]{1,2,0:T(8,128)(2,1)}, u32[]{:S(2)}) copy-start(bf16[1,512,512]{1,2,0:T(8,128)(2,1)} %copy-done.1) | copy-start | bytes 1572868
  (23 other events, 62.8 us)
where the time goes:
time: 172 us
  blocking collectives  125 us (73%)
  other arithmetic  13.9 us (8%)
  starting transfers between devices  12.3 us (7%)
  local copies, waits for them, and re-layouts  9.52 us (6%)
  matrix products  9.3 us (5%)
  between operations  1.78 us (1%)
    psum x1, blocking collectives, on_device(): grad_kernel = lax.psum(jnp.stack(kernel_rows), ('dp', 'seq'))  34.8 us
    all_gather x1, blocking collectives, on_device(): lax.all_gather(values, 'seq', axis=1, tiled=True)  17.6 us
    all_gather x1, blocking collectives, on_device(): lax.all_gather(keys, 'seq', axis=1, tiled=True)  16.6 us
    all_gather x1, blocking collectives, on_device(): lax.all_gather(queries, 'seq', axis=1, tiled=True)  14.8 us
    all_gather x1, blocking collectives, on_device(): lax.all_gather(grad_attended[None], 'seq', axis=1, tiled=True)  14.7 us
    all_gather x1, blocking collectives, on_device(): lax.all_gather(log_total[None], 'seq', axis=2, tiled=True)  13.4 us
    all_gather x1, blocking collectives, on_device(): lax.all_gather(row_delta[None], 'seq', axis=2, tiled=True)  13.3 us
    ppermute x2, starting transfers between devices, extended(): lax.ppermute(lax.slice_in_dim(block, block.shape[dim] - width, None, axis...  9.69 us
  transfers between devices with their start and end apart: 4, of which 0 were waited for; matrix products, arithmetic and copies ran while one was open for 6% of the time, Pallas kernels for 0%

commit v1 on v0

--- a/solution.py
+++ b/solution.py
@@ -1,8 +1,11 @@
+import functools
 import math
 
 import jax
 import jax.numpy as jnp
 from jax import lax
+from jax.experimental import pallas as pl
+from jax.experimental.pallas import tpu as pltpu
 from jax.sharding import PartitionSpec as P
 
 HDIM = 64
@@ -226,6 +229,402 @@
     return (mixed[None], grad_queries, grad_keys, grad_values, grad_kernel)
 
 
+LANES = 128
+PAD = 16
+VMEM = pltpu.VMEM
+MIB = 1024 * 1024
+
+
+def mm(left, right):
+    return lax.dot_general(
+        left, right, (((1,), (0,)), ((), ())), preferred_element_type=jnp.float32
+    )
+
+
+def mm_nt(left, right):
+    return lax.dot_general(
+        left, right, (((1,), (1,)), ((), ())), preferred_element_type=jnp.float32
+    )
+
+
+def rows_at(block, frames):
+    return pl.ds(pl.multiple_of(block * frames, frames), frames)
+
+
+def lanes_at(block):
+    return pl.ds(pl.multiple_of(block * LANES, LANES), LANES)
+
+
+def pack_kernel(ranks, q_ref, k_ref, v_ref, c_ref, *rest):
+    outs, sems = rest[:-1], rest[-1]
+    me = lax.axis_index("seq")
+    copies = []
+    for step in range(1, ranks):
+        lanes = lanes_at(me ^ step)
+        three, one = outs[step - 1], outs[ranks - 1 + step - 1]
+        for place, source in enumerate((q_ref, k_ref, v_ref)):
+            copies.append((source.at[0, :, lanes], three.at[place]))
+        copies.append((c_ref.at[0, :, lanes], one))
+    copies = [
+        pltpu.make_async_copy(source, target, sems.at[number])
+        for number, (source, target) in enumerate(copies)
+    ]
+    for copy in copies:
+        copy.start()
+    for copy in copies:
+        copy.wait()
+
+
+def mask_kernel(length, lens_ref, q_ref, k_ref, v_ref, c_ref, own_ref, col_ref, row_ref, after_ref, before_ref, sems):
+    me = lax.axis_index("seq")
+    lanes = lanes_at(me)
+    copies = [
+        pltpu.make_async_copy(source.at[0, :, lanes], own_ref.at[place], sems.at[place])
+        for place, source in enumerate((q_ref, k_ref, v_ref, c_ref))
+    ]
+    for copy in copies:
+        copy.start()
+    count = lens_ref.shape[1]
+    ends = []
+    running = jnp.int32(0)
+    for number in range(count):
+        running = running + lens_ref[0, number]
+        ends.append(running)
+
+    row_time = lax.broadcasted_iota(jnp.int32, row_ref.shape, 1)
+    row_first = jnp.zeros(row_ref.shape, jnp.int32)
+    for end in ends:
+        row_first = jnp.where(row_time >= end, end, row_first)
+    row_ref[...] = row_first
+
+    chunk = 64
+
+    def some_rows(number, carry):
+        base = pl.multiple_of(number * chunk, chunk)
+        time = base + lax.broadcasted_iota(jnp.int32, (chunk, LANES), 0)
+        first = jnp.zeros((chunk, LANES), jnp.int32)
+        last = jnp.full((chunk, LANES), length, jnp.int32)
+        for end in ends:
+            first = jnp.where(time >= end, end, first)
+        for end in reversed(ends):
+            last = jnp.where(time < end, end, last)
+        rows = pl.ds(base, chunk)
+        col_ref[rows, :] = first
+        after_ref[rows, :] = last - 1 - time
+        before_ref[rows, :] = time - first
+        return carry
+
+    lax.fori_loop(0, length // chunk, some_rows, 0)
+    for copy in copies:
+        copy.wait()
+
+
+def forward_kernel(ranks, frames, *refs):
+    recvs = refs[: ranks - 1]
+    own_ref, col_ref, row_ref, after_ref, before_ref, w_ref = refs[ranks - 1 : ranks + 5]
+    soft_ref, att_ref, att_t_ref, pre_ref, q_ref, k_t_ref, v_ref = refs[ranks + 5 : ranks + 12]
+    k_full, q_full, w_own, w_sem = refs[ranks + 12 :]
+    me = lax.axis_index("seq")
+    length = ranks * frames
+    copy = pltpu.make_async_copy(w_ref.at[:, lanes_at(me)], w_own, w_sem)
+    copy.start()
+    for place, target in enumerate((q_full, k_full, v_ref)):
+        target[rows_at(me, frames), :] = own_ref[place]
+        for step in range(1, ranks):
+            target[rows_at(me ^ step, frames), :] = recvs[step - 1][place]
+    heads = LANES // HDIM
+    lane_head = lax.broadcasted_iota(jnp.int32, (1, LANES), 1) // HDIM
+    scaled = q_full[...].astype(jnp.float32) * (1.0 / math.sqrt(HDIM))
+    for head in range(heads):
+        q_ref[head] = jnp.where(lane_head == head, scaled, 0.0).astype(jnp.bfloat16)
+    k_t_ref[...] = k_full[...].astype(jnp.float32).T.astype(jnp.bfloat16)
+    v_t = v_ref[...].astype(jnp.float32).T.astype(jnp.bfloat16)
+    wide = 256
+    for head in range(heads):
+        for start in range(0, length, wide):
+            cols = slice(start, start + wide)
+            raw = mm_nt(k_full[...], q_ref[head, cols, :])
+            same = jnp.concatenate([col_ref[...]] * (wide // LANES), axis=1) == row_ref[0:1, cols]
+            scores = jnp.where(same, raw, NEGATIVE_FILL)
+            top = jnp.max(scores, axis=0, keepdims=True)
+            powers = jnp.exp(scores - top)
+            share = 1.0 / jnp.sum(powers, axis=0, keepdims=True)
+            soft = (powers * share).astype(jnp.bfloat16)
+            soft_ref[head, :, cols] = soft
+            rows = slice(head * HDIM, (head + 1) * HDIM)
+            att_t_ref[rows, cols] = mm(v_t[rows], soft).astype(jnp.bfloat16).astype(jnp.float32)
+    zeros = jnp.zeros((PAD, LANES), jnp.float32)
+    att_ref[0:PAD, :] = zeros
+    att_ref[PAD : PAD + length, :] = att_t_ref[...].T
+    att_ref[PAD + length :, :] = zeros
+    copy.wait()
+
+    chunk = 64
+
+    def some_rows(number, carry):
+        base = pl.multiple_of(number * chunk, chunk)
+        rows = pl.ds(base, chunk)
+        after, before = after_ref[rows, :], before_ref[rows, :]
+        total = jnp.zeros((chunk, LANES), jnp.float32)
+        for tap in range(KERNEL):
+            off = tap - HALF
+            piece = att_ref[pl.ds(base + (PAD + off), chunk), :]
+            if off > 0:
+                piece = jnp.where(after >= off, piece, 0.0)
+            if off < 0:
+                piece = jnp.where(before >= -off, piece, 0.0)
+            total = total + w_own[tap : tap + 1, :] * piece
+        pre_ref[rows, :] = total
+        return carry
+
+    lax.fori_loop(0, length // chunk, some_rows, 0)
+
+
+def backward_kernel(ranks, frames, *refs):
+    cots = refs[: ranks - 1]
+    own_ref, soft_ref, att_ref, att_t_ref, pre_ref, q_ref, k_t_ref, v_ref, after_ref, before_ref, w_ref = refs[
+        ranks - 1 : ranks + 10
+    ]
+    outs = refs[ranks + 10 : 2 * ranks + 10]
+    taps_ref = refs[2 * ranks + 10]
+    cot, grad_pad, mixed, g_att, res_q, res_k, res_v, tap_sum, w_own, w_sem = refs[2 * ranks + 11 :]
+    me = lax.axis_index("seq")
+    length = ranks * frames
+    copy = pltpu.make_async_copy(w_ref.at[:, lanes_at(me)], w_own, w_sem)
+    copy.start()
+    cot[rows_at(me, frames), :] = own_ref[3]
+    for step in range(1, ranks):
+        cot[rows_at(me ^ step, frames), :] = cots[step - 1][...]
+    zeros = jnp.zeros((PAD, LANES), jnp.float32)
+    grad_pad[0:PAD, :] = zeros
+    grad_pad[PAD + length :, :] = zeros
+    pre = pre_ref[...]
+    gate = jax.nn.sigmoid(pre)
+    mixed[...] = (pre * gate).astype(jnp.bfloat16)
+    conv_grad = cot[...].astype(jnp.float32) * gate * (1.0 + pre * (1.0 - gate))
+    grad_pad[PAD : PAD + length, :] = conv_grad.astype(jnp.bfloat16).astype(jnp.float32)
+    tap_sum[...] = jnp.zeros(tap_sum.shape, jnp.float32)
+    copy.wait()
+
+    chunk = 64
+
+    def some_rows(number, carry):
+        base = pl.multiple_of(number * chunk, chunk)
+        rows = pl.ds(base, chunk)
+        after, before = after_ref[rows, :], before_ref[rows, :]
+        own_att = att_ref[pl.ds(base + PAD, chunk), :]
+        total = jnp.zeros((chunk, LANES), jnp.float32)
+        for tap in range(KERNEL):
+            off = tap - HALF
+            piece = grad_pad[pl.ds(base + (PAD - off), chunk), :]
+            if off > 0:
+                piece = jnp.where(before >= off, piece, 0.0)
+            if off < 0:
+                piece = jnp.where(after >= -off, piece, 0.0)
+            total = total + w_own[tap : tap + 1, :] * piece
+            part = (own_att * piece).reshape(chunk // 8, 8, LANES)
+            tap_sum[tap] = tap_sum[tap] + jnp.sum(part, axis=0)
+        g_att[rows, :] = total.astype(jnp.bfloat16)
+        return carry
+
+    lax.fori_loop(0, length // chunk, some_rows, 0)
+    taps = jnp.sum(tap_sum[...], axis=1).astype(jnp.bfloat16)
+    taps_ref[...] = taps
+
+    heads = LANES // HDIM
+    lane_head = lax.broadcasted_iota(jnp.int32, (1, LANES), 1) // HDIM
+    g_wide = g_att[...].astype(jnp.float32)
+    products_t = (g_wide * att_ref[PAD : PAD + length, :]).T
+    g_heads = [jnp.where(lane_head == head, g_wide, 0.0).astype(jnp.bfloat16) for head in range(heads)]
+    wide = 256
+    grad_v = jnp.zeros((length, LANES), jnp.float32)
+    grad_k = jnp.zeros((length, LANES), jnp.float32)
+    for head in range(heads):
+        rows = slice(head * HDIM, (head + 1) * HDIM)
+        delta = jnp.sum(products_t[rows], axis=0, keepdims=True)
+        for start in range(0, length, wide):
+            cols = slice(start, start + wide)
+            soft = soft_ref[head, :, cols]
+            slopes = mm_nt(v_ref[...], g_heads[head][cols])
+            mixed_grad = (soft.astype(jnp.float32) * (slopes - delta[:, cols])).astype(jnp.bfloat16)
+            grad_v = grad_v + mm(soft, g_heads[head][cols])
+            grad_k = grad_k + mm(mixed_grad, q_ref[head, cols, :])
+            res_q[rows, cols] = mm(k_t_ref[rows, :], mixed_grad) * (1.0 / math.sqrt(HDIM))
+    res_k[...] = grad_k.astype(jnp.bfloat16)
+    res_v[...] = grad_v.astype(jnp.bfloat16)
+    grad_q = res_q[...].T.astype(jnp.bfloat16)
+    g_att[...] = grad_q
+    for step in range(ranks):
+        rows = rows_at(me ^ step, frames)
+        out = outs[step]
+        out[0:frames, :] = mixed[rows, :]
+        out[frames : 2 * frames, :] = g_att[rows, :]
+        out[2 * frames : 3 * frames, :] = res_k[rows, :]
+        out[3 * frames : 4 * frames, :] = res_v[rows, :]
+        out[4 * frames :, :] = taps
+
+
+def spread_kernel(ranks, frames, *refs):
+    blocks = refs[:ranks]
+    others = refs[ranks : 2 * ranks]
+    mixed_ref, q_ref, k_ref, v_ref, taps_ref = refs[2 * ranks : 2 * ranks + 5]
+    me = lax.axis_index("seq")
+    for step in range(ranks):
+        lanes = lanes_at(me ^ step)
+        for place, target in enumerate((mixed_ref, q_ref, k_ref, v_ref)):
+            target[0, :, lanes] = blocks[step][place * frames : (place + 1) * frames, :]
+        both = blocks[step][4 * frames :, :].astype(jnp.float32) + others[step][...].astype(jnp.float32)
+        taps_ref[:, lanes] = both[:KERNEL]
+
+
+def cost(flops, moved):
+    return pl.CostEstimate(flops=flops, bytes_accessed=moved, transcendentals=0)
+
+
+def on_device_heads(queries, keys, values, cotangent, conv_weight, rec_lengths):
+    ranks = lax.axis_size("seq")
+    frames = queries.shape[1]
+    length = ranks * frames
+    heads = LANES // HDIM
+    bf16, f32, i32 = jnp.bfloat16, jnp.float32, jnp.int32
+    struct = jax.ShapeDtypeStruct
+    hbm = pl.BlockSpec(memory_space=pl.ANY)
+    vmem = pl.BlockSpec(memory_space=VMEM)
+    smem = pl.BlockSpec(memory_space=pltpu.SMEM)
+    params = pltpu.CompilerParams(vmem_limit_bytes=24 * MIB)
+    taps = KERNEL + 1
+
+    sends = pl.pallas_call(
+        functools.partial(pack_kernel, ranks),
+        out_shape=[struct((3, frames, LANES), bf16)] * (ranks - 1)
+        + [struct((frames, LANES), bf16)] * (ranks - 1),
+        in_specs=[hbm] * 4,
+        out_specs=[hbm] * (2 * ranks - 2),
+        scratch_shapes=[pltpu.SemaphoreType.DMA((4 * (ranks - 1),))],
+        compiler_params=params,
+        name="pack",
+    )(queries, keys, values, cotangent)
+
+    def swap(array, step):
+        return lax.ppermute(array, "seq", [(rank, rank ^ step) for rank in range(ranks)])
+
+    order = list(range(ranks - 1, 0, -1))
+    received = {step: swap(sends[step - 1], step) for step in order}
+    cots = {step: swap(sends[ranks - 1 + step - 1], step) for step in order}
+
+    own, col, row, after, before = pl.pallas_call(
+        functools.partial(mask_kernel, length),
+        out_shape=[
+            struct((4, frames, LANES), bf16),
+            struct((length, LANES), i32),
+            struct((8, length), i32),
+            struct((length, LANES), i32),
+            struct((length, LANES), i32),
+        ],
+        in_specs=[smem] + [hbm] * 4,
+        out_specs=[vmem] * 5,
+        scratch_shapes=[pltpu.SemaphoreType.DMA((4,))],
+        compiler_params=params,
+        cost_estimate=cost(4 * MIB, MIB),
+        name="masks",
+    )(rec_lengths, queries, keys, values, cotangent)
+
+    soft, att, att_t, pre, q_heads, k_t, v_full = pl.pallas_call(
+        functools.partial(forward_kernel, ranks, frames),
+        out_shape=[
+            struct((heads, length, length), bf16),
+            struct((length + 2 * PAD, LANES), f32),
+            struct((LANES, length), f32),
+            struct((length, LANES), f32),
+            struct((heads, length, LANES), bf16),
+            struct((LANES, length), bf16),
+            struct((length, LANES), bf16),
+        ],
+        in_specs=[vmem] * (ranks + 4) + [hbm],
+        out_specs=[vmem] * 7,
+        scratch_shapes=[
+            VMEM((length, LANES), bf16),
+            VMEM((length, LANES), bf16),
+            VMEM((KERNEL, LANES), f32),
+            pltpu.SemaphoreType.DMA,
+        ],
+        compiler_params=params,
+        cost_estimate=cost(400 * MIB, 3 * MIB),
+        name="forward",
+    )(*[received[step] for step in range(1, ranks)], own, col, row, after, before, conv_weight)
+
+    *blocks, own_taps = pl.pallas_call(
+        functools.partial(backward_kernel, ranks, frames),
+        out_shape=[struct((4 * frames + taps, LANES), bf16)] * ranks + [struct((taps, LANES), bf16)],
+        in_specs=[vmem] * (ranks + 9) + [hbm],
+        out_specs=[vmem] * (ranks + 1),
+        scratch_shapes=[
+            VMEM((length, LANES), bf16),
+            VMEM((length + 2 * PAD, LANES), f32),
+            VMEM((length, LANES), bf16),
+            VMEM((length, LANES), bf16),
+            VMEM((LANES, length), f32),
+            VMEM((length, LANES), bf16),
+            VMEM((length, LANES), bf16),
+            VMEM((taps, 8, LANES), f32),
+            VMEM((KERNEL, LANES), f32),
+            pltpu.SemaphoreType.DMA,
+        ],
+        compiler_params=params,
+        cost_estimate=cost(800 * MIB, 3 * MIB),
+        name="backward",
+    )(
+        *[cots[step] for step in range(1, ranks)],
+        own,
+        soft,
+        att,
+        att_t,
+        pre,
+        q_heads,
+        k_t,
+        v_full,
+        after,
+        before,
+        conv_weight,
+    )
+
+    back = {step: swap(blocks[step], step) for step in order}
+    copies = lax.axis_size("dp")
+    others = {}
+    for step in range(ranks):
+        others[step] = own_taps
+        for shift in range(1, copies):
+            pairs = [
+                (one * ranks + rank, (one + shift) % copies * ranks + (rank ^ step))
+                for one in range(copies)
+                for rank in range(ranks)
+            ]
+            others[step] = lax.ppermute(own_taps, ("dp", "seq"), pairs)
+
+    mixed, grad_q, grad_k, grad_v, grad_taps = pl.pallas_call(
+        functools.partial(spread_kernel, ranks, frames),
+        out_shape=[struct(queries.shape, bf16)] * 4 + [struct(conv_weight.shape, f32)],
+        in_specs=[vmem] * (2 * ranks),
+        out_specs=[vmem] * 5,
+        compiler_params=params,
+        name="spread",
+    )(
+        blocks[0],
+        *[back[step] for step in range(1, ranks)],
+        *[others[step] for step in range(ranks)],
+    )
+    return (mixed, grad_q, grad_k, grad_v, grad_taps)
+
+
+def on_device_any(queries, keys, values, cotangent, conv_weight, rec_lengths):
+    ranks = lax.axis_size("seq")
+    frames, channels = queries.shape[1], queries.shape[2]
+    fits = channels == ranks * LANES and ranks & (ranks - 1) == 0 and frames % LANES == 0
+    if fits and ranks > 1 and ranks * frames <= 1024 and lax.axis_size("dp") == 2:
+        return on_device_heads(queries, keys, values, cotangent, conv_weight, rec_lengths)
+    return on_device(queries, keys, values, cotangent, conv_weight, rec_lengths)
+
+
 def solution(mesh):
     placed = (
         P(("groups", "dp"), "seq", "mp"),
@@ -236,7 +635,7 @@
         P(("groups", "dp"), None),
     )
     return jax.shard_map(
-        on_device,
+        on_device_any,
         mesh=mesh,
         in_specs=placed,
         out_specs=(

time: 172 us -> 48 us (0.28)
  blocking collectives: 125 us -> 0 us
  other arithmetic: 13.9 us -> 0 us
  starting transfers between devices: 12.3 us -> 24.3 us
  waiting for transfers between devices: 0.01 us -> 10 us
  matrix products: 9.3 us -> 0 us
  Pallas kernels: 0 us -> 9.1 us
  local copies, waits for them, and re-layouts: 9.52 us -> 3.62 us
    all_gather x6 -> x0, blocking collectives: 90.3 us -> none  [the longest x1 17.6 us: on_device(): lax.all_gather(values, 'seq', axis=1, tiled=True)]
    psum x1 -> x0, blocking collectives: 34.8 us -> none  [on_device(): grad_kernel = lax.psum(jnp.stack(kernel_rows), ('dp', 'seq'))]
    ppermute x4 -> x13, starting transfers between devices: 12.3 us -> 24.3 us  [the longest x9 15.7 us: swap(): lax.ppermute(array, 'seq', [(rank, rank ^ step) for rank in range(ranks)])]
    ppermute x4 -> x13, waiting for transfers between devices: 0.01 us -> 10 us  [the longest x4 7.17 us: on_device_heads(): others[step] = lax.ppermute(own_taps, ('dp', 'seq'), pairs)]
    dot_general x6 -> x0, matrix products: 9.3 us -> none  [the longest x1 3.04 us: key_grad_step(): jnp.einsum('hqd,hkd->hqk', query_block, k_heads, preferred_element_type=j...]
    pallas_call x0 -> x5, Pallas kernels: none -> 9.1 us  [the longest x1 3.41 us: on_device_heads(): pl.pallas_call(functools.partial(forward_kernel, ranks, frames), out_shap...]
    reduce_sum x9 -> x0, other arithmetic: 6.58 us -> none  [the longest x4 5.63 us: on_device(): kernel_rows.append(jnp.sum(jnp.where(tap_mask, product, 0.0), axis=0))]
    convert_element_type x3 -> x0, other arithmetic: 3.49 us -> none  [the longest x1 2.67 us: on_device(): grad_attended = grad_attended.astype(jnp.bfloat16)]
  transfers between devices with their start and end apart: 4 -> 13, of which waited for: 0 -> 4; matrix products, arithmetic and copies ran while one was open for 6% -> 0% of each run, Pallas kernels for 0% -> 10%
where the time goes in v1:
time: 48 us; the launch traced here: 47.8 us
  starting transfers between devices  24.3 us (51%)
  waiting for transfers between devices  10 us (21%)
  Pallas kernels  9.1 us (19%)
  local copies, waits for them, and re-layouts  3.62 us (8%)
  between operations  0.72 us (2%)
    ppermute x9, starting transfers between devices, swap(): lax.ppermute(array, 'seq', [(rank, rank ^ step) for rank in range(ranks)])  15.7 us
    ppermute x4, starting transfers between devices, on_device_heads(): others[step] = lax.ppermute(own_taps, ('dp', 'seq'), pairs)  8.66 us
    ppermute x4, waiting for transfers between devices, on_device_heads(): others[step] = lax.ppermute(own_taps, ('dp', 'seq'), pairs)  7.17 us
    unnamed x12, local copies, waits for them, and re-layouts  3.62 us
    pallas_call x1, Pallas kernels, on_device_heads(): pl.pallas_call(functools.partial(forward_kernel, ranks, frames), out_shap...  3.41 us
    pallas_call x1, Pallas kernels, on_device_heads(): pl.pallas_call(functools.partial(backward_kernel, ranks, frames), out_sha...  3.3 us
    ppermute x9, waiting for transfers between devices, swap(): lax.ppermute(array, 'seq', [(rank, rank ^ step) for rank in range(ranks)])  2.83 us
    pallas_call x1, Pallas kernels, on_device_heads(): pl.pallas_call(functools.partial(mask_kernel, length), out_shape=[struct(...  1.27 us
  transfers between devices with their start and end apart: 13, of which 4 were waited for; matrix products, arithmetic and copies ran while one was open for 0% of the time, Pallas kernels for 10%

profile of v1, /device:TPU:0, one launch (start us, length us, event | category | flops | bytes accessed | tf_op | source)
XLA Modules:
  0.0 47.8 jit_solution(13009748020908106699)
XLA Ops:
  0.6 0.0 copy-start
  0.6 0.9 %copy-done = bf16[1,128,512]{2,1,0:T(8,128)(2,1)S(1)} copy-done((bf16[1,128,512]{2,1,0:T(8,128)(2,1)S(1)}, bf16[1,128,512]{2,1,0:T(8,128)(2,1)}, u32[]{:S(2)}) %copy-start) | copy-done | bytes 131096
  1.5 0.0 copy-start.1
  1.5 0.9 %copy-done.1 = bf16[1,128,512]{2,1,0:T(8,128)(2,1)S(1)} copy-done((bf16[1,128,512]{2,1,0:T(8,128)(2,1)S(1)}, bf16[1,128,512]{2,1,0:T(8,128)(2,1)}, u32[]{:S(2)}) %copy-start.1) | copy-done | bytes 131096
  2.4 0.0 copy-start.2
  2.4 0.9 %copy-done.2 = bf16[1,128,512]{2,1,0:T(8,128)(2,1)S(1)} copy-done((bf16[1,128,512]{2,1,0:T(8,128)(2,1)S(1)}, bf16[1,128,512]{2,1,0:T(8,128)(2,1)}, u32[]{:S(2)}) %copy-start.2) | copy-done | bytes 131096
  3.3 0.0 copy-start.3
  3.3 0.9 %copy-done.3 = bf16[1,128,512]{2,1,0:T(8,128)(2,1)S(1)} copy-done((bf16[1,128,512]{2,1,0:T(8,128)(2,1)S(1)}, bf16[1,128,512]{2,1,0:T(8,128)(2,1)}, u32[]{:S(2)}) %copy-start.3) | copy-done | bytes 131096
  4.3 0.2 pack.1
  4.5 3.1 %collective-permute-start.3 = (bf16[3,128,128]{2,1,0:T(8,128)(2,1)S(1)}, bf16[3,128,128]{2,1,0:T(8,128)(2,1)S(1)}, u32[]{:S(2)}, u32[]{:S(2)}) collective-permute-start(bf16[3,128,128]{2,1,0:T(8,128)(2,1)S(1)} %get-tuple-element.32), channel_id=1, source_target_pairs={{0,2},{2,0},{4,6},{6,4},{1,3},{3,1},{5,7},{7,5},{8,10},{10,8},{12,... | collective-permute-start | bytes 294920 | tf_op jit(solution)/shard_map/ppermute | solution.py:509
  7.6 2.6 %collective-permute-start.4 = (bf16[3,128,128]{2,1,0:T(8,128)(2,1)S(1)}, bf16[3,128,128]{2,1,0:T(8,128)(2,1)S(1)}, u32[]{:S(2)}, u32[]{:S(2)}) collective-permute-start(bf16[3,128,128]{2,1,0:T(8,128)(2,1)S(1)} %get-tuple-element.33), channel_id=1, source_target_pairs={{0,4},{2,6},{4,0},{6,2},{1,5},{3,7},{5,1},{7,3},{8,12},{10,14},{12... | collective-permute-start | bytes 294920 | tf_op jit(solution)/shard_map/ppermute | solution.py:509
  10.1 0.0 collective-permute-start.5
  10.2 0.0 copy-start.5
  10.2 0.9 %collective-permute-start = (bf16[128,128]{1,0:T(8,128)(2,1)S(1)}, bf16[128,128]{1,0:T(8,128)(2,1)S(1)}, u32[]{:S(2)}, u32[]{:S(2)}) collective-permute-start(bf16[128,128]{1,0:T(8,128)(2,1)S(1)} %get-tuple-element.28), channel_id=1, source_target_pairs={{0,2},{2,0},{4,6},{6,4},{1,3},{3,1},{5,7},{7,5},{8,10},{10,8},{12,... | collective-permute-start | bytes 98312 | tf_op jit(solution)/shard_map/ppermute | solution.py:509
  11.0 0.0 copy-start.4
  11.1 3.5 %collective-permute-start.1 = (bf16[128,128]{1,0:T(8,128)(2,1)S(1)}, bf16[128,128]{1,0:T(8,128)(2,1)S(1)}, u32[]{:S(2)}, u32[]{:S(2)}) collective-permute-start(bf16[128,128]{1,0:T(8,128)(2,1)S(1)} %get-tuple-element.29), channel_id=1, source_target_pairs={{0,4},{2,6},{4,0},{6,2},{1,5},{3,7},{5,1},{7,3},{8,12},{10,14},{12... | collective-permute-start | bytes 98312 | tf_op jit(solution)/shard_map/ppermute | solution.py:509
  14.5 0.0 copy-done.5
  14.5 1.3 %masks.1 = (bf16[4,128,128]{2,1,0:T(8,128)(2,1)S(1)}, s32[512,128]{1,0:T(8,128)S(1)}, s32[8,512]{1,0:T(8,128)S(1)}, s32[512,128]{1,0:T(8,128)S(1)}, s32[512,128]{1,0:T(8,128)S(1)}) custom-call(s32[1,16]{1,0:T(1,128)S(1)} %copy-done.5, bf16[1,128,512]{2,1,0:T(8,128)(2,1)S(1)} %copy-done, bf16[1,128,512]{2,1,0:T(8,128)(2,1)S(1)} %copy-done.1, ...), custom_call_target="tpu_custom_call" | custom-call | flops 4194304 | bytes 1048576 | tf_op jit(solution)/shard_map/masks/pallas_call | solution.py:515
  15.8 0.0 collective-permute-done.3.refs_0_
  15.8 0.1 collective-permute-start.2
  16.0 2.8 %collective-permute-done.4.refs_1_ = bf16[3,128,128]{2,1,0:T(8,128)(2,1)S(1)} collective-permute-done((bf16[3,128,128]{2,1,0:T(8,128)(2,1)S(1)}, bf16[3,128,128]{2,1,0:T(8,128)(2,1)S(1)}, u32[]{:S(2)}, u32[]{:S(2)}) %collective-permute-start.4) | collective-permute-done | bytes 98336 | tf_op jit(solution)/shard_map/ppermute | solution.py:509
  18.8 0.0 collective-permute-done.5.refs_2_
  18.8 0.0 copy-done.4
  18.8 3.4 %forward.1 = (bf16[2,512,512]{2,1,0:T(8,128)(2,1)S(1)}, f32[544,128]{1,0:T(8,128)S(1)}, f32[128,512]{1,0:T(8,128)S(1)}, f32[512,128]{1,0:T(8,128)S(1)}, bf16[2,5...) custom-call(bf16[3,128,128]{2,1,0:T(8,128)(2,1)S(1)} %collective-permute-done.3.refs_0_, ...), custom_call_target="tpu_custom_call" | custom-call | flops 419430400 | bytes 3145728 | tf_op jit(solution)/shard_map/forward/pallas_call | solution.py:532
  22.2 0.0 collective-permute-done.refs_0_
  22.2 0.0 collective-permute-done.1.refs_1_
  22.2 0.0 collective-permute-done.2.refs_2_
  22.2 3.3 %backward.1 = (bf16[544,128]{1,0:T(8,128)(2,1)S(1)}, bf16[544,128]{1,0:T(8,128)(2,1)S(1)}, bf16[544,128]{1,0:T(8,128)(2,1)S(1)}, bf16[544,128]{1,0:T(8,128)(2,1)S(1)}, bf16[32,128]{1,0:T(8,128)(2,1)S(1)}) custom-call(bf16[128,128]{1,0:T(8,128)(2,1)S(1)} %collective-permute-done.refs_0_, bf16[128,128]{1,0:T(8,128)(2,1)S(1)} %collective-permute-done.1.refs_1_, ...), custom_call_target="tpu_custom_call" | custom-call | flops 838860800 | bytes 3145728 | tf_op jit(solution)/shard_map/backward/pallas_call | solution.py:556
  25.6 2.6 %collective-permute-start.6 = (bf16[544,128]{1,0:T(8,128)(2,1)S(1)}, bf16[544,128]{1,0:T(8,128)(2,1)S(1)}, u32[]{:S(2)}, u32[]{:S(2)}) collective-permute-start(bf16[544,128]{1,0:T(8,128)(2,1)S(1)} %get-tuple-element.47), channel_id=1, source_target_pairs={{0,2},{2,0},{4,6},{6,4},{1,3},{3,1},{5,7},{7,5},{8,10},{10,8},{12,... | collective-permute-start | bytes 417800 | tf_op jit(solution)/shard_map/ppermute | solution.py:509
  28.2 1.4 %collective-permute-start.7 = (bf16[544,128]{1,0:T(8,128)(2,1)S(1)}, bf16[544,128]{1,0:T(8,128)(2,1)S(1)}, u32[]{:S(2)}, u32[]{:S(2)}) collective-permute-start(bf16[544,128]{1,0:T(8,128)(2,1)S(1)} %get-tuple-element.48), channel_id=1, source_target_pairs={{0,4},{2,6},{4,0},{6,2},{1,5},{3,7},{5,1},{7,3},{8,12},{10,14},{12... | collective-permute-start | bytes 417800 | tf_op jit(solution)/shard_map/ppermute | solution.py:509
  29.6 1.4 %collective-permute-start.8 = (bf16[544,128]{1,0:T(8,128)(2,1)S(1)}, bf16[544,128]{1,0:T(8,128)(2,1)S(1)}, u32[]{:S(2)}, u32[]{:S(2)}) collective-permute-start(bf16[544,128]{1,0:T(8,128)(2,1)S(1)} %get-tuple-element.49), channel_id=1, source_target_pairs={{0,6},{2,4},{4,2},{6,0},{1,7},{3,5},{5,3},{7,1},{8,14},{10,12},{12... | collective-permute-start | bytes 417800 | tf_op jit(solution)/shard_map/ppermute | solution.py:509
  31.0 3.4 %collective-permute-start.12 = (bf16[32,128]{1,0:T(8,128)(2,1)S(1)}, bf16[32,128]{1,0:T(8,128)(2,1)S(1)}, u32[]{:S(2)}, u32[]{:S(2)}) collective-permute-start(bf16[32,128]{1,0:T(8,128)(2,1)S(1)} %get-tuple-element.50), channel_id=1, source_target_pairs={{0,14},{2,12},{4,10},{6,8},{8,6},{10,4},{12,2},{14,0},{1,15},{3,13... | collective-permute-start | bytes 24584 | tf_op jit(solution)/shard_map/ppermute | solution.py:602
  34.4 0.0 collective-permute-start.11
  34.4 5.0 %collective-permute-done.12.refs_7_ = bf16[32,128]{1,0:T(8,128)(2,1)S(1)} collective-permute-done((bf16[32,128]{1,0:T(8,128)(2,1)S(1)}, bf16[32,128]{1,0:T(8,128)(2,1)S(1)}, u32[]{:S(2)}, u32[]{:S(2)}) %collective-permute-start.12) | collective-permute-done | bytes 8224 | tf_op jit(solution)/shard_map/ppermute | solution.py:602
  39.4 3.8 %collective-permute-start.10 = (bf16[32,128]{1,0:T(8,128)(2,1)S(1)}, bf16[32,128]{1,0:T(8,128)(2,1)S(1)}, u32[]{:S(2)}, u32[]{:S(2)}) collective-permute-start(bf16[32,128]{1,0:T(8,128)(2,1)S(1)} %get-tuple-element.50), channel_id=1, source_target_pairs={{0,10},{2,8},{4,14},{6,12},{8,2},{10,0},{12,6},{14,4},{1,11},{3,9}... | collective-permute-start | bytes 24584 | tf_op jit(solution)/shard_map/ppermute | solution.py:602
  43.2 0.0 collective-permute-done.11.refs_6_
  43.2 1.5 %collective-permute-start.9 = (bf16[32,128]{1,0:T(8,128)(2,1)S(1)}, bf16[32,128]{1,0:T(8,128)(2,1)S(1)}, u32[]{:S(2)}, u32[]{:S(2)}) collective-permute-start(bf16[32,128]{1,0:T(8,128)(2,1)S(1)} %get-tuple-element.50), channel_id=1, source_target_pairs={{0,8},{2,10},{4,12},{6,14},{8,0},{10,2},{12,4},{14,6},{1,9},{3,11}... | collective-permute-start | bytes 24584 | tf_op jit(solution)/shard_map/ppermute | solution.py:602
  44.7 0.1 collective-permute-done.10.refs_5_
  44.8 2.0 %collective-permute-done.9.refs_4_ = bf16[32,128]{1,0:T(8,128)(2,1)S(1)} collective-permute-done((bf16[32,128]{1,0:T(8,128)(2,1)S(1)}, bf16[32,128]{1,0:T(8,128)(2,1)S(1)}, u32[]{:S(2)}, u32[]{:S(2)}) %collective-permute-start.9) | collective-permute-done | bytes 8224 | tf_op jit(solution)/shard_map/ppermute | solution.py:602
  46.9 0.0 collective-permute-done.6.refs_1_
  46.9 0.0 collective-permute-done.7.refs_2_
  46.9 0.0 collective-permute-done.8.refs_3_
  46.9 0.9 %spread.1 = (bf16[1,128,512]{2,1,0:T(8,128)(2,1)}, bf16[1,128,512]{2,1,0:T(8,128)(2,1)}, bf16[1,128,512]{2,1,0:T(8,128)(2,1)}, bf16[1,128,512]{2,1,0:T(8,128)(2,1)}, f32[31,512]{1,0:T(8,128)}) custom-call(bf16[544,128]{1,0:T(8,128)(2,1)S(1)} %get-tuple-element.46.refs_0_, bf16[544,128]{1,0:T(8,128)(2,1)S(1)} %collective-permute-done.6.refs_1_, ...), custom_call_target="tpu_custom_call" | custom-call | tf_op jit(solution)/shard_map/spread/pallas_call | solution.py:604
Async XLA Ops:
  0.6 0.9 %copy-start = (bf16[1,128,512]{2,1,0:T(8,128)(2,1)S(1)}, bf16[1,128,512]{2,1,0:T(8,128)(2,1)}, u32[]{:S(2)}) copy-start(bf16[1,128,512]{2,1,0:T(8,128)(2,1)} %q_ref.3) | copy-start | bytes 393220
  1.5 0.9 %copy-start.1 = (bf16[1,128,512]{2,1,0:T(8,128)(2,1)S(1)}, bf16[1,128,512]{2,1,0:T(8,128)(2,1)}, u32[]{:S(2)}) copy-start(bf16[1,128,512]{2,1,0:T(8,128)(2,1)} %k_ref.3) | copy-start | bytes 393220
  2.4 0.9 %copy-start.2 = (bf16[1,128,512]{2,1,0:T(8,128)(2,1)S(1)}, bf16[1,128,512]{2,1,0:T(8,128)(2,1)}, u32[]{:S(2)}) copy-start(bf16[1,128,512]{2,1,0:T(8,128)(2,1)} %v_ref.3) | copy-start | bytes 393220
  3.3 0.9 %copy-start.3 = (bf16[1,128,512]{2,1,0:T(8,128)(2,1)S(1)}, bf16[1,128,512]{2,1,0:T(8,128)(2,1)}, u32[]{:S(2)}) copy-start(bf16[1,128,512]{2,1,0:T(8,128)(2,1)} %c_ref.3) | copy-start | bytes 393220
  4.5 11.4 %collective-permute-start.3 = (bf16[3,128,128]{2,1,0:T(8,128)(2,1)S(1)}, bf16[3,128,128]{2,1,0:T(8,128)(2,1)S(1)}, u32[]{:S(2)}, u32[]{:S(2)}) collective-permute-start(bf16[3,128,128]{2,1,0:T(8,128)(2,1)S(1)} %get-tuple-element.32), channel_id=1, source_target_pairs={{0,2},{2,0},{4,6},{6,4},{1,3},{3,1},{5,7},{7,5},{8,10},{10,8},{12,... | collective-permute-start | bytes 294920 | tf_op jit(solution)/shard_map/ppermute | solution.py:509
  7.6 11.2 %collective-permute-start.4 = (bf16[3,128,128]{2,1,0:T(8,128)(2,1)S(1)}, bf16[3,128,128]{2,1,0:T(8,128)(2,1)S(1)}, u32[]{:S(2)}, u32[]{:S(2)}) collective-permute-start(bf16[3,128,128]{2,1,0:T(8,128)(2,1)S(1)} %get-tuple-element.33), channel_id=1, source_target_pairs={{0,4},{2,6},{4,0},{6,2},{1,5},{3,7},{5,1},{7,3},{8,12},{10,14},{12... | collective-permute-start | bytes 294920 | tf_op jit(solution)/shard_map/ppermute | solution.py:509
  10.1 8.6 %collective-permute-start.5 = (bf16[3,128,128]{2,1,0:T(8,128)(2,1)S(1)}, bf16[3,128,128]{2,1,0:T(8,128)(2,1)S(1)}, u32[]{:S(2)}, u32[]{:S(2)}) collective-permute-start(bf16[3,128,128]{2,1,0:T(8,128)(2,1)S(1)} %get-tuple-element.34), channel_id=1, source_target_pairs={{0,6},{2,4},{4,2},{6,0},{1,7},{3,5},{5,3},{7,1},{8,14},{10,12},{12... | collective-permute-start | bytes 294920 | tf_op jit(solution)/shard_map/ppermute | solution.py:509
  10.2 4.4 %copy-start.5 = (s32[1,16]{1,0:T(1,128)S(1)}, s32[1,16]{1,0:T(1,128)}, u32[]{:S(2)}) copy-start(s32[1,16]{1,0:T(1,128)} %lens_ref.1) | copy-start | bytes 196
  10.2 12.1 %collective-permute-start = (bf16[128,128]{1,0:T(8,128)(2,1)S(1)}, bf16[128,128]{1,0:T(8,128)(2,1)S(1)}, u32[]{:S(2)}, u32[]{:S(2)}) collective-permute-start(bf16[128,128]{1,0:T(8,128)(2,1)S(1)} %get-tuple-element.28), channel_id=1, source_target_pairs={{0,2},{2,0},{4,6},{6,4},{1,3},{3,1},{5,7},{7,5},{8,10},{10,8},{12,... | collective-permute-start | bytes 98312 | tf_op jit(solution)/shard_map/ppermute | solution.py:509
  11.0 7.7 %copy-start.4 = (f32[31,512]{1,0:T(8,128)S(1)}, f32[31,512]{1,0:T(8,128)}, u32[]{:S(2)}) copy-start(f32[31,512]{1,0:T(8,128)} %refs_13_.1) | copy-start | bytes 190468
  11.1 11.2 %collective-permute-start.1 = (bf16[128,128]{1,0:T(8,128)(2,1)S(1)}, bf16[128,128]{1,0:T(8,128)(2,1)S(1)}, u32[]{:S(2)}, u32[]{:S(2)}) collective-permute-start(bf16[128,128]{1,0:T(8,128)(2,1)S(1)} %get-tuple-element.29), channel_id=1, source_target_pairs={{0,4},{2,6},{4,0},{6,2},{1,5},{3,7},{5,1},{7,3},{8,12},{10,14},{12... | collective-permute-start | bytes 98312 | tf_op jit(solution)/shard_map/ppermute | solution.py:509
  15.8 6.4 %collective-permute-start.2 = (bf16[128,128]{1,0:T(8,128)(2,1)S(1)}, bf16[128,128]{1,0:T(8,128)(2,1)S(1)}, u32[]{:S(2)}, u32[]{:S(2)}) collective-permute-start(bf16[128,128]{1,0:T(8,128)(2,1)S(1)} %get-tuple-element.30), channel_id=1, source_target_pairs={{0,6},{2,4},{4,2},{6,0},{1,7},{3,5},{5,3},{7,1},{8,14},{10,12},{12... | collective-permute-start | bytes 98312 | tf_op jit(solution)/shard_map/ppermute | solution.py:509
  25.6 21.3 %collective-permute-start.6 = (bf16[544,128]{1,0:T(8,128)(2,1)S(1)}, bf16[544,128]{1,0:T(8,128)(2,1)S(1)}, u32[]{:S(2)}, u32[]{:S(2)}) collective-permute-start(bf16[544,128]{1,0:T(8,128)(2,1)S(1)} %get-tuple-element.47), channel_id=1, source_target_pairs={{0,2},{2,0},{4,6},{6,4},{1,3},{3,1},{5,7},{7,5},{8,10},{10,8},{12,... | collective-permute-start | bytes 417800 | tf_op jit(solution)/shard_map/ppermute | solution.py:509
  28.2 18.7 %collective-permute-start.7 = (bf16[544,128]{1,0:T(8,128)(2,1)S(1)}, bf16[544,128]{1,0:T(8,128)(2,1)S(1)}, u32[]{:S(2)}, u32[]{:S(2)}) collective-permute-start(bf16[544,128]{1,0:T(8,128)(2,1)S(1)} %get-tuple-element.48), channel_id=1, source_target_pairs={{0,4},{2,6},{4,0},{6,2},{1,5},{3,7},{5,1},{7,3},{8,12},{10,14},{12... | collective-permute-start | bytes 417800 | tf_op jit(solution)/shard_map/ppermute | solution.py:509
  29.6 17.2 %collective-permute-start.8 = (bf16[544,128]{1,0:T(8,128)(2,1)S(1)}, bf16[544,128]{1,0:T(8,128)(2,1)S(1)}, u32[]{:S(2)}, u32[]{:S(2)}) collective-permute-start(bf16[544,128]{1,0:T(8,128)(2,1)S(1)} %get-tuple-element.49), channel_id=1, source_target_pairs={{0,6},{2,4},{4,2},{6,0},{1,7},{3,5},{5,3},{7,1},{8,14},{10,12},{12... | collective-permute-start | bytes 417800 | tf_op jit(solution)/shard_map/ppermute | solution.py:509
  31.0 8.4 %collective-permute-start.12 = (bf16[32,128]{1,0:T(8,128)(2,1)S(1)}, bf16[32,128]{1,0:T(8,128)(2,1)S(1)}, u32[]{:S(2)}, u32[]{:S(2)}) collective-permute-start(bf16[32,128]{1,0:T(8,128)(2,1)S(1)} %get-tuple-element.50), channel_id=1, source_target_pairs={{0,14},{2,12},{4,10},{6,8},{8,6},{10,4},{12,2},{14,0},{1,15},{3,13... | collective-permute-start | bytes 24584 | tf_op jit(solution)/shard_map/ppermute | solution.py:602
  34.4 8.8 %collective-permute-start.11 = (bf16[32,128]{1,0:T(8,128)(2,1)S(1)}, bf16[32,128]{1,0:T(8,128)(2,1)S(1)}, u32[]{:S(2)}, u32[]{:S(2)}) collective-permute-start(bf16[32,128]{1,0:T(8,128)(2,1)S(1)} %get-tuple-element.50), channel_id=1, source_target_pairs={{0,12},{2,14},{4,8},{6,10},{8,4},{10,6},{12,0},{14,2},{1,13},{3,15... | collective-permute-start | bytes 24584 | tf_op jit(solution)/shard_map/ppermute | solution.py:602
  39.4 5.4 %collective-permute-start.10 = (bf16[32,128]{1,0:T(8,128)(2,1)S(1)}, bf16[32,128]{1,0:T(8,128)(2,1)S(1)}, u32[]{:S(2)}, u32[]{:S(2)}) collective-permute-start(bf16[32,128]{1,0:T(8,128)(2,1)S(1)} %get-tuple-element.50), channel_id=1, source_target_pairs={{0,10},{2,8},{4,14},{6,12},{8,2},{10,0},{12,6},{14,4},{1,11},{3,9}... | collective-permute-start | bytes 24584 | tf_op jit(solution)/shard_map/ppermute | solution.py:602
  43.2 3.7 %collective-permute-start.9 = (bf16[32,128]{1,0:T(8,128)(2,1)S(1)}, bf16[32,128]{1,0:T(8,128)(2,1)S(1)}, u32[]{:S(2)}, u32[]{:S(2)}) collective-permute-start(bf16[32,128]{1,0:T(8,128)(2,1)S(1)} %get-tuple-element.50), channel_id=1, source_target_pairs={{0,8},{2,10},{4,12},{6,14},{8,0},{10,2},{12,4},{14,6},{1,9},{3,11}... | collective-permute-start | bytes 24584 | tf_op jit(solution)/shard_map/ppermute | solution.py:602

commit v2 on v1

--- a/solution.py
+++ b/solution.py
@@ -255,75 +255,75 @@
     return pl.ds(pl.multiple_of(block * LANES, LANES), LANES)
 
 
-def pack_kernel(ranks, q_ref, k_ref, v_ref, c_ref, *rest):
+def pack_kernel(ranks, q_ref, k_ref, v_ref, *rest):
     outs, sems = rest[:-1], rest[-1]
     me = lax.axis_index("seq")
     copies = []
-    for step in range(1, ranks):
-        lanes = lanes_at(me ^ step)
-        three, one = outs[step - 1], outs[ranks - 1 + step - 1]
+    for step in range(ranks - 1, 0, -1):
         for place, source in enumerate((q_ref, k_ref, v_ref)):
-            copies.append((source.at[0, :, lanes], three.at[place]))
-        copies.append((c_ref.at[0, :, lanes], one))
+            copies.append((source.at[0, :, lanes_at(me ^ step)], outs[step - 1].at[place]))
+    run_copies(copies, sems)
+
+
+def run_copies(pairs, sems, meanwhile=None):
     copies = [
         pltpu.make_async_copy(source, target, sems.at[number])
-        for number, (source, target) in enumerate(copies)
+        for number, (source, target) in enumerate(pairs)
     ]
     for copy in copies:
         copy.start()
+    if meanwhile is not None:
+        meanwhile()
     for copy in copies:
         copy.wait()
 
 
-def mask_kernel(length, lens_ref, q_ref, k_ref, v_ref, c_ref, own_ref, col_ref, row_ref, after_ref, before_ref, sems):
+def mask_kernel(ranks, length, lens_ref, q_ref, k_ref, v_ref, c_ref, *refs):
+    cot_refs = refs[: ranks - 1]
+    own_ref, col_ref, row_ref, after_ref, before_ref, sems = refs[ranks - 1 :]
     me = lax.axis_index("seq")
-    lanes = lanes_at(me)
-    copies = [
-        pltpu.make_async_copy(source.at[0, :, lanes], own_ref.at[place], sems.at[place])
-        for place, source in enumerate((q_ref, k_ref, v_ref, c_ref))
-    ]
-    for copy in copies:
-        copy.start()
-    count = lens_ref.shape[1]
-    ends = []
-    running = jnp.int32(0)
-    for number in range(count):
-        running = running + lens_ref[0, number]
-        ends.append(running)
-
-    row_time = lax.broadcasted_iota(jnp.int32, row_ref.shape, 1)
-    row_first = jnp.zeros(row_ref.shape, jnp.int32)
-    for end in ends:
-        row_first = jnp.where(row_time >= end, end, row_first)
-    row_ref[...] = row_first
-
-    chunk = 64
-
-    def some_rows(number, carry):
-        base = pl.multiple_of(number * chunk, chunk)
-        time = base + lax.broadcasted_iota(jnp.int32, (chunk, LANES), 0)
-        first = jnp.zeros((chunk, LANES), jnp.int32)
-        last = jnp.full((chunk, LANES), length, jnp.int32)
+    pairs = [(c_ref.at[0, :, lanes_at(me ^ step)], cot_refs[step - 1]) for step in range(1, ranks)]
+    for place, source in enumerate((q_ref, k_ref, v_ref, c_ref)):
+        pairs.append((source.at[0, :, lanes_at(me)], own_ref.at[place]))
+
+    def extents():
+        ends = []
+        running = jnp.int32(0)
+        for number in range(lens_ref.shape[1]):
+            running = running + lens_ref[0, number]
+            ends.append(running)
+        row_time = lax.broadcasted_iota(jnp.int32, row_ref.shape, 1)
+        row_first = jnp.zeros(row_ref.shape, jnp.int32)
         for end in ends:
-            first = jnp.where(time >= end, end, first)
-        for end in reversed(ends):
-            last = jnp.where(time < end, end, last)
-        rows = pl.ds(base, chunk)
-        col_ref[rows, :] = first
-        after_ref[rows, :] = last - 1 - time
-        before_ref[rows, :] = time - first
-        return carry
-
-    lax.fori_loop(0, length // chunk, some_rows, 0)
-    for copy in copies:
-        copy.wait()
+            row_first = jnp.where(row_time >= end, end, row_first)
+        row_ref[...] = row_first
+        chunk = 64
+
+        def some_rows(number, carry):
+            base = pl.multiple_of(number * chunk, chunk)
+            time = base + lax.broadcasted_iota(jnp.int32, (chunk, LANES), 0)
+            first = jnp.zeros((chunk, LANES), jnp.int32)
+            last = jnp.full((chunk, LANES), length, jnp.int32)
+            for end in ends:
+                first = jnp.where(time >= end, end, first)
+            for end in reversed(ends):
+                last = jnp.where(time < end, end, last)
+            rows = pl.ds(base, chunk)
+            col_ref[rows, :] = first
+            after_ref[rows, :] = last - 1 - time
+            before_ref[rows, :] = time - first
+            return carry
+
+        lax.fori_loop(0, length // chunk, some_rows, 0)
+
+    run_copies(pairs, sems, extents)
 
 
 def forward_kernel(ranks, frames, *refs):
     recvs = refs[: ranks - 1]
     own_ref, col_ref, row_ref, after_ref, before_ref, w_ref = refs[ranks - 1 : ranks + 5]
-    soft_ref, att_ref, att_t_ref, pre_ref, q_ref, k_t_ref, v_ref = refs[ranks + 5 : ranks + 12]
-    k_full, q_full, w_own, w_sem = refs[ranks + 12 :]
+    soft_ref, att_ref, pre_ref, q_ref, k_t_ref, v_ref = refs[ranks + 5 : ranks + 11]
+    att_t_ref, k_full, q_full, w_own, w_sem = refs[ranks + 11 :]
     me = lax.axis_index("seq")
     length = ranks * frames
     copy = pltpu.make_async_copy(w_ref.at[:, lanes_at(me)], w_own, w_sem)
@@ -331,7 +331,7 @@
     for place, target in enumerate((q_full, k_full, v_ref)):
         target[rows_at(me, frames), :] = own_ref[place]
         for step in range(1, ranks):
-            target[rows_at(me ^ step, frames), :] = recvs[step - 1][place]
+            target[rows_at(me ^ step, frames), :] = recvs[ranks - 1 - step][place]
     heads = LANES // HDIM
     lane_head = lax.broadcasted_iota(jnp.int32, (1, LANES), 1) // HDIM
     scaled = q_full[...].astype(jnp.float32) * (1.0 / math.sqrt(HDIM))
@@ -380,27 +380,23 @@
     lax.fori_loop(0, length // chunk, some_rows, 0)
 
 
-def backward_kernel(ranks, frames, *refs):
+def conv_back_kernel(ranks, frames, *refs):
     cots = refs[: ranks - 1]
-    own_ref, soft_ref, att_ref, att_t_ref, pre_ref, q_ref, k_t_ref, v_ref, after_ref, before_ref, w_ref = refs[
-        ranks - 1 : ranks + 10
-    ]
-    outs = refs[ranks + 10 : 2 * ranks + 10]
-    taps_ref = refs[2 * ranks + 10]
-    cot, grad_pad, mixed, g_att, res_q, res_k, res_v, tap_sum, w_own, w_sem = refs[2 * ranks + 11 :]
+    own_ref, att_ref, pre_ref, after_ref, before_ref, w_ref = refs[ranks - 1 : ranks + 5]
+    mixed_ref, g_att, taps_ref, cot, grad_pad, tap_sum, w_own, w_sem = refs[ranks + 5 :]
     me = lax.axis_index("seq")
     length = ranks * frames
     copy = pltpu.make_async_copy(w_ref.at[:, lanes_at(me)], w_own, w_sem)
     copy.start()
     cot[rows_at(me, frames), :] = own_ref[3]
     for step in range(1, ranks):
-        cot[rows_at(me ^ step, frames), :] = cots[step - 1][...]
+        cot[rows_at(me ^ step, frames), :] = cots[ranks - 1 - step][...]
     zeros = jnp.zeros((PAD, LANES), jnp.float32)
     grad_pad[0:PAD, :] = zeros
     grad_pad[PAD + length :, :] = zeros
     pre = pre_ref[...]
     gate = jax.nn.sigmoid(pre)
-    mixed[...] = (pre * gate).astype(jnp.bfloat16)
+    mixed_ref[...] = (pre * gate).astype(jnp.bfloat16)
     conv_grad = cot[...].astype(jnp.float32) * gate * (1.0 + pre * (1.0 - gate))
     grad_pad[PAD : PAD + length, :] = conv_grad.astype(jnp.bfloat16).astype(jnp.float32)
     tap_sum[...] = jnp.zeros(tap_sum.shape, jnp.float32)
@@ -428,9 +424,11 @@
         return carry
 
     lax.fori_loop(0, length // chunk, some_rows, 0)
-    taps = jnp.sum(tap_sum[...], axis=1).astype(jnp.bfloat16)
-    taps_ref[...] = taps
-
+    taps_ref[...] = jnp.sum(tap_sum[...], axis=1)
+
+
+def backward_kernel(soft_ref, att_ref, g_att, q_ref, k_t_ref, v_ref, res_q, res_k, res_v, grad_t):
+    length = v_ref.shape[0]
     heads = LANES // HDIM
     lane_head = lax.broadcasted_iota(jnp.int32, (1, LANES), 1) // HDIM
     g_wide = g_att[...].astype(jnp.float32)
@@ -449,32 +447,43 @@
             mixed_grad = (soft.astype(jnp.float32) * (slopes - delta[:, cols])).astype(jnp.bfloat16)
             grad_v = grad_v + mm(soft, g_heads[head][cols])
             grad_k = grad_k + mm(mixed_grad, q_ref[head, cols, :])
-            res_q[rows, cols] = mm(k_t_ref[rows, :], mixed_grad) * (1.0 / math.sqrt(HDIM))
+            grad_t[rows, cols] = mm(k_t_ref[rows, :], mixed_grad) * (1.0 / math.sqrt(HDIM))
     res_k[...] = grad_k.astype(jnp.bfloat16)
     res_v[...] = grad_v.astype(jnp.bfloat16)
-    grad_q = res_q[...].T.astype(jnp.bfloat16)
-    g_att[...] = grad_q
-    for step in range(ranks):
+    res_q[...] = grad_t[...].T.astype(jnp.bfloat16)
+
+
+def block_kernel(steps, frames, *refs):
+    sources, tap_refs, outs = refs[:4], refs[4 : -len(steps)], refs[-len(steps) :]
+    me = lax.axis_index("seq")
+    taps = tap_refs[0][...]
+    for other in tap_refs[1:]:
+        taps = taps + other[...]
+    for step, out in zip(steps, outs):
         rows = rows_at(me ^ step, frames)
-        out = outs[step]
-        out[0:frames, :] = mixed[rows, :]
-        out[frames : 2 * frames, :] = g_att[rows, :]
-        out[2 * frames : 3 * frames, :] = res_k[rows, :]
-        out[3 * frames : 4 * frames, :] = res_v[rows, :]
-        out[4 * frames :, :] = taps
+        for place, source in enumerate(sources):
+            out[place * frames : (place + 1) * frames, :] = source[rows, :]
+        out[4 * frames :, :] = taps.astype(jnp.bfloat16)
 
 
 def spread_kernel(ranks, frames, *refs):
     blocks = refs[:ranks]
-    others = refs[ranks : 2 * ranks]
-    mixed_ref, q_ref, k_ref, v_ref, taps_ref = refs[2 * ranks : 2 * ranks + 5]
+    targets, taps_ref = refs[ranks : ranks + 4], refs[ranks + 4]
+    sems = refs[-1]
     me = lax.axis_index("seq")
+    pairs = []
     for step in range(ranks):
-        lanes = lanes_at(me ^ step)
-        for place, target in enumerate((mixed_ref, q_ref, k_ref, v_ref)):
-            target[0, :, lanes] = blocks[step][place * frames : (place + 1) * frames, :]
-        both = blocks[step][4 * frames :, :].astype(jnp.float32) + others[step][...].astype(jnp.float32)
-        taps_ref[:, lanes] = both[:KERNEL]
+        for place, target in enumerate(targets):
+            pairs.append(
+                (blocks[step].at[place * frames : (place + 1) * frames, :], target.at[0, :, lanes_at(me ^ step)])
+            )
+
+    def tap_grads():
+        for step in range(ranks):
+            taps = blocks[step][4 * frames :, :].astype(jnp.float32)
+            taps_ref[:, lanes_at(me ^ step)] = taps[:KERNEL]
+
+    run_copies(pairs, sems, tap_grads)
 
 
 def cost(flops, moved):
@@ -488,7 +497,8 @@
     heads = LANES // HDIM
     bf16, f32, i32 = jnp.bfloat16, jnp.float32, jnp.int32
     struct = jax.ShapeDtypeStruct
-    hbm = pl.BlockSpec(memory_space=pl.ANY)
+    hbm = pl.BlockSpec(memory_space=pltpu.HBM)
+    anywhere = pl.BlockSpec(memory_space=pl.ANY)
     vmem = pl.BlockSpec(memory_space=VMEM)
     smem = pl.BlockSpec(memory_space=pltpu.SMEM)
     params = pltpu.CompilerParams(vmem_limit_bytes=24 * MIB)
@@ -496,25 +506,23 @@
 
     sends = pl.pallas_call(
         functools.partial(pack_kernel, ranks),
-        out_shape=[struct((3, frames, LANES), bf16)] * (ranks - 1)
-        + [struct((frames, LANES), bf16)] * (ranks - 1),
-        in_specs=[hbm] * 4,
-        out_specs=[hbm] * (2 * ranks - 2),
-        scratch_shapes=[pltpu.SemaphoreType.DMA((4 * (ranks - 1),))],
-        compiler_params=params,
+        out_shape=[struct((3, frames, LANES), bf16)] * (ranks - 1),
+        in_specs=[hbm] * 3,
+        out_specs=[hbm] * (ranks - 1),
+        scratch_shapes=[pltpu.SemaphoreType.DMA((3 * (ranks - 1),))],
         name="pack",
-    )(queries, keys, values, cotangent)
+    )(queries, keys, values)
 
     def swap(array, step):
         return lax.ppermute(array, "seq", [(rank, rank ^ step) for rank in range(ranks)])
 
     order = list(range(ranks - 1, 0, -1))
     received = {step: swap(sends[step - 1], step) for step in order}
-    cots = {step: swap(sends[ranks - 1 + step - 1], step) for step in order}
-
-    own, col, row, after, before = pl.pallas_call(
-        functools.partial(mask_kernel, length),
-        out_shape=[
+
+    *cot_sends, own, col, row, after, before = pl.pallas_call(
+        functools.partial(mask_kernel, ranks, length),
+        out_shape=[struct((frames, LANES), bf16)] * (ranks - 1)
+        + [
             struct((4, frames, LANES), bf16),
             struct((length, LANES), i32),
             struct((8, length), i32),
@@ -522,27 +530,28 @@
             struct((length, LANES), i32),
         ],
         in_specs=[smem] + [hbm] * 4,
-        out_specs=[vmem] * 5,
-        scratch_shapes=[pltpu.SemaphoreType.DMA((4,))],
+        out_specs=[vmem] * (ranks + 4),
+        scratch_shapes=[pltpu.SemaphoreType.DMA((ranks + 3,))],
         compiler_params=params,
         cost_estimate=cost(4 * MIB, MIB),
         name="masks",
     )(rec_lengths, queries, keys, values, cotangent)
-
-    soft, att, att_t, pre, q_heads, k_t, v_full = pl.pallas_call(
+    cots = {step: swap(cot_sends[step - 1], step) for step in order}
+
+    soft, att, pre, q_heads, k_t, v_full = pl.pallas_call(
         functools.partial(forward_kernel, ranks, frames),
         out_shape=[
             struct((heads, length, length), bf16),
             struct((length + 2 * PAD, LANES), f32),
-            struct((LANES, length), f32),
             struct((length, LANES), f32),
             struct((heads, length, LANES), bf16),
             struct((LANES, length), bf16),
             struct((length, LANES), bf16),
         ],
-        in_specs=[vmem] * (ranks + 4) + [hbm],
-        out_specs=[vmem] * 7,
+        in_specs=[vmem] * (ranks + 4) + [anywhere],
+        out_specs=[vmem] * 6,
         scratch_shapes=[
+            VMEM((LANES, length), f32),
             VMEM((length, LANES), bf16),
             VMEM((length, LANES), bf16),
             VMEM((KERNEL, LANES), f32),
@@ -551,69 +560,69 @@
         compiler_params=params,
         cost_estimate=cost(400 * MIB, 3 * MIB),
         name="forward",
-    )(*[received[step] for step in range(1, ranks)], own, col, row, after, before, conv_weight)
-
-    *blocks, own_taps = pl.pallas_call(
-        functools.partial(backward_kernel, ranks, frames),
-        out_shape=[struct((4 * frames + taps, LANES), bf16)] * ranks + [struct((taps, LANES), bf16)],
-        in_specs=[vmem] * (ranks + 9) + [hbm],
-        out_specs=[vmem] * (ranks + 1),
+    )(*[received[step] for step in order], own, col, row, after, before, conv_weight)
+
+    mixed, g_att, own_taps = pl.pallas_call(
+        functools.partial(conv_back_kernel, ranks, frames),
+        out_shape=[struct((length, LANES), bf16)] * 2 + [struct((taps, LANES), f32)],
+        in_specs=[vmem] * (ranks + 4) + [anywhere],
+        out_specs=[vmem] * 3,
         scratch_shapes=[
             VMEM((length, LANES), bf16),
             VMEM((length + 2 * PAD, LANES), f32),
-            VMEM((length, LANES), bf16),
-            VMEM((length, LANES), bf16),
-            VMEM((LANES, length), f32),
-            VMEM((length, LANES), bf16),
-            VMEM((length, LANES), bf16),
             VMEM((taps, 8, LANES), f32),
             VMEM((KERNEL, LANES), f32),
             pltpu.SemaphoreType.DMA,
         ],
         compiler_params=params,
+        cost_estimate=cost(400 * MIB, 3 * MIB),
+        name="conv_back",
+    )(*[cots[step] for step in order], own, att, pre, after, before, conv_weight)
+
+    copies = lax.axis_size("dp")
+    part_taps = [own_taps] + [
+        lax.ppermute(own_taps, "dp", [(one, (one + shift) % copies) for one in range(copies)])
+        for shift in range(1, copies)
+    ]
+
+    results = pl.pallas_call(
+        backward_kernel,
+        out_shape=[struct((length, LANES), bf16)] * 3,
+        in_specs=[vmem] * 6,
+        out_specs=[vmem] * 3,
+        scratch_shapes=[VMEM((LANES, length), f32)],
+        compiler_params=params,
         cost_estimate=cost(800 * MIB, 3 * MIB),
         name="backward",
-    )(
-        *[cots[step] for step in range(1, ranks)],
-        own,
-        soft,
-        att,
-        att_t,
-        pre,
-        q_heads,
-        k_t,
-        v_full,
-        after,
-        before,
-        conv_weight,
-    )
-
-    back = {step: swap(blocks[step], step) for step in order}
-    copies = lax.axis_size("dp")
-    others = {}
-    for step in range(ranks):
-        others[step] = own_taps
-        for shift in range(1, copies):
-            pairs = [
-                (one * ranks + rank, (one + shift) % copies * ranks + (rank ^ step))
-                for one in range(copies)
-                for rank in range(ranks)
-            ]
-            others[step] = lax.ppermute(own_taps, ("dp", "seq"), pairs)
-
-    mixed, grad_q, grad_k, grad_v, grad_taps = pl.pallas_call(
+    )(soft, att, g_att, q_heads, k_t, v_full)
+
+    def blocks_of(steps):
+        return pl.pallas_call(
+            functools.partial(block_kernel, steps, frames),
+            out_shape=[struct((4 * frames + taps, LANES), bf16)] * len(steps),
+            in_specs=[vmem] * (4 + copies),
+            out_specs=[vmem] * len(steps),
+            compiler_params=params,
+            cost_estimate=cost(MIB, MIB),
+            name="blocks",
+        )(mixed, *results, *part_taps)
+
+    half = ranks // 2
+    far = blocks_of(list(range(half, ranks)))
+    near = blocks_of(list(range(half)))
+    back = {step: swap(far[step - half], step) for step in range(half, ranks)}
+    back |= {step: swap(near[step], step) for step in range(1, half)}
+    back[0] = near[0]
+
+    return pl.pallas_call(
         functools.partial(spread_kernel, ranks, frames),
         out_shape=[struct(queries.shape, bf16)] * 4 + [struct(conv_weight.shape, f32)],
-        in_specs=[vmem] * (2 * ranks),
-        out_specs=[vmem] * 5,
+        in_specs=[vmem] * ranks,
+        out_specs=[hbm] * 4 + [vmem],
+        scratch_shapes=[pltpu.SemaphoreType.DMA((4 * ranks,))],
         compiler_params=params,
         name="spread",
-    )(
-        blocks[0],
-        *[back[step] for step in range(1, ranks)],
-        *[others[step] for step in range(ranks)],
-    )
-    return (mixed, grad_q, grad_k, grad_v, grad_taps)
+    )(*[back[step] for step in range(ranks)])
 
 
 def on_device_any(queries, keys, values, cotangent, conv_weight, rec_lengths):

time: 48 us -> 47.6 us (level)
  Pallas kernels: 9.1 us -> 19.7 us
  starting transfers between devices: 24.3 us -> 16.3 us
  local copies, waits for them, and re-layouts: 3.62 us -> 0.92 us
    pallas_call x1, Pallas kernels: 0.21 us -> 10.1 us  [on_device_heads(): pl.pallas_call(functools.partial(pack_kernel, ranks), out_shape=[struct((...]
    ppermute x4 -> x1, starting transfers between devices: 8.66 us -> 1.56 us  [on_device_heads(): lax.ppermute(own_taps, 'dp', [(one, (one + shift) % copies) for one in ra...]
    ppermute x4 -> x1, waiting for transfers between devices: 7.17 us -> 0.82 us  [on_device_heads(): lax.ppermute(own_taps, 'dp', [(one, (one + shift) % copies) for one in ra...]
    ppermute x9, waiting for transfers between devices: 2.83 us -> 8.97 us  [swap(): lax.ppermute(array, 'seq', [(rank, rank ^ step) for rank in range(ranks)])]
    unnamed x12, local copies, waits for them, and re-layouts: 3.62 us -> 0.92 us
    ppermute x9, starting transfers between devices: 15.7 us -> 14.7 us  [swap(): lax.ppermute(array, 'seq', [(rank, rank ^ step) for rank in range(ranks)])]
    pallas_call x1, Pallas kernels: 0.91 us -> 1.55 us  [on_device_heads(): pl.pallas_call(functools.partial(spread_kernel, ranks, frames), out_shape...]
    pallas_call x2 -> x5, Pallas kernels: 4.57 us -> 4.62 us  [the longest x1 1.82 us: on_device_heads(): pl.pallas_call(functools.partial(conv_back_kernel, ranks, frames), out_sh...]
  transfers between devices with their start and end apart: 13 -> 10, of which waited for: 4 -> 4; matrix products, arithmetic and copies ran while one was open for 0% -> 0% of each run, Pallas kernels for 10% -> 13%
where the time goes in v2:
time: 47.6 us; the launch traced here: 47.4 us
  Pallas kernels  19.7 us (41%)
  starting transfers between devices  16.3 us (34%)
  waiting for transfers between devices  9.79 us (21%)
  local copies, waits for them, and re-layouts  0.92 us (2%)
  between operations  0.75 us (2%)
    ppermute x9, starting transfers between devices, swap(): lax.ppermute(array, 'seq', [(rank, rank ^ step) for rank in range(ranks)])  14.7 us
    pallas_call x1, Pallas kernels, on_device_heads(): pl.pallas_call(functools.partial(pack_kernel, ranks), out_shape=[struct((...  10.1 us
    ppermute x9, waiting for transfers between devices, swap(): lax.ppermute(array, 'seq', [(rank, rank ^ step) for rank in range(ranks)])  8.97 us
    pallas_call x1, Pallas kernels, on_device_heads(): pl.pallas_call(functools.partial(forward_kernel, ranks, frames), out_shap...  3.4 us
    pallas_call x1, Pallas kernels, on_device_heads(): pl.pallas_call(functools.partial(conv_back_kernel, ranks, frames), out_sh...  1.82 us
    ppermute x1, starting transfers between devices, on_device_heads(): lax.ppermute(own_taps, 'dp', [(one, (one + shift) % copies) for one in ra...  1.56 us
    pallas_call x1, Pallas kernels, on_device_heads(): pl.pallas_call(functools.partial(spread_kernel, ranks, frames), out_shape...  1.55 us
    pallas_call x1, Pallas kernels, on_device_heads(): pl.pallas_call(backward_kernel, out_shape=[struct((length, LANES), bf16)]...  1.42 us
  transfers between devices with their start and end apart: 10, of which 4 were waited for; matrix products, arithmetic and copies ran while one was open for 0% of the time, Pallas kernels for 13%

profile of v2, /device:TPU:0, one launch (start us, length us, event | category | flops | bytes accessed | tf_op | source)
XLA Modules:
  0.0 47.4 jit_solution(6397926752339541231)
XLA Ops:
  0.6 0.0 copy-start.2
  0.6 0.0 copy-start.1
  0.7 0.0 copy-start
  0.7 10.1 %pack.1 = (bf16[3,128,128]{2,1,0:T(8,128)(2,1)}, bf16[3,128,128]{2,1,0:T(8,128)(2,1)}, bf16[3,128,128]{2,1,0:T(8,128)(2,1)}) custom-call(bf16[1,128,512]{2,1,0:T(8,128)(2,1)} %q_ref.3, bf16[1,128,512]{2,1,0:T(8,128)(2,1)} %k_ref.3, bf16[1,128,512]{2,1,0:T(8,128)(2,1)} %v_ref.3), custom_call_target="tpu_custom_call" | custom-call | tf_op jit(solution)/shard_map/pack/pallas_call | solution.py:507
  10.8 5.1 %collective-permute-start.3 = (bf16[3,128,128]{2,1,0:T(8,128)(2,1)}, bf16[3,128,128]{2,1,0:T(8,128)(2,1)S(1)}, u32[]{:S(2)}, u32[]{:S(2)}) collective-permute-start(bf16[3,128,128]{2,1,0:T(8,128)(2,1)} %get-tuple-element.36), channel_id=1, source_target_pairs={{0,6},{2,4},{4,2},{6,0},{1,7},{3,5},{5,3},{7,1},{8,14},{10,12},{12... | collective-permute-start | bytes 294920 | tf_op jit(solution)/shard_map/ppermute | solution.py:517
  15.9 0.0 copy-start.4
  15.9 0.0 collective-permute-start.4
  15.9 0.6 %collective-permute-start.5 = (bf16[3,128,128]{2,1,0:T(8,128)(2,1)}, bf16[3,128,128]{2,1,0:T(8,128)(2,1)S(1)}, u32[]{:S(2)}, u32[]{:S(2)}) collective-permute-start(bf16[3,128,128]{2,1,0:T(8,128)(2,1)} %get-tuple-element.38), channel_id=1, source_target_pairs={{0,2},{2,0},{4,6},{6,4},{1,3},{3,1},{5,7},{7,5},{8,10},{10,8},{12,... | collective-permute-start | bytes 294920 | tf_op jit(solution)/shard_map/ppermute | solution.py:517
  16.6 0.0 copy-done.2
  16.6 0.0 copy-done.1
  16.6 0.0 copy-done
  16.6 0.0 copy-done.4
  16.6 0.0 copy-start.3
  16.6 0.9 %copy-done.3 = bf16[1,128,512]{2,1,0:T(8,128)(2,1)S(1)} copy-done((bf16[1,128,512]{2,1,0:T(8,128)(2,1)S(1)}, bf16[1,128,512]{2,1,0:T(8,128)(2,1)}, u32[]{:S(2)}) %copy-start.3) | copy-done | bytes 131096
  17.5 0.0 copy-start.5
  17.5 1.3 %masks.1 = (bf16[128,128]{1,0:T(8,128)(2,1)S(1)}, bf16[128,128]{1,0:T(8,128)(2,1)S(1)}, bf16[128,128]{1,0:T(8,128)(2,1)S(1)}, bf16[4,128,128]{2,1,0:T(8,128)(2,1...) custom-call(s32[1,16]{1,0:T(1,128)S(1)} %copy-done.4, ...), custom_call_target="tpu_custom_call" | custom-call | flops 4194304 | bytes 1048576 | tf_op jit(solution)/shard_map/masks/pallas_call | solution.py:522
  18.8 3.8 %collective-permute-start = (bf16[128,128]{1,0:T(8,128)(2,1)S(1)}, bf16[128,128]{1,0:T(8,128)(2,1)S(1)}, u32[]{:S(2)}, u32[]{:S(2)}) collective-permute-start(bf16[128,128]{1,0:T(8,128)(2,1)S(1)} %get-tuple-element.32), channel_id=1, source_target_pairs={{0,6},{2,4},{4,2},{6,0},{1,7},{3,5},{5,3},{7,1},{8,14},{10,12},{12... | collective-permute-start | bytes 98312 | tf_op jit(solution)/shard_map/ppermute | solution.py:517
  22.6 0.0 collective-permute-start.1
  22.6 0.0 collective-permute-done.3.refs_0_
  22.6 1.5 %collective-permute-start.2 = (bf16[128,128]{1,0:T(8,128)(2,1)S(1)}, bf16[128,128]{1,0:T(8,128)(2,1)S(1)}, u32[]{:S(2)}, u32[]{:S(2)}) collective-permute-start(bf16[128,128]{1,0:T(8,128)(2,1)S(1)} %get-tuple-element.34), channel_id=1, source_target_pairs={{0,2},{2,0},{4,6},{6,4},{1,3},{3,1},{5,7},{7,5},{8,10},{10,8},{12,... | collective-permute-start | bytes 98312 | tf_op jit(solution)/shard_map/ppermute | solution.py:517
  24.2 2.4 %collective-permute-done.4.refs_1_ = bf16[3,128,128]{2,1,0:T(8,128)(2,1)S(1)} collective-permute-done((bf16[3,128,128]{2,1,0:T(8,128)(2,1)}, bf16[3,128,128]{2,1,0:T(8,128)(2,1)S(1)}, u32[]{:S(2)}, u32[]{:S(2)}) %collective-permute-start.4) | collective-permute-done | bytes 98336 | tf_op jit(solution)/shard_map/ppermute | solution.py:517
  26.5 0.0 collective-permute-done.5.refs_2_
  26.5 0.0 copy-done.5
  26.5 3.4 %forward.1 = (bf16[2,512,512]{2,1,0:T(8,128)(2,1)S(1)}, f32[544,128]{1,0:T(8,128)S(1)}, f32[512,128]{1,0:T(8,128)S(1)}, bf16[2,512,128]{2,1,0:T(8,128)(2,1)S(1)}...) custom-call(bf16[3,128,128]{2,1,0:T(8,128)(2,1)S(1)} %collective-permute-done.3.refs_0_, ...), custom_call_target="tpu_custom_call" | custom-call | flops 419430400 | bytes 3145728 | tf_op jit(solution)/shard_map/forward/pallas_call | solution.py:541
  29.9 0.0 collective-permute-done.refs_0_
  30.0 0.0 collective-permute-done.1.refs_1_
  30.0 0.0 collective-permute-done.2.refs_2_
  30.0 1.8 %conv_back.1 = (bf16[512,128]{1,0:T(8,128)(2,1)S(1)}, bf16[512,128]{1,0:T(8,128)(2,1)S(1)}, f32[32,128]{1,0:T(8,128)S(1)}) custom-call(bf16[128,128]{1,0:T(8,128)(2,1)S(1)} %collective-permute-done.refs_0_, bf16[128,128]{1,0:T(8,128)(2,1)S(1)} %collective-permute-done.1.refs_1_, bf16[128,128]{1,0:T(8,128)(2,1)S(1)} %collective-permute-done.2.refs_2_, ...), custom_call_target="tpu_custom_call" | custom-call | flops 419430400 | bytes 3145728 | tf_op jit(solution)/shard_map/conv_back/pallas_call | solution.py:565
  31.8 1.6 %collective-permute-start.6 = (f32[32,128]{1,0:T(8,128)S(1)}, f32[32,128]{1,0:T(8,128)S(1)}, u32[]{:S(2)}, u32[]{:S(2)}) collective-permute-start(f32[32,128]{1,0:T(8,128)S(1)} %get-tuple-element.54.refs_4_), channel_id=1, source_target_pairs={{0,8},{8,0},{1,9},{9,1},{2,10},{10,2},{3,11},{11,3},{4,12},{12,4},... | collective-permute-start | bytes 49160 | tf_op jit(solution)/shard_map/ppermute | solution.py:584
  33.4 1.4 %backward.1 = (bf16[512,128]{1,0:T(8,128)(2,1)S(1)}, bf16[512,128]{1,0:T(8,128)(2,1)S(1)}, bf16[512,128]{1,0:T(8,128)(2,1)S(1)}) custom-call(bf16[2,512,512]{2,1,0:T(8,128)(2,1)S(1)} %get-tuple-element.46.soft_ref, f32[544,128]{1,0:T(8,128)S(1)} %get-tuple-element.43.refs_4_.att_ref, bf16[512,128]{1,0:T(8,128)(2,1)S(1)} %get-tuple-element.47.g_att, ...), custom_call_target="tpu_custom_call" | custom-call | flops 838860800 | bytes 3145728 | tf_op jit(solution)/shard_map/backward/pallas_call | solution.py:588
  34.8 0.8 %collective-permute-done.6.refs_5_ = f32[32,128]{1,0:T(8,128)S(1)} collective-permute-done((f32[32,128]{1,0:T(8,128)S(1)}, f32[32,128]{1,0:T(8,128)S(1)}, u32[]{:S(2)}, u32[]{:S(2)}) %collective-permute-start.6) | collective-permute-done | bytes 16416 | tf_op jit(solution)/shard_map/ppermute | solution.py:584
  35.6 0.1 collective-permute-start.8
  35.7 2.6 %collective-permute-start.9 = (bf16[544,128]{1,0:T(8,128)(2,1)S(1)}, bf16[544,128]{1,0:T(8,128)(2,1)S(1)}, u32[]{:S(2)}, u32[]{:S(2)}) collective-permute-start(bf16[544,128]{1,0:T(8,128)(2,1)S(1)} %get-tuple-element.58), channel_id=1, source_target_pairs={{0,6},{2,4},{4,2},{6,0},{1,7},{3,5},{5,3},{7,1},{8,14},{10,12},{12... | collective-permute-start | bytes 417800 | tf_op jit(solution)/shard_map/ppermute | solution.py:517
  38.3 1.0 %collective-permute-start.7 = (bf16[544,128]{1,0:T(8,128)(2,1)S(1)}, bf16[544,128]{1,0:T(8,128)(2,1)S(1)}, u32[]{:S(2)}, u32[]{:S(2)}) collective-permute-start(bf16[544,128]{1,0:T(8,128)(2,1)S(1)} %get-tuple-element.56), channel_id=1, source_target_pairs={{0,2},{2,0},{4,6},{6,4},{1,3},{3,1},{5,7},{7,5},{8,10},{10,8},{12,... | collective-permute-start | bytes 417800 | tf_op jit(solution)/shard_map/ppermute | solution.py:517
  39.3 6.2 %collective-permute-done.8.refs_2_ = bf16[544,128]{1,0:T(8,128)(2,1)S(1)} collective-permute-done((bf16[544,128]{1,0:T(8,128)(2,1)S(1)}, bf16[544,128]{1,0:T(8,128)(2,1)S(1)}, u32[]{:S(2)}, u32[]{:S(2)}) %collective-permute-start.8) | collective-permute-done | bytes 139296 | tf_op jit(solution)/shard_map/ppermute | solution.py:517
  45.5 0.0 collective-permute-done.9.refs_3_
  45.5 0.4 collective-permute-done.7.refs_1_
  45.9 1.5 %spread.1 = (bf16[1,128,512]{2,1,0:T(8,128)(2,1)}, bf16[1,128,512]{2,1,0:T(8,128)(2,1)}, bf16[1,128,512]{2,1,0:T(8,128)(2,1)}, bf16[1,128,512]{2,1,0:T(8,128)(2,1)}, f32[31,512]{1,0:T(8,128)}) custom-call(bf16[544,128]{1,0:T(8,128)(2,1)S(1)} %get-tuple-element.55.refs_0_, bf16[544,128]{1,0:T(8,128)(2,1)S(1)} %collective-permute-done.7.refs_1_, ...), custom_call_target="tpu_custom_call" | custom-call | tf_op jit(solution)/shard_map/spread/pallas_call | solution.py:617
  (2 shorter events, 0.0 us)
Async XLA Ops:
  0.6 15.9 %copy-start.2 = (bf16[1,128,512]{2,1,0:T(8,128)(2,1)S(1)}, bf16[1,128,512]{2,1,0:T(8,128)(2,1)}, u32[]{:S(2)}) copy-start(bf16[1,128,512]{2,1,0:T(8,128)(2,1)} %v_ref.3) | copy-start | bytes 393220
  0.6 15.9 %copy-start.1 = (bf16[1,128,512]{2,1,0:T(8,128)(2,1)S(1)}, bf16[1,128,512]{2,1,0:T(8,128)(2,1)}, u32[]{:S(2)}) copy-start(bf16[1,128,512]{2,1,0:T(8,128)(2,1)} %k_ref.3) | copy-start | bytes 393220
  0.7 15.9 %copy-start = (bf16[1,128,512]{2,1,0:T(8,128)(2,1)S(1)}, bf16[1,128,512]{2,1,0:T(8,128)(2,1)}, u32[]{:S(2)}) copy-start(bf16[1,128,512]{2,1,0:T(8,128)(2,1)} %q_ref.3) | copy-start | bytes 393220
  10.8 11.8 %collective-permute-start.3 = (bf16[3,128,128]{2,1,0:T(8,128)(2,1)}, bf16[3,128,128]{2,1,0:T(8,128)(2,1)S(1)}, u32[]{:S(2)}, u32[]{:S(2)}) collective-permute-start(bf16[3,128,128]{2,1,0:T(8,128)(2,1)} %get-tuple-element.36), channel_id=1, source_target_pairs={{0,6},{2,4},{4,2},{6,0},{1,7},{3,5},{5,3},{7,1},{8,14},{10,12},{12... | collective-permute-start | bytes 294920 | tf_op jit(solution)/shard_map/ppermute | solution.py:517
  15.9 0.7 %copy-start.4 = (s32[1,16]{1,0:T(1,128)S(1)}, s32[1,16]{1,0:T(1,128)}, u32[]{:S(2)}) copy-start(s32[1,16]{1,0:T(1,128)} %lens_ref.1) | copy-start | bytes 196
  15.9 10.6 %collective-permute-start.4 = (bf16[3,128,128]{2,1,0:T(8,128)(2,1)}, bf16[3,128,128]{2,1,0:T(8,128)(2,1)S(1)}, u32[]{:S(2)}, u32[]{:S(2)}) collective-permute-start(bf16[3,128,128]{2,1,0:T(8,128)(2,1)} %get-tuple-element.37), channel_id=1, source_target_pairs={{0,4},{2,6},{4,0},{6,2},{1,5},{3,7},{5,1},{7,3},{8,12},{10,14},{12... | collective-permute-start | bytes 294920 | tf_op jit(solution)/shard_map/ppermute | solution.py:517
  15.9 10.6 %collective-permute-start.5 = (bf16[3,128,128]{2,1,0:T(8,128)(2,1)}, bf16[3,128,128]{2,1,0:T(8,128)(2,1)S(1)}, u32[]{:S(2)}, u32[]{:S(2)}) collective-permute-start(bf16[3,128,128]{2,1,0:T(8,128)(2,1)} %get-tuple-element.38), channel_id=1, source_target_pairs={{0,2},{2,0},{4,6},{6,4},{1,3},{3,1},{5,7},{7,5},{8,10},{10,8},{12,... | collective-permute-start | bytes 294920 | tf_op jit(solution)/shard_map/ppermute | solution.py:517
  16.6 0.9 %copy-start.3 = (bf16[1,128,512]{2,1,0:T(8,128)(2,1)S(1)}, bf16[1,128,512]{2,1,0:T(8,128)(2,1)}, u32[]{:S(2)}) copy-start(bf16[1,128,512]{2,1,0:T(8,128)(2,1)} %c_ref.1) | copy-start | bytes 393220
  17.5 9.0 %copy-start.5 = (f32[31,512]{1,0:T(8,128)S(1)}, f32[31,512]{1,0:T(8,128)}, u32[]{:S(2)}) copy-start(f32[31,512]{1,0:T(8,128)} %refs_8_.3) | copy-start | bytes 190468
  18.8 11.1 %collective-permute-start = (bf16[128,128]{1,0:T(8,128)(2,1)S(1)}, bf16[128,128]{1,0:T(8,128)(2,1)S(1)}, u32[]{:S(2)}, u32[]{:S(2)}) collective-permute-start(bf16[128,128]{1,0:T(8,128)(2,1)S(1)} %get-tuple-element.32), channel_id=1, source_target_pairs={{0,6},{2,4},{4,2},{6,0},{1,7},{3,5},{5,3},{7,1},{8,14},{10,12},{12... | collective-permute-start | bytes 98312 | tf_op jit(solution)/shard_map/ppermute | solution.py:517
  22.6 7.3 %collective-permute-start.1 = (bf16[128,128]{1,0:T(8,128)(2,1)S(1)}, bf16[128,128]{1,0:T(8,128)(2,1)S(1)}, u32[]{:S(2)}, u32[]{:S(2)}) collective-permute-start(bf16[128,128]{1,0:T(8,128)(2,1)S(1)} %get-tuple-element.33), channel_id=1, source_target_pairs={{0,4},{2,6},{4,0},{6,2},{1,5},{3,7},{5,1},{7,3},{8,12},{10,14},{12... | collective-permute-start | bytes 98312 | tf_op jit(solution)/shard_map/ppermute | solution.py:517
  22.6 7.3 %collective-permute-start.2 = (bf16[128,128]{1,0:T(8,128)(2,1)S(1)}, bf16[128,128]{1,0:T(8,128)(2,1)S(1)}, u32[]{:S(2)}, u32[]{:S(2)}) collective-permute-start(bf16[128,128]{1,0:T(8,128)(2,1)S(1)} %get-tuple-element.34), channel_id=1, source_target_pairs={{0,2},{2,0},{4,6},{6,4},{1,3},{3,1},{5,7},{7,5},{8,10},{10,8},{12,... | collective-permute-start | bytes 98312 | tf_op jit(solution)/shard_map/ppermute | solution.py:517
  31.8 3.8 %collective-permute-start.6 = (f32[32,128]{1,0:T(8,128)S(1)}, f32[32,128]{1,0:T(8,128)S(1)}, u32[]{:S(2)}, u32[]{:S(2)}) collective-permute-start(f32[32,128]{1,0:T(8,128)S(1)} %get-tuple-element.54.refs_4_), channel_id=1, source_target_pairs={{0,8},{8,0},{1,9},{9,1},{2,10},{10,2},{3,11},{11,3},{4,12},{12,4},... | collective-permute-start | bytes 49160 | tf_op jit(solution)/shard_map/ppermute | solution.py:584
  35.6 9.9 %collective-permute-start.8 = (bf16[544,128]{1,0:T(8,128)(2,1)S(1)}, bf16[544,128]{1,0:T(8,128)(2,1)S(1)}, u32[]{:S(2)}, u32[]{:S(2)}) collective-permute-start(bf16[544,128]{1,0:T(8,128)(2,1)S(1)} %get-tuple-element.57), channel_id=1, source_target_pairs={{0,4},{2,6},{4,0},{6,2},{1,5},{3,7},{5,1},{7,3},{8,12},{10,14},{12... | collective-permute-start | bytes 417800 | tf_op jit(solution)/shard_map/ppermute | solution.py:517
  35.7 9.8 %collective-permute-start.9 = (bf16[544,128]{1,0:T(8,128)(2,1)S(1)}, bf16[544,128]{1,0:T(8,128)(2,1)S(1)}, u32[]{:S(2)}, u32[]{:S(2)}) collective-permute-start(bf16[544,128]{1,0:T(8,128)(2,1)S(1)} %get-tuple-element.58), channel_id=1, source_target_pairs={{0,6},{2,4},{4,2},{6,0},{1,7},{3,5},{5,3},{7,1},{8,14},{10,12},{12... | collective-permute-start | bytes 417800 | tf_op jit(solution)/shard_map/ppermute | solution.py:517
  38.3 7.5 %collective-permute-start.7 = (bf16[544,128]{1,0:T(8,128)(2,1)S(1)}, bf16[544,128]{1,0:T(8,128)(2,1)S(1)}, u32[]{:S(2)}, u32[]{:S(2)}) collective-permute-start(bf16[544,128]{1,0:T(8,128)(2,1)S(1)} %get-tuple-element.56), channel_id=1, source_target_pairs={{0,2},{2,0},{4,6},{6,4},{1,3},{3,1},{5,7},{7,5},{8,10},{10,8},{12,... | collective-permute-start | bytes 417800 | tf_op jit(solution)/shard_map/ppermute | solution.py:517

commit v3 on v2

--- a/solution.py
+++ b/solution.py
@@ -256,13 +256,13 @@
 
 
 def pack_kernel(ranks, q_ref, k_ref, v_ref, *rest):
-    outs, sems = rest[:-1], rest[-1]
+    outs, (whole, sems) = rest[:-2], rest[-2:]
     me = lax.axis_index("seq")
-    copies = []
+    sources = (q_ref, k_ref, v_ref)
+    run_copies([(source.at[0], whole.at[place]) for place, source in enumerate(sources)], sems)
     for step in range(ranks - 1, 0, -1):
-        for place, source in enumerate((q_ref, k_ref, v_ref)):
-            copies.append((source.at[0, :, lanes_at(me ^ step)], outs[step - 1].at[place]))
-    run_copies(copies, sems)
+        for place in range(len(sources)):
+            outs[step - 1][place] = whole[place, :, lanes_at(me ^ step)]
 
 
 def run_copies(pairs, sems, meanwhile=None):
@@ -469,21 +469,13 @@
 def spread_kernel(ranks, frames, *refs):
     blocks = refs[:ranks]
     targets, taps_ref = refs[ranks : ranks + 4], refs[ranks + 4]
-    sems = refs[-1]
     me = lax.axis_index("seq")
-    pairs = []
     for step in range(ranks):
+        lanes = lanes_at(me ^ step)
         for place, target in enumerate(targets):
-            pairs.append(
-                (blocks[step].at[place * frames : (place + 1) * frames, :], target.at[0, :, lanes_at(me ^ step)])
-            )
-
-    def tap_grads():
-        for step in range(ranks):
-            taps = blocks[step][4 * frames :, :].astype(jnp.float32)
-            taps_ref[:, lanes_at(me ^ step)] = taps[:KERNEL]
-
-    run_copies(pairs, sems, tap_grads)
+            target[0, :, lanes] = blocks[step][place * frames : (place + 1) * frames, :]
+        taps = blocks[step][4 * frames :, :].astype(jnp.float32)
+        taps_ref[:, lanes] = taps[:KERNEL]
 
 
 def cost(flops, moved):
@@ -508,8 +500,9 @@
         functools.partial(pack_kernel, ranks),
         out_shape=[struct((3, frames, LANES), bf16)] * (ranks - 1),
         in_specs=[hbm] * 3,
-        out_specs=[hbm] * (ranks - 1),
-        scratch_shapes=[pltpu.SemaphoreType.DMA((3 * (ranks - 1),))],
+        out_specs=[vmem] * (ranks - 1),
+        scratch_shapes=[VMEM((3,) + queries.shape[1:], bf16), pltpu.SemaphoreType.DMA((3,))],
+        compiler_params=pltpu.CompilerParams(vmem_limit_bytes=54912 * 1024),
         name="pack",
     )(queries, keys, values)
 
@@ -618,8 +611,7 @@
         functools.partial(spread_kernel, ranks, frames),
         out_shape=[struct(queries.shape, bf16)] * 4 + [struct(conv_weight.shape, f32)],
         in_specs=[vmem] * ranks,
-        out_specs=[hbm] * 4 + [vmem],
-        scratch_shapes=[pltpu.SemaphoreType.DMA((4 * ranks,))],
+        out_specs=[vmem] * 5,
         compiler_params=params,
         name="spread",
     )(*[back[step] for step in range(ranks)])

time: 47.6 us -> 37.7 us (0.79)
  Pallas kernels: 19.7 us -> 10.1 us
    pallas_call x1, Pallas kernels: 10.1 us -> 1.16 us  [on_device_heads(): pl.pallas_call(functools.partial(pack_kernel, ranks), out_shape=[struct((...]
    pallas_call x1, Pallas kernels: 1.55 us -> 0.9 us  [on_device_heads(): pl.pallas_call(functools.partial(spread_kernel, ranks, frames), out_shape...]
  transfers between devices with their start and end apart: 10 -> 10, of which waited for: 4 -> 4; matrix products, arithmetic and copies ran while one was open for 0% -> 0% of each run, Pallas kernels for 13% -> 16%
where the time goes in v3:
time: 37.7 us; the launch traced here: 37.5 us
  starting transfers between devices  16.1 us (43%)
  Pallas kernels  10.1 us (27%)
  waiting for transfers between devices  9.73 us (26%)
  local copies, waits for them, and re-layouts  0.92 us (2%)
  between operations  0.75 us (2%)
    ppermute x9, starting transfers between devices, swap(): lax.ppermute(array, 'seq', [(rank, rank ^ step) for rank in range(ranks)])  14.5 us
    ppermute x9, waiting for transfers between devices, swap(): lax.ppermute(array, 'seq', [(rank, rank ^ step) for rank in range(ranks)])  8.91 us
    pallas_call x1, Pallas kernels, on_device_heads(): pl.pallas_call(functools.partial(forward_kernel, ranks, frames), out_shap...  3.4 us
    pallas_call x1, Pallas kernels, on_device_heads(): pl.pallas_call(functools.partial(conv_back_kernel, ranks, frames), out_sh...  1.82 us
    ppermute x1, starting transfers between devices, on_device_heads(): lax.ppermute(own_taps, 'dp', [(one, (one + shift) % copies) for one in ra...  1.55 us
    pallas_call x1, Pallas kernels, on_device_heads(): pl.pallas_call(backward_kernel, out_shape=[struct((length, LANES), bf16)]...  1.43 us
    pallas_call x1, Pallas kernels, on_device_heads(): pl.pallas_call(functools.partial(mask_kernel, ranks, length), out_shape=[...  1.32 us
    pallas_call x1, Pallas kernels, on_device_heads(): pl.pallas_call(functools.partial(pack_kernel, ranks), out_shape=[struct((...  1.16 us
  transfers between devices with their start and end apart: 10, of which 4 were waited for; matrix products, arithmetic and copies ran while one was open for 0% of the time, Pallas kernels for 16%

profile of v3, /device:TPU:0, one launch (start us, length us, event | category | flops | bytes accessed | tf_op | source)
XLA Modules:
  0.0 37.5 jit_solution(313690463242711032)
XLA Ops:
  0.6 0.0 copy-start.2
  0.6 0.0 copy-start.1
  0.7 0.0 copy-start
  0.7 1.2 %pack.1 = (bf16[3,128,128]{2,1,0:T(8,128)(2,1)S(1)}, bf16[3,128,128]{2,1,0:T(8,128)(2,1)S(1)}, bf16[3,128,128]{2,1,0:T(8,128)(2,1)S(1)}) custom-call(bf16[1,128,512]{2,1,0:T(8,128)(2,1)} %q_ref.3, bf16[1,128,512]{2,1,0:T(8,128)(2,1)} %k_ref.3, bf16[1,128,512]{2,1,0:T(8,128)(2,1)} %v_ref.3), custom_call_target="tpu_custom_call" | custom-call | tf_op jit(solution)/shard_map/pack/pallas_call | solution.py:499
  1.8 5.1 %collective-permute-start.3 = (bf16[3,128,128]{2,1,0:T(8,128)(2,1)S(1)}, bf16[3,128,128]{2,1,0:T(8,128)(2,1)S(1)}, u32[]{:S(2)}, u32[]{:S(2)}) collective-permute-start(bf16[3,128,128]{2,1,0:T(8,128)(2,1)S(1)} %get-tuple-element.36), channel_id=1, source_target_pairs={{0,6},{2,4},{4,2},{6,0},{1,7},{3,5},{5,3},{7,1},{8,14},{10,12},{12... | collective-permute-start | bytes 294920 | tf_op jit(solution)/shard_map/ppermute | solution.py:510
  6.9 0.0 copy-start.4
  6.9 0.0 collective-permute-start.4
  6.9 0.6 %collective-permute-start.5 = (bf16[3,128,128]{2,1,0:T(8,128)(2,1)S(1)}, bf16[3,128,128]{2,1,0:T(8,128)(2,1)S(1)}, u32[]{:S(2)}, u32[]{:S(2)}) collective-permute-start(bf16[3,128,128]{2,1,0:T(8,128)(2,1)S(1)} %get-tuple-element.38), channel_id=1, source_target_pairs={{0,2},{2,0},{4,6},{6,4},{1,3},{3,1},{5,7},{7,5},{8,10},{10,8},{12,... | collective-permute-start | bytes 294920 | tf_op jit(solution)/shard_map/ppermute | solution.py:510
  7.6 0.0 copy-done.2
  7.6 0.0 copy-done.1
  7.6 0.0 copy-done
  7.6 0.0 copy-done.4
  7.6 0.0 copy-start.3
  7.6 0.9 %copy-done.3 = bf16[1,128,512]{2,1,0:T(8,128)(2,1)S(1)} copy-done((bf16[1,128,512]{2,1,0:T(8,128)(2,1)S(1)}, bf16[1,128,512]{2,1,0:T(8,128)(2,1)}, u32[]{:S(2)}) %copy-start.3) | copy-done | bytes 131096
  8.5 0.0 copy-start.5
  8.5 1.3 %masks.1 = (bf16[128,128]{1,0:T(8,128)(2,1)S(1)}, bf16[128,128]{1,0:T(8,128)(2,1)S(1)}, bf16[128,128]{1,0:T(8,128)(2,1)S(1)}, bf16[4,128,128]{2,1,0:T(8,128)(2,1...) custom-call(s32[1,16]{1,0:T(1,128)S(1)} %copy-done.4, ...), custom_call_target="tpu_custom_call" | custom-call | flops 4194304 | bytes 1048576 | tf_op jit(solution)/shard_map/masks/pallas_call | solution.py:515
  9.9 3.8 %collective-permute-start = (bf16[128,128]{1,0:T(8,128)(2,1)S(1)}, bf16[128,128]{1,0:T(8,128)(2,1)S(1)}, u32[]{:S(2)}, u32[]{:S(2)}) collective-permute-start(bf16[128,128]{1,0:T(8,128)(2,1)S(1)} %get-tuple-element.32), channel_id=1, source_target_pairs={{0,6},{2,4},{4,2},{6,0},{1,7},{3,5},{5,3},{7,1},{8,14},{10,12},{12... | collective-permute-start | bytes 98312 | tf_op jit(solution)/shard_map/ppermute | solution.py:510
  13.7 0.0 collective-permute-start.1
  13.7 0.0 collective-permute-done.3.refs_0_
  13.7 1.3 %collective-permute-start.2 = (bf16[128,128]{1,0:T(8,128)(2,1)S(1)}, bf16[128,128]{1,0:T(8,128)(2,1)S(1)}, u32[]{:S(2)}, u32[]{:S(2)}) collective-permute-start(bf16[128,128]{1,0:T(8,128)(2,1)S(1)} %get-tuple-element.34), channel_id=1, source_target_pairs={{0,2},{2,0},{4,6},{6,4},{1,3},{3,1},{5,7},{7,5},{8,10},{10,8},{12,... | collective-permute-start | bytes 98312 | tf_op jit(solution)/shard_map/ppermute | solution.py:510
  15.0 2.3 %collective-permute-done.4.refs_1_ = bf16[3,128,128]{2,1,0:T(8,128)(2,1)S(1)} collective-permute-done((bf16[3,128,128]{2,1,0:T(8,128)(2,1)S(1)}, bf16[3,128,128]{2,1,0:T(8,128)(2,1)S(1)}, u32[]{:S(2)}, u32[]{:S(2)}) %collective-permute-start.4) | collective-permute-done | bytes 98336 | tf_op jit(solution)/shard_map/ppermute | solution.py:510
  17.3 0.0 collective-permute-done.5.refs_2_
  17.3 0.0 copy-done.5
  17.3 3.4 %forward.1 = (bf16[2,512,512]{2,1,0:T(8,128)(2,1)S(1)}, f32[544,128]{1,0:T(8,128)S(1)}, f32[512,128]{1,0:T(8,128)S(1)}, bf16[2,512,128]{2,1,0:T(8,128)(2,1)S(1)}...) custom-call(bf16[3,128,128]{2,1,0:T(8,128)(2,1)S(1)} %collective-permute-done.3.refs_0_, ...), custom_call_target="tpu_custom_call" | custom-call | flops 419430400 | bytes 3145728 | tf_op jit(solution)/shard_map/forward/pallas_call | solution.py:534
  20.7 0.0 collective-permute-done.refs_0_
  20.7 0.0 collective-permute-done.1.refs_1_
  20.8 0.0 collective-permute-done.2.refs_2_
  20.8 1.8 %conv_back.1 = (bf16[512,128]{1,0:T(8,128)(2,1)S(1)}, bf16[512,128]{1,0:T(8,128)(2,1)S(1)}, f32[32,128]{1,0:T(8,128)S(1)}) custom-call(bf16[128,128]{1,0:T(8,128)(2,1)S(1)} %collective-permute-done.refs_0_, bf16[128,128]{1,0:T(8,128)(2,1)S(1)} %collective-permute-done.1.refs_1_, bf16[128,128]{1,0:T(8,128)(2,1)S(1)} %collective-permute-done.2.refs_2_, ...), custom_call_target="tpu_custom_call" | custom-call | flops 419430400 | bytes 3145728 | tf_op jit(solution)/shard_map/conv_back/pallas_call | solution.py:558
  22.6 1.6 %collective-permute-start.6 = (f32[32,128]{1,0:T(8,128)S(1)}, f32[32,128]{1,0:T(8,128)S(1)}, u32[]{:S(2)}, u32[]{:S(2)}) collective-permute-start(f32[32,128]{1,0:T(8,128)S(1)} %get-tuple-element.54.refs_4_), channel_id=1, source_target_pairs={{0,8},{8,0},{1,9},{9,1},{2,10},{10,2},{3,11},{11,3},{4,12},{12,4},... | collective-permute-start | bytes 49160 | tf_op jit(solution)/shard_map/ppermute | solution.py:577
  24.2 1.4 %backward.1 = (bf16[512,128]{1,0:T(8,128)(2,1)S(1)}, bf16[512,128]{1,0:T(8,128)(2,1)S(1)}, bf16[512,128]{1,0:T(8,128)(2,1)S(1)}) custom-call(bf16[2,512,512]{2,1,0:T(8,128)(2,1)S(1)} %get-tuple-element.46.soft_ref, f32[544,128]{1,0:T(8,128)S(1)} %get-tuple-element.43.refs_4_.att_ref, bf16[512,128]{1,0:T(8,128)(2,1)S(1)} %get-tuple-element.47.g_att, ...), custom_call_target="tpu_custom_call" | custom-call | flops 838860800 | bytes 3145728 | tf_op jit(solution)/shard_map/backward/pallas_call | solution.py:581
  25.6 0.8 %collective-permute-done.6.refs_5_ = f32[32,128]{1,0:T(8,128)S(1)} collective-permute-done((f32[32,128]{1,0:T(8,128)S(1)}, f32[32,128]{1,0:T(8,128)S(1)}, u32[]{:S(2)}, u32[]{:S(2)}) %collective-permute-start.6) | collective-permute-done | bytes 16416 | tf_op jit(solution)/shard_map/ppermute | solution.py:577
  26.4 0.1 collective-permute-start.8
  26.5 2.6 %collective-permute-start.9 = (bf16[544,128]{1,0:T(8,128)(2,1)S(1)}, bf16[544,128]{1,0:T(8,128)(2,1)S(1)}, u32[]{:S(2)}, u32[]{:S(2)}) collective-permute-start(bf16[544,128]{1,0:T(8,128)(2,1)S(1)} %get-tuple-element.58), channel_id=1, source_target_pairs={{0,6},{2,4},{4,2},{6,0},{1,7},{3,5},{5,3},{7,1},{8,14},{10,12},{12... | collective-permute-start | bytes 417800 | tf_op jit(solution)/shard_map/ppermute | solution.py:510
  29.1 1.0 %collective-permute-start.7 = (bf16[544,128]{1,0:T(8,128)(2,1)S(1)}, bf16[544,128]{1,0:T(8,128)(2,1)S(1)}, u32[]{:S(2)}, u32[]{:S(2)}) collective-permute-start(bf16[544,128]{1,0:T(8,128)(2,1)S(1)} %get-tuple-element.56), channel_id=1, source_target_pairs={{0,2},{2,0},{4,6},{6,4},{1,3},{3,1},{5,7},{7,5},{8,10},{10,8},{12,... | collective-permute-start | bytes 417800 | tf_op jit(solution)/shard_map/ppermute | solution.py:510
  30.1 6.2 %collective-permute-done.8.refs_2_ = bf16[544,128]{1,0:T(8,128)(2,1)S(1)} collective-permute-done((bf16[544,128]{1,0:T(8,128)(2,1)S(1)}, bf16[544,128]{1,0:T(8,128)(2,1)S(1)}, u32[]{:S(2)}, u32[]{:S(2)}) %collective-permute-start.8) | collective-permute-done | bytes 139296 | tf_op jit(solution)/shard_map/ppermute | solution.py:510
  36.3 0.0 collective-permute-done.9.refs_3_
  36.3 0.3 collective-permute-done.7.refs_1_
  36.6 0.9 %spread.1 = (bf16[1,128,512]{2,1,0:T(8,128)(2,1)}, bf16[1,128,512]{2,1,0:T(8,128)(2,1)}, bf16[1,128,512]{2,1,0:T(8,128)(2,1)}, bf16[1,128,512]{2,1,0:T(8,128)(2,1)}, f32[31,512]{1,0:T(8,128)}) custom-call(bf16[544,128]{1,0:T(8,128)(2,1)S(1)} %get-tuple-element.55.refs_0_, bf16[544,128]{1,0:T(8,128)(2,1)S(1)} %collective-permute-done.7.refs_1_, ...), custom_call_target="tpu_custom_call" | custom-call | tf_op jit(solution)/shard_map/spread/pallas_call | solution.py:610
  (2 shorter events, 0.0 us)
Async XLA Ops:
  0.6 7.0 %copy-start.2 = (bf16[1,128,512]{2,1,0:T(8,128)(2,1)S(1)}, bf16[1,128,512]{2,1,0:T(8,128)(2,1)}, u32[]{:S(2)}) copy-start(bf16[1,128,512]{2,1,0:T(8,128)(2,1)} %v_ref.3) | copy-start | bytes 393220
  0.6 7.0 %copy-start.1 = (bf16[1,128,512]{2,1,0:T(8,128)(2,1)S(1)}, bf16[1,128,512]{2,1,0:T(8,128)(2,1)}, u32[]{:S(2)}) copy-start(bf16[1,128,512]{2,1,0:T(8,128)(2,1)} %k_ref.3) | copy-start | bytes 393220
  0.7 7.0 %copy-start = (bf16[1,128,512]{2,1,0:T(8,128)(2,1)S(1)}, bf16[1,128,512]{2,1,0:T(8,128)(2,1)}, u32[]{:S(2)}) copy-start(bf16[1,128,512]{2,1,0:T(8,128)(2,1)} %q_ref.3) | copy-start | bytes 393220
  1.8 11.8 %collective-permute-start.3 = (bf16[3,128,128]{2,1,0:T(8,128)(2,1)S(1)}, bf16[3,128,128]{2,1,0:T(8,128)(2,1)S(1)}, u32[]{:S(2)}, u32[]{:S(2)}) collective-permute-start(bf16[3,128,128]{2,1,0:T(8,128)(2,1)S(1)} %get-tuple-element.36), channel_id=1, source_target_pairs={{0,6},{2,4},{4,2},{6,0},{1,7},{3,5},{5,3},{7,1},{8,14},{10,12},{12... | collective-permute-start | bytes 294920 | tf_op jit(solution)/shard_map/ppermute | solution.py:510
  6.9 0.7 %copy-start.4 = (s32[1,16]{1,0:T(1,128)S(1)}, s32[1,16]{1,0:T(1,128)}, u32[]{:S(2)}) copy-start(s32[1,16]{1,0:T(1,128)} %lens_ref.1) | copy-start | bytes 196
  6.9 10.4 %collective-permute-start.4 = (bf16[3,128,128]{2,1,0:T(8,128)(2,1)S(1)}, bf16[3,128,128]{2,1,0:T(8,128)(2,1)S(1)}, u32[]{:S(2)}, u32[]{:S(2)}) collective-permute-start(bf16[3,128,128]{2,1,0:T(8,128)(2,1)S(1)} %get-tuple-element.37), channel_id=1, source_target_pairs={{0,4},{2,6},{4,0},{6,2},{1,5},{3,7},{5,1},{7,3},{8,12},{10,14},{12... | collective-permute-start | bytes 294920 | tf_op jit(solution)/shard_map/ppermute | solution.py:510
  6.9 10.4 %collective-permute-start.5 = (bf16[3,128,128]{2,1,0:T(8,128)(2,1)S(1)}, bf16[3,128,128]{2,1,0:T(8,128)(2,1)S(1)}, u32[]{:S(2)}, u32[]{:S(2)}) collective-permute-start(bf16[3,128,128]{2,1,0:T(8,128)(2,1)S(1)} %get-tuple-element.38), channel_id=1, source_target_pairs={{0,2},{2,0},{4,6},{6,4},{1,3},{3,1},{5,7},{7,5},{8,10},{10,8},{12,... | collective-permute-start | bytes 294920 | tf_op jit(solution)/shard_map/ppermute | solution.py:510
  7.6 0.9 %copy-start.3 = (bf16[1,128,512]{2,1,0:T(8,128)(2,1)S(1)}, bf16[1,128,512]{2,1,0:T(8,128)(2,1)}, u32[]{:S(2)}) copy-start(bf16[1,128,512]{2,1,0:T(8,128)(2,1)} %c_ref.1) | copy-start | bytes 393220
  8.5 8.8 %copy-start.5 = (f32[31,512]{1,0:T(8,128)S(1)}, f32[31,512]{1,0:T(8,128)}, u32[]{:S(2)}) copy-start(f32[31,512]{1,0:T(8,128)} %refs_8_.3) | copy-start | bytes 190468
  9.9 10.9 %collective-permute-start = (bf16[128,128]{1,0:T(8,128)(2,1)S(1)}, bf16[128,128]{1,0:T(8,128)(2,1)S(1)}, u32[]{:S(2)}, u32[]{:S(2)}) collective-permute-start(bf16[128,128]{1,0:T(8,128)(2,1)S(1)} %get-tuple-element.32), channel_id=1, source_target_pairs={{0,6},{2,4},{4,2},{6,0},{1,7},{3,5},{5,3},{7,1},{8,14},{10,12},{12... | collective-permute-start | bytes 98312 | tf_op jit(solution)/shard_map/ppermute | solution.py:510
  13.7 7.1 %collective-permute-start.1 = (bf16[128,128]{1,0:T(8,128)(2,1)S(1)}, bf16[128,128]{1,0:T(8,128)(2,1)S(1)}, u32[]{:S(2)}, u32[]{:S(2)}) collective-permute-start(bf16[128,128]{1,0:T(8,128)(2,1)S(1)} %get-tuple-element.33), channel_id=1, source_target_pairs={{0,4},{2,6},{4,0},{6,2},{1,5},{3,7},{5,1},{7,3},{8,12},{10,14},{12... | collective-permute-start | bytes 98312 | tf_op jit(solution)/shard_map/ppermute | solution.py:510
  13.7 7.1 %collective-permute-start.2 = (bf16[128,128]{1,0:T(8,128)(2,1)S(1)}, bf16[128,128]{1,0:T(8,128)(2,1)S(1)}, u32[]{:S(2)}, u32[]{:S(2)}) collective-permute-start(bf16[128,128]{1,0:T(8,128)(2,1)S(1)} %get-tuple-element.34), channel_id=1, source_target_pairs={{0,2},{2,0},{4,6},{6,4},{1,3},{3,1},{5,7},{7,5},{8,10},{10,8},{12,... | collective-permute-start | bytes 98312 | tf_op jit(solution)/shard_map/ppermute | solution.py:510
  22.6 3.8 %collective-permute-start.6 = (f32[32,128]{1,0:T(8,128)S(1)}, f32[32,128]{1,0:T(8,128)S(1)}, u32[]{:S(2)}, u32[]{:S(2)}) collective-permute-start(f32[32,128]{1,0:T(8,128)S(1)} %get-tuple-element.54.refs_4_), channel_id=1, source_target_pairs={{0,8},{8,0},{1,9},{9,1},{2,10},{10,2},{3,11},{11,3},{4,12},{12,4},... | collective-permute-start | bytes 49160 | tf_op jit(solution)/shard_map/ppermute | solution.py:577
  26.4 9.9 %collective-permute-start.8 = (bf16[544,128]{1,0:T(8,128)(2,1)S(1)}, bf16[544,128]{1,0:T(8,128)(2,1)S(1)}, u32[]{:S(2)}, u32[]{:S(2)}) collective-permute-start(bf16[544,128]{1,0:T(8,128)(2,1)S(1)} %get-tuple-element.57), channel_id=1, source_target_pairs={{0,4},{2,6},{4,0},{6,2},{1,5},{3,7},{5,1},{7,3},{8,12},{10,14},{12... | collective-permute-start | bytes 417800 | tf_op jit(solution)/shard_map/ppermute | solution.py:510
  26.5 9.8 %collective-permute-start.9 = (bf16[544,128]{1,0:T(8,128)(2,1)S(1)}, bf16[544,128]{1,0:T(8,128)(2,1)S(1)}, u32[]{:S(2)}, u32[]{:S(2)}) collective-permute-start(bf16[544,128]{1,0:T(8,128)(2,1)S(1)} %get-tuple-element.58), channel_id=1, source_target_pairs={{0,6},{2,4},{4,2},{6,0},{1,7},{3,5},{5,3},{7,1},{8,14},{10,12},{12... | collective-permute-start | bytes 417800 | tf_op jit(solution)/shard_map/ppermute | solution.py:510
  29.1 7.5 %collective-permute-start.7 = (bf16[544,128]{1,0:T(8,128)(2,1)S(1)}, bf16[544,128]{1,0:T(8,128)(2,1)S(1)}, u32[]{:S(2)}, u32[]{:S(2)}) collective-permute-start(bf16[544,128]{1,0:T(8,128)(2,1)S(1)} %get-tuple-element.56), channel_id=1, source_target_pairs={{0,2},{2,0},{4,6},{6,4},{1,3},{3,1},{5,7},{7,5},{8,10},{10,8},{12,... | collective-permute-start | bytes 417800 | tf_op jit(solution)/shard_map/ppermute | solution.py:510

commit v4 on v3

--- a/solution.py
+++ b/solution.py
@@ -380,10 +380,18 @@
     lax.fori_loop(0, length // chunk, some_rows, 0)
 
 
+def split_heads(wide):
+    lane_head = lax.broadcasted_iota(jnp.int32, (1, LANES), 1) // HDIM
+    return [jnp.where(lane_head == head, wide, 0.0).astype(jnp.bfloat16) for head in range(LANES // HDIM)]
+
+
 def conv_back_kernel(ranks, frames, *refs):
+    half = ranks // 2
     cots = refs[: ranks - 1]
-    own_ref, att_ref, pre_ref, after_ref, before_ref, w_ref = refs[ranks - 1 : ranks + 5]
-    mixed_ref, g_att, taps_ref, cot, grad_pad, tap_sum, w_own, w_sem = refs[ranks + 5 :]
+    own_ref, pre_ref, after_ref, before_ref, soft_ref, w_ref = refs[ranks - 1 : ranks + 5]
+    mixed_ref, g_att, res_v, grad_pad = refs[ranks + 5 : ranks + 9]
+    early = refs[ranks + 9 : ranks + 9 + half]
+    cot, w_own, w_sem = refs[ranks + 9 + half :]
     me = lax.axis_index("seq")
     length = ranks * frames
     copy = pltpu.make_async_copy(w_ref.at[:, lanes_at(me)], w_own, w_sem)
@@ -399,16 +407,13 @@
     mixed_ref[...] = (pre * gate).astype(jnp.bfloat16)
     conv_grad = cot[...].astype(jnp.float32) * gate * (1.0 + pre * (1.0 - gate))
     grad_pad[PAD : PAD + length, :] = conv_grad.astype(jnp.bfloat16).astype(jnp.float32)
-    tap_sum[...] = jnp.zeros(tap_sum.shape, jnp.float32)
     copy.wait()
-
     chunk = 64
 
     def some_rows(number, carry):
         base = pl.multiple_of(number * chunk, chunk)
         rows = pl.ds(base, chunk)
         after, before = after_ref[rows, :], before_ref[rows, :]
-        own_att = att_ref[pl.ds(base + PAD, chunk), :]
         total = jnp.zeros((chunk, LANES), jnp.float32)
         for tap in range(KERNEL):
             off = tap - HALF
@@ -418,43 +423,69 @@
             if off < 0:
                 piece = jnp.where(after >= -off, piece, 0.0)
             total = total + w_own[tap : tap + 1, :] * piece
-            part = (own_att * piece).reshape(chunk // 8, 8, LANES)
-            tap_sum[tap] = tap_sum[tap] + jnp.sum(part, axis=0)
         g_att[rows, :] = total.astype(jnp.bfloat16)
         return carry
 
     lax.fori_loop(0, length // chunk, some_rows, 0)
+    g_heads = split_heads(g_att[...].astype(jnp.float32))
+    grad_v = mm(soft_ref[0], g_heads[0])
+    for head in range(1, LANES // HDIM):
+        grad_v = grad_v + mm(soft_ref[head], g_heads[head])
+    res_v[...] = grad_v.astype(jnp.bfloat16)
+    for step, out in zip(range(half, ranks), early):
+        rows = rows_at(me ^ step, frames)
+        out[0:frames, :] = mixed_ref[rows, :]
+        out[frames:, :] = res_v[rows, :]
+
+
+def taps_kernel(att_ref, grad_pad, after_ref, before_ref, taps_ref, tap_sum):
+    length = after_ref.shape[0]
+    tap_sum[...] = jnp.zeros(tap_sum.shape, jnp.float32)
+    chunk = 64
+
+    def some_rows(number, carry):
+        base = pl.multiple_of(number * chunk, chunk)
+        rows = pl.ds(base, chunk)
+        after, before = after_ref[rows, :], before_ref[rows, :]
+        own_grad = grad_pad[pl.ds(base + PAD, chunk), :]
+        for tap in range(KERNEL):
+            off = tap - HALF
+            piece = att_ref[pl.ds(base + (PAD + off), chunk), :]
+            if off > 0:
+                piece = jnp.where(after >= off, piece, 0.0)
+            if off < 0:
+                piece = jnp.where(before >= -off, piece, 0.0)
+            part = (own_grad * piece).reshape(chunk // 8, 8, LANES)
+            tap_sum[tap] = tap_sum[tap] + jnp.sum(part, axis=0)
+        return carry
+
+    lax.fori_loop(0, length // chunk, some_rows, 0)
     taps_ref[...] = jnp.sum(tap_sum[...], axis=1)
 
 
-def backward_kernel(soft_ref, att_ref, g_att, q_ref, k_t_ref, v_ref, res_q, res_k, res_v, grad_t):
+def backward_kernel(soft_ref, att_ref, g_att, q_ref, k_t_ref, v_ref, res_q, res_k, grad_t):
     length = v_ref.shape[0]
-    heads = LANES // HDIM
-    lane_head = lax.broadcasted_iota(jnp.int32, (1, LANES), 1) // HDIM
     g_wide = g_att[...].astype(jnp.float32)
     products_t = (g_wide * att_ref[PAD : PAD + length, :]).T
-    g_heads = [jnp.where(lane_head == head, g_wide, 0.0).astype(jnp.bfloat16) for head in range(heads)]
+    g_heads = split_heads(g_wide)
     wide = 256
-    grad_v = jnp.zeros((length, LANES), jnp.float32)
     grad_k = jnp.zeros((length, LANES), jnp.float32)
-    for head in range(heads):
+    for head in range(LANES // HDIM):
         rows = slice(head * HDIM, (head + 1) * HDIM)
         delta = jnp.sum(products_t[rows], axis=0, keepdims=True)
         for start in range(0, length, wide):
             cols = slice(start, start + wide)
-            soft = soft_ref[head, :, cols]
             slopes = mm_nt(v_ref[...], g_heads[head][cols])
-            mixed_grad = (soft.astype(jnp.float32) * (slopes - delta[:, cols])).astype(jnp.bfloat16)
-            grad_v = grad_v + mm(soft, g_heads[head][cols])
+            soft = soft_ref[head, :, cols].astype(jnp.float32)
+            mixed_grad = (soft * (slopes - delta[:, cols])).astype(jnp.bfloat16)
             grad_k = grad_k + mm(mixed_grad, q_ref[head, cols, :])
             grad_t[rows, cols] = mm(k_t_ref[rows, :], mixed_grad) * (1.0 / math.sqrt(HDIM))
     res_k[...] = grad_k.astype(jnp.bfloat16)
-    res_v[...] = grad_v.astype(jnp.bfloat16)
     res_q[...] = grad_t[...].T.astype(jnp.bfloat16)
 
 
-def block_kernel(steps, frames, *refs):
-    sources, tap_refs, outs = refs[:4], refs[4 : -len(steps)], refs[-len(steps) :]
+def block_kernel(steps, frames, count, *refs):
+    sources, tap_refs, outs = refs[:count], refs[count : -len(steps)], refs[-len(steps) :]
     me = lax.axis_index("seq")
     taps = tap_refs[0][...]
     for other in tap_refs[1:]:
@@ -463,18 +494,32 @@
         rows = rows_at(me ^ step, frames)
         for place, source in enumerate(sources):
             out[place * frames : (place + 1) * frames, :] = source[rows, :]
-        out[4 * frames :, :] = taps.astype(jnp.bfloat16)
+        out[count * frames :, :] = taps.astype(jnp.bfloat16)
+
+
+def stage_kernel(*refs):
+    half = len(refs) // 2
+    for source, target in zip(refs[:half], refs[half:]):
+        target[...] = source[...]
 
 
 def spread_kernel(ranks, frames, *refs):
-    blocks = refs[:ranks]
-    targets, taps_ref = refs[ranks : ranks + 4], refs[ranks + 4]
+    half = ranks // 2
+    near, far, early = refs[:half], refs[half:ranks], refs[ranks : ranks + half]
+    targets, taps_ref = refs[ranks + half : ranks + half + 4], refs[ranks + half + 4]
     me = lax.axis_index("seq")
     for step in range(ranks):
         lanes = lanes_at(me ^ step)
-        for place, target in enumerate(targets):
-            target[0, :, lanes] = blocks[step][place * frames : (place + 1) * frames, :]
-        taps = blocks[step][4 * frames :, :].astype(jnp.float32)
+        if step < half:
+            parts = [(near[step], place) for place in range(4)]
+            last = near[step], 4
+        else:
+            late, soon = far[step - half], early[step - half]
+            parts = [(late, 0), (late, 1), (soon, 0), (soon, 1)]
+            last = late, 2
+        for target, (source, place) in zip(targets, parts):
+            target[0, :, lanes] = source[place * frames : (place + 1) * frames, :]
+        taps = last[0][last[1] * frames :, :].astype(jnp.float32)
         taps_ref[:, lanes] = taps[:KERNEL]
 
 
@@ -555,66 +600,89 @@
         name="forward",
     )(*[received[step] for step in order], own, col, row, after, before, conv_weight)
 
-    mixed, g_att, own_taps = pl.pallas_call(
+    half = ranks // 2
+    wide = struct((length, LANES), bf16)
+    mixed, g_att, grad_v, grad_pad, *early = pl.pallas_call(
         functools.partial(conv_back_kernel, ranks, frames),
-        out_shape=[struct((length, LANES), bf16)] * 2 + [struct((taps, LANES), f32)],
+        out_shape=[wide] * 3
+        + [struct((length + 2 * PAD, LANES), f32)]
+        + [struct((2 * frames, LANES), bf16)] * half,
         in_specs=[vmem] * (ranks + 4) + [anywhere],
-        out_specs=[vmem] * 3,
+        out_specs=[vmem] * (4 + half),
         scratch_shapes=[
             VMEM((length, LANES), bf16),
-            VMEM((length + 2 * PAD, LANES), f32),
-            VMEM((taps, 8, LANES), f32),
             VMEM((KERNEL, LANES), f32),
             pltpu.SemaphoreType.DMA,
         ],
         compiler_params=params,
         cost_estimate=cost(400 * MIB, 3 * MIB),
         name="conv_back",
-    )(*[cots[step] for step in order], own, att, pre, after, before, conv_weight)
-
+    )(*[cots[step] for step in order], own, pre, after, before, soft, conv_weight)
+    early = [swap(early[step - half], step) for step in range(half, ranks)]
+
+    own_taps = pl.pallas_call(
+        taps_kernel,
+        out_shape=struct((taps, LANES), f32),
+        in_specs=[vmem] * 4,
+        out_specs=vmem,
+        scratch_shapes=[VMEM((taps, 8, LANES), f32)],
+        compiler_params=params,
+        cost_estimate=cost(MIB, MIB // 64),
+        name="taps",
+    )(att, grad_pad, after, before)
     copies = lax.axis_size("dp")
     part_taps = [own_taps] + [
         lax.ppermute(own_taps, "dp", [(one, (one + shift) % copies) for one in range(copies)])
         for shift in range(1, copies)
     ]
 
-    results = pl.pallas_call(
+    grad_q, grad_k = pl.pallas_call(
         backward_kernel,
-        out_shape=[struct((length, LANES), bf16)] * 3,
+        out_shape=[wide] * 2,
         in_specs=[vmem] * 6,
-        out_specs=[vmem] * 3,
+        out_specs=[vmem] * 2,
         scratch_shapes=[VMEM((LANES, length), f32)],
         compiler_params=params,
-        cost_estimate=cost(800 * MIB, 3 * MIB),
+        cost_estimate=cost(MIB, MIB // 64),
         name="backward",
     )(soft, att, g_att, q_heads, k_t, v_full)
 
-    def blocks_of(steps):
+    def blocks_of(steps, *sources):
+        rows = len(sources) * frames + taps
         return pl.pallas_call(
-            functools.partial(block_kernel, steps, frames),
-            out_shape=[struct((4 * frames + taps, LANES), bf16)] * len(steps),
-            in_specs=[vmem] * (4 + copies),
+            functools.partial(block_kernel, steps, frames, len(sources)),
+            out_shape=[struct((rows, LANES), bf16)] * len(steps),
+            in_specs=[vmem] * (len(sources) + copies),
             out_specs=[vmem] * len(steps),
             compiler_params=params,
-            cost_estimate=cost(MIB, MIB),
+            cost_estimate=cost(MIB, MIB // 64),
             name="blocks",
-        )(mixed, *results, *part_taps)
-
-    half = ranks // 2
-    far = blocks_of(list(range(half, ranks)))
-    near = blocks_of(list(range(half)))
-    back = {step: swap(far[step - half], step) for step in range(half, ranks)}
-    back |= {step: swap(near[step], step) for step in range(1, half)}
-    back[0] = near[0]
-
-    return pl.pallas_call(
+        )(*sources, *part_taps)
+
+    far = blocks_of(range(half, ranks), grad_q, grad_k)
+    near = blocks_of(range(half), grad_q, grad_k, mixed, grad_v)
+    far = [swap(far[step - half], step) for step in range(half, ranks)]
+    near = [near[0]] + [swap(near[step], step) for step in range(1, half)]
+
+    early = pl.pallas_call(
+        stage_kernel,
+        out_shape=[struct((2 * frames, LANES), bf16)] * half,
+        in_specs=[vmem] * half,
+        out_specs=[vmem] * half,
+        compiler_params=params,
+        cost_estimate=cost(16384 * MIB, 64 * MIB),
+        name="stage",
+    )(*early)
+
+    grad_q, grad_k, mixed, grad_v, grad_taps = pl.pallas_call(
         functools.partial(spread_kernel, ranks, frames),
         out_shape=[struct(queries.shape, bf16)] * 4 + [struct(conv_weight.shape, f32)],
-        in_specs=[vmem] * ranks,
+        in_specs=[vmem] * (ranks + half),
         out_specs=[vmem] * 5,
         compiler_params=params,
         name="spread",
-    )(*[back[step] for step in range(ranks)])
+    )(*near, *far, *early)
+    return (mixed, grad_q, grad_k, grad_v, grad_taps)
 
 
 def on_device_any(queries, keys, values, cotangent, conv_weight, rec_lengths):

time: 37.7 us -> 40.4 us (1.072)
  starting transfers between devices: 16.1 us -> 18.7 us
  Pallas kernels: 10.1 us -> 11.1 us
  waiting for transfers between devices: 9.73 us -> 8.79 us
    ppermute x9 -> x11, starting transfers between devices: 14.5 us -> 17.2 us  [swap(): lax.ppermute(array, 'seq', [(rank, rank ^ step) for rank in range(ranks)])]
    pallas_call x3 -> x5, Pallas kernels: 1.48 us -> 2.56 us  [the longest x1 1.39 us: on_device_heads(): pl.pallas_call(backward_kernel, out_shape=[wide] * 2, in_specs=[vmem] * 6...]
    ppermute x9 -> x11, waiting for transfers between devices: 8.91 us -> 7.94 us  [swap(): lax.ppermute(array, 'seq', [(rank, rank ^ step) for rank in range(ranks)])]
  transfers between devices with their start and end apart: 10 -> 12, of which waited for: 4 -> 5; matrix products, arithmetic and copies ran while one was open for 0% -> 0% of each run, Pallas kernels for 16% -> 18%
where the time goes in v4:
time: 40.4 us; the launch traced here: 40.3 us
  starting transfers between devices  18.7 us (46%)
  Pallas kernels  11.1 us (27%)
  waiting for transfers between devices  8.79 us (22%)
  local copies, waits for them, and re-layouts  0.92 us (2%)
  between operations  0.77 us (2%)
    ppermute x11, starting transfers between devices, swap(): lax.ppermute(array, 'seq', [(rank, rank ^ step) for rank in range(ranks)])  17.2 us
    ppermute x11, waiting for transfers between devices, swap(): lax.ppermute(array, 'seq', [(rank, rank ^ step) for rank in range(ranks)])  7.94 us
    pallas_call x1, Pallas kernels, on_device_heads(): pl.pallas_call(functools.partial(forward_kernel, ranks, frames), out_shap...  3.42 us
    pallas_call x1, Pallas kernels, on_device_heads(): pl.pallas_call(functools.partial(conv_back_kernel, ranks, frames), out_sh...  1.71 us
    ppermute x1, starting transfers between devices, on_device_heads(): lax.ppermute(own_taps, 'dp', [(one, (one + shift) % copies) for one in ra...  1.56 us
    pallas_call x1, Pallas kernels, on_device_heads(): pl.pallas_call(backward_kernel, out_shape=[wide] * 2, in_specs=[vmem] * 6...  1.39 us
    pallas_call x1, Pallas kernels, on_device_heads(): pl.pallas_call(functools.partial(mask_kernel, ranks, length), out_shape=[...  1.32 us
    pallas_call x1, Pallas kernels, on_device_heads(): pl.pallas_call(functools.partial(pack_kernel, ranks), out_shape=[struct((...  1.16 us
  transfers between devices with their start and end apart: 12, of which 5 were waited for; matrix products, arithmetic and copies ran while one was open for 0% of the time, Pallas kernels for 18%

profile of v4, /device:TPU:0, one launch (start us, length us, event | category | flops | bytes accessed | tf_op | source)
XLA Modules:
  0.0 40.3 jit_solution(1858620802368750169)
XLA Ops:
  0.6 0.0 copy-start.2
  0.6 0.0 copy-start.1
  0.7 0.0 copy-start
  0.7 1.2 %pack.1 = (bf16[3,128,128]{2,1,0:T(8,128)(2,1)S(1)}, bf16[3,128,128]{2,1,0:T(8,128)(2,1)S(1)}, bf16[3,128,128]{2,1,0:T(8,128)(2,1)S(1)}) custom-call(bf16[1,128,512]{2,1,0:T(8,128)(2,1)} %q_ref.3, bf16[1,128,512]{2,1,0:T(8,128)(2,1)} %k_ref.3, bf16[1,128,512]{2,1,0:T(8,128)(2,1)} %v_ref.3), custom_call_target="tpu_custom_call" | custom-call | tf_op jit(solution)/shard_map/pack/pallas_call | solution.py:544
  1.8 5.1 %collective-permute-start = (bf16[3,128,128]{2,1,0:T(8,128)(2,1)S(1)}, bf16[3,128,128]{2,1,0:T(8,128)(2,1)S(1)}, u32[]{:S(2)}, u32[]{:S(2)}) collective-permute-start(bf16[3,128,128]{2,1,0:T(8,128)(2,1)S(1)} %get-tuple-element.41), channel_id=1, source_target_pairs={{0,6},{2,4},{4,2},{6,0},{1,7},{3,5},{5,3},{7,1},{8,14},{10,12},{12... | collective-permute-start | bytes 294920 | tf_op jit(solution)/shard_map/ppermute | solution.py:555
  6.9 0.0 copy-start.5
  6.9 0.0 collective-permute-start.1
  6.9 0.6 %collective-permute-start.2 = (bf16[3,128,128]{2,1,0:T(8,128)(2,1)S(1)}, bf16[3,128,128]{2,1,0:T(8,128)(2,1)S(1)}, u32[]{:S(2)}, u32[]{:S(2)}) collective-permute-start(bf16[3,128,128]{2,1,0:T(8,128)(2,1)S(1)} %get-tuple-element.43), channel_id=1, source_target_pairs={{0,2},{2,0},{4,6},{6,4},{1,3},{3,1},{5,7},{7,5},{8,10},{10,8},{12,... | collective-permute-start | bytes 294920 | tf_op jit(solution)/shard_map/ppermute | solution.py:555
  7.6 0.0 copy-done.2
  7.6 0.0 copy-done.1
  7.6 0.0 copy-done
  7.6 0.0 copy-done.5
  7.6 0.0 copy-start.3
  7.6 0.9 %copy-done.3 = bf16[1,128,512]{2,1,0:T(8,128)(2,1)S(1)} copy-done((bf16[1,128,512]{2,1,0:T(8,128)(2,1)S(1)}, bf16[1,128,512]{2,1,0:T(8,128)(2,1)}, u32[]{:S(2)}) %copy-start.3) | copy-done | bytes 131096
  8.5 0.0 copy-start.4
  8.5 1.3 %masks.1 = (bf16[128,128]{1,0:T(8,128)(2,1)S(1)}, bf16[128,128]{1,0:T(8,128)(2,1)S(1)}, bf16[128,128]{1,0:T(8,128)(2,1)S(1)}, bf16[4,128,128]{2,1,0:T(8,128)(2,1...) custom-call(s32[1,16]{1,0:T(1,128)S(1)} %copy-done.5, ...), custom_call_target="tpu_custom_call" | custom-call | flops 4194304 | bytes 1048576 | tf_op jit(solution)/shard_map/masks/pallas_call | solution.py:560
  9.9 3.8 %collective-permute-start.3 = (bf16[128,128]{1,0:T(8,128)(2,1)S(1)}, bf16[128,128]{1,0:T(8,128)(2,1)S(1)}, u32[]{:S(2)}, u32[]{:S(2)}) collective-permute-start(bf16[128,128]{1,0:T(8,128)(2,1)S(1)} %get-tuple-element.51), channel_id=1, source_target_pairs={{0,6},{2,4},{4,2},{6,0},{1,7},{3,5},{5,3},{7,1},{8,14},{10,12},{12... | collective-permute-start | bytes 98312 | tf_op jit(solution)/shard_map/ppermute | solution.py:555
  13.7 0.0 collective-permute-start.4
  13.7 0.0 collective-permute-done.refs_0_
  13.7 1.3 %collective-permute-start.5 = (bf16[128,128]{1,0:T(8,128)(2,1)S(1)}, bf16[128,128]{1,0:T(8,128)(2,1)S(1)}, u32[]{:S(2)}, u32[]{:S(2)}) collective-permute-start(bf16[128,128]{1,0:T(8,128)(2,1)S(1)} %get-tuple-element.53), channel_id=1, source_target_pairs={{0,2},{2,0},{4,6},{6,4},{1,3},{3,1},{5,7},{7,5},{8,10},{10,8},{12,... | collective-permute-start | bytes 98312 | tf_op jit(solution)/shard_map/ppermute | solution.py:555
  15.0 2.3 %collective-permute-done.1.refs_1_ = bf16[3,128,128]{2,1,0:T(8,128)(2,1)S(1)} collective-permute-done((bf16[3,128,128]{2,1,0:T(8,128)(2,1)S(1)}, bf16[3,128,128]{2,1,0:T(8,128)(2,1)S(1)}, u32[]{:S(2)}, u32[]{:S(2)}) %collective-permute-start.1) | collective-permute-done | bytes 98336 | tf_op jit(solution)/shard_map/ppermute | solution.py:555
  17.3 0.0 collective-permute-done.2.refs_2_
  17.3 0.0 copy-done.4
  17.3 3.4 %forward.1 = (bf16[2,512,512]{2,1,0:T(8,128)(2,1)S(1)}, f32[544,128]{1,0:T(8,128)S(1)}, f32[512,128]{1,0:T(8,128)S(1)}, bf16[2,512,128]{2,1,0:T(8,128)(2,1)S(1)}...) custom-call(bf16[3,128,128]{2,1,0:T(8,128)(2,1)S(1)} %collective-permute-done.refs_0_, ...), custom_call_target="tpu_custom_call" | custom-call | flops 419430400 | bytes 3145728 | tf_op jit(solution)/shard_map/forward/pallas_call | solution.py:579
  20.7 0.0 collective-permute-done.3.refs_0_
  20.8 0.0 collective-permute-done.4.refs_1_
  20.8 0.0 collective-permute-done.5.refs_2_
  20.8 1.7 %conv_back.1 = (bf16[512,128]{1,0:T(8,128)(2,1)S(1)}, bf16[512,128]{1,0:T(8,128)(2,1)S(1)}, bf16[512,128]{1,0:T(8,128)(2,1)S(1)}, f32[544,128]{1,0:T(8,128)S(1)}...) custom-call(bf16[128,128]{1,0:T(8,128)(2,1)S(1)} %collective-permute-done.3.refs_0_, ...), custom_call_target="tpu_custom_call" | custom-call | flops 419430400 | bytes 3145728 | tf_op jit(solution)/shard_map/conv_back/pallas_call | solution.py:605
  22.5 0.1 collective-permute-start.10
  22.6 2.6 %collective-permute-start.11 = (bf16[256,128]{1,0:T(8,128)(2,1)S(1)}, bf16[256,128]{1,0:T(8,128)(2,1)S(1)}, u32[]{:S(2)}, u32[]{:S(2)}) collective-permute-start(bf16[256,128]{1,0:T(8,128)(2,1)S(1)} %get-tuple-element.69), channel_id=1, source_target_pairs={{0,6},{2,4},{4,2},{6,0},{1,7},{3,5},{5,3},{7,1},{8,14},{10,12},{12... | collective-permute-start | bytes 196616 | tf_op jit(solution)/shard_map/ppermute | solution.py:555
  25.2 1.1 %taps.1.refs_4_.refs_2_ = f32[32,128]{1,0:T(8,128)S(1)} custom-call(f32[544,128]{1,0:T(8,128)S(1)} %get-tuple-element.50.att_ref, f32[544,128]{1,0:T(8,128)S(1)} %get-tuple-element.63.grad_pad, s32[512,128]{1,0:T(8,128)S(1)} %get-tuple-element.47.refs_6_.refs_5_.after_ref, s32[512,128]{1,0:T(8,128)S(1)} %get-tuple-element.48.refs_7_.refs_6_.before_ref), custom_call_target="tpu_custom_call" | custom-call | flops 1048576 | bytes 16384 | tf_op jit(solution)/shard_map/taps/pallas_call | solution.py:623
  26.3 1.6 %collective-permute-start.6 = (f32[32,128]{1,0:T(8,128)S(1)}, f32[32,128]{1,0:T(8,128)S(1)}, u32[]{:S(2)}, u32[]{:S(2)}) collective-permute-start(f32[32,128]{1,0:T(8,128)S(1)} %taps.1.refs_4_.refs_2_), channel_id=1, source_target_pairs={{0,8},{8,0},{1,9},{9,1},{2,10},{10,2},{3,11},{11,3},{4,12},{12,4},... | collective-permute-start | bytes 49160 | tf_op jit(solution)/shard_map/ppermute | solution.py:635
  27.9 1.4 %backward.1 = (bf16[512,128]{1,0:T(8,128)(2,1)S(1)}, bf16[512,128]{1,0:T(8,128)(2,1)S(1)}) custom-call(bf16[2,512,512]{2,1,0:T(8,128)(2,1)S(1)} %get-tuple-element.49.refs_7_.soft_ref, f32[544,128]{1,0:T(8,128)S(1)} %get-tuple-element.50.att_ref, bf16[512,128]{1,0:T(8,128)(2,1)S(1)} %get-tuple-element.55.g_att, ...), custom_call_target="tpu_custom_call" | custom-call | flops 1048576 | bytes 16384 | tf_op jit(solution)/shard_map/backward/pallas_call | solution.py:639
  29.3 0.8 %collective-permute-done.6.refs_5_.refs_3_ = f32[32,128]{1,0:T(8,128)S(1)} collective-permute-done((f32[32,128]{1,0:T(8,128)S(1)}, f32[32,128]{1,0:T(8,128)S(1)}, u32[]{:S(2)}, u32[]{:S(2)}) %collective-permute-start.6) | collective-permute-done | bytes 16416 | tf_op jit(solution)/shard_map/ppermute | solution.py:635
  30.1 2.0 %collective-permute-start.8 = (bf16[288,128]{1,0:T(8,128)(2,1)S(1)}, bf16[288,128]{1,0:T(8,128)(2,1)S(1)}, u32[]{:S(2)}, u32[]{:S(2)}) collective-permute-start(bf16[288,128]{1,0:T(8,128)(2,1)S(1)} %get-tuple-element.66), channel_id=1, source_target_pairs={{0,4},{2,6},{4,0},{6,2},{1,5},{3,7},{5,1},{7,3},{8,12},{10,14},{12... | collective-permute-start | bytes 221192 | tf_op jit(solution)/shard_map/ppermute | solution.py:555
  32.1 1.3 %collective-permute-start.9 = (bf16[288,128]{1,0:T(8,128)(2,1)S(1)}, bf16[288,128]{1,0:T(8,128)(2,1)S(1)}, u32[]{:S(2)}, u32[]{:S(2)}) collective-permute-start(bf16[288,128]{1,0:T(8,128)(2,1)S(1)} %get-tuple-element.67), channel_id=1, source_target_pairs={{0,6},{2,4},{4,2},{6,0},{1,7},{3,5},{5,3},{7,1},{8,14},{10,12},{12... | collective-permute-start | bytes 221192 | tf_op jit(solution)/shard_map/ppermute | solution.py:555
  33.5 0.3 collective-permute-start.7
  33.8 0.0 collective-permute-done.10.refs_0_
  33.8 0.0 collective-permute-done.11.refs_1_
  33.8 2.4 %collective-permute-done.8.refs_2_ = bf16[288,128]{1,0:T(8,128)(2,1)S(1)} collective-permute-done((bf16[288,128]{1,0:T(8,128)(2,1)S(1)}, bf16[288,128]{1,0:T(8,128)(2,1)S(1)}, u32[]{:S(2)}, u32[]{:S(2)}) %collective-permute-start.8) | collective-permute-done | bytes 73760 | tf_op jit(solution)/shard_map/ppermute | solution.py:555
  36.2 2.2 %collective-permute-done.9.refs_3_ = bf16[288,128]{1,0:T(8,128)(2,1)S(1)} collective-permute-done((bf16[288,128]{1,0:T(8,128)(2,1)S(1)}, bf16[288,128]{1,0:T(8,128)(2,1)S(1)}, u32[]{:S(2)}, u32[]{:S(2)}) %collective-permute-start.9) | collective-permute-done | bytes 73760 | tf_op jit(solution)/shard_map/ppermute | solution.py:555
  38.4 1.0 %collective-permute-done.7.refs_1_ = bf16[544,128]{1,0:T(8,128)(2,1)S(1)} collective-permute-done((bf16[544,128]{1,0:T(8,128)(2,1)S(1)}, bf16[544,128]{1,0:T(8,128)(2,1)S(1)}, u32[]{:S(2)}, u32[]{:S(2)}) %collective-permute-start.7) | collective-permute-done | bytes 139296 | tf_op jit(solution)/shard_map/ppermute | solution.py:555
  39.4 0.9 %spread.1 = (bf16[1,128,512]{2,1,0:T(8,128)(2,1)}, bf16[1,128,512]{2,1,0:T(8,128)(2,1)}, bf16[1,128,512]{2,1,0:T(8,128)(2,1)}, bf16[1,128,512]{2,1,0:T(8,128)(2,1)}, f32[31,512]{1,0:T(8,128)}) custom-call(bf16[544,128]{1,0:T(8,128)(2,1)S(1)} %get-tuple-element.64.refs_0_, bf16[544,128]{1,0:T(8,128)(2,1)S(1)} %collective-permute-done.7.refs_1_, ...), custom_call_target="tpu_custom_call" | custom-call | tf_op jit(solution)/shard_map/spread/pallas_call | solution.py:677
  (3 shorter events, 0.0 us)
Async XLA Ops:
  0.6 7.0 %copy-start.2 = (bf16[1,128,512]{2,1,0:T(8,128)(2,1)S(1)}, bf16[1,128,512]{2,1,0:T(8,128)(2,1)}, u32[]{:S(2)}) copy-start(bf16[1,128,512]{2,1,0:T(8,128)(2,1)} %v_ref.3) | copy-start | bytes 393220
  0.6 7.0 %copy-start.1 = (bf16[1,128,512]{2,1,0:T(8,128)(2,1)S(1)}, bf16[1,128,512]{2,1,0:T(8,128)(2,1)}, u32[]{:S(2)}) copy-start(bf16[1,128,512]{2,1,0:T(8,128)(2,1)} %k_ref.3) | copy-start | bytes 393220
  0.7 7.0 %copy-start = (bf16[1,128,512]{2,1,0:T(8,128)(2,1)S(1)}, bf16[1,128,512]{2,1,0:T(8,128)(2,1)}, u32[]{:S(2)}) copy-start(bf16[1,128,512]{2,1,0:T(8,128)(2,1)} %q_ref.3) | copy-start | bytes 393220
  1.8 11.8 %collective-permute-start = (bf16[3,128,128]{2,1,0:T(8,128)(2,1)S(1)}, bf16[3,128,128]{2,1,0:T(8,128)(2,1)S(1)}, u32[]{:S(2)}, u32[]{:S(2)}) collective-permute-start(bf16[3,128,128]{2,1,0:T(8,128)(2,1)S(1)} %get-tuple-element.41), channel_id=1, source_target_pairs={{0,6},{2,4},{4,2},{6,0},{1,7},{3,5},{5,3},{7,1},{8,14},{10,12},{12... | collective-permute-start | bytes 294920 | tf_op jit(solution)/shard_map/ppermute | solution.py:555
  6.9 0.7 %copy-start.5 = (s32[1,16]{1,0:T(1,128)S(1)}, s32[1,16]{1,0:T(1,128)}, u32[]{:S(2)}) copy-start(s32[1,16]{1,0:T(1,128)} %lens_ref.1) | copy-start | bytes 196
  6.9 10.4 %collective-permute-start.1 = (bf16[3,128,128]{2,1,0:T(8,128)(2,1)S(1)}, bf16[3,128,128]{2,1,0:T(8,128)(2,1)S(1)}, u32[]{:S(2)}, u32[]{:S(2)}) collective-permute-start(bf16[3,128,128]{2,1,0:T(8,128)(2,1)S(1)} %get-tuple-element.42), channel_id=1, source_target_pairs={{0,4},{2,6},{4,0},{6,2},{1,5},{3,7},{5,1},{7,3},{8,12},{10,14},{12... | collective-permute-start | bytes 294920 | tf_op jit(solution)/shard_map/ppermute | solution.py:555
  6.9 10.4 %collective-permute-start.2 = (bf16[3,128,128]{2,1,0:T(8,128)(2,1)S(1)}, bf16[3,128,128]{2,1,0:T(8,128)(2,1)S(1)}, u32[]{:S(2)}, u32[]{:S(2)}) collective-permute-start(bf16[3,128,128]{2,1,0:T(8,128)(2,1)S(1)} %get-tuple-element.43), channel_id=1, source_target_pairs={{0,2},{2,0},{4,6},{6,4},{1,3},{3,1},{5,7},{7,5},{8,10},{10,8},{12,... | collective-permute-start | bytes 294920 | tf_op jit(solution)/shard_map/ppermute | solution.py:555
  7.6 0.9 %copy-start.3 = (bf16[1,128,512]{2,1,0:T(8,128)(2,1)S(1)}, bf16[1,128,512]{2,1,0:T(8,128)(2,1)}, u32[]{:S(2)}) copy-start(bf16[1,128,512]{2,1,0:T(8,128)(2,1)} %c_ref.1) | copy-start | bytes 393220
  8.5 8.8 %copy-start.4 = (f32[31,512]{1,0:T(8,128)S(1)}, f32[31,512]{1,0:T(8,128)}, u32[]{:S(2)}) copy-start(f32[31,512]{1,0:T(8,128)} %refs_8_.3) | copy-start | bytes 190468
  9.9 10.9 %collective-permute-start.3 = (bf16[128,128]{1,0:T(8,128)(2,1)S(1)}, bf16[128,128]{1,0:T(8,128)(2,1)S(1)}, u32[]{:S(2)}, u32[]{:S(2)}) collective-permute-start(bf16[128,128]{1,0:T(8,128)(2,1)S(1)} %get-tuple-element.51), channel_id=1, source_target_pairs={{0,6},{2,4},{4,2},{6,0},{1,7},{3,5},{5,3},{7,1},{8,14},{10,12},{12... | collective-permute-start | bytes 98312 | tf_op jit(solution)/shard_map/ppermute | solution.py:555
  13.7 7.1 %collective-permute-start.4 = (bf16[128,128]{1,0:T(8,128)(2,1)S(1)}, bf16[128,128]{1,0:T(8,128)(2,1)S(1)}, u32[]{:S(2)}, u32[]{:S(2)}) collective-permute-start(bf16[128,128]{1,0:T(8,128)(2,1)S(1)} %get-tuple-element.52), channel_id=1, source_target_pairs={{0,4},{2,6},{4,0},{6,2},{1,5},{3,7},{5,1},{7,3},{8,12},{10,14},{12... | collective-permute-start | bytes 98312 | tf_op jit(solution)/shard_map/ppermute | solution.py:555
  13.7 7.1 %collective-permute-start.5 = (bf16[128,128]{1,0:T(8,128)(2,1)S(1)}, bf16[128,128]{1,0:T(8,128)(2,1)S(1)}, u32[]{:S(2)}, u32[]{:S(2)}) collective-permute-start(bf16[128,128]{1,0:T(8,128)(2,1)S(1)} %get-tuple-element.53), channel_id=1, source_target_pairs={{0,2},{2,0},{4,6},{6,4},{1,3},{3,1},{5,7},{7,5},{8,10},{10,8},{12,... | collective-permute-start | bytes 98312 | tf_op jit(solution)/shard_map/ppermute | solution.py:555
  22.5 11.3 %collective-permute-start.10 = (bf16[256,128]{1,0:T(8,128)(2,1)S(1)}, bf16[256,128]{1,0:T(8,128)(2,1)S(1)}, u32[]{:S(2)}, u32[]{:S(2)}) collective-permute-start(bf16[256,128]{1,0:T(8,128)(2,1)S(1)} %get-tuple-element.68), channel_id=1, source_target_pairs={{0,4},{2,6},{4,0},{6,2},{1,5},{3,7},{5,1},{7,3},{8,12},{10,14},{12... | collective-permute-start | bytes 196616 | tf_op jit(solution)/shard_map/ppermute | solution.py:555
  22.6 11.2 %collective-permute-start.11 = (bf16[256,128]{1,0:T(8,128)(2,1)S(1)}, bf16[256,128]{1,0:T(8,128)(2,1)S(1)}, u32[]{:S(2)}, u32[]{:S(2)}) collective-permute-start(bf16[256,128]{1,0:T(8,128)(2,1)S(1)} %get-tuple-element.69), channel_id=1, source_target_pairs={{0,6},{2,4},{4,2},{6,0},{1,7},{3,5},{5,3},{7,1},{8,14},{10,12},{12... | collective-permute-start | bytes 196616 | tf_op jit(solution)/shard_map/ppermute | solution.py:555
  26.3 3.8 %collective-permute-start.6 = (f32[32,128]{1,0:T(8,128)S(1)}, f32[32,128]{1,0:T(8,128)S(1)}, u32[]{:S(2)}, u32[]{:S(2)}) collective-permute-start(f32[32,128]{1,0:T(8,128)S(1)} %taps.1.refs_4_.refs_2_), channel_id=1, source_target_pairs={{0,8},{8,0},{1,9},{9,1},{2,10},{10,2},{3,11},{11,3},{4,12},{12,4},... | collective-permute-start | bytes 49160 | tf_op jit(solution)/shard_map/ppermute | solution.py:635
  30.1 6.1 %collective-permute-start.8 = (bf16[288,128]{1,0:T(8,128)(2,1)S(1)}, bf16[288,128]{1,0:T(8,128)(2,1)S(1)}, u32[]{:S(2)}, u32[]{:S(2)}) collective-permute-start(bf16[288,128]{1,0:T(8,128)(2,1)S(1)} %get-tuple-element.66), channel_id=1, source_target_pairs={{0,4},{2,6},{4,0},{6,2},{1,5},{3,7},{5,1},{7,3},{8,12},{10,14},{12... | collective-permute-start | bytes 221192 | tf_op jit(solution)/shard_map/ppermute | solution.py:555
  32.1 6.3 %collective-permute-start.9 = (bf16[288,128]{1,0:T(8,128)(2,1)S(1)}, bf16[288,128]{1,0:T(8,128)(2,1)S(1)}, u32[]{:S(2)}, u32[]{:S(2)}) collective-permute-start(bf16[288,128]{1,0:T(8,128)(2,1)S(1)} %get-tuple-element.67), channel_id=1, source_target_pairs={{0,6},{2,4},{4,2},{6,0},{1,7},{3,5},{5,3},{7,1},{8,14},{10,12},{12... | collective-permute-start | bytes 221192 | tf_op jit(solution)/shard_map/ppermute | solution.py:555
  33.5 5.9 %collective-permute-start.7 = (bf16[544,128]{1,0:T(8,128)(2,1)S(1)}, bf16[544,128]{1,0:T(8,128)(2,1)S(1)}, u32[]{:S(2)}, u32[]{:S(2)}) collective-permute-start(bf16[544,128]{1,0:T(8,128)(2,1)S(1)} %get-tuple-element.65), channel_id=1, source_target_pairs={{0,2},{2,0},{4,6},{6,4},{1,3},{3,1},{5,7},{7,5},{8,10},{10,8},{12,... | collective-permute-start | bytes 417800 | tf_op jit(solution)/shard_map/ppermute | solution.py:555

commit v5 on v4

--- a/solution.py
+++ b/solution.py
@@ -255,14 +255,20 @@
     return pl.ds(pl.multiple_of(block * LANES, LANES), LANES)
 
 
-def pack_kernel(ranks, q_ref, k_ref, v_ref, *rest):
-    outs, (whole, sems) = rest[:-2], rest[-2:]
+def partners(ranks):
+    middle = ranks // 2
+    return [middle] + [step for step in range(ranks - 1, 0, -1) if step != middle]
+
+
+def pack_kernel(ranks, q_ref, k_ref, v_ref, c_ref, *rest):
+    outs, whole, sems = rest[: ranks - 1], *rest[ranks - 1 :]
     me = lax.axis_index("seq")
-    sources = (q_ref, k_ref, v_ref)
+    sources = (q_ref, k_ref, v_ref, c_ref)
     run_copies([(source.at[0], whole.at[place]) for place, source in enumerate(sources)], sems)
-    for step in range(ranks - 1, 0, -1):
-        for place in range(len(sources)):
-            outs[step - 1][place] = whole[place, :, lanes_at(me ^ step)]
+    for step in range(1, ranks):
+        lanes = lanes_at(me ^ step)
+        for place in range(outs[step - 1].shape[0]):
+            outs[step - 1][place] = whole[place, :, lanes]
 
 
 def run_copies(pairs, sems, meanwhile=None):
@@ -279,12 +285,14 @@
 
 
 def mask_kernel(ranks, length, lens_ref, q_ref, k_ref, v_ref, c_ref, *refs):
-    cot_refs = refs[: ranks - 1]
-    own_ref, col_ref, row_ref, after_ref, before_ref, sems = refs[ranks - 1 :]
+    late_ref, own_ref, col_ref, row_ref, after_ref, before_ref, sems = refs
     me = lax.axis_index("seq")
-    pairs = [(c_ref.at[0, :, lanes_at(me ^ step)], cot_refs[step - 1]) for step in range(1, ranks)]
-    for place, source in enumerate((q_ref, k_ref, v_ref, c_ref)):
-        pairs.append((source.at[0, :, lanes_at(me)], own_ref.at[place]))
+    lanes = lanes_at(me)
+    pairs = [
+        (source.at[0, :, lanes], own_ref.at[place])
+        for place, source in enumerate((q_ref, k_ref, v_ref, c_ref))
+    ]
+    pairs.append((c_ref.at[0, :, lanes_at(me ^ (ranks // 2))], late_ref))
 
     def extents():
         ends = []
@@ -320,7 +328,7 @@
 
 
 def forward_kernel(ranks, frames, *refs):
-    recvs = refs[: ranks - 1]
+    recvs = dict(zip(partners(ranks), refs))
     own_ref, col_ref, row_ref, after_ref, before_ref, w_ref = refs[ranks - 1 : ranks + 5]
     soft_ref, att_ref, pre_ref, q_ref, k_t_ref, v_ref = refs[ranks + 5 : ranks + 11]
     att_t_ref, k_full, q_full, w_own, w_sem = refs[ranks + 11 :]
@@ -331,7 +339,7 @@
     for place, target in enumerate((q_full, k_full, v_ref)):
         target[rows_at(me, frames), :] = own_ref[place]
         for step in range(1, ranks):
-            target[rows_at(me ^ step, frames), :] = recvs[ranks - 1 - step][place]
+            target[rows_at(me ^ step, frames), :] = recvs[step][place]
     heads = LANES // HDIM
     lane_head = lax.broadcasted_iota(jnp.int32, (1, LANES), 1) // HDIM
     scaled = q_full[...].astype(jnp.float32) * (1.0 / math.sqrt(HDIM))
@@ -386,19 +394,18 @@
 
 
 def conv_back_kernel(ranks, frames, *refs):
-    half = ranks // 2
     cots = refs[: ranks - 1]
     own_ref, pre_ref, after_ref, before_ref, soft_ref, w_ref = refs[ranks - 1 : ranks + 5]
-    mixed_ref, g_att, res_v, grad_pad = refs[ranks + 5 : ranks + 9]
-    early = refs[ranks + 9 : ranks + 9 + half]
-    cot, w_own, w_sem = refs[ranks + 9 + half :]
+    mixed_ref, g_att, res_v, grad_pad, early = refs[ranks + 5 : ranks + 10]
+    cot, w_own, w_sem = refs[ranks + 10 :]
     me = lax.axis_index("seq")
     length = ranks * frames
     copy = pltpu.make_async_copy(w_ref.at[:, lanes_at(me)], w_own, w_sem)
     copy.start()
     cot[rows_at(me, frames), :] = own_ref[3]
     for step in range(1, ranks):
-        cot[rows_at(me ^ step, frames), :] = cots[ranks - 1 - step][...]
+        block = cots[step - 1]
+        cot[rows_at(me ^ step, frames), :] = block[...] if step == ranks // 2 else block[3]
     zeros = jnp.zeros((PAD, LANES), jnp.float32)
     grad_pad[0:PAD, :] = zeros
     grad_pad[PAD + length :, :] = zeros
@@ -432,10 +439,9 @@
     for head in range(1, LANES // HDIM):
         grad_v = grad_v + mm(soft_ref[head], g_heads[head])
     res_v[...] = grad_v.astype(jnp.bfloat16)
-    for step, out in zip(range(half, ranks), early):
-        rows = rows_at(me ^ step, frames)
-        out[0:frames, :] = mixed_ref[rows, :]
-        out[frames:, :] = res_v[rows, :]
+    rows = rows_at(me ^ (ranks // 2), frames)
+    early[0:frames, :] = mixed_ref[rows, :]
+    early[frames:, :] = res_v[rows, :]
 
 
 def taps_kernel(att_ref, grad_pad, after_ref, before_ref, taps_ref, tap_sum):
@@ -497,29 +503,22 @@
         out[count * frames :, :] = taps.astype(jnp.bfloat16)
 
 
-def stage_kernel(*refs):
-    half = len(refs) // 2
-    for source, target in zip(refs[:half], refs[half:]):
-        target[...] = source[...]
+def stage_kernel(source, target):
+    target[...] = source[...]
 
 
 def spread_kernel(ranks, frames, *refs):
-    half = ranks // 2
-    near, far, early = refs[:half], refs[half:ranks], refs[ranks : ranks + half]
-    targets, taps_ref = refs[ranks + half : ranks + half + 4], refs[ranks + half + 4]
+    blocks, early = refs[:ranks], refs[ranks]
+    targets, taps_ref = refs[ranks + 1 : ranks + 5], refs[ranks + 5]
     me = lax.axis_index("seq")
     for step in range(ranks):
         lanes = lanes_at(me ^ step)
-        if step < half:
-            parts = [(near[step], place) for place in range(4)]
-            last = near[step], 4
-        else:
-            late, soon = far[step - half], early[step - half]
-            parts = [(late, 0), (late, 1), (soon, 0), (soon, 1)]
-            last = late, 2
+        parts = [(blocks[step], place) for place in range(4)]
+        if step == ranks // 2:
+            parts[2:] = [(early, 0), (early, 1)]
         for target, (source, place) in zip(targets, parts):
             target[0, :, lanes] = source[place * frames : (place + 1) * frames, :]
-        taps = last[0][last[1] * frames :, :].astype(jnp.float32)
+        taps = blocks[step][-(KERNEL + 1) :, :].astype(jnp.float32)
         taps_ref[:, lanes] = taps[:KERNEL]
 
 
@@ -541,26 +540,31 @@
     params = pltpu.CompilerParams(vmem_limit_bytes=24 * MIB)
     taps = KERNEL + 1
 
+    middle = ranks // 2
+    light = partners(ranks)[1:]
+
     sends = pl.pallas_call(
         functools.partial(pack_kernel, ranks),
-        out_shape=[struct((3, frames, LANES), bf16)] * (ranks - 1),
-        in_specs=[hbm] * 3,
+        out_shape=[
+            struct((3 if step == middle else 4, frames, LANES), bf16) for step in range(1, ranks)
+        ],
+        in_specs=[hbm] * 4,
         out_specs=[vmem] * (ranks - 1),
-        scratch_shapes=[VMEM((3,) + queries.shape[1:], bf16), pltpu.SemaphoreType.DMA((3,))],
-        compiler_params=pltpu.CompilerParams(vmem_limit_bytes=54912 * 1024),
+        scratch_shapes=[VMEM((4,) + queries.shape[1:], bf16), pltpu.SemaphoreType.DMA((4,))],
+        compiler_params=pltpu.CompilerParams(vmem_limit_bytes=54832 * 1024),
         name="pack",
-    )(queries, keys, values)
+    )(queries, keys, values, cotangent)
 
     def swap(array, step):
         return lax.ppermute(array, "seq", [(rank, rank ^ step) for rank in range(ranks)])
 
-    order = list(range(ranks - 1, 0, -1))
+    order = partners(ranks)
     received = {step: swap(sends[step - 1], step) for step in order}
 
-    *cot_sends, own, col, row, after, before = pl.pallas_call(
+    late_send, own, col, row, after, before = pl.pallas_call(
         functools.partial(mask_kernel, ranks, length),
-        out_shape=[struct((frames, LANES), bf16)] * (ranks - 1)
-        + [
+        out_shape=[
+            struct((frames, LANES), bf16),
             struct((4, frames, LANES), bf16),
             struct((length, LANES), i32),
             struct((8, length), i32),
@@ -568,13 +572,13 @@
             struct((length, LANES), i32),
         ],
         in_specs=[smem] + [hbm] * 4,
-        out_specs=[vmem] * (ranks + 4),
-        scratch_shapes=[pltpu.SemaphoreType.DMA((ranks + 3,))],
+        out_specs=[vmem] * 6,
+        scratch_shapes=[pltpu.SemaphoreType.DMA((5,))],
         compiler_params=params,
-        cost_estimate=cost(4 * MIB, MIB),
+        cost_estimate=cost(16384 * MIB, 64 * MIB),
         name="masks",
     )(rec_lengths, queries, keys, values, cotangent)
-    cots = {step: swap(cot_sends[step - 1], step) for step in order}
+    cots = received | {middle: swap(late_send, middle)}
 
     soft, att, pre, q_heads, k_t, v_full = pl.pallas_call(
         functools.partial(forward_kernel, ranks, frames),
@@ -600,15 +604,14 @@
         name="forward",
     )(*[received[step] for step in order], own, col, row, after, before, conv_weight)
 
-    half = ranks // 2
     wide = struct((length, LANES), bf16)
-    mixed, g_att, grad_v, grad_pad, *early = pl.pallas_call(
+    mixed, g_att, grad_v, grad_pad, early = pl.pallas_call(
         functools.partial(conv_back_kernel, ranks, frames),
         out_shape=[wide] * 3
         + [struct((length + 2 * PAD, LANES), f32)]
-        + [struct((2 * frames, LANES), bf16)] * half,
+        + [struct((2 * frames, LANES), bf16)],
         in_specs=[vmem] * (ranks + 4) + [anywhere],
-        out_specs=[vmem] * (4 + half),
+        out_specs=[vmem] * 5,
         scratch_shapes=[
             VMEM((length, LANES), bf16),
             VMEM((KERNEL, LANES), f32),
@@ -617,8 +620,8 @@
         compiler_params=params,
         cost_estimate=cost(400 * MIB, 3 * MIB),
         name="conv_back",
-    )(*[cots[step] for step in order], own, pre, after, before, soft, conv_weight)
-    early = [swap(early[step - half], step) for step in range(half, ranks)]
+    )(*[cots[step] for step in range(1, ranks)], own, pre, after, before, soft, conv_weight)
+    early = swap(early, middle)
 
     own_taps = pl.pallas_call(
         taps_kernel,
@@ -659,29 +662,29 @@
             name="blocks",
         )(*sources, *part_taps)
 
-    far = blocks_of(range(half, ranks), grad_q, grad_k)
-    near = blocks_of(range(half), grad_q, grad_k, mixed, grad_v)
-    far = [swap(far[step - half], step) for step in range(half, ranks)]
-    near = [near[0]] + [swap(near[step], step) for step in range(1, half)]
+    (blocks,) = blocks_of([middle], grad_q, grad_k)
+    rest = blocks_of([0] + light, grad_q, grad_k, mixed, grad_v)
+    blocks = {middle: swap(blocks, middle), 0: rest[0]}
+    blocks |= {step: swap(rest[1 + number], step) for number, step in enumerate(light)}
 
     early = pl.pallas_call(
         stage_kernel,
-        out_shape=[struct((2 * frames, LANES), bf16)] * half,
-        in_specs=[vmem] * half,
-        out_specs=[vmem] * half,
+        out_shape=struct((2 * frames, LANES), bf16),
+        in_specs=[vmem],
+        out_specs=vmem,
         compiler_params=params,
         cost_estimate=cost(16384 * MIB, 64 * MIB),
         name="stage",
-    )(*early)
+    )(early)
 
     grad_q, grad_k, mixed, grad_v, grad_taps = pl.pallas_call(
         functools.partial(spread_kernel, ranks, frames),
         out_shape=[struct(queries.shape, bf16)] * 4 + [struct(conv_weight.shape, f32)],
-        in_specs=[vmem] * (ranks + half),
+        in_specs=[vmem] * (ranks + 1),
         out_specs=[vmem] * 5,
         compiler_params=params,
         name="spread",
-    )(*near, *far, *early)
+    )(*[blocks[step] for step in range(ranks)], early)
     return (mixed, grad_q, grad_k, grad_v, grad_taps)
 
 

time: 40.4 us -> 41.7 us (1.032)
  waiting for transfers between devices: 8.79 us -> 10.7 us
  local copies, waits for them, and re-layouts: 0.92 us -> 0.02 us
    ppermute x11 -> x8, waiting for transfers between devices: 7.94 us -> 9.86 us  [swap(): lax.ppermute(array, 'seq', [(rank, rank ^ step) for rank in range(ranks)])]
    unnamed x12, local copies, waits for them, and re-layouts: 0.92 us -> 0.02 us
    ppermute x11 -> x8, starting transfers between devices: 17.2 us -> 17.3 us  [swap(): lax.ppermute(array, 'seq', [(rank, rank ^ step) for rank in range(ranks)])]
  transfers between devices with their start and end apart: 12 -> 9, of which waited for: 5 -> 5; matrix products, arithmetic and copies ran while one was open for 0% -> 0% of each run, Pallas kernels for 18% -> 18%
where the time goes in v5:
time: 41.7 us; the launch traced here: 41.5 us
  starting transfers between devices  18.9 us (45%)
  Pallas kernels  11.2 us (27%)
  waiting for transfers between devices  10.7 us (26%)
  between operations  0.75 us (2%)
    ppermute x8, starting transfers between devices, swap(): lax.ppermute(array, 'seq', [(rank, rank ^ step) for rank in range(ranks)])  17.3 us
    ppermute x8, waiting for transfers between devices, swap(): lax.ppermute(array, 'seq', [(rank, rank ^ step) for rank in range(ranks)])  9.86 us
    pallas_call x1, Pallas kernels, on_device_heads(): pl.pallas_call(functools.partial(forward_kernel, ranks, frames), out_shap...  3.43 us
    pallas_call x1, Pallas kernels, on_device_heads(): pl.pallas_call(functools.partial(conv_back_kernel, ranks, frames), out_sh...  1.72 us
    ppermute x1, starting transfers between devices, on_device_heads(): lax.ppermute(own_taps, 'dp', [(one, (one + shift) % copies) for one in ra...  1.56 us
    pallas_call x1, Pallas kernels, on_device_heads(): pl.pallas_call(backward_kernel, out_shape=[wide] * 2, in_specs=[vmem] * 6...  1.39 us
    pallas_call x1, Pallas kernels, on_device_heads(): pl.pallas_call(functools.partial(mask_kernel, ranks, length), out_shape=[...  1.29 us
    pallas_call x1, Pallas kernels, on_device_heads(): pl.pallas_call(functools.partial(pack_kernel, ranks), out_shape=[struct((...  1.25 us
  transfers between devices with their start and end apart: 9, of which 5 were waited for; matrix products, arithmetic and copies ran while one was open for 0% of the time, Pallas kernels for 18%

profile of v5, /device:TPU:0, one launch (start us, length us, event | category | flops | bytes accessed | tf_op | source)
XLA Modules:
  0.0 41.5 jit_solution(3066910350990490303)
XLA Ops:
  0.6 0.0 copy-start.3
  0.6 0.0 copy-start.2
  0.7 0.0 copy-start.1
  0.7 0.0 copy-start
  0.7 1.2 %pack.1 = (bf16[4,128,128]{2,1,0:T(8,128)(2,1)S(1)}, bf16[3,128,128]{2,1,0:T(8,128)(2,1)S(1)}, bf16[4,128,128]{2,1,0:T(8,128)(2,1)S(1)}) custom-call(bf16[1,128,512]{2,1,0:T(8,128)(2,1)} %q_ref.3, bf16[1,128,512]{2,1,0:T(8,128)(2,1)} %k_ref.3, bf16[1,128,512]{2,1,0:T(8,128)(2,1)} %v_ref.3, bf16[1,128,512]{2,1,0:T(8,128)(2,1)} %c_ref.3), custom_call_target="tpu_custom_call" | custom-call | tf_op jit(solution)/shard_map/pack/pallas_call | solution.py:546
  1.9 4.1 %collective-permute-start = (bf16[3,128,128]{2,1,0:T(8,128)(2,1)S(1)}, bf16[3,128,128]{2,1,0:T(8,128)(2,1)S(1)}, u32[]{:S(2)}, u32[]{:S(2)}) collective-permute-start(bf16[3,128,128]{2,1,0:T(8,128)(2,1)S(1)} %get-tuple-element.35), channel_id=1, source_target_pairs={{0,4},{2,6},{4,0},{6,2},{1,5},{3,7},{5,1},{7,3},{8,12},{10,14},{12... | collective-permute-start | bytes 294920 | tf_op jit(solution)/shard_map/ppermute | solution.py:559
  6.0 0.0 copy-start.5
  6.0 1.3 %collective-permute-start.1 = (bf16[4,128,128]{2,1,0:T(8,128)(2,1)S(1)}, bf16[4,128,128]{2,1,0:T(8,128)(2,1)S(1)}, u32[]{:S(2)}, u32[]{:S(2)}) collective-permute-start(bf16[4,128,128]{2,1,0:T(8,128)(2,1)S(1)} %get-tuple-element.36), channel_id=1, source_target_pairs={{0,6},{2,4},{4,2},{6,0},{1,7},{3,5},{5,3},{7,1},{8,14},{10,12},{12... | collective-permute-start | bytes 393224 | tf_op jit(solution)/shard_map/ppermute | solution.py:559
  7.4 0.0 copy-start.4
  7.4 0.2 collective-permute-start.2
  7.6 0.0 copy-done.3
  7.6 0.0 copy-done.2
  7.6 0.0 copy-done.1
  7.6 0.0 copy-done
  7.6 0.0 copy-done.5
  7.6 1.3 %masks.1 = (bf16[128,128]{1,0:T(8,128)(2,1)S(1)}, bf16[4,128,128]{2,1,0:T(8,128)(2,1)S(1)}, s32[512,128]{1,0:T(8,128)S(1)}, s32[8,512]{1,0:T(8,128)S(1)}, s32[51...) custom-call(s32[1,16]{1,0:T(1,128)S(1)} %copy-done.5, bf16[1,128,512]{2,1,0:T(8,128)(2,1)S(1)} %copy-done, ...), custom_call_target="tpu_custom_call" | custom-call | flops 17179869184 | bytes 67108864 | tf_op jit(solution)/shard_map/masks/pallas_call | solution.py:564
  8.9 2.9 %collective-permute-start.3 = (bf16[128,128]{1,0:T(8,128)(2,1)S(1)}, bf16[128,128]{1,0:T(8,128)(2,1)S(1)}, u32[]{:S(2)}, u32[]{:S(2)}) collective-permute-start(bf16[128,128]{1,0:T(8,128)(2,1)S(1)} %get-tuple-element.45), channel_id=1, source_target_pairs={{0,4},{2,6},{4,0},{6,2},{1,5},{3,7},{5,1},{7,3},{8,12},{10,14},{12... | collective-permute-start | bytes 98312 | tf_op jit(solution)/shard_map/ppermute | solution.py:559
  11.8 3.2 %collective-permute-done.refs_0_ = bf16[3,128,128]{2,1,0:T(8,128)(2,1)S(1)} collective-permute-done((bf16[3,128,128]{2,1,0:T(8,128)(2,1)S(1)}, bf16[3,128,128]{2,1,0:T(8,128)(2,1)S(1)}, u32[]{:S(2)}, u32[]{:S(2)}) %collective-permute-start) | collective-permute-done | bytes 98336 | tf_op jit(solution)/shard_map/ppermute | solution.py:559
  15.0 0.0 collective-permute-done.1.refs_1_.refs_2_
  15.0 0.9 %collective-permute-done.2.refs_2_.refs_0_ = bf16[4,128,128]{2,1,0:T(8,128)(2,1)S(1)} collective-permute-done((bf16[4,128,128]{2,1,0:T(8,128)(2,1)S(1)}, bf16[4,128,128]{2,1,0:T(8,128)(2,1)S(1)}, u32[]{:S(2)}, u32[]{:S(2)}) %collective-permute-start.2) | collective-permute-done | bytes 131104 | tf_op jit(solution)/shard_map/ppermute | solution.py:559
  15.8 0.0 copy-done.4
  15.8 3.4 %forward.1 = (bf16[2,512,512]{2,1,0:T(8,128)(2,1)S(1)}, f32[544,128]{1,0:T(8,128)S(1)}, f32[512,128]{1,0:T(8,128)S(1)}, bf16[2,512,128]{2,1,0:T(8,128)(2,1)S(1)}...) custom-call(bf16[3,128,128]{2,1,0:T(8,128)(2,1)S(1)} %collective-permute-done.refs_0_, ...), custom_call_target="tpu_custom_call" | custom-call | flops 419430400 | bytes 3145728 | tf_op jit(solution)/shard_map/forward/pallas_call | solution.py:583
  19.3 0.0 collective-permute-done.3.refs_1_
  19.3 1.7 %conv_back.1 = (bf16[512,128]{1,0:T(8,128)(2,1)S(1)}, bf16[512,128]{1,0:T(8,128)(2,1)S(1)}, bf16[512,128]{1,0:T(8,128)(2,1)S(1)}, f32[544,128]{1,0:T(8,128)S(1)}, bf16[256,128]{1,0:T(8,128)(2,1)S(1)}) custom-call(bf16[4,128,128]{2,1,0:T(8,128)(2,1)S(1)} %collective-permute-done.2.refs_2_.refs_0_, bf16[128,128]{1,0:T(8,128)(2,1)S(1)} %collective-permute-done.3.refs_1_, ...), custom_call_target="tpu_custom_call" | custom-call | flops 419430400 | bytes 3145728 | tf_op jit(solution)/shard_map/conv_back/pallas_call | solution.py:608
  21.0 4.2 %collective-permute-start.8 = (bf16[256,128]{1,0:T(8,128)(2,1)S(1)}, bf16[256,128]{1,0:T(8,128)(2,1)S(1)}, u32[]{:S(2)}, u32[]{:S(2)}) collective-permute-start(bf16[256,128]{1,0:T(8,128)(2,1)S(1)} %get-tuple-element.59), channel_id=1, source_target_pairs={{0,4},{2,6},{4,0},{6,2},{1,5},{3,7},{5,1},{7,3},{8,12},{10,14},{12... | collective-permute-start | bytes 196616 | tf_op jit(solution)/shard_map/ppermute | solution.py:559
  25.3 1.2 %taps.1.refs_4_.refs_2_ = f32[32,128]{1,0:T(8,128)S(1)} custom-call(f32[544,128]{1,0:T(8,128)S(1)} %get-tuple-element.44.att_ref, f32[544,128]{1,0:T(8,128)S(1)} %get-tuple-element.55.grad_pad, s32[512,128]{1,0:T(8,128)S(1)} %get-tuple-element.41.refs_6_.refs_5_.after_ref, s32[512,128]{1,0:T(8,128)S(1)} %get-tuple-element.42.refs_7_.refs_6_.before_ref), custom_call_target="tpu_custom_call" | custom-call | flops 1048576 | bytes 16384 | tf_op jit(solution)/shard_map/taps/pallas_call | solution.py:626
  26.4 1.6 %collective-permute-start.4 = (f32[32,128]{1,0:T(8,128)S(1)}, f32[32,128]{1,0:T(8,128)S(1)}, u32[]{:S(2)}, u32[]{:S(2)}) collective-permute-start(f32[32,128]{1,0:T(8,128)S(1)} %taps.1.refs_4_.refs_2_), channel_id=1, source_target_pairs={{0,8},{8,0},{1,9},{9,1},{2,10},{10,2},{3,11},{11,3},{4,12},{12,4},... | collective-permute-start | bytes 49160 | tf_op jit(solution)/shard_map/ppermute | solution.py:638
  28.0 1.4 %backward.1 = (bf16[512,128]{1,0:T(8,128)(2,1)S(1)}, bf16[512,128]{1,0:T(8,128)(2,1)S(1)}) custom-call(bf16[2,512,512]{2,1,0:T(8,128)(2,1)S(1)} %get-tuple-element.43.refs_7_.soft_ref, f32[544,128]{1,0:T(8,128)S(1)} %get-tuple-element.44.att_ref, bf16[512,128]{1,0:T(8,128)(2,1)S(1)} %get-tuple-element.47.g_att, ...), custom_call_target="tpu_custom_call" | custom-call | flops 1048576 | bytes 16384 | tf_op jit(solution)/shard_map/backward/pallas_call | solution.py:642
  29.4 0.8 %collective-permute-done.4.refs_5_.refs_3_ = f32[32,128]{1,0:T(8,128)S(1)} collective-permute-done((f32[32,128]{1,0:T(8,128)S(1)}, f32[32,128]{1,0:T(8,128)S(1)}, u32[]{:S(2)}, u32[]{:S(2)}) %collective-permute-start.4) | collective-permute-done | bytes 16416 | tf_op jit(solution)/shard_map/ppermute | solution.py:638
  30.3 0.1 collective-permute-start.6
  30.4 1.2 %collective-permute-start.5 = (bf16[544,128]{1,0:T(8,128)(2,1)S(1)}, bf16[544,128]{1,0:T(8,128)(2,1)S(1)}, u32[]{:S(2)}, u32[]{:S(2)}) collective-permute-start(bf16[544,128]{1,0:T(8,128)(2,1)S(1)} %get-tuple-element.57), channel_id=1, source_target_pairs={{0,2},{2,0},{4,6},{6,4},{1,3},{3,1},{5,7},{7,5},{8,10},{10,8},{12,... | collective-permute-start | bytes 417800 | tf_op jit(solution)/shard_map/ppermute | solution.py:559
  31.5 3.3 %collective-permute-start.7 = (bf16[544,128]{1,0:T(8,128)(2,1)S(1)}, bf16[544,128]{1,0:T(8,128)(2,1)S(1)}, u32[]{:S(2)}, u32[]{:S(2)}) collective-permute-start(bf16[544,128]{1,0:T(8,128)(2,1)S(1)} %get-tuple-element.58), channel_id=1, source_target_pairs={{0,6},{2,4},{4,2},{6,0},{1,7},{3,5},{5,3},{7,1},{8,14},{10,12},{12... | collective-permute-start | bytes 417800 | tf_op jit(solution)/shard_map/ppermute | solution.py:559
  34.8 0.0 collective-permute-done.8.source
  34.8 2.2 %collective-permute-done.6.refs_2_ = bf16[288,128]{1,0:T(8,128)(2,1)S(1)} collective-permute-done((bf16[288,128]{1,0:T(8,128)(2,1)S(1)}, bf16[288,128]{1,0:T(8,128)(2,1)S(1)}, u32[]{:S(2)}, u32[]{:S(2)}) %collective-permute-start.6) | collective-permute-done | bytes 73760 | tf_op jit(solution)/shard_map/ppermute | solution.py:559
  37.0 0.0 collective-permute-done.5.refs_1_
  37.0 3.6 %collective-permute-done.7.refs_3_ = bf16[544,128]{1,0:T(8,128)(2,1)S(1)} collective-permute-done((bf16[544,128]{1,0:T(8,128)(2,1)S(1)}, bf16[544,128]{1,0:T(8,128)(2,1)S(1)}, u32[]{:S(2)}, u32[]{:S(2)}) %collective-permute-start.7) | collective-permute-done | bytes 139296 | tf_op jit(solution)/shard_map/ppermute | solution.py:559
  40.6 0.9 %spread.1 = (bf16[1,128,512]{2,1,0:T(8,128)(2,1)}, bf16[1,128,512]{2,1,0:T(8,128)(2,1)}, bf16[1,128,512]{2,1,0:T(8,128)(2,1)}, bf16[1,128,512]{2,1,0:T(8,128)(2,1)}, f32[31,512]{1,0:T(8,128)}) custom-call(bf16[544,128]{1,0:T(8,128)(2,1)S(1)} %get-tuple-element.56.refs_0_, bf16[544,128]{1,0:T(8,128)(2,1)S(1)} %collective-permute-done.5.refs_1_, ...), custom_call_target="tpu_custom_call" | custom-call | tf_op jit(solution)/shard_map/spread/pallas_call | solution.py:680
  (3 shorter events, 0.1 us)
Async XLA Ops:
  0.6 7.0 %copy-start.3 = (bf16[1,128,512]{2,1,0:T(8,128)(2,1)S(1)}, bf16[1,128,512]{2,1,0:T(8,128)(2,1)}, u32[]{:S(2)}) copy-start(bf16[1,128,512]{2,1,0:T(8,128)(2,1)} %c_ref.3) | copy-start | bytes 393220
  0.6 7.0 %copy-start.2 = (bf16[1,128,512]{2,1,0:T(8,128)(2,1)S(1)}, bf16[1,128,512]{2,1,0:T(8,128)(2,1)}, u32[]{:S(2)}) copy-start(bf16[1,128,512]{2,1,0:T(8,128)(2,1)} %v_ref.3) | copy-start | bytes 393220
  0.7 7.0 %copy-start.1 = (bf16[1,128,512]{2,1,0:T(8,128)(2,1)S(1)}, bf16[1,128,512]{2,1,0:T(8,128)(2,1)}, u32[]{:S(2)}) copy-start(bf16[1,128,512]{2,1,0:T(8,128)(2,1)} %k_ref.3) | copy-start | bytes 393220
  0.7 7.0 %copy-start = (bf16[1,128,512]{2,1,0:T(8,128)(2,1)S(1)}, bf16[1,128,512]{2,1,0:T(8,128)(2,1)}, u32[]{:S(2)}) copy-start(bf16[1,128,512]{2,1,0:T(8,128)(2,1)} %q_ref.3) | copy-start | bytes 393220
  1.9 13.0 %collective-permute-start = (bf16[3,128,128]{2,1,0:T(8,128)(2,1)S(1)}, bf16[3,128,128]{2,1,0:T(8,128)(2,1)S(1)}, u32[]{:S(2)}, u32[]{:S(2)}) collective-permute-start(bf16[3,128,128]{2,1,0:T(8,128)(2,1)S(1)} %get-tuple-element.35), channel_id=1, source_target_pairs={{0,4},{2,6},{4,0},{6,2},{1,5},{3,7},{5,1},{7,3},{8,12},{10,14},{12... | collective-permute-start | bytes 294920 | tf_op jit(solution)/shard_map/ppermute | solution.py:559
  6.0 1.6 %copy-start.5 = (s32[1,16]{1,0:T(1,128)S(1)}, s32[1,16]{1,0:T(1,128)}, u32[]{:S(2)}) copy-start(s32[1,16]{1,0:T(1,128)} %lens_ref.1) | copy-start | bytes 196
  6.0 8.9 %collective-permute-start.1 = (bf16[4,128,128]{2,1,0:T(8,128)(2,1)S(1)}, bf16[4,128,128]{2,1,0:T(8,128)(2,1)S(1)}, u32[]{:S(2)}, u32[]{:S(2)}) collective-permute-start(bf16[4,128,128]{2,1,0:T(8,128)(2,1)S(1)} %get-tuple-element.36), channel_id=1, source_target_pairs={{0,6},{2,4},{4,2},{6,0},{1,7},{3,5},{5,3},{7,1},{8,14},{10,12},{12... | collective-permute-start | bytes 393224 | tf_op jit(solution)/shard_map/ppermute | solution.py:559
  7.4 8.5 %copy-start.4 = (f32[31,512]{1,0:T(8,128)S(1)}, f32[31,512]{1,0:T(8,128)}, u32[]{:S(2)}) copy-start(f32[31,512]{1,0:T(8,128)} %refs_8_.3) | copy-start | bytes 190468
  7.4 8.5 %collective-permute-start.2 = (bf16[4,128,128]{2,1,0:T(8,128)(2,1)S(1)}, bf16[4,128,128]{2,1,0:T(8,128)(2,1)S(1)}, u32[]{:S(2)}, u32[]{:S(2)}) collective-permute-start(bf16[4,128,128]{2,1,0:T(8,128)(2,1)S(1)} %get-tuple-element.37), channel_id=1, source_target_pairs={{0,2},{2,0},{4,6},{6,4},{1,3},{3,1},{5,7},{7,5},{8,10},{10,8},{12,... | collective-permute-start | bytes 393224 | tf_op jit(solution)/shard_map/ppermute | solution.py:559
  8.9 10.4 %collective-permute-start.3 = (bf16[128,128]{1,0:T(8,128)(2,1)S(1)}, bf16[128,128]{1,0:T(8,128)(2,1)S(1)}, u32[]{:S(2)}, u32[]{:S(2)}) collective-permute-start(bf16[128,128]{1,0:T(8,128)(2,1)S(1)} %get-tuple-element.45), channel_id=1, source_target_pairs={{0,4},{2,6},{4,0},{6,2},{1,5},{3,7},{5,1},{7,3},{8,12},{10,14},{12... | collective-permute-start | bytes 98312 | tf_op jit(solution)/shard_map/ppermute | solution.py:559
  21.0 13.8 %collective-permute-start.8 = (bf16[256,128]{1,0:T(8,128)(2,1)S(1)}, bf16[256,128]{1,0:T(8,128)(2,1)S(1)}, u32[]{:S(2)}, u32[]{:S(2)}) collective-permute-start(bf16[256,128]{1,0:T(8,128)(2,1)S(1)} %get-tuple-element.59), channel_id=1, source_target_pairs={{0,4},{2,6},{4,0},{6,2},{1,5},{3,7},{5,1},{7,3},{8,12},{10,14},{12... | collective-permute-start | bytes 196616 | tf_op jit(solution)/shard_map/ppermute | solution.py:559
  26.4 3.8 %collective-permute-start.4 = (f32[32,128]{1,0:T(8,128)S(1)}, f32[32,128]{1,0:T(8,128)S(1)}, u32[]{:S(2)}, u32[]{:S(2)}) collective-permute-start(f32[32,128]{1,0:T(8,128)S(1)} %taps.1.refs_4_.refs_2_), channel_id=1, source_target_pairs={{0,8},{8,0},{1,9},{9,1},{2,10},{10,2},{3,11},{11,3},{4,12},{12,4},... | collective-permute-start | bytes 49160 | tf_op jit(solution)/shard_map/ppermute | solution.py:638
  30.3 6.7 %collective-permute-start.6 = (bf16[288,128]{1,0:T(8,128)(2,1)S(1)}, bf16[288,128]{1,0:T(8,128)(2,1)S(1)}, u32[]{:S(2)}, u32[]{:S(2)}) collective-permute-start(bf16[288,128]{1,0:T(8,128)(2,1)S(1)} %blocks.3), channel_id=1, source_target_pairs={{0,4},{2,6},{4,0},{6,2},{1,5},{3,7},{5,1},{7,3},{8,12},{10,14},{12... | collective-permute-start | bytes 221192 | tf_op jit(solution)/shard_map/ppermute | solution.py:559
  30.4 6.6 %collective-permute-start.5 = (bf16[544,128]{1,0:T(8,128)(2,1)S(1)}, bf16[544,128]{1,0:T(8,128)(2,1)S(1)}, u32[]{:S(2)}, u32[]{:S(2)}) collective-permute-start(bf16[544,128]{1,0:T(8,128)(2,1)S(1)} %get-tuple-element.57), channel_id=1, source_target_pairs={{0,2},{2,0},{4,6},{6,4},{1,3},{3,1},{5,7},{7,5},{8,10},{10,8},{12,... | collective-permute-start | bytes 417800 | tf_op jit(solution)/shard_map/ppermute | solution.py:559
  31.5 9.1 %collective-permute-start.7 = (bf16[544,128]{1,0:T(8,128)(2,1)S(1)}, bf16[544,128]{1,0:T(8,128)(2,1)S(1)}, u32[]{:S(2)}, u32[]{:S(2)}) collective-permute-start(bf16[544,128]{1,0:T(8,128)(2,1)S(1)} %get-tuple-element.58), channel_id=1, source_target_pairs={{0,6},{2,4},{4,2},{6,0},{1,7},{3,5},{5,3},{7,1},{8,14},{10,12},{12... | collective-permute-start | bytes 417800 | tf_op jit(solution)/shard_map/ppermute | solution.py:559

commit v6 on v3

--- a/solution.py
+++ b/solution.py
@@ -255,10 +255,10 @@
     return pl.ds(pl.multiple_of(block * LANES, LANES), LANES)
 
 
-def pack_kernel(ranks, q_ref, k_ref, v_ref, *rest):
+def pack_kernel(ranks, q_ref, k_ref, v_ref, c_ref, *rest):
     outs, (whole, sems) = rest[:-2], rest[-2:]
     me = lax.axis_index("seq")
-    sources = (q_ref, k_ref, v_ref)
+    sources = (q_ref, k_ref, v_ref, c_ref)
     run_copies([(source.at[0], whole.at[place]) for place, source in enumerate(sources)], sems)
     for step in range(ranks - 1, 0, -1):
         for place in range(len(sources)):
@@ -278,13 +278,13 @@
         copy.wait()
 
 
-def mask_kernel(ranks, length, lens_ref, q_ref, k_ref, v_ref, c_ref, *refs):
-    cot_refs = refs[: ranks - 1]
-    own_ref, col_ref, row_ref, after_ref, before_ref, sems = refs[ranks - 1 :]
-    me = lax.axis_index("seq")
-    pairs = [(c_ref.at[0, :, lanes_at(me ^ step)], cot_refs[step - 1]) for step in range(1, ranks)]
-    for place, source in enumerate((q_ref, k_ref, v_ref, c_ref)):
-        pairs.append((source.at[0, :, lanes_at(me)], own_ref.at[place]))
+def mask_kernel(length, lens_ref, q_ref, k_ref, v_ref, c_ref, *refs):
+    own_ref, col_ref, row_ref, after_ref, before_ref, sems = refs
+    lanes = lanes_at(lax.axis_index("seq"))
+    pairs = [
+        (source.at[0, :, lanes], own_ref.at[place])
+        for place, source in enumerate((q_ref, k_ref, v_ref, c_ref))
+    ]
 
     def extents():
         ends = []
@@ -320,18 +320,23 @@
 
 
 def forward_kernel(ranks, frames, *refs):
-    recvs = refs[: ranks - 1]
+    recvs = dict(zip(range(ranks - 1, 0, -1), refs))
     own_ref, col_ref, row_ref, after_ref, before_ref, w_ref = refs[ranks - 1 : ranks + 5]
-    soft_ref, att_ref, pre_ref, q_ref, k_t_ref, v_ref = refs[ranks + 5 : ranks + 11]
-    att_t_ref, k_full, q_full, w_own, w_sem = refs[ranks + 11 :]
+    soft_ref, att_ref, q_ref, k_t_ref, v_ref, mixed_ref, g_att, taps_ref = refs[ranks + 5 : ranks + 13]
+    att_t_ref, k_full, q_full, cot, grad_pad, tap_sum, w_own, w_sem = refs[ranks + 13 :]
     me = lax.axis_index("seq")
     length = ranks * frames
     copy = pltpu.make_async_copy(w_ref.at[:, lanes_at(me)], w_own, w_sem)
     copy.start()
-    for place, target in enumerate((q_full, k_full, v_ref)):
+    for place, target in enumerate((q_full, k_full, v_ref, cot)):
         target[rows_at(me, frames), :] = own_ref[place]
         for step in range(1, ranks):
-            target[rows_at(me ^ step, frames), :] = recvs[ranks - 1 - step][place]
+            target[rows_at(me ^ step, frames), :] = recvs[step][place]
+    zeros = jnp.zeros((PAD, LANES), jnp.float32)
+    for padded in (att_ref, grad_pad):
+        padded[0:PAD, :] = zeros
+        padded[PAD + length :, :] = zeros
+    tap_sum[...] = jnp.zeros(tap_sum.shape, jnp.float32)
     heads = LANES // HDIM
     lane_head = lax.broadcasted_iota(jnp.int32, (1, LANES), 1) // HDIM
     scaled = q_full[...].astype(jnp.float32) * (1.0 / math.sqrt(HDIM))
@@ -353,77 +358,48 @@
             soft_ref[head, :, cols] = soft
             rows = slice(head * HDIM, (head + 1) * HDIM)
             att_t_ref[rows, cols] = mm(v_t[rows], soft).astype(jnp.bfloat16).astype(jnp.float32)
-    zeros = jnp.zeros((PAD, LANES), jnp.float32)
-    att_ref[0:PAD, :] = zeros
     att_ref[PAD : PAD + length, :] = att_t_ref[...].T
-    att_ref[PAD + length :, :] = zeros
     copy.wait()
-
     chunk = 64
 
-    def some_rows(number, carry):
+    def masked(source, base, off, low, high):
+        piece = source[pl.ds(base + (PAD + off), chunk), :]
+        if off > 0:
+            piece = jnp.where(high >= off, piece, 0.0)
+        if off < 0:
+            piece = jnp.where(low >= -off, piece, 0.0)
+        return piece
+
+    def conv_rows(number, carry):
         base = pl.multiple_of(number * chunk, chunk)
         rows = pl.ds(base, chunk)
         after, before = after_ref[rows, :], before_ref[rows, :]
-        total = jnp.zeros((chunk, LANES), jnp.float32)
+        pre = jnp.zeros((chunk, LANES), jnp.float32)
         for tap in range(KERNEL):
-            off = tap - HALF
-            piece = att_ref[pl.ds(base + (PAD + off), chunk), :]
-            if off > 0:
-                piece = jnp.where(after >= off, piece, 0.0)
-            if off < 0:
-                piece = jnp.where(before >= -off, piece, 0.0)
-            total = total + w_own[tap : tap + 1, :] * piece
-        pre_ref[rows, :] = total
+            pre = pre + w_own[tap : tap + 1, :] * masked(att_ref, base, tap - HALF, before, after)
+        gate = jax.nn.sigmoid(pre)
+        mixed_ref[rows, :] = (pre * gate).astype(jnp.bfloat16)
+        conv_grad = cot[rows, :].astype(jnp.float32) * gate * (1.0 + pre * (1.0 - gate))
+        grad_pad[pl.ds(base + PAD, chunk), :] = conv_grad.astype(jnp.bfloat16).astype(jnp.float32)
         return carry
 
-    lax.fori_loop(0, length // chunk, some_rows, 0)
-
-
-def conv_back_kernel(ranks, frames, *refs):
-    cots = refs[: ranks - 1]
-    own_ref, att_ref, pre_ref, after_ref, before_ref, w_ref = refs[ranks - 1 : ranks + 5]
-    mixed_ref, g_att, taps_ref, cot, grad_pad, tap_sum, w_own, w_sem = refs[ranks + 5 :]
-    me = lax.axis_index("seq")
-    length = ranks * frames
-    copy = pltpu.make_async_copy(w_ref.at[:, lanes_at(me)], w_own, w_sem)
-    copy.start()
-    cot[rows_at(me, frames), :] = own_ref[3]
-    for step in range(1, ranks):
-        cot[rows_at(me ^ step, frames), :] = cots[ranks - 1 - step][...]
-    zeros = jnp.zeros((PAD, LANES), jnp.float32)
-    grad_pad[0:PAD, :] = zeros
-    grad_pad[PAD + length :, :] = zeros
-    pre = pre_ref[...]
-    gate = jax.nn.sigmoid(pre)
-    mixed_ref[...] = (pre * gate).astype(jnp.bfloat16)
-    conv_grad = cot[...].astype(jnp.float32) * gate * (1.0 + pre * (1.0 - gate))
-    grad_pad[PAD : PAD + length, :] = conv_grad.astype(jnp.bfloat16).astype(jnp.float32)
-    tap_sum[...] = jnp.zeros(tap_sum.shape, jnp.float32)
-    copy.wait()
-
-    chunk = 64
-
-    def some_rows(number, carry):
+    lax.fori_loop(0, length // chunk, conv_rows, 0)
+
+    def back_rows(number, carry):
         base = pl.multiple_of(number * chunk, chunk)
         rows = pl.ds(base, chunk)
         after, before = after_ref[rows, :], before_ref[rows, :]
         own_att = att_ref[pl.ds(base + PAD, chunk), :]
         total = jnp.zeros((chunk, LANES), jnp.float32)
         for tap in range(KERNEL):
-            off = tap - HALF
-            piece = grad_pad[pl.ds(base + (PAD - off), chunk), :]
-            if off > 0:
-                piece = jnp.where(before >= off, piece, 0.0)
-            if off < 0:
-                piece = jnp.where(after >= -off, piece, 0.0)
+            piece = masked(grad_pad, base, HALF - tap, before, after)
             total = total + w_own[tap : tap + 1, :] * piece
             part = (own_att * piece).reshape(chunk // 8, 8, LANES)
             tap_sum[tap] = tap_sum[tap] + jnp.sum(part, axis=0)
         g_att[rows, :] = total.astype(jnp.bfloat16)
         return carry
 
-    lax.fori_loop(0, length // chunk, some_rows, 0)
+    lax.fori_loop(0, length // chunk, back_rows, 0)
     taps_ref[...] = jnp.sum(tap_sum[...], axis=1)
 
 
@@ -467,7 +443,7 @@
 
 
 def spread_kernel(ranks, frames, *refs):
-    blocks = refs[:ranks]
+    blocks = refs[:ranks][::-1]
     targets, taps_ref = refs[ranks : ranks + 4], refs[ranks + 4]
     me = lax.axis_index("seq")
     for step in range(ranks):
@@ -498,24 +474,22 @@
 
     sends = pl.pallas_call(
         functools.partial(pack_kernel, ranks),
-        out_shape=[struct((3, frames, LANES), bf16)] * (ranks - 1),
-        in_specs=[hbm] * 3,
+        out_shape=[struct((4, frames, LANES), bf16)] * (ranks - 1),
+        in_specs=[hbm] * 4,
         out_specs=[vmem] * (ranks - 1),
-        scratch_shapes=[VMEM((3,) + queries.shape[1:], bf16), pltpu.SemaphoreType.DMA((3,))],
-        compiler_params=pltpu.CompilerParams(vmem_limit_bytes=54912 * 1024),
+        scratch_shapes=[VMEM((4,) + queries.shape[1:], bf16), pltpu.SemaphoreType.DMA((4,))],
+        compiler_params=pltpu.CompilerParams(vmem_limit_bytes=54784 * 1024),
         name="pack",
-    )(queries, keys, values)
+    )(queries, keys, values, cotangent)
 
     def swap(array, step):
         return lax.ppermute(array, "seq", [(rank, rank ^ step) for rank in range(ranks)])
 
-    order = list(range(ranks - 1, 0, -1))
-    received = {step: swap(sends[step - 1], step) for step in order}
-
-    *cot_sends, own, col, row, after, before = pl.pallas_call(
-        functools.partial(mask_kernel, ranks, length),
-        out_shape=[struct((frames, LANES), bf16)] * (ranks - 1)
-        + [
+    received = [swap(sends[step - 1], step) for step in range(ranks - 1, 0, -1)]
+
+    own, col, row, after, before = pl.pallas_call(
+        functools.partial(mask_kernel, length),
+        out_shape=[
             struct((4, frames, LANES), bf16),
             struct((length, LANES), i32),
             struct((8, length), i32),
@@ -523,54 +497,43 @@
             struct((length, LANES), i32),
         ],
         in_specs=[smem] + [hbm] * 4,
-        out_specs=[vmem] * (ranks + 4),
-        scratch_shapes=[pltpu.SemaphoreType.DMA((ranks + 3,))],
+        out_specs=[vmem] * 5,
+        scratch_shapes=[pltpu.SemaphoreType.DMA((4,))],
         compiler_params=params,
-        cost_estimate=cost(4 * MIB, MIB),
+        cost_estimate=cost(16384 * MIB, 64 * MIB),
         name="masks",
     )(rec_lengths, queries, keys, values, cotangent)
-    cots = {step: swap(cot_sends[step - 1], step) for step in order}
-
-    soft, att, pre, q_heads, k_t, v_full = pl.pallas_call(
+
+    wide = struct((length, LANES), bf16)
+    padded = (length + 2 * PAD, LANES)
+    soft, att, q_heads, k_t, v_full, mixed, g_att, own_taps = pl.pallas_call(
         functools.partial(forward_kernel, ranks, frames),
         out_shape=[
             struct((heads, length, length), bf16),
-            struct((length + 2 * PAD, LANES), f32),
-            struct((length, LANES), f32),
+            struct(padded, f32),
             struct((heads, length, LANES), bf16),
             struct((LANES, length), bf16),
-            struct((length, LANES), bf16),
+            wide,
+            wide,
+            wide,
+            struct((taps, LANES), f32),
         ],
         in_specs=[vmem] * (ranks + 4) + [anywhere],
-        out_specs=[vmem] * 6,
+        out_specs=[vmem] * 8,
         scratch_shapes=[
             VMEM((LANES, length), f32),
             VMEM((length, LANES), bf16),
             VMEM((length, LANES), bf16),
-            VMEM((KERNEL, LANES), f32),
-            pltpu.SemaphoreType.DMA,
-        ],
-        compiler_params=params,
-        cost_estimate=cost(400 * MIB, 3 * MIB),
-        name="forward",
-    )(*[received[step] for step in order], own, col, row, after, before, conv_weight)
-
-    mixed, g_att, own_taps = pl.pallas_call(
-        functools.partial(conv_back_kernel, ranks, frames),
-        out_shape=[struct((length, LANES), bf16)] * 2 + [struct((taps, LANES), f32)],
-        in_specs=[vmem] * (ranks + 4) + [anywhere],
-        out_specs=[vmem] * 3,
-        scratch_shapes=[
             VMEM((length, LANES), bf16),
-            VMEM((length + 2 * PAD, LANES), f32),
+            VMEM(padded, f32),
             VMEM((taps, 8, LANES), f32),
             VMEM((KERNEL, LANES), f32),
             pltpu.SemaphoreType.DMA,
         ],
         compiler_params=params,
-        cost_estimate=cost(400 * MIB, 3 * MIB),
-        name="conv_back",
-    )(*[cots[step] for step in order], own, att, pre, after, before, conv_weight)
+        cost_estimate=cost(800 * MIB, 3 * MIB),
+        name="forward",
+    )(*received, own, col, row, after, before, conv_weight)
 
     copies = lax.axis_size("dp")
     part_taps = [own_taps] + [
@@ -589,23 +552,17 @@
         name="backward",
     )(soft, att, g_att, q_heads, k_t, v_full)
 
-    def blocks_of(steps):
-        return pl.pallas_call(
-            functools.partial(block_kernel, steps, frames),
-            out_shape=[struct((4 * frames + taps, LANES), bf16)] * len(steps),
-            in_specs=[vmem] * (4 + copies),
-            out_specs=[vmem] * len(steps),
-            compiler_params=params,
-            cost_estimate=cost(MIB, MIB),
-            name="blocks",
-        )(mixed, *results, *part_taps)
-
-    half = ranks // 2
-    far = blocks_of(list(range(half, ranks)))
-    near = blocks_of(list(range(half)))
-    back = {step: swap(far[step - half], step) for step in range(half, ranks)}
-    back |= {step: swap(near[step], step) for step in range(1, half)}
-    back[0] = near[0]
+    steps = list(range(ranks - 1, -1, -1))
+    blocks = pl.pallas_call(
+        functools.partial(block_kernel, steps, frames),
+        out_shape=[struct((4 * frames + taps, LANES), bf16)] * ranks,
+        in_specs=[vmem] * (4 + copies),
+        out_specs=[vmem] * ranks,
+        compiler_params=params,
+        cost_estimate=cost(MIB, MIB),
+        name="blocks",
+    )(mixed, *results, *part_taps)
+    back = [swap(block, step) if step else block for block, step in zip(blocks, steps)]
 
     return pl.pallas_call(
         functools.partial(spread_kernel, ranks, frames),
@@ -614,7 +571,7 @@
         out_specs=[vmem] * 5,
         compiler_params=params,
         name="spread",
-    )(*[back[step] for step in range(ranks)])
+    )(*back)
 
 
 def on_device_any(queries, keys, values, cotangent, conv_weight, rec_lengths):

time: 37.7 us -> 41.2 us (1.093)
  waiting for transfers between devices: 9.73 us -> 18.5 us
  starting transfers between devices: 16.1 us -> 11.8 us
  local copies, waits for them, and re-layouts: 0.92 us -> 0.02 us
    ppermute x9 -> x6, waiting for transfers between devices: 8.91 us -> 17.6 us  [swap(): lax.ppermute(array, 'seq', [(rank, rank ^ step) for rank in range(ranks)])]
    ppermute x9 -> x6, starting transfers between devices: 14.5 us -> 10.2 us  [swap(): lax.ppermute(array, 'seq', [(rank, rank ^ step) for rank in range(ranks)])]
    pallas_call x4 -> x2, Pallas kernels: 3.19 us -> 1.31 us  [the longest x1 1.27 us: on_device_heads(): pl.pallas_call(functools.partial(mask_kernel, length), out_shape=[struct(...]
    pallas_call x1, Pallas kernels: 3.4 us -> 5.14 us  [on_device_heads(): pl.pallas_call(functools.partial(forward_kernel, ranks, frames), out_shap...]
    unnamed x12, local copies, waits for them, and re-layouts: 0.92 us -> 0.02 us
  transfers between devices with their start and end apart: 10 -> 7, of which waited for: 4 -> 5; matrix products, arithmetic and copies ran while one was open for 0% -> 0% of each run, Pallas kernels for 16% -> 7%
where the time goes in v6:
time: 41.2 us; the launch traced here: 41 us
  waiting for transfers between devices  18.5 us (45%)
  starting transfers between devices  11.8 us (29%)
  Pallas kernels  10 us (24%)
  between operations  0.71 us (2%)
    ppermute x6, waiting for transfers between devices, swap(): lax.ppermute(array, 'seq', [(rank, rank ^ step) for rank in range(ranks)])  17.6 us
    ppermute x6, starting transfers between devices, swap(): lax.ppermute(array, 'seq', [(rank, rank ^ step) for rank in range(ranks)])  10.2 us
    pallas_call x1, Pallas kernels, on_device_heads(): pl.pallas_call(functools.partial(forward_kernel, ranks, frames), out_shap...  5.14 us
    ppermute x1, starting transfers between devices, on_device_heads(): lax.ppermute(own_taps, 'dp', [(one, (one + shift) % copies) for one in ra...  1.56 us
    pallas_call x1, Pallas kernels, on_device_heads(): pl.pallas_call(backward_kernel, out_shape=[struct((length, LANES), bf16)]...  1.43 us
    pallas_call x1, Pallas kernels, on_device_heads(): pl.pallas_call(functools.partial(mask_kernel, length), out_shape=[struct(...  1.27 us
    pallas_call x1, Pallas kernels, on_device_heads(): pl.pallas_call(functools.partial(pack_kernel, ranks), out_shape=[struct((...  1.25 us
    pallas_call x1, Pallas kernels, on_device_heads(): pl.pallas_call(functools.partial(spread_kernel, ranks, frames), out_shape...  0.9 us
  transfers between devices with their start and end apart: 7, of which 5 were waited for; matrix products, arithmetic and copies ran while one was open for 0% of the time, Pallas kernels for 7%

profile of v6, /device:TPU:0, one launch (start us, length us, event | category | flops | bytes accessed | tf_op | source)
XLA Modules:
  0.0 41.0 jit_solution(8588039089441145117)
XLA Ops:
  0.6 0.0 copy-start.3
  0.6 0.0 copy-start.2
  0.7 0.0 copy-start.1
  0.7 0.0 copy-start
  0.7 1.3 %pack.1 = (bf16[4,128,128]{2,1,0:T(8,128)(2,1)S(1)}, bf16[4,128,128]{2,1,0:T(8,128)(2,1)S(1)}, bf16[4,128,128]{2,1,0:T(8,128)(2,1)S(1)}) custom-call(bf16[1,128,512]{2,1,0:T(8,128)(2,1)} %q_ref.3, bf16[1,128,512]{2,1,0:T(8,128)(2,1)} %k_ref.3, bf16[1,128,512]{2,1,0:T(8,128)(2,1)} %v_ref.3, bf16[1,128,512]{2,1,0:T(8,128)(2,1)} %c_ref.3), custom_call_target="tpu_custom_call" | custom-call | tf_op jit(solution)/shard_map/pack/pallas_call | solution.py:475
  1.9 5.1 %collective-permute-start = (bf16[4,128,128]{2,1,0:T(8,128)(2,1)S(1)}, bf16[4,128,128]{2,1,0:T(8,128)(2,1)S(1)}, u32[]{:S(2)}, u32[]{:S(2)}) collective-permute-start(bf16[4,128,128]{2,1,0:T(8,128)(2,1)S(1)} %get-tuple-element.28), channel_id=1, source_target_pairs={{0,6},{2,4},{4,2},{6,0},{1,7},{3,5},{5,3},{7,1},{8,14},{10,12},{12... | collective-permute-start | bytes 393224 | tf_op jit(solution)/shard_map/ppermute | solution.py:486
  7.0 0.0 copy-start.5
  7.1 0.0 collective-permute-start.1
  7.1 0.0 copy-start.4
  7.1 0.6 %collective-permute-start.2 = (bf16[4,128,128]{2,1,0:T(8,128)(2,1)S(1)}, bf16[4,128,128]{2,1,0:T(8,128)(2,1)S(1)}, u32[]{:S(2)}, u32[]{:S(2)}) collective-permute-start(bf16[4,128,128]{2,1,0:T(8,128)(2,1)S(1)} %get-tuple-element.30), channel_id=1, source_target_pairs={{0,2},{2,0},{4,6},{6,4},{1,3},{3,1},{5,7},{7,5},{8,10},{10,8},{12,... | collective-permute-start | bytes 393224 | tf_op jit(solution)/shard_map/ppermute | solution.py:486
  7.7 0.0 copy-done.3
  7.7 0.0 copy-done.2
  7.7 0.0 copy-done.1
  7.7 0.0 copy-done
  7.7 0.0 copy-done.5
  7.7 1.3 %masks.1 = (bf16[4,128,128]{2,1,0:T(8,128)(2,1)S(1)}, s32[512,128]{1,0:T(8,128)S(1)}, s32[8,512]{1,0:T(8,128)S(1)}, s32[512,128]{1,0:T(8,128)S(1)}, s32[512,128]{1,0:T(8,128)S(1)}) custom-call(s32[1,16]{1,0:T(1,128)S(1)} %copy-done.5, bf16[1,128,512]{2,1,0:T(8,128)(2,1)S(1)} %copy-done, bf16[1,128,512]{2,1,0:T(8,128)(2,1)S(1)} %copy-done.1, ...), custom_call_target="tpu_custom_call" | custom-call | flops 17179869184 | bytes 67108864 | tf_op jit(solution)/shard_map/masks/pallas_call | solution.py:490
  9.0 2.5 %collective-permute-done.refs_0_ = bf16[4,128,128]{2,1,0:T(8,128)(2,1)S(1)} collective-permute-done((bf16[4,128,128]{2,1,0:T(8,128)(2,1)S(1)}, bf16[4,128,128]{2,1,0:T(8,128)(2,1)S(1)}, u32[]{:S(2)}, u32[]{:S(2)}) %collective-permute-start) | collective-permute-done | bytes 131104 | tf_op jit(solution)/shard_map/ppermute | solution.py:486
  11.5 6.6 %collective-permute-done.1.refs_1_ = bf16[4,128,128]{2,1,0:T(8,128)(2,1)S(1)} collective-permute-done((bf16[4,128,128]{2,1,0:T(8,128)(2,1)S(1)}, bf16[4,128,128]{2,1,0:T(8,128)(2,1)S(1)}, u32[]{:S(2)}, u32[]{:S(2)}) %collective-permute-start.1) | collective-permute-done | bytes 131104 | tf_op jit(solution)/shard_map/ppermute | solution.py:486
  18.1 0.0 collective-permute-done.2.refs_2_
  18.1 0.0 copy-done.4
  18.1 5.1 %forward.1 = (bf16[2,512,512]{2,1,0:T(8,128)(2,1)S(1)}, f32[544,128]{1,0:T(8,128)S(1)}, bf16[2,512,128]{2,1,0:T(8,128)(2,1)S(1)}, bf16[128,512]{1,0:T(8,128)(2,1...) custom-call(bf16[4,128,128]{2,1,0:T(8,128)(2,1)S(1)} %collective-per, ...), custom_call_target="tpu_custom_call" | custom-call | flops 838860800 | bytes 3145728 | tf_op jit(solution)/shard_map/forward/pallas_call | solution.py:509
  23.3 1.6 %collective-permute-start.3 = (f32[32,128]{1,0:T(8,128)S(1)}, f32[32,128]{1,0:T(8,128)S(1)}, u32[]{:S(2)}, u32[]{:S(2)}) collective-permute-start(f32[32,128]{1,0:T(8,128)S(1)} %get-tuple-element.46.refs_4_), channel_id=1, source_target_pairs={{0,8},{8,0},{1,9},{9,1},{2,10},{10,2},{3,11},{11,3},{4,12},{12,4},... | collective-permute-start | bytes 49160 | tf_op jit(solution)/shard_map/ppermute | solution.py:540
  24.8 1.4 %backward.1 = (bf16[512,128]{1,0:T(8,128)(2,1)S(1)}, bf16[512,128]{1,0:T(8,128)(2,1)S(1)}, bf16[512,128]{1,0:T(8,128)(2,1)S(1)}) custom-call(bf16[2,512,512]{2,1,0:T(8,128)(2,1)S(1)} %get-tuple-element.37.soft_ref, f32[544,128]{1,0:T(8,128)S(1)} %get-tuple-element.38.att_ref, bf16[512,128]{1,0:T(8,128)(2,1)S(1)} %get-tuple-element.39.g_att, ...), custom_call_target="tpu_custom_call" | custom-call | flops 838860800 | bytes 3145728 | tf_op jit(solution)/shard_map/backward/pallas_call | solution.py:544
  26.3 0.8 %collective-permute-done.3.refs_5_ = f32[32,128]{1,0:T(8,128)S(1)} collective-permute-done((f32[32,128]{1,0:T(8,128)S(1)}, f32[32,128]{1,0:T(8,128)S(1)}, u32[]{:S(2)}, u32[]{:S(2)}) %collective-permute-start.3) | collective-permute-done | bytes 16416 | tf_op jit(solution)/shard_map/ppermute | solution.py:540
  27.1 2.5 %collective-permute-start.4 = (bf16[544,128]{1,0:T(8,128)(2,1)S(1)}, bf16[544,128]{1,0:T(8,128)(2,1)S(1)}, u32[]{:S(2)}, u32[]{:S(2)}) collective-permute-start(bf16[544,128]{1,0:T(8,128)(2,1)S(1)} %get-tuple-element.47), channel_id=1, source_target_pairs={{0,6},{2,4},{4,2},{6,0},{1,7},{3,5},{5,3},{7,1},{8,14},{10,12},{12... | collective-permute-start | bytes 417800 | tf_op jit(solution)/shard_map/ppermute | solution.py:486
  29.7 0.0 collective-permute-start.5
  29.7 1.9 %collective-permute-start.6 = (bf16[544,128]{1,0:T(8,128)(2,1)S(1)}, bf16[544,128]{1,0:T(8,128)(2,1)S(1)}, u32[]{:S(2)}, u32[]{:S(2)}) collective-permute-start(bf16[544,128]{1,0:T(8,128)(2,1)S(1)} %get-tuple-element.49), channel_id=1, source_target_pairs={{0,2},{2,0},{4,6},{6,4},{1,3},{3,1},{5,7},{7,5},{8,10},{10,8},{12,... | collective-permute-start | bytes 417800 | tf_op jit(solution)/shard_map/ppermute | solution.py:486
  31.6 4.0 %collective-permute-done.4.refs_0_ = bf16[544,128]{1,0:T(8,128)(2,1)S(1)} collective-permute-done((bf16[544,128]{1,0:T(8,128)(2,1)S(1)}, bf16[544,128]{1,0:T(8,128)(2,1)S(1)}, u32[]{:S(2)}, u32[]{:S(2)}) %collective-permute-start.4) | collective-permute-done | bytes 139296 | tf_op jit(solution)/shard_map/ppermute | solution.py:486
  35.6 4.5 %collective-permute-done.5.refs_1_ = bf16[544,128]{1,0:T(8,128)(2,1)S(1)} collective-permute-done((bf16[544,128]{1,0:T(8,128)(2,1)S(1)}, bf16[544,128]{1,0:T(8,128)(2,1)S(1)}, u32[]{:S(2)}, u32[]{:S(2)}) %collective-permute-start.5) | collective-permute-done | bytes 139296 | tf_op jit(solution)/shard_map/ppermute | solution.py:486
  40.1 0.0 collective-permute-done.6.refs_2_
  40.1 0.9 %spread.1 = (bf16[1,128,512]{2,1,0:T(8,128)(2,1)}, bf16[1,128,512]{2,1,0:T(8,128)(2,1)}, bf16[1,128,512]{2,1,0:T(8,128)(2,1)}, bf16[1,128,512]{2,1,0:T(8,128)(2,1)}, f32[31,512]{1,0:T(8,128)}) custom-call(bf16[544,128]{1,0:T(8,128)(2,1)S(1)} %collective-permute-done.4.refs_0_, bf16[544,128]{1,0:T(8,128)(2,1)S(1)} %collective-permute-done.5.refs_1_, ...), custom_call_target="tpu_custom_call" | custom-call | tf_op jit(solution)/shard_map/spread/pallas_call | solution.py:567
  (1 shorter events, 0.0 us)
Async XLA Ops:
  0.6 7.1 %copy-start.3 = (bf16[1,128,512]{2,1,0:T(8,128)(2,1)S(1)}, bf16[1,128,512]{2,1,0:T(8,128)(2,1)}, u32[]{:S(2)}) copy-start(bf16[1,128,512]{2,1,0:T(8,128)(2,1)} %c_ref.3) | copy-start | bytes 393220
  0.6 7.1 %copy-start.2 = (bf16[1,128,512]{2,1,0:T(8,128)(2,1)S(1)}, bf16[1,128,512]{2,1,0:T(8,128)(2,1)}, u32[]{:S(2)}) copy-start(bf16[1,128,512]{2,1,0:T(8,128)(2,1)} %v_ref.3) | copy-start | bytes 393220
  0.7 7.1 %copy-start.1 = (bf16[1,128,512]{2,1,0:T(8,128)(2,1)S(1)}, bf16[1,128,512]{2,1,0:T(8,128)(2,1)}, u32[]{:S(2)}) copy-start(bf16[1,128,512]{2,1,0:T(8,128)(2,1)} %k_ref.3) | copy-start | bytes 393220
  0.7 7.1 %copy-start = (bf16[1,128,512]{2,1,0:T(8,128)(2,1)S(1)}, bf16[1,128,512]{2,1,0:T(8,128)(2,1)}, u32[]{:S(2)}) copy-start(bf16[1,128,512]{2,1,0:T(8,128)(2,1)} %q_ref.3) | copy-start | bytes 393220
  1.9 9.5 %collective-permute-start = (bf16[4,128,128]{2,1,0:T(8,128)(2,1)S(1)}, bf16[4,128,128]{2,1,0:T(8,128)(2,1)S(1)}, u32[]{:S(2)}, u32[]{:S(2)}) collective-permute-start(bf16[4,128,128]{2,1,0:T(8,128)(2,1)S(1)} %get-tuple-element.28), channel_id=1, source_target_pairs={{0,6},{2,4},{4,2},{6,0},{1,7},{3,5},{5,3},{7,1},{8,14},{10,12},{12... | collective-permute-start | bytes 393224 | tf_op jit(solution)/shard_map/ppermute | solution.py:486
  7.0 0.7 %copy-start.5 = (s32[1,16]{1,0:T(1,128)S(1)}, s32[1,16]{1,0:T(1,128)}, u32[]{:S(2)}) copy-start(s32[1,16]{1,0:T(1,128)} %lens_ref.1) | copy-start | bytes 196
  7.1 11.1 %collective-permute-start.1 = (bf16[4,128,128]{2,1,0:T(8,128)(2,1)S(1)}, bf16[4,128,128]{2,1,0:T(8,128)(2,1)S(1)}, u32[]{:S(2)}, u32[]{:S(2)}) collective-permute-start(bf16[4,128,128]{2,1,0:T(8,128)(2,1)S(1)} %get-tuple-element.29), channel_id=1, source_target_pairs={{0,4},{2,6},{4,0},{6,2},{1,5},{3,7},{5,1},{7,3},{8,12},{10,14},{12... | collective-permute-start | bytes 393224 | tf_op jit(solution)/shard_map/ppermute | solution.py:486
  7.1 11.1 %copy-start.4 = (f32[31,512]{1,0:T(8,128)S(1)}, f32[31,512]{1,0:T(8,128)}, u32[]{:S(2)}) copy-start(f32[31,512]{1,0:T(8,128)} %refs_8_.1) | copy-start | bytes 190468
  7.1 11.1 %collective-permute-start.2 = (bf16[4,128,128]{2,1,0:T(8,128)(2,1)S(1)}, bf16[4,128,128]{2,1,0:T(8,128)(2,1)S(1)}, u32[]{:S(2)}, u32[]{:S(2)}) collective-permute-start(bf16[4,128,128]{2,1,0:T(8,128)(2,1)S(1)} %get-tuple-element.30), channel_id=1, source_target_pairs={{0,2},{2,0},{4,6},{6,4},{1,3},{3,1},{5,7},{7,5},{8,10},{10,8},{12,... | collective-permute-start | bytes 393224 | tf_op jit(solution)/shard_map/ppermute | solution.py:486
  23.3 3.8 %collective-permute-start.3 = (f32[32,128]{1,0:T(8,128)S(1)}, f32[32,128]{1,0:T(8,128)S(1)}, u32[]{:S(2)}, u32[]{:S(2)}) collective-permute-start(f32[32,128]{1,0:T(8,128)S(1)} %get-tuple-element.46.refs_4_), channel_id=1, source_target_pairs={{0,8},{8,0},{1,9},{9,1},{2,10},{10,2},{3,11},{11,3},{4,12},{12,4},... | collective-permute-start | bytes 49160 | tf_op jit(solution)/shard_map/ppermute | solution.py:540
  27.1 8.5 %collective-permute-start.4 = (bf16[544,128]{1,0:T(8,128)(2,1)S(1)}, bf16[544,128]{1,0:T(8,128)(2,1)S(1)}, u32[]{:S(2)}, u32[]{:S(2)}) collective-permute-start(bf16[544,128]{1,0:T(8,128)(2,1)S(1)} %get-tuple-element.47), channel_id=1, source_target_pairs={{0,6},{2,4},{4,2},{6,0},{1,7},{3,5},{5,3},{7,1},{8,14},{10,12},{12... | collective-permute-start | bytes 417800 | tf_op jit(solution)/shard_map/ppermute | solution.py:486
  29.7 10.4 %collective-permute-start.5 = (bf16[544,128]{1,0:T(8,128)(2,1)S(1)}, bf16[544,128]{1,0:T(8,128)(2,1)S(1)}, u32[]{:S(2)}, u32[]{:S(2)}) collective-permute-start(bf16[544,128]{1,0:T(8,128)(2,1)S(1)} %get-tuple-element.48), channel_id=1, source_target_pairs={{0,4},{2,6},{4,0},{6,2},{1,5},{3,7},{5,1},{7,3},{8,12},{10,14},{12... | collective-permute-start | bytes 417800 | tf_op jit(solution)/shard_map/ppermute | solution.py:486
  29.7 10.4 %collective-permute-start.6 = (bf16[544,128]{1,0:T(8,128)(2,1)S(1)}, bf16[544,128]{1,0:T(8,128)(2,1)S(1)}, u32[]{:S(2)}, u32[]{:S(2)}) collective-permute-start(bf16[544,128]{1,0:T(8,128)(2,1)S(1)} %get-tuple-element.49), channel_id=1, source_target_pairs={{0,2},{2,0},{4,6},{6,4},{1,3},{3,1},{5,7},{7,5},{8,10},{10,8},{12,... | collective-permute-start | bytes 417800 | tf_op jit(solution)/shard_map/ppermute | solution.py:486

commit v7 on v3

--- a/solution.py
+++ b/solution.py
@@ -339,7 +339,7 @@
         q_ref[head] = jnp.where(lane_head == head, scaled, 0.0).astype(jnp.bfloat16)
     k_t_ref[...] = k_full[...].astype(jnp.float32).T.astype(jnp.bfloat16)
     v_t = v_ref[...].astype(jnp.float32).T.astype(jnp.bfloat16)
-    wide = 256
+    wide = 512
     for head in range(heads):
         for start in range(0, length, wide):
             cols = slice(start, start + wide)
@@ -434,7 +434,7 @@
     g_wide = g_att[...].astype(jnp.float32)
     products_t = (g_wide * att_ref[PAD : PAD + length, :]).T
     g_heads = [jnp.where(lane_head == head, g_wide, 0.0).astype(jnp.bfloat16) for head in range(heads)]
-    wide = 256
+    wide = 512
     grad_v = jnp.zeros((length, LANES), jnp.float32)
     grad_k = jnp.zeros((length, LANES), jnp.float32)
     for head in range(heads):

time: 37.7 us -> 37 us (0.981)
  Pallas kernels: 10.1 us -> 9.16 us
    pallas_call x1, Pallas kernels: 3.4 us -> 2.6 us  [on_device_heads(): pl.pallas_call(functools.partial(forward_kernel, ranks, frames), out_shap...]
  transfers between devices with their start and end apart: 10 -> 10, of which waited for: 4 -> 4; matrix products, arithmetic and copies ran while one was open for 0% -> 0% of each run, Pallas kernels for 16% -> 14%
where the time goes in v7:
time: 37 us; the launch traced here: 36.9 us
  starting transfers between devices  16.1 us (44%)
  waiting for transfers between devices  9.98 us (27%)
  Pallas kernels  9.16 us (25%)
  local copies, waits for them, and re-layouts  0.92 us (2%)
  between operations  0.75 us (2%)
    ppermute x9, starting transfers between devices, swap(): lax.ppermute(array, 'seq', [(rank, rank ^ step) for rank in range(ranks)])  14.5 us
    ppermute x9, waiting for transfers between devices, swap(): lax.ppermute(array, 'seq', [(rank, rank ^ step) for rank in range(ranks)])  9.05 us
    pallas_call x1, Pallas kernels, on_device_heads(): pl.pallas_call(functools.partial(forward_kernel, ranks, frames), out_shap...  2.6 us
    pallas_call x1, Pallas kernels, on_device_heads(): pl.pallas_call(functools.partial(conv_back_kernel, ranks, frames), out_sh...  1.82 us
    ppermute x1, starting transfers between devices, on_device_heads(): lax.ppermute(own_taps, 'dp', [(one, (one + shift) % copies) for one in ra...  1.56 us
    pallas_call x1, Pallas kernels, on_device_heads(): pl.pallas_call(functools.partial(mask_kernel, ranks, length), out_shape=[...  1.32 us
    pallas_call x1, Pallas kernels, on_device_heads(): pl.pallas_call(backward_kernel, out_shape=[struct((length, LANES), bf16)]...  1.3 us
    pallas_call x1, Pallas kernels, on_device_heads(): pl.pallas_call(functools.partial(pack_kernel, ranks), out_shape=[struct((...  1.16 us
  transfers between devices with their start and end apart: 10, of which 4 were waited for; matrix products, arithmetic and copies ran while one was open for 0% of the time, Pallas kernels for 14%

profile of v7, /device:TPU:0, one launch (start us, length us, event | category | flops | bytes accessed | tf_op | source)
XLA Modules:
  0.0 36.9 jit_solution(4138464015793235346)
XLA Ops:
  0.6 0.0 copy-start.2
  0.6 0.0 copy-start.1
  0.7 0.0 copy-start
  0.7 1.2 %pack.1 = (bf16[3,128,128]{2,1,0:T(8,128)(2,1)S(1)}, bf16[3,128,128]{2,1,0:T(8,128)(2,1)S(1)}, bf16[3,128,128]{2,1,0:T(8,128)(2,1)S(1)}) custom-call(bf16[1,128,512]{2,1,0:T(8,128)(2,1)} %q_ref.3, bf16[1,128,512]{2,1,0:T(8,128)(2,1)} %k_ref.3, bf16[1,128,512]{2,1,0:T(8,128)(2,1)} %v_ref.3), custom_call_target="tpu_custom_call" | custom-call | tf_op jit(solution)/shard_map/pack/pallas_call | solution.py:499
  1.8 5.1 %collective-permute-start.3 = (bf16[3,128,128]{2,1,0:T(8,128)(2,1)S(1)}, bf16[3,128,128]{2,1,0:T(8,128)(2,1)S(1)}, u32[]{:S(2)}, u32[]{:S(2)}) collective-permute-start(bf16[3,128,128]{2,1,0:T(8,128)(2,1)S(1)} %get-tuple-element.36), channel_id=1, source_target_pairs={{0,6},{2,4},{4,2},{6,0},{1,7},{3,5},{5,3},{7,1},{8,14},{10,12},{12... | collective-permute-start | bytes 294920 | tf_op jit(solution)/shard_map/ppermute | solution.py:510
  6.9 0.0 copy-start.4
  6.9 0.0 collective-permute-start.4
  6.9 0.6 %collective-permute-start.5 = (bf16[3,128,128]{2,1,0:T(8,128)(2,1)S(1)}, bf16[3,128,128]{2,1,0:T(8,128)(2,1)S(1)}, u32[]{:S(2)}, u32[]{:S(2)}) collective-permute-start(bf16[3,128,128]{2,1,0:T(8,128)(2,1)S(1)} %get-tuple-element.38), channel_id=1, source_target_pairs={{0,2},{2,0},{4,6},{6,4},{1,3},{3,1},{5,7},{7,5},{8,10},{10,8},{12,... | collective-permute-start | bytes 294920 | tf_op jit(solution)/shard_map/ppermute | solution.py:510
  7.6 0.0 copy-done.2
  7.6 0.0 copy-done.1
  7.6 0.0 copy-done
  7.6 0.0 copy-done.4
  7.6 0.0 copy-start.3
  7.6 0.9 %copy-done.3 = bf16[1,128,512]{2,1,0:T(8,128)(2,1)S(1)} copy-done((bf16[1,128,512]{2,1,0:T(8,128)(2,1)S(1)}, bf16[1,128,512]{2,1,0:T(8,128)(2,1)}, u32[]{:S(2)}) %copy-start.3) | copy-done | bytes 131096
  8.5 0.0 copy-start.5
  8.5 1.3 %masks.1 = (bf16[128,128]{1,0:T(8,128)(2,1)S(1)}, bf16[128,128]{1,0:T(8,128)(2,1)S(1)}, bf16[128,128]{1,0:T(8,128)(2,1)S(1)}, bf16[4,128,128]{2,1,0:T(8,128)(2,1...) custom-call(s32[1,16]{1,0:T(1,128)S(1)} %copy-done.4, ...), custom_call_target="tpu_custom_call" | custom-call | flops 4194304 | bytes 1048576 | tf_op jit(solution)/shard_map/masks/pallas_call | solution.py:515
  9.9 3.8 %collective-permute-start = (bf16[128,128]{1,0:T(8,128)(2,1)S(1)}, bf16[128,128]{1,0:T(8,128)(2,1)S(1)}, u32[]{:S(2)}, u32[]{:S(2)}) collective-permute-start(bf16[128,128]{1,0:T(8,128)(2,1)S(1)} %get-tuple-element.32), channel_id=1, source_target_pairs={{0,6},{2,4},{4,2},{6,0},{1,7},{3,5},{5,3},{7,1},{8,14},{10,12},{12... | collective-permute-start | bytes 98312 | tf_op jit(solution)/shard_map/ppermute | solution.py:510
  13.7 0.0 collective-permute-start.1
  13.7 0.0 collective-permute-done.3.refs_0_
  13.7 1.3 %collective-permute-start.2 = (bf16[128,128]{1,0:T(8,128)(2,1)S(1)}, bf16[128,128]{1,0:T(8,128)(2,1)S(1)}, u32[]{:S(2)}, u32[]{:S(2)}) collective-permute-start(bf16[128,128]{1,0:T(8,128)(2,1)S(1)} %get-tuple-element.34), channel_id=1, source_target_pairs={{0,2},{2,0},{4,6},{6,4},{1,3},{3,1},{5,7},{7,5},{8,10},{10,8},{12,... | collective-permute-start | bytes 98312 | tf_op jit(solution)/shard_map/ppermute | solution.py:510
  15.0 2.3 %collective-permute-done.4.refs_1_ = bf16[3,128,128]{2,1,0:T(8,128)(2,1)S(1)} collective-permute-done((bf16[3,128,128]{2,1,0:T(8,128)(2,1)S(1)}, bf16[3,128,128]{2,1,0:T(8,128)(2,1)S(1)}, u32[]{:S(2)}, u32[]{:S(2)}) %collective-permute-start.4) | collective-permute-done | bytes 98336 | tf_op jit(solution)/shard_map/ppermute | solution.py:510
  17.3 0.0 collective-permute-done.5.refs_2_
  17.3 0.0 copy-done.5
  17.3 2.6 %forward.1 = (bf16[2,512,512]{2,1,0:T(8,128)(2,1)S(1)}, f32[544,128]{1,0:T(8,128)S(1)}, f32[512,128]{1,0:T(8,128)S(1)}, bf16[2,512,128]{2,1,0:T(8,128)(2,1)S(1)}...) custom-call(bf16[3,128,128]{2,1,0:T(8,128)(2,1)S(1)} %collective-permute-done.3.refs_0_, ...), custom_call_target="tpu_custom_call" | custom-call | flops 419430400 | bytes 3145728 | tf_op jit(solution)/shard_map/forward/pallas_call | solution.py:534
  19.9 0.0 collective-permute-done.refs_0_
  19.9 0.0 collective-permute-done.1.refs_1_
  20.0 0.0 collective-permute-done.2.refs_2_
  20.0 1.8 %conv_back.1 = (bf16[512,128]{1,0:T(8,128)(2,1)S(1)}, bf16[512,128]{1,0:T(8,128)(2,1)S(1)}, f32[32,128]{1,0:T(8,128)S(1)}) custom-call(bf16[128,128]{1,0:T(8,128)(2,1)S(1)} %collective-permute-done.refs_0_, bf16[128,128]{1,0:T(8,128)(2,1)S(1)} %collective-permute-done.1.refs_1_, bf16[128,128]{1,0:T(8,128)(2,1)S(1)} %collective-permute-done.2.refs_2_, ...), custom_call_target="tpu_custom_call" | custom-call | flops 419430400 | bytes 3145728 | tf_op jit(solution)/shard_map/conv_back/pallas_call | solution.py:558
  21.8 1.6 %collective-permute-start.6 = (f32[32,128]{1,0:T(8,128)S(1)}, f32[32,128]{1,0:T(8,128)S(1)}, u32[]{:S(2)}, u32[]{:S(2)}) collective-permute-start(f32[32,128]{1,0:T(8,128)S(1)} %get-tuple-element.54.refs_4_), channel_id=1, source_target_pairs={{0,8},{8,0},{1,9},{9,1},{2,10},{10,2},{3,11},{11,3},{4,12},{12,4},... | collective-permute-start | bytes 49160 | tf_op jit(solution)/shard_map/ppermute | solution.py:577
  23.4 1.3 %backward.1 = (bf16[512,128]{1,0:T(8,128)(2,1)S(1)}, bf16[512,128]{1,0:T(8,128)(2,1)S(1)}, bf16[512,128]{1,0:T(8,128)(2,1)S(1)}) custom-call(bf16[2,512,512]{2,1,0:T(8,128)(2,1)S(1)} %get-tuple-element.46.soft_ref, f32[544,128]{1,0:T(8,128)S(1)} %get-tuple-element.43.refs_4_.att_ref, bf16[512,128]{1,0:T(8,128)(2,1)S(1)} %get-tuple-element.47.g_att, ...), custom_call_target="tpu_custom_call" | custom-call | flops 838860800 | bytes 3145728 | tf_op jit(solution)/shard_map/backward/pallas_call | solution.py:581
  24.7 0.9 %collective-permute-done.6.refs_5_ = f32[32,128]{1,0:T(8,128)S(1)} collective-permute-done((f32[32,128]{1,0:T(8,128)S(1)}, f32[32,128]{1,0:T(8,128)S(1)}, u32[]{:S(2)}, u32[]{:S(2)}) %collective-permute-start.6) | collective-permute-done | bytes 16416 | tf_op jit(solution)/shard_map/ppermute | solution.py:577
  25.6 0.6 %collective-permute-start.8 = (bf16[544,128]{1,0:T(8,128)(2,1)S(1)}, bf16[544,128]{1,0:T(8,128)(2,1)S(1)}, u32[]{:S(2)}, u32[]{:S(2)}) collective-permute-start(bf16[544,128]{1,0:T(8,128)(2,1)S(1)} %get-tuple-element.57), channel_id=1, source_target_pairs={{0,4},{2,6},{4,0},{6,2},{1,5},{3,7},{5,1},{7,3},{8,12},{10,14},{12... | collective-permute-start | bytes 417800 | tf_op jit(solution)/shard_map/ppermute | solution.py:510
  26.2 2.1 %collective-permute-start.9 = (bf16[544,128]{1,0:T(8,128)(2,1)S(1)}, bf16[544,128]{1,0:T(8,128)(2,1)S(1)}, u32[]{:S(2)}, u32[]{:S(2)}) collective-permute-start(bf16[544,128]{1,0:T(8,128)(2,1)S(1)} %get-tuple-element.58), channel_id=1, source_target_pairs={{0,6},{2,4},{4,2},{6,0},{1,7},{3,5},{5,3},{7,1},{8,14},{10,12},{12... | collective-permute-start | bytes 417800 | tf_op jit(solution)/shard_map/ppermute | solution.py:510
  28.3 0.9 %collective-permute-start.7 = (bf16[544,128]{1,0:T(8,128)(2,1)S(1)}, bf16[544,128]{1,0:T(8,128)(2,1)S(1)}, u32[]{:S(2)}, u32[]{:S(2)}) collective-permute-start(bf16[544,128]{1,0:T(8,128)(2,1)S(1)} %get-tuple-element.56), channel_id=1, source_target_pairs={{0,2},{2,0},{4,6},{6,4},{1,3},{3,1},{5,7},{7,5},{8,10},{10,8},{12,... | collective-permute-start | bytes 417800 | tf_op jit(solution)/shard_map/ppermute | solution.py:510
  29.3 6.2 %collective-permute-done.8.refs_2_ = bf16[544,128]{1,0:T(8,128)(2,1)S(1)} collective-permute-done((bf16[544,128]{1,0:T(8,128)(2,1)S(1)}, bf16[544,128]{1,0:T(8,128)(2,1)S(1)}, u32[]{:S(2)}, u32[]{:S(2)}) %collective-permute-start.8) | collective-permute-done | bytes 139296 | tf_op jit(solution)/shard_map/ppermute | solution.py:510
  35.4 0.0 collective-permute-done.9.refs_3_
  35.4 0.5 %collective-permute-done.7.refs_1_ = bf16[544,128]{1,0:T(8,128)(2,1)S(1)} collective-permute-done((bf16[544,128]{1,0:T(8,128)(2,1)S(1)}, bf16[544,128]{1,0:T(8,128)(2,1)S(1)}, u32[]{:S(2)}, u32[]{:S(2)}) %collective-permute-start.7) | collective-permute-done | bytes 139296 | tf_op jit(solution)/shard_map/ppermute | solution.py:510
  36.0 0.9 %spread.1 = (bf16[1,128,512]{2,1,0:T(8,128)(2,1)}, bf16[1,128,512]{2,1,0:T(8,128)(2,1)}, bf16[1,128,512]{2,1,0:T(8,128)(2,1)}, bf16[1,128,512]{2,1,0:T(8,128)(2,1)}, f32[31,512]{1,0:T(8,128)}) custom-call(bf16[544,128]{1,0:T(8,128)(2,1)S(1)} %get-tuple-element.55.refs_0_, bf16[544,128]{1,0:T(8,128)(2,1)S(1)} %collective-permute-done.7.refs_1_, ...), custom_call_target="tpu_custom_call" | custom-call | tf_op jit(solution)/shard_map/spread/pallas_call | solution.py:610
  (2 shorter events, 0.0 us)
Async XLA Ops:
  0.6 7.0 %copy-start.2 = (bf16[1,128,512]{2,1,0:T(8,128)(2,1)S(1)}, bf16[1,128,512]{2,1,0:T(8,128)(2,1)}, u32[]{:S(2)}) copy-start(bf16[1,128,512]{2,1,0:T(8,128)(2,1)} %v_ref.3) | copy-start | bytes 393220
  0.6 7.0 %copy-start.1 = (bf16[1,128,512]{2,1,0:T(8,128)(2,1)S(1)}, bf16[1,128,512]{2,1,0:T(8,128)(2,1)}, u32[]{:S(2)}) copy-start(bf16[1,128,512]{2,1,0:T(8,128)(2,1)} %k_ref.3) | copy-start | bytes 393220
  0.7 7.0 %copy-start = (bf16[1,128,512]{2,1,0:T(8,128)(2,1)S(1)}, bf16[1,128,512]{2,1,0:T(8,128)(2,1)}, u32[]{:S(2)}) copy-start(bf16[1,128,512]{2,1,0:T(8,128)(2,1)} %q_ref.3) | copy-start | bytes 393220
  1.8 11.8 %collective-permute-start.3 = (bf16[3,128,128]{2,1,0:T(8,128)(2,1)S(1)}, bf16[3,128,128]{2,1,0:T(8,128)(2,1)S(1)}, u32[]{:S(2)}, u32[]{:S(2)}) collective-permute-start(bf16[3,128,128]{2,1,0:T(8,128)(2,1)S(1)} %get-tuple-element.36), channel_id=1, source_target_pairs={{0,6},{2,4},{4,2},{6,0},{1,7},{3,5},{5,3},{7,1},{8,14},{10,12},{12... | collective-permute-start | bytes 294920 | tf_op jit(solution)/shard_map/ppermute | solution.py:510
  6.9 0.7 %copy-start.4 = (s32[1,16]{1,0:T(1,128)S(1)}, s32[1,16]{1,0:T(1,128)}, u32[]{:S(2)}) copy-start(s32[1,16]{1,0:T(1,128)} %lens_ref.1) | copy-start | bytes 196
  6.9 10.4 %collective-permute-start.4 = (bf16[3,128,128]{2,1,0:T(8,128)(2,1)S(1)}, bf16[3,128,128]{2,1,0:T(8,128)(2,1)S(1)}, u32[]{:S(2)}, u32[]{:S(2)}) collective-permute-start(bf16[3,128,128]{2,1,0:T(8,128)(2,1)S(1)} %get-tuple-element.37), channel_id=1, source_target_pairs={{0,4},{2,6},{4,0},{6,2},{1,5},{3,7},{5,1},{7,3},{8,12},{10,14},{12... | collective-permute-start | bytes 294920 | tf_op jit(solution)/shard_map/ppermute | solution.py:510
  6.9 10.4 %collective-permute-start.5 = (bf16[3,128,128]{2,1,0:T(8,128)(2,1)S(1)}, bf16[3,128,128]{2,1,0:T(8,128)(2,1)S(1)}, u32[]{:S(2)}, u32[]{:S(2)}) collective-permute-start(bf16[3,128,128]{2,1,0:T(8,128)(2,1)S(1)} %get-tuple-element.38), channel_id=1, source_target_pairs={{0,2},{2,0},{4,6},{6,4},{1,3},{3,1},{5,7},{7,5},{8,10},{10,8},{12,... | collective-permute-start | bytes 294920 | tf_op jit(solution)/shard_map/ppermute | solution.py:510
  7.6 0.9 %copy-start.3 = (bf16[1,128,512]{2,1,0:T(8,128)(2,1)S(1)}, bf16[1,128,512]{2,1,0:T(8,128)(2,1)}, u32[]{:S(2)}) copy-start(bf16[1,128,512]{2,1,0:T(8,128)(2,1)} %c_ref.1) | copy-start | bytes 393220
  8.5 8.8 %copy-start.5 = (f32[31,512]{1,0:T(8,128)S(1)}, f32[31,512]{1,0:T(8,128)}, u32[]{:S(2)}) copy-start(f32[31,512]{1,0:T(8,128)} %refs_8_.3) | copy-start | bytes 190468
  9.9 10.1 %collective-permute-start = (bf16[128,128]{1,0:T(8,128)(2,1)S(1)}, bf16[128,128]{1,0:T(8,128)(2,1)S(1)}, u32[]{:S(2)}, u32[]{:S(2)}) collective-permute-start(bf16[128,128]{1,0:T(8,128)(2,1)S(1)} %get-tuple-element.32), channel_id=1, source_target_pairs={{0,6},{2,4},{4,2},{6,0},{1,7},{3,5},{5,3},{7,1},{8,14},{10,12},{12... | collective-permute-start | bytes 98312 | tf_op jit(solution)/shard_map/ppermute | solution.py:510
  13.7 6.3 %collective-permute-start.1 = (bf16[128,128]{1,0:T(8,128)(2,1)S(1)}, bf16[128,128]{1,0:T(8,128)(2,1)S(1)}, u32[]{:S(2)}, u32[]{:S(2)}) collective-permute-start(bf16[128,128]{1,0:T(8,128)(2,1)S(1)} %get-tuple-element.33), channel_id=1, source_target_pairs={{0,4},{2,6},{4,0},{6,2},{1,5},{3,7},{5,1},{7,3},{8,12},{10,14},{12... | collective-permute-start | bytes 98312 | tf_op jit(solution)/shard_map/ppermute | solution.py:510
  13.7 6.3 %collective-permute-start.2 = (bf16[128,128]{1,0:T(8,128)(2,1)S(1)}, bf16[128,128]{1,0:T(8,128)(2,1)S(1)}, u32[]{:S(2)}, u32[]{:S(2)}) collective-permute-start(bf16[128,128]{1,0:T(8,128)(2,1)S(1)} %get-tuple-element.34), channel_id=1, source_target_pairs={{0,2},{2,0},{4,6},{6,4},{1,3},{3,1},{5,7},{7,5},{8,10},{10,8},{12,... | collective-permute-start | bytes 98312 | tf_op jit(solution)/shard_map/ppermute | solution.py:510
  21.8 3.8 %collective-permute-start.6 = (f32[32,128]{1,0:T(8,128)S(1)}, f32[32,128]{1,0:T(8,128)S(1)}, u32[]{:S(2)}, u32[]{:S(2)}) collective-permute-start(f32[32,128]{1,0:T(8,128)S(1)} %get-tuple-element.54.refs_4_), channel_id=1, source_target_pairs={{0,8},{8,0},{1,9},{9,1},{2,10},{10,2},{3,11},{11,3},{4,12},{12,4},... | collective-permute-start | bytes 49160 | tf_op jit(solution)/shard_map/ppermute | solution.py:577
  25.6 9.8 %collective-permute-start.8 = (bf16[544,128]{1,0:T(8,128)(2,1)S(1)}, bf16[544,128]{1,0:T(8,128)(2,1)S(1)}, u32[]{:S(2)}, u32[]{:S(2)}) collective-permute-start(bf16[544,128]{1,0:T(8,128)(2,1)S(1)} %get-tuple-element.57), channel_id=1, source_target_pairs={{0,4},{2,6},{4,0},{6,2},{1,5},{3,7},{5,1},{7,3},{8,12},{10,14},{12... | collective-permute-start | bytes 417800 | tf_op jit(solution)/shard_map/ppermute | solution.py:510
  26.2 9.2 %collective-permute-start.9 = (bf16[544,128]{1,0:T(8,128)(2,1)S(1)}, bf16[544,128]{1,0:T(8,128)(2,1)S(1)}, u32[]{:S(2)}, u32[]{:S(2)}) collective-permute-start(bf16[544,128]{1,0:T(8,128)(2,1)S(1)} %get-tuple-element.58), channel_id=1, source_target_pairs={{0,6},{2,4},{4,2},{6,0},{1,7},{3,5},{5,3},{7,1},{8,14},{10,12},{12... | collective-permute-start | bytes 417800 | tf_op jit(solution)/shard_map/ppermute | solution.py:510
  28.3 7.6 %collective-permute-start.7 = (bf16[544,128]{1,0:T(8,128)(2,1)S(1)}, bf16[544,128]{1,0:T(8,128)(2,1)S(1)}, u32[]{:S(2)}, u32[]{:S(2)}) collective-permute-start(bf16[544,128]{1,0:T(8,128)(2,1)S(1)} %get-tuple-element.56), channel_id=1, source_target_pairs={{0,2},{2,0},{4,6},{6,4},{1,3},{3,1},{5,7},{7,5},{8,10},{10,8},{12,... | collective-permute-start | bytes 417800 | tf_op jit(solution)/shard_map/ppermute | solution.py:510

commit v8 on v7

--- a/solution.py
+++ b/solution.py
@@ -467,7 +467,7 @@
 
 
 def spread_kernel(ranks, frames, *refs):
-    blocks = refs[:ranks]
+    blocks = refs[:ranks][::-1]
     targets, taps_ref = refs[ranks : ranks + 4], refs[ranks + 4]
     me = lax.axis_index("seq")
     for step in range(ranks):
@@ -589,23 +589,17 @@
         name="backward",
     )(soft, att, g_att, q_heads, k_t, v_full)
 
-    def blocks_of(steps):
-        return pl.pallas_call(
-            functools.partial(block_kernel, steps, frames),
-            out_shape=[struct((4 * frames + taps, LANES), bf16)] * len(steps),
-            in_specs=[vmem] * (4 + copies),
-            out_specs=[vmem] * len(steps),
-            compiler_params=params,
-            cost_estimate=cost(MIB, MIB),
-            name="blocks",
-        )(mixed, *results, *part_taps)
-
-    half = ranks // 2
-    far = blocks_of(list(range(half, ranks)))
-    near = blocks_of(list(range(half)))
-    back = {step: swap(far[step - half], step) for step in range(half, ranks)}
-    back |= {step: swap(near[step], step) for step in range(1, half)}
-    back[0] = near[0]
+    steps = list(range(ranks - 1, -1, -1))
+    blocks = pl.pallas_call(
+        functools.partial(block_kernel, steps, frames),
+        out_shape=[struct((4 * frames + taps, LANES), bf16)] * ranks,
+        in_specs=[vmem] * (4 + copies),
+        out_specs=[vmem] * ranks,
+        compiler_params=params,
+        cost_estimate=cost(MIB, MIB),
+        name="blocks",
+    )(mixed, *results, *part_taps)
+    back = [swap(block, step) if step else block for block, step in zip(blocks, steps)]
 
     return pl.pallas_call(
         functools.partial(spread_kernel, ranks, frames),
@@ -614,7 +608,7 @@
         out_specs=[vmem] * 5,
         compiler_params=params,
         name="spread",
-    )(*[back[step] for step in range(ranks)])
+    )(*back)
 
 
 def on_device_any(queries, keys, values, cotangent, conv_weight, rec_lengths):

time: 37 us -> 37.9 us (1.024)
  starting transfers between devices: 16.1 us -> 16.9 us
    ppermute x9, starting transfers between devices: 14.5 us -> 15.3 us  [swap(): lax.ppermute(array, 'seq', [(rank, rank ^ step) for rank in range(ranks)])]
where the time goes in v8:
time: 37.9 us; the launch traced here: 37.7 us
  starting transfers between devices  16.9 us (45%)
  waiting for transfers between devices  9.98 us (26%)
  Pallas kernels  9.15 us (24%)
  local copies, waits for them, and re-layouts  0.92 us (2%)
  between operations  0.74 us (2%)
    ppermute x9, starting transfers between devices, swap(): lax.ppermute(array, 'seq', [(rank, rank ^ step) for rank in range(ranks)])  15.3 us
    ppermute x9, waiting for transfers between devices, swap(): lax.ppermute(array, 'seq', [(rank, rank ^ step) for rank in range(ranks)])  9.05 us
    pallas_call x1, Pallas kernels, on_device_heads(): pl.pallas_call(functools.partial(forward_kernel, ranks, frames), out_shap...  2.6 us
    pallas_call x1, Pallas kernels, on_device_heads(): pl.pallas_call(functools.partial(conv_back_kernel, ranks, frames), out_sh...  1.82 us
    ppermute x1, starting transfers between devices, on_device_heads(): lax.ppermute(own_taps, 'dp', [(one, (one + shift) % copies) for one in ra...  1.56 us
    pallas_call x1, Pallas kernels, on_device_heads(): pl.pallas_call(functools.partial(mask_kernel, ranks, length), out_shape=[...  1.32 us
    pallas_call x1, Pallas kernels, on_device_heads(): pl.pallas_call(backward_kernel, out_shape=[struct((length, LANES), bf16)]...  1.3 us
    pallas_call x1, Pallas kernels, on_device_heads(): pl.pallas_call(functools.partial(pack_kernel, ranks), out_shape=[struct((...  1.16 us
  transfers between devices with their start and end apart: 10, of which 4 were waited for; matrix products, arithmetic and copies ran while one was open for 0% of the time, Pallas kernels for 14%

profile of v8, /device:TPU:0, one launch (start us, length us, event | category | flops | bytes accessed | tf_op | source)
XLA Modules:
  0.0 37.7 jit_solution(1956947121158941603)
XLA Ops:
  0.6 0.0 copy-start.2
  0.6 0.0 copy-start.1
  0.7 0.0 copy-start
  0.7 1.2 %pack.1 = (bf16[3,128,128]{2,1,0:T(8,128)(2,1)S(1)}, bf16[3,128,128]{2,1,0:T(8,128)(2,1)S(1)}, bf16[3,128,128]{2,1,0:T(8,128)(2,1)S(1)}) custom-call(bf16[1,128,512]{2,1,0:T(8,128)(2,1)} %q_ref.3, bf16[1,128,512]{2,1,0:T(8,128)(2,1)} %k_ref.3, bf16[1,128,512]{2,1,0:T(8,128)(2,1)} %v_ref.3), custom_call_target="tpu_custom_call" | custom-call | tf_op jit(solution)/shard_map/pack/pallas_call | solution.py:499
  1.8 5.1 %collective-permute-start.3 = (bf16[3,128,128]{2,1,0:T(8,128)(2,1)S(1)}, bf16[3,128,128]{2,1,0:T(8,128)(2,1)S(1)}, u32[]{:S(2)}, u32[]{:S(2)}) collective-permute-start(bf16[3,128,128]{2,1,0:T(8,128)(2,1)S(1)} %get-tuple-element.36), channel_id=1, source_target_pairs={{0,6},{2,4},{4,2},{6,0},{1,7},{3,5},{5,3},{7,1},{8,14},{10,12},{12... | collective-permute-start | bytes 294920 | tf_op jit(solution)/shard_map/ppermute | solution.py:510
  6.9 0.0 copy-start.4
  6.9 0.0 collective-permute-start.4
  6.9 0.6 %collective-permute-start.5 = (bf16[3,128,128]{2,1,0:T(8,128)(2,1)S(1)}, bf16[3,128,128]{2,1,0:T(8,128)(2,1)S(1)}, u32[]{:S(2)}, u32[]{:S(2)}) collective-permute-start(bf16[3,128,128]{2,1,0:T(8,128)(2,1)S(1)} %get-tuple-element.38), channel_id=1, source_target_pairs={{0,2},{2,0},{4,6},{6,4},{1,3},{3,1},{5,7},{7,5},{8,10},{10,8},{12,... | collective-permute-start | bytes 294920 | tf_op jit(solution)/shard_map/ppermute | solution.py:510
  7.6 0.0 copy-done.2
  7.6 0.0 copy-done.1
  7.6 0.0 copy-done
  7.6 0.0 copy-done.4
  7.6 0.0 copy-start.3
  7.6 0.9 %copy-done.3 = bf16[1,128,512]{2,1,0:T(8,128)(2,1)S(1)} copy-done((bf16[1,128,512]{2,1,0:T(8,128)(2,1)S(1)}, bf16[1,128,512]{2,1,0:T(8,128)(2,1)}, u32[]{:S(2)}) %copy-start.3) | copy-done | bytes 131096
  8.5 0.0 copy-start.5
  8.5 1.3 %masks.1 = (bf16[128,128]{1,0:T(8,128)(2,1)S(1)}, bf16[128,128]{1,0:T(8,128)(2,1)S(1)}, bf16[128,128]{1,0:T(8,128)(2,1)S(1)}, bf16[4,128,128]{2,1,0:T(8,128)(2,1...) custom-call(s32[1,16]{1,0:T(1,128)S(1)} %copy-done.4, ...), custom_call_target="tpu_custom_call" | custom-call | flops 4194304 | bytes 1048576 | tf_op jit(solution)/shard_map/masks/pallas_call | solution.py:515
  9.9 3.8 %collective-permute-start = (bf16[128,128]{1,0:T(8,128)(2,1)S(1)}, bf16[128,128]{1,0:T(8,128)(2,1)S(1)}, u32[]{:S(2)}, u32[]{:S(2)}) collective-permute-start(bf16[128,128]{1,0:T(8,128)(2,1)S(1)} %get-tuple-element.32), channel_id=1, source_target_pairs={{0,6},{2,4},{4,2},{6,0},{1,7},{3,5},{5,3},{7,1},{8,14},{10,12},{12... | collective-permute-start | bytes 98312 | tf_op jit(solution)/shard_map/ppermute | solution.py:510
  13.7 0.0 collective-permute-start.1
  13.7 0.0 collective-permute-done.3.refs_0_
  13.7 1.3 %collective-permute-start.2 = (bf16[128,128]{1,0:T(8,128)(2,1)S(1)}, bf16[128,128]{1,0:T(8,128)(2,1)S(1)}, u32[]{:S(2)}, u32[]{:S(2)}) collective-permute-start(bf16[128,128]{1,0:T(8,128)(2,1)S(1)} %get-tuple-element.34), channel_id=1, source_target_pairs={{0,2},{2,0},{4,6},{6,4},{1,3},{3,1},{5,7},{7,5},{8,10},{10,8},{12,... | collective-permute-start | bytes 98312 | tf_op jit(solution)/shard_map/ppermute | solution.py:510
  15.0 2.3 %collective-permute-done.4.refs_1_ = bf16[3,128,128]{2,1,0:T(8,128)(2,1)S(1)} collective-permute-done((bf16[3,128,128]{2,1,0:T(8,128)(2,1)S(1)}, bf16[3,128,128]{2,1,0:T(8,128)(2,1)S(1)}, u32[]{:S(2)}, u32[]{:S(2)}) %collective-permute-start.4) | collective-permute-done | bytes 98336 | tf_op jit(solution)/shard_map/ppermute | solution.py:510
  17.3 0.0 collective-permute-done.5.refs_2_
  17.3 0.0 copy-done.5
  17.3 2.6 %forward.1 = (bf16[2,512,512]{2,1,0:T(8,128)(2,1)S(1)}, f32[544,128]{1,0:T(8,128)S(1)}, f32[512,128]{1,0:T(8,128)S(1)}, bf16[2,512,128]{2,1,0:T(8,128)(2,1)S(1)}...) custom-call(bf16[3,128,128]{2,1,0:T(8,128)(2,1)S(1)} %collective-permute-done.3.refs_0_, ...), custom_call_target="tpu_custom_call" | custom-call | flops 419430400 | bytes 3145728 | tf_op jit(solution)/shard_map/forward/pallas_call | solution.py:534
  19.9 0.0 collective-permute-done.refs_0_
  19.9 0.0 collective-permute-done.1.refs_1_
  20.0 0.0 collective-permute-done.2.refs_2_
  20.0 1.8 %conv_back.1 = (bf16[512,128]{1,0:T(8,128)(2,1)S(1)}, bf16[512,128]{1,0:T(8,128)(2,1)S(1)}, f32[32,128]{1,0:T(8,128)S(1)}) custom-call(bf16[128,128]{1,0:T(8,128)(2,1)S(1)} %collective-permute-done.refs_0_, bf16[128,128]{1,0:T(8,128)(2,1)S(1)} %collective-permute-done.1.refs_1_, bf16[128,128]{1,0:T(8,128)(2,1)S(1)} %collective-permute-done.2.refs_2_, ...), custom_call_target="tpu_custom_call" | custom-call | flops 419430400 | bytes 3145728 | tf_op jit(solution)/shard_map/conv_back/pallas_call | solution.py:558
  21.8 1.6 %collective-permute-start.6 = (f32[32,128]{1,0:T(8,128)S(1)}, f32[32,128]{1,0:T(8,128)S(1)}, u32[]{:S(2)}, u32[]{:S(2)}) collective-permute-start(f32[32,128]{1,0:T(8,128)S(1)} %get-tuple-element.54.refs_4_), channel_id=1, source_target_pairs={{0,8},{8,0},{1,9},{9,1},{2,10},{10,2},{3,11},{11,3},{4,12},{12,4},... | collective-permute-start | bytes 49160 | tf_op jit(solution)/shard_map/ppermute | solution.py:577
  23.4 1.3 %backward.1 = (bf16[512,128]{1,0:T(8,128)(2,1)S(1)}, bf16[512,128]{1,0:T(8,128)(2,1)S(1)}, bf16[512,128]{1,0:T(8,128)(2,1)S(1)}) custom-call(bf16[2,512,512]{2,1,0:T(8,128)(2,1)S(1)} %get-tuple-element.46.soft_ref, f32[544,128]{1,0:T(8,128)S(1)} %get-tuple-element.43.refs_4_.att_ref, bf16[512,128]{1,0:T(8,128)(2,1)S(1)} %get-tuple-element.47.g_att, ...), custom_call_target="tpu_custom_call" | custom-call | flops 838860800 | bytes 3145728 | tf_op jit(solution)/shard_map/backward/pallas_call | solution.py:581
  24.7 0.9 %collective-permute-done.6.refs_5_ = f32[32,128]{1,0:T(8,128)S(1)} collective-permute-done((f32[32,128]{1,0:T(8,128)S(1)}, f32[32,128]{1,0:T(8,128)S(1)}, u32[]{:S(2)}, u32[]{:S(2)}) %collective-permute-start.6) | collective-permute-done | bytes 16416 | tf_op jit(solution)/shard_map/ppermute | solution.py:577
  25.6 2.6 %collective-permute-start.7 = (bf16[544,128]{1,0:T(8,128)(2,1)S(1)}, bf16[544,128]{1,0:T(8,128)(2,1)S(1)}, u32[]{:S(2)}, u32[]{:S(2)}) collective-permute-start(bf16[544,128]{1,0:T(8,128)(2,1)S(1)} %get-tuple-element.55), channel_id=1, source_target_pairs={{0,6},{2,4},{4,2},{6,0},{1,7},{3,5},{5,3},{7,1},{8,14},{10,12},{12... | collective-permute-start | bytes 417800 | tf_op jit(solution)/shard_map/ppermute | solution.py:510
  28.2 0.0 collective-permute-start.8
  28.2 1.9 %collective-permute-start.9 = (bf16[544,128]{1,0:T(8,128)(2,1)S(1)}, bf16[544,128]{1,0:T(8,128)(2,1)S(1)}, u32[]{:S(2)}, u32[]{:S(2)}) collective-permute-start(bf16[544,128]{1,0:T(8,128)(2,1)S(1)} %get-tuple-element.57), channel_id=1, source_target_pairs={{0,2},{2,0},{4,6},{6,4},{1,3},{3,1},{5,7},{7,5},{8,10},{10,8},{12,... | collective-permute-start | bytes 417800 | tf_op jit(solution)/shard_map/ppermute | solution.py:510
  30.1 2.7 %collective-permute-done.7.refs_0_ = bf16[544,128]{1,0:T(8,128)(2,1)S(1)} collective-permute-done((bf16[544,128]{1,0:T(8,128)(2,1)S(1)}, bf16[544,128]{1,0:T(8,128)(2,1)S(1)}, u32[]{:S(2)}, u32[]{:S(2)}) %collective-permute-start.7) | collective-permute-done | bytes 139296 | tf_op jit(solution)/shard_map/ppermute | solution.py:510
  32.8 4.0 %collective-permute-done.8.refs_1_ = bf16[544,128]{1,0:T(8,128)(2,1)S(1)} collective-permute-done((bf16[544,128]{1,0:T(8,128)(2,1)S(1)}, bf16[544,128]{1,0:T(8,128)(2,1)S(1)}, u32[]{:S(2)}, u32[]{:S(2)}) %collective-permute-start.8) | collective-permute-done | bytes 139296 | tf_op jit(solution)/shard_map/ppermute | solution.py:510
  36.8 0.0 collective-permute-done.9.refs_2_
  36.8 0.9 %spread.1 = (bf16[1,128,512]{2,1,0:T(8,128)(2,1)}, bf16[1,128,512]{2,1,0:T(8,128)(2,1)}, bf16[1,128,512]{2,1,0:T(8,128)(2,1)}, bf16[1,128,512]{2,1,0:T(8,128)(2,1)}, f32[31,512]{1,0:T(8,128)}) custom-call(bf16[544,128]{1,0:T(8,128)(2,1)S(1)} %collective-permute-done.7.refs_0_, bf16[544,128]{1,0:T(8,128)(2,1)S(1)} %collective-permute-done.8.refs_1_, ...), custom_call_target="tpu_custom_call" | custom-call | tf_op jit(solution)/shard_map/spread/pallas_call | solution.py:604
  (1 shorter events, 0.0 us)
Async XLA Ops:
  0.6 7.0 %copy-start.2 = (bf16[1,128,512]{2,1,0:T(8,128)(2,1)S(1)}, bf16[1,128,512]{2,1,0:T(8,128)(2,1)}, u32[]{:S(2)}) copy-start(bf16[1,128,512]{2,1,0:T(8,128)(2,1)} %v_ref.3) | copy-start | bytes 393220
  0.6 7.0 %copy-start.1 = (bf16[1,128,512]{2,1,0:T(8,128)(2,1)S(1)}, bf16[1,128,512]{2,1,0:T(8,128)(2,1)}, u32[]{:S(2)}) copy-start(bf16[1,128,512]{2,1,0:T(8,128)(2,1)} %k_ref.3) | copy-start | bytes 393220
  0.7 7.0 %copy-start = (bf16[1,128,512]{2,1,0:T(8,128)(2,1)S(1)}, bf16[1,128,512]{2,1,0:T(8,128)(2,1)}, u32[]{:S(2)}) copy-start(bf16[1,128,512]{2,1,0:T(8,128)(2,1)} %q_ref.3) | copy-start | bytes 393220
  1.8 11.8 %collective-permute-start.3 = (bf16[3,128,128]{2,1,0:T(8,128)(2,1)S(1)}, bf16[3,128,128]{2,1,0:T(8,128)(2,1)S(1)}, u32[]{:S(2)}, u32[]{:S(2)}) collective-permute-start(bf16[3,128,128]{2,1,0:T(8,128)(2,1)S(1)} %get-tuple-element.36), channel_id=1, source_target_pairs={{0,6},{2,4},{4,2},{6,0},{1,7},{3,5},{5,3},{7,1},{8,14},{10,12},{12... | collective-permute-start | bytes 294920 | tf_op jit(solution)/shard_map/ppermute | solution.py:510
  6.9 0.7 %copy-start.4 = (s32[1,16]{1,0:T(1,128)S(1)}, s32[1,16]{1,0:T(1,128)}, u32[]{:S(2)}) copy-start(s32[1,16]{1,0:T(1,128)} %lens_ref.1) | copy-start | bytes 196
  6.9 10.4 %collective-permute-start.4 = (bf16[3,128,128]{2,1,0:T(8,128)(2,1)S(1)}, bf16[3,128,128]{2,1,0:T(8,128)(2,1)S(1)}, u32[]{:S(2)}, u32[]{:S(2)}) collective-permute-start(bf16[3,128,128]{2,1,0:T(8,128)(2,1)S(1)} %get-tuple-element.37), channel_id=1, source_target_pairs={{0,4},{2,6},{4,0},{6,2},{1,5},{3,7},{5,1},{7,3},{8,12},{10,14},{12... | collective-permute-start | bytes 294920 | tf_op jit(solution)/shard_map/ppermute | solution.py:510
  6.9 10.4 %collective-permute-start.5 = (bf16[3,128,128]{2,1,0:T(8,128)(2,1)S(1)}, bf16[3,128,128]{2,1,0:T(8,128)(2,1)S(1)}, u32[]{:S(2)}, u32[]{:S(2)}) collective-permute-start(bf16[3,128,128]{2,1,0:T(8,128)(2,1)S(1)} %get-tuple-element.38), channel_id=1, source_target_pairs={{0,2},{2,0},{4,6},{6,4},{1,3},{3,1},{5,7},{7,5},{8,10},{10,8},{12,... | collective-permute-start | bytes 294920 | tf_op jit(solution)/shard_map/ppermute | solution.py:510
  7.6 0.9 %copy-start.3 = (bf16[1,128,512]{2,1,0:T(8,128)(2,1)S(1)}, bf16[1,128,512]{2,1,0:T(8,128)(2,1)}, u32[]{:S(2)}) copy-start(bf16[1,128,512]{2,1,0:T(8,128)(2,1)} %c_ref.1) | copy-start | bytes 393220
  8.5 8.8 %copy-start.5 = (f32[31,512]{1,0:T(8,128)S(1)}, f32[31,512]{1,0:T(8,128)}, u32[]{:S(2)}) copy-start(f32[31,512]{1,0:T(8,128)} %refs_8_.3) | copy-start | bytes 190468
  9.9 10.1 %collective-permute-start = (bf16[128,128]{1,0:T(8,128)(2,1)S(1)}, bf16[128,128]{1,0:T(8,128)(2,1)S(1)}, u32[]{:S(2)}, u32[]{:S(2)}) collective-permute-start(bf16[128,128]{1,0:T(8,128)(2,1)S(1)} %get-tuple-element.32), channel_id=1, source_target_pairs={{0,6},{2,4},{4,2},{6,0},{1,7},{3,5},{5,3},{7,1},{8,14},{10,12},{12... | collective-permute-start | bytes 98312 | tf_op jit(solution)/shard_map/ppermute | solution.py:510
  13.7 6.3 %collective-permute-start.1 = (bf16[128,128]{1,0:T(8,128)(2,1)S(1)}, bf16[128,128]{1,0:T(8,128)(2,1)S(1)}, u32[]{:S(2)}, u32[]{:S(2)}) collective-permute-start(bf16[128,128]{1,0:T(8,128)(2,1)S(1)} %get-tuple-element.33), channel_id=1, source_target_pairs={{0,4},{2,6},{4,0},{6,2},{1,5},{3,7},{5,1},{7,3},{8,12},{10,14},{12... | collective-permute-start | bytes 98312 | tf_op jit(solution)/shard_map/ppermute | solution.py:510
  13.7 6.3 %collective-permute-start.2 = (bf16[128,128]{1,0:T(8,128)(2,1)S(1)}, bf16[128,128]{1,0:T(8,128)(2,1)S(1)}, u32[]{:S(2)}, u32[]{:S(2)}) collective-permute-start(bf16[128,128]{1,0:T(8,128)(2,1)S(1)} %get-tuple-element.34), channel_id=1, source_target_pairs={{0,2},{2,0},{4,6},{6,4},{1,3},{3,1},{5,7},{7,5},{8,10},{10,8},{12,... | collective-permute-start | bytes 98312 | tf_op jit(solution)/shard_map/ppermute | solution.py:510
  21.8 3.8 %collective-permute-start.6 = (f32[32,128]{1,0:T(8,128)S(1)}, f32[32,128]{1,0:T(8,128)S(1)}, u32[]{:S(2)}, u32[]{:S(2)}) collective-permute-start(f32[32,128]{1,0:T(8,128)S(1)} %get-tuple-element.54.refs_4_), channel_id=1, source_target_pairs={{0,8},{8,0},{1,9},{9,1},{2,10},{10,2},{3,11},{11,3},{4,12},{12,4},... | collective-permute-start | bytes 49160 | tf_op jit(solution)/shard_map/ppermute | solution.py:577
  25.6 7.1 %collective-permute-start.7 = (bf16[544,128]{1,0:T(8,128)(2,1)S(1)}, bf16[544,128]{1,0:T(8,128)(2,1)S(1)}, u32[]{:S(2)}, u32[]{:S(2)}) collective-permute-start(bf16[544,128]{1,0:T(8,128)(2,1)S(1)} %get-tuple-element.55), channel_id=1, source_target_pairs={{0,6},{2,4},{4,2},{6,0},{1,7},{3,5},{5,3},{7,1},{8,14},{10,12},{12... | collective-permute-start | bytes 417800 | tf_op jit(solution)/shard_map/ppermute | solution.py:510
  28.2 8.6 %collective-permute-start.8 = (bf16[544,128]{1,0:T(8,128)(2,1)S(1)}, bf16[544,128]{1,0:T(8,128)(2,1)S(1)}, u32[]{:S(2)}, u32[]{:S(2)}) collective-permute-start(bf16[544,128]{1,0:T(8,128)(2,1)S(1)} %get-tuple-element.56), channel_id=1, source_target_pairs={{0,4},{2,6},{4,0},{6,2},{1,5},{3,7},{5,1},{7,3},{8,12},{10,14},{12... | collective-permute-start | bytes 417800 | tf_op jit(solution)/shard_map/ppermute | solution.py:510
  28.2 8.6 %collective-permute-start.9 = (bf16[544,128]{1,0:T(8,128)(2,1)S(1)}, bf16[544,128]{1,0:T(8,128)(2,1)S(1)}, u32[]{:S(2)}, u32[]{:S(2)}) collective-permute-start(bf16[544,128]{1,0:T(8,128)(2,1)S(1)} %get-tuple-element.57), channel_id=1, source_target_pairs={{0,2},{2,0},{4,6},{6,4},{1,3},{3,1},{5,7},{7,5},{8,10},{10,8},{12,... | collective-permute-start | bytes 417800 | tf_op jit(solution)/shard_map/ppermute | solution.py:510

commit v9 on v7

--- a/solution.py
+++ b/solution.py
@@ -255,6 +255,11 @@
     return pl.ds(pl.multiple_of(block * LANES, LANES), LANES)
 
 
+def partners(ranks):
+    middle = ranks // 2
+    return [middle] + [step for step in range(ranks - 1, 0, -1) if step != middle]
+
+
 def pack_kernel(ranks, q_ref, k_ref, v_ref, *rest):
     outs, (whole, sems) = rest[:-2], rest[-2:]
     me = lax.axis_index("seq")
@@ -320,7 +325,7 @@
 
 
 def forward_kernel(ranks, frames, *refs):
-    recvs = refs[: ranks - 1]
+    recvs = dict(zip(partners(ranks), refs))
     own_ref, col_ref, row_ref, after_ref, before_ref, w_ref = refs[ranks - 1 : ranks + 5]
     soft_ref, att_ref, pre_ref, q_ref, k_t_ref, v_ref = refs[ranks + 5 : ranks + 11]
     att_t_ref, k_full, q_full, w_own, w_sem = refs[ranks + 11 :]
@@ -331,7 +336,7 @@
     for place, target in enumerate((q_full, k_full, v_ref)):
         target[rows_at(me, frames), :] = own_ref[place]
         for step in range(1, ranks):
-            target[rows_at(me ^ step, frames), :] = recvs[ranks - 1 - step][place]
+            target[rows_at(me ^ step, frames), :] = recvs[step][place]
     heads = LANES // HDIM
     lane_head = lax.broadcasted_iota(jnp.int32, (1, LANES), 1) // HDIM
     scaled = q_full[...].astype(jnp.float32) * (1.0 / math.sqrt(HDIM))
@@ -381,7 +386,7 @@
 
 
 def conv_back_kernel(ranks, frames, *refs):
-    cots = refs[: ranks - 1]
+    cots = dict(zip(partners(ranks), refs))
     own_ref, att_ref, pre_ref, after_ref, before_ref, w_ref = refs[ranks - 1 : ranks + 5]
     mixed_ref, g_att, taps_ref, cot, grad_pad, tap_sum, w_own, w_sem = refs[ranks + 5 :]
     me = lax.axis_index("seq")
@@ -390,7 +395,7 @@
     copy.start()
     cot[rows_at(me, frames), :] = own_ref[3]
     for step in range(1, ranks):
-        cot[rows_at(me ^ step, frames), :] = cots[ranks - 1 - step][...]
+        cot[rows_at(me ^ step, frames), :] = cots[step][...]
     zeros = jnp.zeros((PAD, LANES), jnp.float32)
     grad_pad[0:PAD, :] = zeros
     grad_pad[PAD + length :, :] = zeros
@@ -509,7 +514,7 @@
     def swap(array, step):
         return lax.ppermute(array, "seq", [(rank, rank ^ step) for rank in range(ranks)])
 
-    order = list(range(ranks - 1, 0, -1))
+    order = partners(ranks)
     received = {step: swap(sends[step - 1], step) for step in order}
 
     *cot_sends, own, col, row, after, before = pl.pallas_call(

time: 37 us -> 38.5 us (1.041)
  waiting for transfers between devices: 9.98 us -> 11.6 us
    ppermute x9, waiting for transfers between devices: 9.05 us -> 10.9 us  [swap(): lax.ppermute(array, 'seq', [(rank, rank ^ step) for rank in range(ranks)])]
  transfers between devices with their start and end apart: 10 -> 10, of which waited for: 4 -> 6; matrix products, arithmetic and copies ran while one was open for 0% -> 0% of each run, Pallas kernels for 14% -> 14%
where the time goes in v9:
time: 38.5 us; the launch traced here: 38.4 us
  starting transfers between devices  15.9 us (41%)
  waiting for transfers between devices  11.6 us (30%)
  Pallas kernels  9.15 us (24%)
  local copies, waits for them, and re-layouts  0.92 us (2%)
  between operations  0.73 us (2%)
    ppermute x9, starting transfers between devices, swap(): lax.ppermute(array, 'seq', [(rank, rank ^ step) for rank in range(ranks)])  14.2 us
    ppermute x9, waiting for transfers between devices, swap(): lax.ppermute(array, 'seq', [(rank, rank ^ step) for rank in range(ranks)])  10.9 us
    pallas_call x1, Pallas kernels, on_device_heads(): pl.pallas_call(functools.partial(forward_kernel, ranks, frames), out_shap...  2.61 us
    pallas_call x1, Pallas kernels, on_device_heads(): pl.pallas_call(functools.partial(conv_back_kernel, ranks, frames), out_sh...  1.81 us
    ppermute x1, starting transfers between devices, on_device_heads(): lax.ppermute(own_taps, 'dp', [(one, (one + shift) % copies) for one in ra...  1.78 us
    pallas_call x1, Pallas kernels, on_device_heads(): pl.pallas_call(functools.partial(mask_kernel, ranks, length), out_shape=[...  1.32 us
    pallas_call x1, Pallas kernels, on_device_heads(): pl.pallas_call(backward_kernel, out_shape=[struct((length, LANES), bf16)]...  1.31 us
    pallas_call x1, Pallas kernels, on_device_heads(): pl.pallas_call(functools.partial(pack_kernel, ranks), out_shape=[struct((...  1.16 us
  transfers between devices with their start and end apart: 10, of which 6 were waited for; matrix products, arithmetic and copies ran while one was open for 0% of the time, Pallas kernels for 14%

profile of v9, /device:TPU:0, one launch (start us, length us, event | category | flops | bytes accessed | tf_op | source)
XLA Modules:
  0.0 38.4 jit_solution(13144316698453153070)
XLA Ops:
  0.6 0.0 copy-start.2
  0.6 0.0 copy-start.1
  0.7 0.0 copy-start
  0.7 1.2 %pack.1 = (bf16[3,128,128]{2,1,0:T(8,128)(2,1)S(1)}, bf16[3,128,128]{2,1,0:T(8,128)(2,1)S(1)}, bf16[3,128,128]{2,1,0:T(8,128)(2,1)S(1)}) custom-call(bf16[1,128,512]{2,1,0:T(8,128)(2,1)} %q_ref.3, bf16[1,128,512]{2,1,0:T(8,128)(2,1)} %k_ref.3, bf16[1,128,512]{2,1,0:T(8,128)(2,1)} %v_ref.3), custom_call_target="tpu_custom_call" | custom-call | tf_op jit(solution)/shard_map/pack/pallas_call | solution.py:504
  1.8 4.1 %collective-permute-start.3 = (bf16[3,128,128]{2,1,0:T(8,128)(2,1)S(1)}, bf16[3,128,128]{2,1,0:T(8,128)(2,1)S(1)}, u32[]{:S(2)}, u32[]{:S(2)}) collective-permute-start(bf16[3,128,128]{2,1,0:T(8,128)(2,1)S(1)} %get-tuple-element.36), channel_id=1, source_target_pairs={{0,4},{2,6},{4,0},{6,2},{1,5},{3,7},{5,1},{7,3},{8,12},{10,14},{12... | collective-permute-start | bytes 294920 | tf_op jit(solution)/shard_map/ppermute | solution.py:515
  5.9 0.0 copy-start.4
  5.9 1.3 %collective-permute-start.4 = (bf16[3,128,128]{2,1,0:T(8,128)(2,1)S(1)}, bf16[3,128,128]{2,1,0:T(8,128)(2,1)S(1)}, u32[]{:S(2)}, u32[]{:S(2)}) collective-permute-start(bf16[3,128,128]{2,1,0:T(8,128)(2,1)S(1)} %get-tuple-element.37), channel_id=1, source_target_pairs={{0,6},{2,4},{4,2},{6,0},{1,7},{3,5},{5,3},{7,1},{8,14},{10,12},{12... | collective-permute-start | bytes 294920 | tf_op jit(solution)/shard_map/ppermute | solution.py:515
  7.3 0.2 collective-permute-start.5
  7.5 0.0 copy-done.2
  7.5 0.0 copy-done.1
  7.5 0.0 copy-done
  7.5 0.0 copy-done.4
  7.5 0.0 copy-start.3
  7.5 0.9 %copy-done.3 = bf16[1,128,512]{2,1,0:T(8,128)(2,1)S(1)} copy-done((bf16[1,128,512]{2,1,0:T(8,128)(2,1)S(1)}, bf16[1,128,512]{2,1,0:T(8,128)(2,1)}, u32[]{:S(2)}) %copy-start.3) | copy-done | bytes 131096
  8.4 0.0 copy-start.5
  8.4 1.3 %masks.1 = (bf16[128,128]{1,0:T(8,128)(2,1)S(1)}, bf16[128,128]{1,0:T(8,128)(2,1)S(1)}, bf16[128,128]{1,0:T(8,128)(2,1)S(1)}, bf16[4,128,128]{2,1,0:T(8,128)(2,1...) custom-call(s32[1,16]{1,0:T(1,128)S(1)} %copy-done.4, ...), custom_call_target="tpu_custom_call" | custom-call | flops 4194304 | bytes 1048576 | tf_op jit(solution)/shard_map/masks/pallas_call | solution.py:520
  9.8 2.9 %collective-permute-start = (bf16[128,128]{1,0:T(8,128)(2,1)S(1)}, bf16[128,128]{1,0:T(8,128)(2,1)S(1)}, u32[]{:S(2)}, u32[]{:S(2)}) collective-permute-start(bf16[128,128]{1,0:T(8,128)(2,1)S(1)} %get-tuple-element.32), channel_id=1, source_target_pairs={{0,4},{2,6},{4,0},{6,2},{1,5},{3,7},{5,1},{7,3},{8,12},{10,14},{12... | collective-permute-start | bytes 98312 | tf_op jit(solution)/shard_map/ppermute | solution.py:515
  12.6 1.3 %collective-permute-start.1 = (bf16[128,128]{1,0:T(8,128)(2,1)S(1)}, bf16[128,128]{1,0:T(8,128)(2,1)S(1)}, u32[]{:S(2)}, u32[]{:S(2)}) collective-permute-start(bf16[128,128]{1,0:T(8,128)(2,1)S(1)} %get-tuple-element.33), channel_id=1, source_target_pairs={{0,6},{2,4},{4,2},{6,0},{1,7},{3,5},{5,3},{7,1},{8,14},{10,12},{12... | collective-permute-start | bytes 98312 | tf_op jit(solution)/shard_map/ppermute | solution.py:515
  14.0 0.0 collective-permute-done.3.refs_0_
  14.0 0.0 collective-permute-start.2
  14.0 0.0 collective-permute-done.4.refs_1_
  14.0 0.3 collective-permute-done.5.refs_2_
  14.3 0.0 copy-done.5
  14.3 2.6 %forward.1 = (bf16[2,512,512]{2,1,0:T(8,128)(2,1)S(1)}, f32[544,128]{1,0:T(8,128)S(1)}, f32[512,128]{1,0:T(8,128)S(1)}, bf16[2,512,128]{2,1,0:T(8,128)(2,1)S(1)}...) custom-call(bf16[3,128,128]{2,1,0:T(8,128)(2,1)S(1)} %collective-permute-done.3.refs_0_, ...), custom_call_target="tpu_custom_call" | custom-call | flops 419430400 | bytes 3145728 | tf_op jit(solution)/shard_map/forward/pallas_call | solution.py:539
  17.0 0.2 collective-permute-done.refs_0_
  17.2 1.2 %collective-permute-done.1.refs_1_ = bf16[128,128]{1,0:T(8,128)(2,1)S(1)} collective-permute-done((bf16[128,128]{1,0:T(8,128)(2,1)S(1)}, bf16[128,128]{1,0:T(8,128)(2,1)S(1)}, u32[]{:S(2)}, u32[]{:S(2)}) %collective-permute-start.1) | collective-permute-done | bytes 32800 | tf_op jit(solution)/shard_map/ppermute | solution.py:515
  18.4 0.0 collective-permute-done.2.refs_2_
  18.4 1.8 %conv_back.1 = (bf16[512,128]{1,0:T(8,128)(2,1)S(1)}, bf16[512,128]{1,0:T(8,128)(2,1)S(1)}, f32[32,128]{1,0:T(8,128)S(1)}) custom-call(bf16[128,128]{1,0:T(8,128)(2,1)S(1)} %collective-permute-done.refs_0_, bf16[128,128]{1,0:T(8,128)(2,1)S(1)} %collective-permute-done.1.refs_1_, bf16[128,128]{1,0:T(8,128)(2,1)S(1)} %collective-permute-done.2.refs_2_, ...), custom_call_target="tpu_custom_call" | custom-call | flops 419430400 | bytes 3145728 | tf_op jit(solution)/shard_map/conv_back/pallas_call | solution.py:563
  20.2 1.8 %collective-permute-start.6 = (f32[32,128]{1,0:T(8,128)S(1)}, f32[32,128]{1,0:T(8,128)S(1)}, u32[]{:S(2)}, u32[]{:S(2)}) collective-permute-start(f32[32,128]{1,0:T(8,128)S(1)} %get-tuple-element.54.refs_4_), channel_id=1, source_target_pairs={{0,8},{8,0},{1,9},{9,1},{2,10},{10,2},{3,11},{11,3},{4,12},{12,4},... | collective-permute-start | bytes 49160 | tf_op jit(solution)/shard_map/ppermute | solution.py:582
  22.0 1.3 %backward.1 = (bf16[512,128]{1,0:T(8,128)(2,1)S(1)}, bf16[512,128]{1,0:T(8,128)(2,1)S(1)}, bf16[512,128]{1,0:T(8,128)(2,1)S(1)}) custom-call(bf16[2,512,512]{2,1,0:T(8,128)(2,1)S(1)} %get-tuple-element.46.soft_ref, f32[544,128]{1,0:T(8,128)S(1)} %get-tuple-element.43.refs_4_.att_ref, bf16[512,128]{1,0:T(8,128)(2,1)S(1)} %get-tuple-element.47.g_att, ...), custom_call_target="tpu_custom_call" | custom-call | flops 838860800 | bytes 3145728 | tf_op jit(solution)/shard_map/backward/pallas_call | solution.py:586
  23.3 0.7 %collective-permute-done.6.refs_5_ = f32[32,128]{1,0:T(8,128)S(1)} collective-permute-done((f32[32,128]{1,0:T(8,128)S(1)}, f32[32,128]{1,0:T(8,128)S(1)}, u32[]{:S(2)}, u32[]{:S(2)}) %collective-permute-start.6) | collective-permute-done | bytes 16416 | tf_op jit(solution)/shard_map/ppermute | solution.py:582
  24.1 3.5 %collective-permute-start.8 = (bf16[544,128]{1,0:T(8,128)(2,1)S(1)}, bf16[544,128]{1,0:T(8,128)(2,1)S(1)}, u32[]{:S(2)}, u32[]{:S(2)}) collective-permute-start(bf16[544,128]{1,0:T(8,128)(2,1)S(1)} %get-tuple-element.57), channel_id=1, source_target_pairs={{0,4},{2,6},{4,0},{6,2},{1,5},{3,7},{5,1},{7,3},{8,12},{10,14},{12... | collective-permute-start | bytes 417800 | tf_op jit(solution)/shard_map/ppermute | solution.py:515
  27.6 0.5 %collective-permute-start.9 = (bf16[544,128]{1,0:T(8,128)(2,1)S(1)}, bf16[544,128]{1,0:T(8,128)(2,1)S(1)}, u32[]{:S(2)}, u32[]{:S(2)}) collective-permute-start(bf16[544,128]{1,0:T(8,128)(2,1)S(1)} %get-tuple-element.58), channel_id=1, source_target_pairs={{0,6},{2,4},{4,2},{6,0},{1,7},{3,5},{5,3},{7,1},{8,14},{10,12},{12... | collective-permute-start | bytes 417800 | tf_op jit(solution)/shard_map/ppermute | solution.py:515
  28.2 0.2 collective-permute-start.7
  28.3 8.3 %collective-permute-done.8.refs_2_ = bf16[544,128]{1,0:T(8,128)(2,1)S(1)} collective-permute-done((bf16[544,128]{1,0:T(8,128)(2,1)S(1)}, bf16[544,128]{1,0:T(8,128)(2,1)S(1)}, u32[]{:S(2)}, u32[]{:S(2)}) %collective-permute-start.8) | collective-permute-done | bytes 139296 | tf_op jit(solution)/shard_map/ppermute | solution.py:515
  36.7 0.0 collective-permute-done.9.refs_3_
  36.7 0.8 %collective-permute-done.7.refs_1_ = bf16[544,128]{1,0:T(8,128)(2,1)S(1)} collective-permute-done((bf16[544,128]{1,0:T(8,128)(2,1)S(1)}, bf16[544,128]{1,0:T(8,128)(2,1)S(1)}, u32[]{:S(2)}, u32[]{:S(2)}) %collective-permute-start.7) | collective-permute-done | bytes 139296 | tf_op jit(solution)/shard_map/ppermute | solution.py:515
  37.5 0.9 %spread.1 = (bf16[1,128,512]{2,1,0:T(8,128)(2,1)}, bf16[1,128,512]{2,1,0:T(8,128)(2,1)}, bf16[1,128,512]{2,1,0:T(8,128)(2,1)}, bf16[1,128,512]{2,1,0:T(8,128)(2,1)}, f32[31,512]{1,0:T(8,128)}) custom-call(bf16[544,128]{1,0:T(8,128)(2,1)S(1)} %get-tuple-element.55.refs_0_, bf16[544,128]{1,0:T(8,128)(2,1)S(1)} %collective-permute-done.7.refs_1_, ...), custom_call_target="tpu_custom_call" | custom-call | tf_op jit(solution)/shard_map/spread/pallas_call | solution.py:615
  (2 shorter events, 0.0 us)
Async XLA Ops:
  0.6 6.9 %copy-start.2 = (bf16[1,128,512]{2,1,0:T(8,128)(2,1)S(1)}, bf16[1,128,512]{2,1,0:T(8,128)(2,1)}, u32[]{:S(2)}) copy-start(bf16[1,128,512]{2,1,0:T(8,128)(2,1)} %v_ref.3) | copy-start | bytes 393220
  0.6 6.9 %copy-start.1 = (bf16[1,128,512]{2,1,0:T(8,128)(2,1)S(1)}, bf16[1,128,512]{2,1,0:T(8,128)(2,1)}, u32[]{:S(2)}) copy-start(bf16[1,128,512]{2,1,0:T(8,128)(2,1)} %k_ref.3) | copy-start | bytes 393220
  0.7 6.9 %copy-start = (bf16[1,128,512]{2,1,0:T(8,128)(2,1)S(1)}, bf16[1,128,512]{2,1,0:T(8,128)(2,1)}, u32[]{:S(2)}) copy-start(bf16[1,128,512]{2,1,0:T(8,128)(2,1)} %q_ref.3) | copy-start | bytes 393220
  1.8 12.2 %collective-permute-start.3 = (bf16[3,128,128]{2,1,0:T(8,128)(2,1)S(1)}, bf16[3,128,128]{2,1,0:T(8,128)(2,1)S(1)}, u32[]{:S(2)}, u32[]{:S(2)}) collective-permute-start(bf16[3,128,128]{2,1,0:T(8,128)(2,1)S(1)} %get-tuple-element.36), channel_id=1, source_target_pairs={{0,4},{2,6},{4,0},{6,2},{1,5},{3,7},{5,1},{7,3},{8,12},{10,14},{12... | collective-permute-start | bytes 294920 | tf_op jit(solution)/shard_map/ppermute | solution.py:515
  5.9 1.6 %copy-start.4 = (s32[1,16]{1,0:T(1,128)S(1)}, s32[1,16]{1,0:T(1,128)}, u32[]{:S(2)}) copy-start(s32[1,16]{1,0:T(1,128)} %lens_ref.1) | copy-start | bytes 196
  5.9 8.1 %collective-permute-start.4 = (bf16[3,128,128]{2,1,0:T(8,128)(2,1)S(1)}, bf16[3,128,128]{2,1,0:T(8,128)(2,1)S(1)}, u32[]{:S(2)}, u32[]{:S(2)}) collective-permute-start(bf16[3,128,128]{2,1,0:T(8,128)(2,1)S(1)} %get-tuple-element.37), channel_id=1, source_target_pairs={{0,6},{2,4},{4,2},{6,0},{1,7},{3,5},{5,3},{7,1},{8,14},{10,12},{12... | collective-permute-start | bytes 294920 | tf_op jit(solution)/shard_map/ppermute | solution.py:515
  7.3 7.1 %collective-permute-start.5 = (bf16[3,128,128]{2,1,0:T(8,128)(2,1)S(1)}, bf16[3,128,128]{2,1,0:T(8,128)(2,1)S(1)}, u32[]{:S(2)}, u32[]{:S(2)}) collective-permute-start(bf16[3,128,128]{2,1,0:T(8,128)(2,1)S(1)} %get-tuple-element.38), channel_id=1, source_target_pairs={{0,2},{2,0},{4,6},{6,4},{1,3},{3,1},{5,7},{7,5},{8,10},{10,8},{12,... | collective-permute-start | bytes 294920 | tf_op jit(solution)/shard_map/ppermute | solution.py:515
  7.5 0.9 %copy-start.3 = (bf16[1,128,512]{2,1,0:T(8,128)(2,1)S(1)}, bf16[1,128,512]{2,1,0:T(8,128)(2,1)}, u32[]{:S(2)}) copy-start(bf16[1,128,512]{2,1,0:T(8,128)(2,1)} %c_ref.1) | copy-start | bytes 393220
  8.4 5.9 %copy-start.5 = (f32[31,512]{1,0:T(8,128)S(1)}, f32[31,512]{1,0:T(8,128)}, u32[]{:S(2)}) copy-start(f32[31,512]{1,0:T(8,128)} %refs_8_.3) | copy-start | bytes 190468
  9.8 7.4 %collective-permute-start = (bf16[128,128]{1,0:T(8,128)(2,1)S(1)}, bf16[128,128]{1,0:T(8,128)(2,1)S(1)}, u32[]{:S(2)}, u32[]{:S(2)}) collective-permute-start(bf16[128,128]{1,0:T(8,128)(2,1)S(1)} %get-tuple-element.32), channel_id=1, source_target_pairs={{0,4},{2,6},{4,0},{6,2},{1,5},{3,7},{5,1},{7,3},{8,12},{10,14},{12... | collective-permute-start | bytes 98312 | tf_op jit(solution)/shard_map/ppermute | solution.py:515
  12.6 5.8 %collective-permute-start.1 = (bf16[128,128]{1,0:T(8,128)(2,1)S(1)}, bf16[128,128]{1,0:T(8,128)(2,1)S(1)}, u32[]{:S(2)}, u32[]{:S(2)}) collective-permute-start(bf16[128,128]{1,0:T(8,128)(2,1)S(1)} %get-tuple-element.33), channel_id=1, source_target_pairs={{0,6},{2,4},{4,2},{6,0},{1,7},{3,5},{5,3},{7,1},{8,14},{10,12},{12... | collective-permute-start | bytes 98312 | tf_op jit(solution)/shard_map/ppermute | solution.py:515
  14.0 4.4 %collective-permute-start.2 = (bf16[128,128]{1,0:T(8,128)(2,1)S(1)}, bf16[128,128]{1,0:T(8,128)(2,1)S(1)}, u32[]{:S(2)}, u32[]{:S(2)}) collective-permute-start(bf16[128,128]{1,0:T(8,128)(2,1)S(1)} %get-tuple-element.34), channel_id=1, source_target_pairs={{0,2},{2,0},{4,6},{6,4},{1,3},{3,1},{5,7},{7,5},{8,10},{10,8},{12,... | collective-permute-start | bytes 98312 | tf_op jit(solution)/shard_map/ppermute | solution.py:515
  20.2 3.8 %collective-permute-start.6 = (f32[32,128]{1,0:T(8,128)S(1)}, f32[32,128]{1,0:T(8,128)S(1)}, u32[]{:S(2)}, u32[]{:S(2)}) collective-permute-start(f32[32,128]{1,0:T(8,128)S(1)} %get-tuple-element.54.refs_4_), channel_id=1, source_target_pairs={{0,8},{8,0},{1,9},{9,1},{2,10},{10,2},{3,11},{11,3},{4,12},{12,4},... | collective-permute-start | bytes 49160 | tf_op jit(solution)/shard_map/ppermute | solution.py:582
  24.1 12.6 %collective-permute-start.8 = (bf16[544,128]{1,0:T(8,128)(2,1)S(1)}, bf16[544,128]{1,0:T(8,128)(2,1)S(1)}, u32[]{:S(2)}, u32[]{:S(2)}) collective-permute-start(bf16[544,128]{1,0:T(8,128)(2,1)S(1)} %get-tuple-element.57), channel_id=1, source_target_pairs={{0,4},{2,6},{4,0},{6,2},{1,5},{3,7},{5,1},{7,3},{8,12},{10,14},{12... | collective-permute-start | bytes 417800 | tf_op jit(solution)/shard_map/ppermute | solution.py:515
  27.6 9.1 %collective-permute-start.9 = (bf16[544,128]{1,0:T(8,128)(2,1)S(1)}, bf16[544,128]{1,0:T(8,128)(2,1)S(1)}, u32[]{:S(2)}, u32[]{:S(2)}) collective-permute-start(bf16[544,128]{1,0:T(8,128)(2,1)S(1)} %get-tuple-element.58), channel_id=1, source_target_pairs={{0,6},{2,4},{4,2},{6,0},{1,7},{3,5},{5,3},{7,1},{8,14},{10,12},{12... | collective-permute-start | bytes 417800 | tf_op jit(solution)/shard_map/ppermute | solution.py:515
  28.2 9.3 %collective-permute-start.7 = (bf16[544,128]{1,0:T(8,128)(2,1)S(1)}, bf16[544,128]{1,0:T(8,128)(2,1)S(1)}, u32[]{:S(2)}, u32[]{:S(2)}) collective-permute-start(bf16[544,128]{1,0:T(8,128)(2,1)S(1)} %get-tuple-element.56), channel_id=1, source_target_pairs={{0,2},{2,0},{4,6},{6,4},{1,3},{3,1},{5,7},{7,5},{8,10},{10,8},{12,... | collective-permute-start | bytes 417800 | tf_op jit(solution)/shard_map/ppermute | solution.py:515

commit v10 on v7

--- a/solution.py
+++ b/solution.py
@@ -256,13 +256,13 @@
 
 
 def pack_kernel(ranks, q_ref, k_ref, v_ref, *rest):
-    outs, (whole, sems) = rest[:-2], rest[-2:]
+    outs, sems = rest[:-1], rest[-1]
     me = lax.axis_index("seq")
-    sources = (q_ref, k_ref, v_ref)
-    run_copies([(source.at[0], whole.at[place]) for place, source in enumerate(sources)], sems)
+    pairs = []
     for step in range(ranks - 1, 0, -1):
-        for place in range(len(sources)):
-            outs[step - 1][place] = whole[place, :, lanes_at(me ^ step)]
+        for place, source in enumerate((q_ref, k_ref, v_ref)):
+            pairs.append((source.at[0, :, lanes_at(me ^ step)], outs[step - 1].at[place]))
+    run_copies(pairs, sems)
 
 
 def run_copies(pairs, sems, meanwhile=None):
@@ -380,74 +380,84 @@
     lax.fori_loop(0, length // chunk, some_rows, 0)
 
 
-def conv_back_kernel(ranks, frames, *refs):
+def masked(source, base, chunk, off, before, after):
+    piece = source[pl.ds(base + (PAD + off), chunk), :]
+    if off > 0:
+        piece = jnp.where(after >= off, piece, 0.0)
+    if off < 0:
+        piece = jnp.where(before >= -off, piece, 0.0)
+    return piece
+
+
+def taps_kernel(ranks, frames, *refs):
     cots = refs[: ranks - 1]
-    own_ref, att_ref, pre_ref, after_ref, before_ref, w_ref = refs[ranks - 1 : ranks + 5]
-    mixed_ref, g_att, taps_ref, cot, grad_pad, tap_sum, w_own, w_sem = refs[ranks + 5 :]
+    own_ref, att_ref, pre_ref, after_ref, before_ref = refs[ranks - 1 : ranks + 4]
+    mixed_ref, grad_pad, taps_ref, cot, tap_sum = refs[ranks + 4 :]
     me = lax.axis_index("seq")
     length = ranks * frames
-    copy = pltpu.make_async_copy(w_ref.at[:, lanes_at(me)], w_own, w_sem)
-    copy.start()
     cot[rows_at(me, frames), :] = own_ref[3]
     for step in range(1, ranks):
         cot[rows_at(me ^ step, frames), :] = cots[ranks - 1 - step][...]
     zeros = jnp.zeros((PAD, LANES), jnp.float32)
     grad_pad[0:PAD, :] = zeros
     grad_pad[PAD + length :, :] = zeros
-    pre = pre_ref[...]
-    gate = jax.nn.sigmoid(pre)
-    mixed_ref[...] = (pre * gate).astype(jnp.bfloat16)
-    conv_grad = cot[...].astype(jnp.float32) * gate * (1.0 + pre * (1.0 - gate))
-    grad_pad[PAD : PAD + length, :] = conv_grad.astype(jnp.bfloat16).astype(jnp.float32)
     tap_sum[...] = jnp.zeros(tap_sum.shape, jnp.float32)
+    chunk = 64
+
+    def some_rows(number, carry):
+        base = pl.multiple_of(number * chunk, chunk)
+        rows = pl.ds(base, chunk)
+        pre = pre_ref[rows, :]
+        gate = jax.nn.sigmoid(pre)
+        mixed_ref[rows, :] = (pre * gate).astype(jnp.bfloat16)
+        conv_grad = cot[rows, :].astype(jnp.float32) * gate * (1.0 + pre * (1.0 - gate))
+        conv_grad = conv_grad.astype(jnp.bfloat16).astype(jnp.float32)
+        grad_pad[pl.ds(base + PAD, chunk), :] = conv_grad
+        after, before = after_ref[rows, :], before_ref[rows, :]
+        for tap in range(KERNEL):
+            part = conv_grad * masked(att_ref, base, chunk, tap - HALF, before, after)
+            tap_sum[tap] = tap_sum[tap] + jnp.sum(part.reshape(chunk // 8, 8, LANES), axis=0)
+        return carry
+
+    lax.fori_loop(0, length // chunk, some_rows, 0)
+    taps_ref[...] = jnp.sum(tap_sum[...], axis=1)
+
+
+def backward_kernel(soft_ref, att_ref, grad_pad, after_ref, before_ref, q_ref, k_t_ref, v_ref, w_ref, *refs):
+    res_q, res_k, res_v, g_att, grad_t, w_own, w_sem = refs
+    length = v_ref.shape[0]
+    copy = pltpu.make_async_copy(w_ref.at[:, lanes_at(lax.axis_index("seq"))], w_own, w_sem)
+    copy.start()
     copy.wait()
-
     chunk = 64
 
     def some_rows(number, carry):
         base = pl.multiple_of(number * chunk, chunk)
         rows = pl.ds(base, chunk)
         after, before = after_ref[rows, :], before_ref[rows, :]
-        own_att = att_ref[pl.ds(base + PAD, chunk), :]
         total = jnp.zeros((chunk, LANES), jnp.float32)
         for tap in range(KERNEL):
-            off = tap - HALF
-            piece = grad_pad[pl.ds(base + (PAD - off), chunk), :]
-            if off > 0:
-                piece = jnp.where(before >= off, piece, 0.0)
-            if off < 0:
-                piece = jnp.where(after >= -off, piece, 0.0)
-            total = total + w_own[tap : tap + 1, :] * piece
-            part = (own_att * piece).reshape(chunk // 8, 8, LANES)
-            tap_sum[tap] = tap_sum[tap] + jnp.sum(part, axis=0)
+            total = total + w_own[tap : tap + 1, :] * masked(grad_pad, base, chunk, HALF - tap, before, after)
         g_att[rows, :] = total.astype(jnp.bfloat16)
         return carry
 
     lax.fori_loop(0, length // chunk, some_rows, 0)
-    taps_ref[...] = jnp.sum(tap_sum[...], axis=1)
-
-
-def backward_kernel(soft_ref, att_ref, g_att, q_ref, k_t_ref, v_ref, res_q, res_k, res_v, grad_t):
-    length = v_ref.shape[0]
     heads = LANES // HDIM
     lane_head = lax.broadcasted_iota(jnp.int32, (1, LANES), 1) // HDIM
     g_wide = g_att[...].astype(jnp.float32)
     products_t = (g_wide * att_ref[PAD : PAD + length, :]).T
-    g_heads = [jnp.where(lane_head == head, g_wide, 0.0).astype(jnp.bfloat16) for head in range(heads)]
-    wide = 512
     grad_v = jnp.zeros((length, LANES), jnp.float32)
     grad_k = jnp.zeros((length, LANES), jnp.float32)
     for head in range(heads):
         rows = slice(head * HDIM, (head + 1) * HDIM)
+        g_head = jnp.where(lane_head == head, g_wide, 0.0).astype(jnp.bfloat16)
         delta = jnp.sum(products_t[rows], axis=0, keepdims=True)
-        for start in range(0, length, wide):
-            cols = slice(start, start + wide)
-            soft = soft_ref[head, :, cols]
-            slopes = mm_nt(v_ref[...], g_heads[head][cols])
-            mixed_grad = (soft.astype(jnp.float32) * (slopes - delta[:, cols])).astype(jnp.bfloat16)
-            grad_v = grad_v + mm(soft, g_heads[head][cols])
-            grad_k = grad_k + mm(mixed_grad, q_ref[head, cols, :])
-            grad_t[rows, cols] = mm(k_t_ref[rows, :], mixed_grad) * (1.0 / math.sqrt(HDIM))
+        soft = soft_ref[head]
+        slopes = mm_nt(v_ref[...], g_head)
+        mixed_grad = (soft.astype(jnp.float32) * (slopes - delta)).astype(jnp.bfloat16)
+        grad_v = grad_v + mm(soft, g_head)
+        grad_k = grad_k + mm(mixed_grad, q_ref[head])
+        grad_t[rows, :] = mm(k_t_ref[rows, :], mixed_grad) * (1.0 / math.sqrt(HDIM))
     res_k[...] = grad_k.astype(jnp.bfloat16)
     res_v[...] = grad_v.astype(jnp.bfloat16)
     res_q[...] = grad_t[...].T.astype(jnp.bfloat16)
@@ -501,7 +511,7 @@
         out_shape=[struct((3, frames, LANES), bf16)] * (ranks - 1),
         in_specs=[hbm] * 3,
         out_specs=[vmem] * (ranks - 1),
-        scratch_shapes=[VMEM((3,) + queries.shape[1:], bf16), pltpu.SemaphoreType.DMA((3,))],
+        scratch_shapes=[pltpu.SemaphoreType.DMA((3 * (ranks - 1),))],
         compiler_params=pltpu.CompilerParams(vmem_limit_bytes=54912 * 1024),
         name="pack",
     )(queries, keys, values)
@@ -555,22 +565,20 @@
         name="forward",
     )(*[received[step] for step in order], own, col, row, after, before, conv_weight)
 
-    mixed, g_att, own_taps = pl.pallas_call(
-        functools.partial(conv_back_kernel, ranks, frames),
-        out_shape=[struct((length, LANES), bf16)] * 2 + [struct((taps, LANES), f32)],
-        in_specs=[vmem] * (ranks + 4) + [anywhere],
+    mixed, grad_pad, own_taps = pl.pallas_call(
+        functools.partial(taps_kernel, ranks, frames),
+        out_shape=[
+            struct((length, LANES), bf16),
+            struct((length + 2 * PAD, LANES), f32),
+            struct((taps, LANES), f32),
+        ],
+        in_specs=[vmem] * (ranks + 4),
         out_specs=[vmem] * 3,
-        scratch_shapes=[
-            VMEM((length, LANES), bf16),
-            VMEM((length + 2 * PAD, LANES), f32),
-            VMEM((taps, 8, LANES), f32),
-            VMEM((KERNEL, LANES), f32),
-            pltpu.SemaphoreType.DMA,
-        ],
+        scratch_shapes=[VMEM((length, LANES), bf16), VMEM((taps, 8, LANES), f32)],
         compiler_params=params,
         cost_estimate=cost(400 * MIB, 3 * MIB),
-        name="conv_back",
-    )(*[cots[step] for step in order], own, att, pre, after, before, conv_weight)
+        name="taps",
+    )(*[cots[step] for step in order], own, att, pre, after, before)
 
     copies = lax.axis_size("dp")
     part_taps = [own_taps] + [
@@ -581,13 +589,18 @@
     results = pl.pallas_call(
         backward_kernel,
         out_shape=[struct((length, LANES), bf16)] * 3,
-        in_specs=[vmem] * 6,
+        in_specs=[vmem] * 8 + [anywhere],
         out_specs=[vmem] * 3,
-        scratch_shapes=[VMEM((LANES, length), f32)],
+        scratch_shapes=[
+            VMEM((length, LANES), bf16),
+            VMEM((LANES, length), f32),
+            VMEM((KERNEL, LANES), f32),
+            pltpu.SemaphoreType.DMA,
+        ],
         compiler_params=params,
         cost_estimate=cost(800 * MIB, 3 * MIB),
         name="backward",
-    )(soft, att, g_att, q_heads, k_t, v_full)
+    )(soft, att, grad_pad, after, before, q_heads, k_t, v_full, conv_weight)
 
     def blocks_of(steps):
         return pl.pallas_call(

time: 37 us -> 36.8 us (level)
  waiting for transfers between devices: 9.98 us -> 9.33 us
  Pallas kernels: 9.16 us -> 9.57 us
    pallas_call x1, Pallas kernels: 1.3 us -> 2.41 us  [on_device_heads(): pl.pallas_call(backward_kernel, out_shape=[struct((length, LANES), bf16)]...]
    ppermute x1, waiting for transfers between devices: 0.93 us -> 0.01 us  [on_device_heads(): lax.ppermute(own_taps, 'dp', [(one, (one + shift) % copies) for one in ra...]
    pallas_call x1, Pallas kernels: 1.82 us -> 1.24 us  [on_device_heads(): pl.pallas_call(functools.partial(taps_kernel, ranks, frames), out_shape=[...]
  transfers between devices with their start and end apart: 10 -> 10, of which waited for: 4 -> 3; matrix products, arithmetic and copies ran while one was open for 0% -> 0% of each run, Pallas kernels for 14% -> 17%
where the time goes in v10:
time: 36.8 us; the launch traced here: 36.6 us
  starting transfers between devices  16.1 us (44%)
  Pallas kernels  9.57 us (26%)
  waiting for transfers between devices  9.33 us (25%)
  local copies, waits for them, and re-layouts  0.92 us (2%)
  between operations  0.76 us (2%)
    ppermute x9, starting transfers between devices, swap(): lax.ppermute(array, 'seq', [(rank, rank ^ step) for rank in range(ranks)])  14.5 us
    ppermute x9, waiting for transfers between devices, swap(): lax.ppermute(array, 'seq', [(rank, rank ^ step) for rank in range(ranks)])  9.33 us
    pallas_call x1, Pallas kernels, on_device_heads(): pl.pallas_call(functools.partial(forward_kernel, ranks, frames), out_shap...  2.6 us
    pallas_call x1, Pallas kernels, on_device_heads(): pl.pallas_call(backward_kernel, out_shape=[struct((length, LANES), bf16)]...  2.41 us
    ppermute x1, starting transfers between devices, on_device_heads(): lax.ppermute(own_taps, 'dp', [(one, (one + shift) % copies) for one in ra...  1.56 us
    pallas_call x1, Pallas kernels, on_device_heads(): pl.pallas_call(functools.partial(mask_kernel, ranks, length), out_shape=[...  1.32 us
    pallas_call x1, Pallas kernels, on_device_heads(): pl.pallas_call(functools.partial(taps_kernel, ranks, frames), out_shape=[...  1.24 us
    pallas_call x1, Pallas kernels, on_device_heads(): pl.pallas_call(functools.partial(pack_kernel, ranks), out_shape=[struct((...  1.04 us
  transfers between devices with their start and end apart: 10, of which 3 were waited for; matrix products, arithmetic and copies ran while one was open for 0% of the time, Pallas kernels for 17%

profile of v10, /device:TPU:0, one launch (start us, length us, event | category | flops | bytes accessed | tf_op | source)
XLA Modules:
  0.0 36.6 jit_solution(428212904011674180)
XLA Ops:
  0.6 0.0 copy-start.2
  0.6 0.0 copy-start.1
  0.7 0.0 copy-start
  0.7 1.0 %pack.1 = (bf16[3,128,128]{2,1,0:T(8,128)(2,1)S(1)}, bf16[3,128,128]{2,1,0:T(8,128)(2,1)S(1)}, bf16[3,128,128]{2,1,0:T(8,128)(2,1)S(1)}) custom-call(bf16[1,128,512]{2,1,0:T(8,128)(2,1)} %q_ref.3, bf16[1,128,512]{2,1,0:T(8,128)(2,1)} %k_ref.3, bf16[1,128,512]{2,1,0:T(8,128)(2,1)} %v_ref.3), custom_call_target="tpu_custom_call" | custom-call | tf_op jit(solution)/shard_map/pack/pallas_call | solution.py:509
  1.7 5.1 %collective-permute-start.3 = (bf16[3,128,128]{2,1,0:T(8,128)(2,1)S(1)}, bf16[3,128,128]{2,1,0:T(8,128)(2,1)S(1)}, u32[]{:S(2)}, u32[]{:S(2)}) collective-permute-start(bf16[3,128,128]{2,1,0:T(8,128)(2,1)S(1)} %get-tuple-element.36), channel_id=1, source_target_pairs={{0,6},{2,4},{4,2},{6,0},{1,7},{3,5},{5,3},{7,1},{8,14},{10,12},{12... | collective-permute-start | bytes 294920 | tf_op jit(solution)/shard_map/ppermute | solution.py:520
  6.8 0.0 copy-start.4
  6.8 0.0 collective-permute-start.4
  6.8 0.6 %collective-permute-start.5 = (bf16[3,128,128]{2,1,0:T(8,128)(2,1)S(1)}, bf16[3,128,128]{2,1,0:T(8,128)(2,1)S(1)}, u32[]{:S(2)}, u32[]{:S(2)}) collective-permute-start(bf16[3,128,128]{2,1,0:T(8,128)(2,1)S(1)} %get-tuple-element.38), channel_id=1, source_target_pairs={{0,2},{2,0},{4,6},{6,4},{1,3},{3,1},{5,7},{7,5},{8,10},{10,8},{12,... | collective-permute-start | bytes 294920 | tf_op jit(solution)/shard_map/ppermute | solution.py:520
  7.5 0.0 copy-done.2
  7.5 0.0 copy-done.1
  7.5 0.0 copy-done
  7.5 0.0 copy-done.4
  7.5 0.0 copy-start.3
  7.5 0.9 %copy-done.3 = bf16[1,128,512]{2,1,0:T(8,128)(2,1)S(1)} copy-done((bf16[1,128,512]{2,1,0:T(8,128)(2,1)S(1)}, bf16[1,128,512]{2,1,0:T(8,128)(2,1)}, u32[]{:S(2)}) %copy-start.3) | copy-done | bytes 131096
  8.4 0.0 copy-start.5
  8.4 1.3 %masks.1 = (bf16[128,128]{1,0:T(8,128)(2,1)S(1)}, bf16[128,128]{1,0:T(8,128)(2,1)S(1)}, bf16[128,128]{1,0:T(8,128)(2,1)S(1)}, bf16[4,128,128]{2,1,0:T(8,128)(2,1...) custom-call(s32[1,16]{1,0:T(1,128)S(1)} %copy-done.4, ...), custom_call_target="tpu_custom_call" | custom-call | flops 4194304 | bytes 1048576 | tf_op jit(solution)/shard_map/masks/pallas_call | solution.py:525
  9.7 3.8 %collective-permute-start = (bf16[128,128]{1,0:T(8,128)(2,1)S(1)}, bf16[128,128]{1,0:T(8,128)(2,1)S(1)}, u32[]{:S(2)}, u32[]{:S(2)}) collective-permute-start(bf16[128,128]{1,0:T(8,128)(2,1)S(1)} %get-tuple-element.32), channel_id=1, source_target_pairs={{0,6},{2,4},{4,2},{6,0},{1,7},{3,5},{5,3},{7,1},{8,14},{10,12},{12... | collective-permute-start | bytes 98312 | tf_op jit(solution)/shard_map/ppermute | solution.py:520
  13.5 0.0 collective-permute-start.1
  13.5 0.0 collective-permute-done.3.refs_0_
  13.5 1.3 %collective-permute-start.2 = (bf16[128,128]{1,0:T(8,128)(2,1)S(1)}, bf16[128,128]{1,0:T(8,128)(2,1)S(1)}, u32[]{:S(2)}, u32[]{:S(2)}) collective-permute-start(bf16[128,128]{1,0:T(8,128)(2,1)S(1)} %get-tuple-element.34), channel_id=1, source_target_pairs={{0,2},{2,0},{4,6},{6,4},{1,3},{3,1},{5,7},{7,5},{8,10},{10,8},{12,... | collective-permute-start | bytes 98312 | tf_op jit(solution)/shard_map/ppermute | solution.py:520
  14.9 2.3 %collective-permute-done.4.refs_1_ = bf16[3,128,128]{2,1,0:T(8,128)(2,1)S(1)} collective-permute-done((bf16[3,128,128]{2,1,0:T(8,128)(2,1)S(1)}, bf16[3,128,128]{2,1,0:T(8,128)(2,1)S(1)}, u32[]{:S(2)}, u32[]{:S(2)}) %collective-permute-start.4) | collective-permute-done | bytes 98336 | tf_op jit(solution)/shard_map/ppermute | solution.py:520
  17.2 0.0 collective-permute-done.5.refs_2_
  17.2 0.0 copy-done.5
  17.2 2.6 %forward.1 = (bf16[2,512,512]{2,1,0:T(8,128)(2,1)S(1)}, f32[544,128]{1,0:T(8,128)S(1)}, f32[512,128]{1,0:T(8,128)S(1)}, bf16[2,512,128]{2,1,0:T(8,128)(2,1)S(1)}...) custom-call(bf16[3,128,128]{2,1,0:T(8,128)(2,1)S(1)} %collective-permute-done.3.refs_0_, ...), custom_call_target="tpu_custom_call" | custom-call | flops 419430400 | bytes 3145728 | tf_op jit(solution)/shard_map/forward/pallas_call | solution.py:544
  19.8 0.0 collective-permute-done.refs_0_
  19.8 0.0 collective-permute-done.1.refs_1_
  19.8 0.0 collective-permute-done.2.refs_2_
  19.8 1.2 %taps.1 = (bf16[512,128]{1,0:T(8,128)(2,1)S(1)}, f32[544,128]{1,0:T(8,128)S(1)}, f32[32,128]{1,0:T(8,128)S(1)}) custom-call(bf16[128,128]{1,0:T(8,128)(2,1)S(1)} %collective-permute-done.refs_0_, bf16[128,128]{1,0:T(8,128)(2,1)S(1)} %collective-permute-done.1.refs_1_, bf16[128,128]{1,0:T(8,128)(2,1)S(1)} %collective-permute-done.2.refs_2_, ...), custom_call_target="tpu_custom_call" | custom-call | flops 419430400 | bytes 3145728 | tf_op jit(solution)/shard_map/taps/pallas_call | solution.py:568
  21.1 1.6 %collective-permute-start.6 = (f32[32,128]{1,0:T(8,128)S(1)}, f32[32,128]{1,0:T(8,128)S(1)}, u32[]{:S(2)}, u32[]{:S(2)}) collective-permute-start(f32[32,128]{1,0:T(8,128)S(1)} %get-tuple-element.54.refs_4_), channel_id=1, source_target_pairs={{0,8},{8,0},{1,9},{9,1},{2,10},{10,2},{3,11},{11,3},{4,12},{12,4},... | collective-permute-start | bytes 49160 | tf_op jit(solution)/shard_map/ppermute | solution.py:585
  22.7 2.4 %backward.1 = (bf16[512,128]{1,0:T(8,128)(2,1)S(1)}, bf16[512,128]{1,0:T(8,128)(2,1)S(1)}, bf16[512,128]{1,0:T(8,128)(2,1)S(1)}) custom-call(bf16[2,512,512]{2,1,0:T(8,128)(2,1)S(1)} %get-tuple-element.46.soft_ref, f32[544,128]{1,0:T(8,128)S(1)} %get-tuple-element.43.refs_4_.att_ref, f32[544,128]{1,0:T(8,128)S(1)} %get-tuple-element.47.grad_pad, ...), custom_call_target="tpu_custom_call" | custom-call | flops 838860800 | bytes 3145728 | tf_op jit(solution)/shard_map/backward/pallas_call | solution.py:589
  25.1 0.0 collective-permute-done.6.refs_5_
  25.1 0.6 %collective-permute-start.8 = (bf16[544,128]{1,0:T(8,128)(2,1)S(1)}, bf16[544,128]{1,0:T(8,128)(2,1)S(1)}, u32[]{:S(2)}, u32[]{:S(2)}) collective-permute-start(bf16[544,128]{1,0:T(8,128)(2,1)S(1)} %get-tuple-element.57), channel_id=1, source_target_pairs={{0,4},{2,6},{4,0},{6,2},{1,5},{3,7},{5,1},{7,3},{8,12},{10,14},{12... | collective-permute-start | bytes 417800 | tf_op jit(solution)/shard_map/ppermute | solution.py:520
  25.7 2.1 %collective-permute-start.9 = (bf16[544,128]{1,0:T(8,128)(2,1)S(1)}, bf16[544,128]{1,0:T(8,128)(2,1)S(1)}, u32[]{:S(2)}, u32[]{:S(2)}) collective-permute-start(bf16[544,128]{1,0:T(8,128)(2,1)S(1)} %get-tuple-element.58), channel_id=1, source_target_pairs={{0,6},{2,4},{4,2},{6,0},{1,7},{3,5},{5,3},{7,1},{8,14},{10,12},{12... | collective-permute-start | bytes 417800 | tf_op jit(solution)/shard_map/ppermute | solution.py:520
  27.8 1.0 %collective-permute-start.7 = (bf16[544,128]{1,0:T(8,128)(2,1)S(1)}, bf16[544,128]{1,0:T(8,128)(2,1)S(1)}, u32[]{:S(2)}, u32[]{:S(2)}) collective-permute-start(bf16[544,128]{1,0:T(8,128)(2,1)S(1)} %get-tuple-element.56), channel_id=1, source_target_pairs={{0,2},{2,0},{4,6},{6,4},{1,3},{3,1},{5,7},{7,5},{8,10},{10,8},{12,... | collective-permute-start | bytes 417800 | tf_op jit(solution)/shard_map/ppermute | solution.py:520
  28.8 6.8 %collective-permute-done.8.refs_2_ = bf16[544,128]{1,0:T(8,128)(2,1)S(1)} collective-permute-done((bf16[544,128]{1,0:T(8,128)(2,1)S(1)}, bf16[544,128]{1,0:T(8,128)(2,1)S(1)}, u32[]{:S(2)}, u32[]{:S(2)}) %collective-permute-start.8) | collective-permute-done | bytes 139296 | tf_op jit(solution)/shard_map/ppermute | solution.py:520
  35.5 0.0 collective-permute-done.9.refs_3_
  35.5 0.2 collective-permute-done.7.refs_1_
  35.7 0.9 %spread.1 = (bf16[1,128,512]{2,1,0:T(8,128)(2,1)}, bf16[1,128,512]{2,1,0:T(8,128)(2,1)}, bf16[1,128,512]{2,1,0:T(8,128)(2,1)}, bf16[1,128,512]{2,1,0:T(8,128)(2,1)}, f32[31,512]{1,0:T(8,128)}) custom-call(bf16[544,128]{1,0:T(8,128)(2,1)S(1)} %get-tuple-element.55.refs_0_, bf16[544,128]{1,0:T(8,128)(2,1)S(1)} %collective-permute-done.7.refs_1_, ...), custom_call_target="tpu_custom_call" | custom-call | tf_op jit(solution)/shard_map/spread/pallas_call | solution.py:623
  (2 shorter events, 0.1 us)
Async XLA Ops:
  0.6 6.8 %copy-start.2 = (bf16[1,128,512]{2,1,0:T(8,128)(2,1)S(1)}, bf16[1,128,512]{2,1,0:T(8,128)(2,1)}, u32[]{:S(2)}) copy-start(bf16[1,128,512]{2,1,0:T(8,128)(2,1)} %v_ref.3) | copy-start | bytes 393220
  0.6 6.8 %copy-start.1 = (bf16[1,128,512]{2,1,0:T(8,128)(2,1)S(1)}, bf16[1,128,512]{2,1,0:T(8,128)(2,1)}, u32[]{:S(2)}) copy-start(bf16[1,128,512]{2,1,0:T(8,128)(2,1)} %k_ref.3) | copy-start | bytes 393220
  0.7 6.8 %copy-start = (bf16[1,128,512]{2,1,0:T(8,128)(2,1)S(1)}, bf16[1,128,512]{2,1,0:T(8,128)(2,1)}, u32[]{:S(2)}) copy-start(bf16[1,128,512]{2,1,0:T(8,128)(2,1)} %q_ref.3) | copy-start | bytes 393220
  1.7 11.8 %collective-permute-start.3 = (bf16[3,128,128]{2,1,0:T(8,128)(2,1)S(1)}, bf16[3,128,128]{2,1,0:T(8,128)(2,1)S(1)}, u32[]{:S(2)}, u32[]{:S(2)}) collective-permute-start(bf16[3,128,128]{2,1,0:T(8,128)(2,1)S(1)} %get-tuple-element.36), channel_id=1, source_target_pairs={{0,6},{2,4},{4,2},{6,0},{1,7},{3,5},{5,3},{7,1},{8,14},{10,12},{12... | collective-permute-start | bytes 294920 | tf_op jit(solution)/shard_map/ppermute | solution.py:520
  6.8 0.7 %copy-start.4 = (s32[1,16]{1,0:T(1,128)S(1)}, s32[1,16]{1,0:T(1,128)}, u32[]{:S(2)}) copy-start(s32[1,16]{1,0:T(1,128)} %lens_ref.1) | copy-start | bytes 196
  6.8 10.4 %collective-permute-start.4 = (bf16[3,128,128]{2,1,0:T(8,128)(2,1)S(1)}, bf16[3,128,128]{2,1,0:T(8,128)(2,1)S(1)}, u32[]{:S(2)}, u32[]{:S(2)}) collective-permute-start(bf16[3,128,128]{2,1,0:T(8,128)(2,1)S(1)} %get-tuple-element.37), channel_id=1, source_target_pairs={{0,4},{2,6},{4,0},{6,2},{1,5},{3,7},{5,1},{7,3},{8,12},{10,14},{12... | collective-permute-start | bytes 294920 | tf_op jit(solution)/shard_map/ppermute | solution.py:520
  6.8 10.4 %collective-permute-start.5 = (bf16[3,128,128]{2,1,0:T(8,128)(2,1)S(1)}, bf16[3,128,128]{2,1,0:T(8,128)(2,1)S(1)}, u32[]{:S(2)}, u32[]{:S(2)}) collective-permute-start(bf16[3,128,128]{2,1,0:T(8,128)(2,1)S(1)} %get-tuple-element.38), channel_id=1, source_target_pairs={{0,2},{2,0},{4,6},{6,4},{1,3},{3,1},{5,7},{7,5},{8,10},{10,8},{12,... | collective-permute-start | bytes 294920 | tf_op jit(solution)/shard_map/ppermute | solution.py:520
  7.5 0.9 %copy-start.3 = (bf16[1,128,512]{2,1,0:T(8,128)(2,1)S(1)}, bf16[1,128,512]{2,1,0:T(8,128)(2,1)}, u32[]{:S(2)}) copy-start(bf16[1,128,512]{2,1,0:T(8,128)(2,1)} %c_ref.1) | copy-start | bytes 393220
  8.4 8.8 %copy-start.5 = (f32[31,512]{1,0:T(8,128)S(1)}, f32[31,512]{1,0:T(8,128)}, u32[]{:S(2)}) copy-start(f32[31,512]{1,0:T(8,128)} %w_ref.1) | copy-start | bytes 190468
  9.7 10.1 %collective-permute-start = (bf16[128,128]{1,0:T(8,128)(2,1)S(1)}, bf16[128,128]{1,0:T(8,128)(2,1)S(1)}, u32[]{:S(2)}, u32[]{:S(2)}) collective-permute-start(bf16[128,128]{1,0:T(8,128)(2,1)S(1)} %get-tuple-element.32), channel_id=1, source_target_pairs={{0,6},{2,4},{4,2},{6,0},{1,7},{3,5},{5,3},{7,1},{8,14},{10,12},{12... | collective-permute-start | bytes 98312 | tf_op jit(solution)/shard_map/ppermute | solution.py:520
  13.5 6.3 %collective-permute-start.1 = (bf16[128,128]{1,0:T(8,128)(2,1)S(1)}, bf16[128,128]{1,0:T(8,128)(2,1)S(1)}, u32[]{:S(2)}, u32[]{:S(2)}) collective-permute-start(bf16[128,128]{1,0:T(8,128)(2,1)S(1)} %get-tuple-element.33), channel_id=1, source_target_pairs={{0,4},{2,6},{4,0},{6,2},{1,5},{3,7},{5,1},{7,3},{8,12},{10,14},{12... | collective-permute-start | bytes 98312 | tf_op jit(solution)/shard_map/ppermute | solution.py:520
  13.5 6.3 %collective-permute-start.2 = (bf16[128,128]{1,0:T(8,128)(2,1)S(1)}, bf16[128,128]{1,0:T(8,128)(2,1)S(1)}, u32[]{:S(2)}, u32[]{:S(2)}) collective-permute-start(bf16[128,128]{1,0:T(8,128)(2,1)S(1)} %get-tuple-element.34), channel_id=1, source_target_pairs={{0,2},{2,0},{4,6},{6,4},{1,3},{3,1},{5,7},{7,5},{8,10},{10,8},{12,... | collective-permute-start | bytes 98312 | tf_op jit(solution)/shard_map/ppermute | solution.py:520
  21.1 4.0 %collective-permute-start.6 = (f32[32,128]{1,0:T(8,128)S(1)}, f32[32,128]{1,0:T(8,128)S(1)}, u32[]{:S(2)}, u32[]{:S(2)}) collective-permute-start(f32[32,128]{1,0:T(8,128)S(1)} %get-tuple-element.54.refs_4_), channel_id=1, source_target_pairs={{0,8},{8,0},{1,9},{9,1},{2,10},{10,2},{3,11},{11,3},{4,12},{12,4},... | collective-permute-start | bytes 49160 | tf_op jit(solution)/shard_map/ppermute | solution.py:585
  25.1 10.4 %collective-permute-start.8 = (bf16[544,128]{1,0:T(8,128)(2,1)S(1)}, bf16[544,128]{1,0:T(8,128)(2,1)S(1)}, u32[]{:S(2)}, u32[]{:S(2)}) collective-permute-start(bf16[544,128]{1,0:T(8,128)(2,1)S(1)} %get-tuple-element.57), channel_id=1, source_target_pairs={{0,4},{2,6},{4,0},{6,2},{1,5},{3,7},{5,1},{7,3},{8,12},{10,14},{12... | collective-permute-start | bytes 417800 | tf_op jit(solution)/shard_map/ppermute | solution.py:520
  25.7 9.8 %collective-permute-start.9 = (bf16[544,128]{1,0:T(8,128)(2,1)S(1)}, bf16[544,128]{1,0:T(8,128)(2,1)S(1)}, u32[]{:S(2)}, u32[]{:S(2)}) collective-permute-start(bf16[544,128]{1,0:T(8,128)(2,1)S(1)} %get-tuple-element.58), channel_id=1, source_target_pairs={{0,6},{2,4},{4,2},{6,0},{1,7},{3,5},{5,3},{7,1},{8,14},{10,12},{12... | collective-permute-start | bytes 417800 | tf_op jit(solution)/shard_map/ppermute | solution.py:520
  27.8 7.9 %collective-permute-start.7 = (bf16[544,128]{1,0:T(8,128)(2,1)S(1)}, bf16[544,128]{1,0:T(8,128)(2,1)S(1)}, u32[]{:S(2)}, u32[]{:S(2)}) collective-permute-start(bf16[544,128]{1,0:T(8,128)(2,1)S(1)} %get-tuple-element.56), channel_id=1, source_target_pairs={{0,2},{2,0},{4,6},{6,4},{1,3},{3,1},{5,7},{7,5},{8,10},{10,8},{12,... | collective-permute-start | bytes 417800 | tf_op jit(solution)/shard_map/ppermute | solution.py:520

commit v11 on v10

--- a/solution.py
+++ b/solution.py
@@ -253,6 +253,11 @@
 
 def lanes_at(block):
     return pl.ds(pl.multiple_of(block * LANES, LANES), LANES)
+
+
+def late_order(ranks):
+    middle = ranks // 2
+    return [step for step in range(ranks - 1, 0, -1) if step != middle] + [middle]
 
 
 def pack_kernel(ranks, q_ref, k_ref, v_ref, *rest):
@@ -390,14 +395,14 @@
 
 
 def taps_kernel(ranks, frames, *refs):
-    cots = refs[: ranks - 1]
+    cots = dict(zip(late_order(ranks), refs))
     own_ref, att_ref, pre_ref, after_ref, before_ref = refs[ranks - 1 : ranks + 4]
     mixed_ref, grad_pad, taps_ref, cot, tap_sum = refs[ranks + 4 :]
     me = lax.axis_index("seq")
     length = ranks * frames
     cot[rows_at(me, frames), :] = own_ref[3]
     for step in range(1, ranks):
-        cot[rows_at(me ^ step, frames), :] = cots[ranks - 1 - step][...]
+        cot[rows_at(me ^ step, frames), :] = cots[step][...]
     zeros = jnp.zeros((PAD, LANES), jnp.float32)
     grad_pad[0:PAD, :] = zeros
     grad_pad[PAD + length :, :] = zeros
@@ -578,7 +583,7 @@
         compiler_params=params,
         cost_estimate=cost(400 * MIB, 3 * MIB),
         name="taps",
-    )(*[cots[step] for step in order], own, att, pre, after, before)
+    )(*[cots[step] for step in late_order(ranks)], own, att, pre, after, before)
 
     copies = lax.axis_size("dp")
     part_taps = [own_taps] + [

time: 36.8 us -> 37.2 us (1.011)
  starting transfers between devices: 16.1 us -> 16.9 us
  waiting for transfers between devices: 9.33 us -> 8.81 us
    ppermute x9, starting transfers between devices: 14.5 us -> 15.4 us  [swap(): lax.ppermute(array, 'seq', [(rank, rank ^ step) for rank in range(ranks)])]
    ppermute x9, waiting for transfers between devices: 9.33 us -> 8.81 us  [swap(): lax.ppermute(array, 'seq', [(rank, rank ^ step) for rank in range(ranks)])]
where the time goes in v11:
time: 37.2 us; the launch traced here: 37 us
  starting transfers between devices  16.9 us (45%)
  Pallas kernels  9.57 us (26%)
  waiting for transfers between devices  8.81 us (24%)
  local copies, waits for them, and re-layouts  0.92 us (2%)
  between operations  0.77 us (2%)
    ppermute x9, starting transfers between devices, swap(): lax.ppermute(array, 'seq', [(rank, rank ^ step) for rank in range(ranks)])  15.4 us
    ppermute x9, waiting for transfers between devices, swap(): lax.ppermute(array, 'seq', [(rank, rank ^ step) for rank in range(ranks)])  8.81 us
    pallas_call x1, Pallas kernels, on_device_heads(): pl.pallas_call(functools.partial(forward_kernel, ranks, frames), out_shap...  2.6 us
    pallas_call x1, Pallas kernels, on_device_heads(): pl.pallas_call(backward_kernel, out_shape=[struct((length, LANES), bf16)]...  2.41 us
    ppermute x1, starting transfers between devices, on_device_heads(): lax.ppermute(own_taps, 'dp', [(one, (one + shift) % copies) for one in ra...  1.57 us
    pallas_call x1, Pallas kernels, on_device_heads(): pl.pallas_call(functools.partial(mask_kernel, ranks, length), out_shape=[...  1.32 us
    pallas_call x1, Pallas kernels, on_device_heads(): pl.pallas_call(functools.partial(taps_kernel, ranks, frames), out_shape=[...  1.24 us
    pallas_call x1, Pallas kernels, on_device_heads(): pl.pallas_call(functools.partial(pack_kernel, ranks), out_shape=[struct((...  1.04 us
  transfers between devices with their start and end apart: 10, of which 3 were waited for; matrix products, arithmetic and copies ran while one was open for 0% of the time, Pallas kernels for 17%

profile of v11, /device:TPU:0, one launch (start us, length us, event | category | flops | bytes accessed | tf_op | source)
XLA Modules:
  0.0 37.0 jit_solution(4542910594812021808)
XLA Ops:
  0.6 0.0 copy-start.2
  0.6 0.0 copy-start.1
  0.7 0.0 copy-start
  0.7 1.0 %pack.1 = (bf16[3,128,128]{2,1,0:T(8,128)(2,1)S(1)}, bf16[3,128,128]{2,1,0:T(8,128)(2,1)S(1)}, bf16[3,128,128]{2,1,0:T(8,128)(2,1)S(1)}) custom-call(bf16[1,128,512]{2,1,0:T(8,128)(2,1)} %q_ref.3, bf16[1,128,512]{2,1,0:T(8,128)(2,1)} %k_ref.3, bf16[1,128,512]{2,1,0:T(8,128)(2,1)} %v_ref.3), custom_call_target="tpu_custom_call" | custom-call | tf_op jit(solution)/shard_map/pack/pallas_call | solution.py:514
  1.7 5.1 %collective-permute-start.3 = (bf16[3,128,128]{2,1,0:T(8,128)(2,1)S(1)}, bf16[3,128,128]{2,1,0:T(8,128)(2,1)S(1)}, u32[]{:S(2)}, u32[]{:S(2)}) collective-permute-start(bf16[3,128,128]{2,1,0:T(8,128)(2,1)S(1)} %get-tuple-element.36), channel_id=1, source_target_pairs={{0,6},{2,4},{4,2},{6,0},{1,7},{3,5},{5,3},{7,1},{8,14},{10,12},{12... | collective-permute-start | bytes 294920 | tf_op jit(solution)/shard_map/ppermute | solution.py:525
  6.8 0.0 copy-start.4
  6.8 0.0 collective-permute-start.4
  6.8 0.6 %collective-permute-start.5 = (bf16[3,128,128]{2,1,0:T(8,128)(2,1)S(1)}, bf16[3,128,128]{2,1,0:T(8,128)(2,1)S(1)}, u32[]{:S(2)}, u32[]{:S(2)}) collective-permute-start(bf16[3,128,128]{2,1,0:T(8,128)(2,1)S(1)} %get-tuple-element.38), channel_id=1, source_target_pairs={{0,2},{2,0},{4,6},{6,4},{1,3},{3,1},{5,7},{7,5},{8,10},{10,8},{12,... | collective-permute-start | bytes 294920 | tf_op jit(solution)/shard_map/ppermute | solution.py:525
  7.5 0.0 copy-done.2
  7.5 0.0 copy-done.1
  7.5 0.0 copy-done
  7.5 0.0 copy-done.4
  7.5 0.0 copy-start.3
  7.5 0.9 %copy-done.3 = bf16[1,128,512]{2,1,0:T(8,128)(2,1)S(1)} copy-done((bf16[1,128,512]{2,1,0:T(8,128)(2,1)S(1)}, bf16[1,128,512]{2,1,0:T(8,128)(2,1)}, u32[]{:S(2)}) %copy-start.3) | copy-done | bytes 131096
  8.4 0.0 copy-start.5
  8.4 1.3 %masks.1 = (bf16[128,128]{1,0:T(8,128)(2,1)S(1)}, bf16[128,128]{1,0:T(8,128)(2,1)S(1)}, bf16[128,128]{1,0:T(8,128)(2,1)S(1)}, bf16[4,128,128]{2,1,0:T(8,128)(2,1...) custom-call(s32[1,16]{1,0:T(1,128)S(1)} %copy-done.4, ...), custom_call_target="tpu_custom_call" | custom-call | flops 4194304 | bytes 1048576 | tf_op jit(solution)/shard_map/masks/pallas_call | solution.py:530
  9.7 3.8 %collective-permute-start = (bf16[128,128]{1,0:T(8,128)(2,1)S(1)}, bf16[128,128]{1,0:T(8,128)(2,1)S(1)}, u32[]{:S(2)}, u32[]{:S(2)}) collective-permute-start(bf16[128,128]{1,0:T(8,128)(2,1)S(1)} %get-tuple-element.32), channel_id=1, source_target_pairs={{0,6},{2,4},{4,2},{6,0},{1,7},{3,5},{5,3},{7,1},{8,14},{10,12},{12... | collective-permute-start | bytes 98312 | tf_op jit(solution)/shard_map/ppermute | solution.py:525
  13.5 0.0 collective-permute-start.1
  13.5 0.0 collective-permute-done.3.refs_0_
  13.5 2.1 %collective-permute-start.2 = (bf16[128,128]{1,0:T(8,128)(2,1)S(1)}, bf16[128,128]{1,0:T(8,128)(2,1)S(1)}, u32[]{:S(2)}, u32[]{:S(2)}) collective-permute-start(bf16[128,128]{1,0:T(8,128)(2,1)S(1)} %get-tuple-element.34), channel_id=1, source_target_pairs={{0,4},{2,6},{4,0},{6,2},{1,5},{3,7},{5,1},{7,3},{8,12},{10,14},{12... | collective-permute-start | bytes 98312 | tf_op jit(solution)/shard_map/ppermute | solution.py:525
  15.7 0.9 %collective-permute-done.4.refs_1_ = bf16[3,128,128]{2,1,0:T(8,128)(2,1)S(1)} collective-permute-done((bf16[3,128,128]{2,1,0:T(8,128)(2,1)S(1)}, bf16[3,128,128]{2,1,0:T(8,128)(2,1)S(1)}, u32[]{:S(2)}, u32[]{:S(2)}) %collective-permute-start.4) | collective-permute-done | bytes 98336 | tf_op jit(solution)/shard_map/ppermute | solution.py:525
  16.6 0.0 collective-permute-done.5.refs_2_
  16.6 0.0 copy-done.5
  16.6 2.6 %forward.1 = (bf16[2,512,512]{2,1,0:T(8,128)(2,1)S(1)}, f32[544,128]{1,0:T(8,128)S(1)}, f32[512,128]{1,0:T(8,128)S(1)}, bf16[2,512,128]{2,1,0:T(8,128)(2,1)S(1)}...) custom-call(bf16[3,128,128]{2,1,0:T(8,128)(2,1)S(1)} %collective-permute-done.3.refs_0_, ...), custom_call_target="tpu_custom_call" | custom-call | flops 419430400 | bytes 3145728 | tf_op jit(solution)/shard_map/forward/pallas_call | solution.py:549
  19.2 0.0 collective-permute-done.refs_0_
  19.2 0.0 collective-permute-done.1.refs_1_
  19.2 0.0 collective-permute-done.2.refs_2_
  19.2 1.2 %taps.1 = (bf16[512,128]{1,0:T(8,128)(2,1)S(1)}, f32[544,128]{1,0:T(8,128)S(1)}, f32[32,128]{1,0:T(8,128)S(1)}) custom-call(bf16[128,128]{1,0:T(8,128)(2,1)S(1)} %collective-permute-done.refs_0_, bf16[128,128]{1,0:T(8,128)(2,1)S(1)} %collective-permute-done.1.refs_1_, bf16[128,128]{1,0:T(8,128)(2,1)S(1)} %collective-permute-done.2.refs_2_, ...), custom_call_target="tpu_custom_call" | custom-call | flops 419430400 | bytes 3145728 | tf_op jit(solution)/shard_map/taps/pallas_call | solution.py:573
  20.4 1.6 %collective-permute-start.6 = (f32[32,128]{1,0:T(8,128)S(1)}, f32[32,128]{1,0:T(8,128)S(1)}, u32[]{:S(2)}, u32[]{:S(2)}) collective-permute-start(f32[32,128]{1,0:T(8,128)S(1)} %get-tuple-element.54.refs_4_), channel_id=1, source_target_pairs={{0,8},{8,0},{1,9},{9,1},{2,10},{10,2},{3,11},{11,3},{4,12},{12,4},... | collective-permute-start | bytes 49160 | tf_op jit(solution)/shard_map/ppermute | solution.py:590
  22.0 2.4 %backward.1 = (bf16[512,128]{1,0:T(8,128)(2,1)S(1)}, bf16[512,128]{1,0:T(8,128)(2,1)S(1)}, bf16[512,128]{1,0:T(8,128)(2,1)S(1)}) custom-call(bf16[2,512,512]{2,1,0:T(8,128)(2,1)S(1)} %get-tuple-element.46.soft_ref, f32[544,128]{1,0:T(8,128)S(1)} %get-tuple-element.43.refs_4_.att_ref, f32[544,128]{1,0:T(8,128)S(1)} %get-tuple-element.47.grad_pad, ...), custom_call_target="tpu_custom_call" | custom-call | flops 838860800 | bytes 3145728 | tf_op jit(solution)/shard_map/backward/pallas_call | solution.py:594
  24.4 0.0 collective-permute-done.6.refs_5_
  24.5 1.3 %collective-permute-start.8 = (bf16[544,128]{1,0:T(8,128)(2,1)S(1)}, bf16[544,128]{1,0:T(8,128)(2,1)S(1)}, u32[]{:S(2)}, u32[]{:S(2)}) collective-permute-start(bf16[544,128]{1,0:T(8,128)(2,1)S(1)} %get-tuple-element.57), channel_id=1, source_target_pairs={{0,4},{2,6},{4,0},{6,2},{1,5},{3,7},{5,1},{7,3},{8,12},{10,14},{12... | collective-permute-start | bytes 417800 | tf_op jit(solution)/shard_map/ppermute | solution.py:525
  25.8 2.2 %collective-permute-start.9 = (bf16[544,128]{1,0:T(8,128)(2,1)S(1)}, bf16[544,128]{1,0:T(8,128)(2,1)S(1)}, u32[]{:S(2)}, u32[]{:S(2)}) collective-permute-start(bf16[544,128]{1,0:T(8,128)(2,1)S(1)} %get-tuple-element.58), channel_id=1, source_target_pairs={{0,6},{2,4},{4,2},{6,0},{1,7},{3,5},{5,3},{7,1},{8,14},{10,12},{12... | collective-permute-start | bytes 417800 | tf_op jit(solution)/shard_map/ppermute | solution.py:525
  28.1 0.1 collective-permute-start.7
  28.2 6.9 %collective-permute-done.8.refs_2_ = bf16[544,128]{1,0:T(8,128)(2,1)S(1)} collective-permute-done((bf16[544,128]{1,0:T(8,128)(2,1)S(1)}, bf16[544,128]{1,0:T(8,128)(2,1)S(1)}, u32[]{:S(2)}, u32[]{:S(2)}) %collective-permute-start.8) | collective-permute-done | bytes 139296 | tf_op jit(solution)/shard_map/ppermute | solution.py:525
  35.0 0.0 collective-permute-done.9.refs_3_
  35.0 1.1 %collective-permute-done.7.refs_1_ = bf16[544,128]{1,0:T(8,128)(2,1)S(1)} collective-permute-done((bf16[544,128]{1,0:T(8,128)(2,1)S(1)}, bf16[544,128]{1,0:T(8,128)(2,1)S(1)}, u32[]{:S(2)}, u32[]{:S(2)}) %collective-permute-start.7) | collective-permute-done | bytes 139296 | tf_op jit(solution)/shard_map/ppermute | solution.py:525
  36.1 0.9 %spread.1 = (bf16[1,128,512]{2,1,0:T(8,128)(2,1)}, bf16[1,128,512]{2,1,0:T(8,128)(2,1)}, bf16[1,128,512]{2,1,0:T(8,128)(2,1)}, bf16[1,128,512]{2,1,0:T(8,128)(2,1)}, f32[31,512]{1,0:T(8,128)}) custom-call(bf16[544,128]{1,0:T(8,128)(2,1)S(1)} %get-tuple-element.55.refs_0_, bf16[544,128]{1,0:T(8,128)(2,1)S(1)} %collective-permute-done.7.refs_1_, ...), custom_call_target="tpu_custom_call" | custom-call | tf_op jit(solution)/shard_map/spread/pallas_call | solution.py:628
  (2 shorter events, 0.1 us)
Async XLA Ops:
  0.6 6.8 %copy-start.2 = (bf16[1,128,512]{2,1,0:T(8,128)(2,1)S(1)}, bf16[1,128,512]{2,1,0:T(8,128)(2,1)}, u32[]{:S(2)}) copy-start(bf16[1,128,512]{2,1,0:T(8,128)(2,1)} %v_ref.3) | copy-start | bytes 393220
  0.6 6.8 %copy-start.1 = (bf16[1,128,512]{2,1,0:T(8,128)(2,1)S(1)}, bf16[1,128,512]{2,1,0:T(8,128)(2,1)}, u32[]{:S(2)}) copy-start(bf16[1,128,512]{2,1,0:T(8,128)(2,1)} %k_ref.3) | copy-start | bytes 393220
  0.7 6.8 %copy-start = (bf16[1,128,512]{2,1,0:T(8,128)(2,1)S(1)}, bf16[1,128,512]{2,1,0:T(8,128)(2,1)}, u32[]{:S(2)}) copy-start(bf16[1,128,512]{2,1,0:T(8,128)(2,1)} %q_ref.3) | copy-start | bytes 393220
  1.7 11.8 %collective-permute-start.3 = (bf16[3,128,128]{2,1,0:T(8,128)(2,1)S(1)}, bf16[3,128,128]{2,1,0:T(8,128)(2,1)S(1)}, u32[]{:S(2)}, u32[]{:S(2)}) collective-permute-start(bf16[3,128,128]{2,1,0:T(8,128)(2,1)S(1)} %get-tuple-element.36), channel_id=1, source_target_pairs={{0,6},{2,4},{4,2},{6,0},{1,7},{3,5},{5,3},{7,1},{8,14},{10,12},{12... | collective-permute-start | bytes 294920 | tf_op jit(solution)/shard_map/ppermute | solution.py:525
  6.8 0.7 %copy-start.4 = (s32[1,16]{1,0:T(1,128)S(1)}, s32[1,16]{1,0:T(1,128)}, u32[]{:S(2)}) copy-start(s32[1,16]{1,0:T(1,128)} %lens_ref.1) | copy-start | bytes 196
  6.8 9.7 %collective-permute-start.4 = (bf16[3,128,128]{2,1,0:T(8,128)(2,1)S(1)}, bf16[3,128,128]{2,1,0:T(8,128)(2,1)S(1)}, u32[]{:S(2)}, u32[]{:S(2)}) collective-permute-start(bf16[3,128,128]{2,1,0:T(8,128)(2,1)S(1)} %get-tuple-element.37), channel_id=1, source_target_pairs={{0,4},{2,6},{4,0},{6,2},{1,5},{3,7},{5,1},{7,3},{8,12},{10,14},{12... | collective-permute-start | bytes 294920 | tf_op jit(solution)/shard_map/ppermute | solution.py:525
  6.8 9.7 %collective-permute-start.5 = (bf16[3,128,128]{2,1,0:T(8,128)(2,1)S(1)}, bf16[3,128,128]{2,1,0:T(8,128)(2,1)S(1)}, u32[]{:S(2)}, u32[]{:S(2)}) collective-permute-start(bf16[3,128,128]{2,1,0:T(8,128)(2,1)S(1)} %get-tuple-element.38), channel_id=1, source_target_pairs={{0,2},{2,0},{4,6},{6,4},{1,3},{3,1},{5,7},{7,5},{8,10},{10,8},{12,... | collective-permute-start | bytes 294920 | tf_op jit(solution)/shard_map/ppermute | solution.py:525
  7.5 0.9 %copy-start.3 = (bf16[1,128,512]{2,1,0:T(8,128)(2,1)S(1)}, bf16[1,128,512]{2,1,0:T(8,128)(2,1)}, u32[]{:S(2)}) copy-start(bf16[1,128,512]{2,1,0:T(8,128)(2,1)} %c_ref.1) | copy-start | bytes 393220
  8.4 8.2 %copy-start.5 = (f32[31,512]{1,0:T(8,128)S(1)}, f32[31,512]{1,0:T(8,128)}, u32[]{:S(2)}) copy-start(f32[31,512]{1,0:T(8,128)} %w_ref.1) | copy-start | bytes 190468
  9.7 9.4 %collective-permute-start = (bf16[128,128]{1,0:T(8,128)(2,1)S(1)}, bf16[128,128]{1,0:T(8,128)(2,1)S(1)}, u32[]{:S(2)}, u32[]{:S(2)}) collective-permute-start(bf16[128,128]{1,0:T(8,128)(2,1)S(1)} %get-tuple-element.32), channel_id=1, source_target_pairs={{0,6},{2,4},{4,2},{6,0},{1,7},{3,5},{5,3},{7,1},{8,14},{10,12},{12... | collective-permute-start | bytes 98312 | tf_op jit(solution)/shard_map/ppermute | solution.py:525
  13.5 5.7 %collective-permute-start.1 = (bf16[128,128]{1,0:T(8,128)(2,1)S(1)}, bf16[128,128]{1,0:T(8,128)(2,1)S(1)}, u32[]{:S(2)}, u32[]{:S(2)}) collective-permute-start(bf16[128,128]{1,0:T(8,128)(2,1)S(1)} %get-tuple-element.33), channel_id=1, source_target_pairs={{0,2},{2,0},{4,6},{6,4},{1,3},{3,1},{5,7},{7,5},{8,10},{10,8},{12,... | collective-permute-start | bytes 98312 | tf_op jit(solution)/shard_map/ppermute | solution.py:525
  13.5 5.7 %collective-permute-start.2 = (bf16[128,128]{1,0:T(8,128)(2,1)S(1)}, bf16[128,128]{1,0:T(8,128)(2,1)S(1)}, u32[]{:S(2)}, u32[]{:S(2)}) collective-permute-start(bf16[128,128]{1,0:T(8,128)(2,1)S(1)} %get-tuple-element.34), channel_id=1, source_target_pairs={{0,4},{2,6},{4,0},{6,2},{1,5},{3,7},{5,1},{7,3},{8,12},{10,14},{12... | collective-permute-start | bytes 98312 | tf_op jit(solution)/shard_map/ppermute | solution.py:525
  20.4 4.0 %collective-permute-start.6 = (f32[32,128]{1,0:T(8,128)S(1)}, f32[32,128]{1,0:T(8,128)S(1)}, u32[]{:S(2)}, u32[]{:S(2)}) collective-permute-start(f32[32,128]{1,0:T(8,128)S(1)} %get-tuple-element.54.refs_4_), channel_id=1, source_target_pairs={{0,8},{8,0},{1,9},{9,1},{2,10},{10,2},{3,11},{11,3},{4,12},{12,4},... | collective-permute-start | bytes 49160 | tf_op jit(solution)/shard_map/ppermute | solution.py:590
  24.5 10.5 %collective-permute-start.8 = (bf16[544,128]{1,0:T(8,128)(2,1)S(1)}, bf16[544,128]{1,0:T(8,128)(2,1)S(1)}, u32[]{:S(2)}, u32[]{:S(2)}) collective-permute-start(bf16[544,128]{1,0:T(8,128)(2,1)S(1)} %get-tuple-element.57), channel_id=1, source_target_pairs={{0,4},{2,6},{4,0},{6,2},{1,5},{3,7},{5,1},{7,3},{8,12},{10,14},{12... | collective-permute-start | bytes 417800 | tf_op jit(solution)/shard_map/ppermute | solution.py:525
  25.8 9.2 %collective-permute-start.9 = (bf16[544,128]{1,0:T(8,128)(2,1)S(1)}, bf16[544,128]{1,0:T(8,128)(2,1)S(1)}, u32[]{:S(2)}, u32[]{:S(2)}) collective-permute-start(bf16[544,128]{1,0:T(8,128)(2,1)S(1)} %get-tuple-element.58), channel_id=1, source_target_pairs={{0,6},{2,4},{4,2},{6,0},{1,7},{3,5},{5,3},{7,1},{8,14},{10,12},{12... | collective-permute-start | bytes 417800 | tf_op jit(solution)/shard_map/ppermute | solution.py:525
  28.1 8.0 %collective-permute-start.7 = (bf16[544,128]{1,0:T(8,128)(2,1)S(1)}, bf16[544,128]{1,0:T(8,128)(2,1)S(1)}, u32[]{:S(2)}, u32[]{:S(2)}) collective-permute-start(bf16[544,128]{1,0:T(8,128)(2,1)S(1)} %get-tuple-element.56), channel_id=1, source_target_pairs={{0,2},{2,0},{4,6},{6,4},{1,3},{3,1},{5,7},{7,5},{8,10},{10,8},{12,... | collective-permute-start | bytes 417800 | tf_op jit(solution)/shard_map/ppermute | solution.py:525

commit v12 on v10

--- a/solution.py
+++ b/solution.py
@@ -253,6 +253,17 @@
 
 def lanes_at(block):
     return pl.ds(pl.multiple_of(block * LANES, LANES), LANES)
+
+
+def turns(ranks):
+    middle = ranks // 2
+    even = [middle] + [step for step in range(ranks - 1, 0, -1) if step != middle]
+    return list(zip(even, even[1:] + even[:1]))
+
+
+def step_of(turn):
+    even, odd = turn
+    return jnp.where(lax.axis_index("mp") % 2 == 0, even, odd)
 
 
 def pack_kernel(ranks, q_ref, k_ref, v_ref, *rest):
@@ -469,22 +480,23 @@
     taps = tap_refs[0][...]
     for other in tap_refs[1:]:
         taps = taps + other[...]
-    for step, out in zip(steps, outs):
-        rows = rows_at(me ^ step, frames)
+    for turn, out in zip(steps, outs):
+        rows = rows_at(me ^ step_of(turn), frames)
         for place, source in enumerate(sources):
             out[place * frames : (place + 1) * frames, :] = source[rows, :]
         out[4 * frames :, :] = taps.astype(jnp.bfloat16)
 
 
-def spread_kernel(ranks, frames, *refs):
+def spread_kernel(steps, frames, *refs):
+    ranks = len(steps)
     blocks = refs[:ranks]
     targets, taps_ref = refs[ranks : ranks + 4], refs[ranks + 4]
     me = lax.axis_index("seq")
-    for step in range(ranks):
-        lanes = lanes_at(me ^ step)
+    for turn, block in zip(steps, blocks):
+        lanes = lanes_at(me ^ step_of(turn))
         for place, target in enumerate(targets):
-            target[0, :, lanes] = blocks[step][place * frames : (place + 1) * frames, :]
-        taps = blocks[step][4 * frames :, :].astype(jnp.float32)
+            target[0, :, lanes] = block[place * frames : (place + 1) * frames, :]
+        taps = block[4 * frames :, :].astype(jnp.float32)
         taps_ref[:, lanes] = taps[:KERNEL]
 
 
@@ -613,21 +625,30 @@
             name="blocks",
         )(mixed, *results, *part_taps)
 
-    half = ranks // 2
-    far = blocks_of(list(range(half, ranks)))
-    near = blocks_of(list(range(half)))
-    back = {step: swap(far[step - half], step) for step in range(half, ranks)}
-    back |= {step: swap(near[step], step) for step in range(1, half)}
-    back[0] = near[0]
+    cores = lax.axis_size("mp")
+
+    def exchange(array, turn):
+        pairs = [
+            (rank * cores + core, (rank ^ turn[core % 2]) * cores + core)
+            for rank in range(ranks)
+            for core in range(cores)
+        ]
+        return lax.ppermute(array, ("seq", "mp"), pairs)
+
+    order = turns(ranks)
+    first, last = order[: ranks // 2], order[ranks // 2 :]
+    far = blocks_of(first)
+    *near, kept = blocks_of(last + [(0, 0)])
+    back = [exchange(block, turn) for block, turn in zip([*far, *near], order)]
 
     return pl.pallas_call(
-        functools.partial(spread_kernel, ranks, frames),
+        functools.partial(spread_kernel, order + [(0, 0)], frames),
         out_shape=[struct(queries.shape, bf16)] * 4 + [struct(conv_weight.shape, f32)],
         in_specs=[vmem] * ranks,
         out_specs=[vmem] * 5,
         compiler_params=params,
         name="spread",
-    )(*[back[step] for step in range(ranks)])
+    )(*back, kept)
 
 
 def on_device_any(queries, keys, values, cotangent, conv_weight, rec_lengths):

time: 36.8 us -> 36.8 us (level)
  waiting for transfers between devices: 9.33 us -> 8.43 us
  starting transfers between devices: 16.1 us -> 16.9 us
    ppermute x9 -> x6, waiting for transfers between devices: 9.33 us -> 2.36 us  [swap(): lax.ppermute(array, 'seq', [(rank, rank ^ step) for rank in range(ranks)])]
    ppermute x0 -> x3, waiting for transfers between devices: none -> 6.08 us  [exchange(): return lax.ppermute(array, ('seq', 'mp'), pairs)]
    ppermute x0 -> x3, starting transfers between devices: none -> 4.49 us  [exchange(): return lax.ppermute(array, ('seq', 'mp'), pairs)]
    ppermute x9 -> x6, starting transfers between devices: 14.5 us -> 10.9 us  [swap(): lax.ppermute(array, 'seq', [(rank, rank ^ step) for rank in range(ranks)])]
where the time goes in v12:
time: 36.8 us; the launch traced here: 36.6 us
  starting transfers between devices  16.9 us (46%)
  Pallas kernels  9.58 us (26%)
  waiting for transfers between devices  8.43 us (23%)
  local copies, waits for them, and re-layouts  0.92 us (2%)
  between operations  0.77 us (2%)
    ppermute x6, starting transfers between devices, swap(): lax.ppermute(array, 'seq', [(rank, rank ^ step) for rank in range(ranks)])  10.9 us
    ppermute x3, waiting for transfers between devices, exchange(): return lax.ppermute(array, ('seq', 'mp'), pairs)  6.08 us
    ppermute x3, starting transfers between devices, exchange(): return lax.ppermute(array, ('seq', 'mp'), pairs)  4.49 us
    pallas_call x1, Pallas kernels, on_device_heads(): pl.pallas_call(functools.partial(forward_kernel, ranks, frames), out_shap...  2.6 us
    pallas_call x1, Pallas kernels, on_device_heads(): pl.pallas_call(backward_kernel, out_shape=[struct((length, LANES), bf16)]...  2.41 us
    ppermute x6, waiting for transfers between devices, swap(): lax.ppermute(array, 'seq', [(rank, rank ^ step) for rank in range(ranks)])  2.36 us
    ppermute x1, starting transfers between devices, on_device_heads(): lax.ppermute(own_taps, 'dp', [(one, (one + shift) % copies) for one in ra...  1.56 us
    pallas_call x1, Pallas kernels, on_device_heads(): pl.pallas_call(functools.partial(mask_kernel, ranks, length), out_shape=[...  1.32 us
  transfers between devices with their start and end apart: 10, of which 3 were waited for; matrix products, arithmetic and copies ran while one was open for 0% of the time, Pallas kernels for 17%

profile of v12, /device:TPU:0, one launch (start us, length us, event | category | flops | bytes accessed | tf_op | source)
XLA Modules:
  0.0 36.6 jit_solution(14859567962378117479)
XLA Ops:
  0.6 0.0 copy-start.2
  0.6 0.0 copy-start.1
  0.7 0.0 copy-start
  0.7 1.0 %pack.1 = (bf16[3,128,128]{2,1,0:T(8,128)(2,1)S(1)}, bf16[3,128,128]{2,1,0:T(8,128)(2,1)S(1)}, bf16[3,128,128]{2,1,0:T(8,128)(2,1)S(1)}) custom-call(bf16[1,128,512]{2,1,0:T(8,128)(2,1)} %q_ref.3, bf16[1,128,512]{2,1,0:T(8,128)(2,1)} %k_ref.3, bf16[1,128,512]{2,1,0:T(8,128)(2,1)} %v_ref.3), custom_call_target="tpu_custom_call" | custom-call | tf_op jit(solution)/shard_map/pack/pallas_call | solution.py:521
  1.7 5.1 %collective-permute-start.3 = (bf16[3,128,128]{2,1,0:T(8,128)(2,1)S(1)}, bf16[3,128,128]{2,1,0:T(8,128)(2,1)S(1)}, u32[]{:S(2)}, u32[]{:S(2)}) collective-permute-start(bf16[3,128,128]{2,1,0:T(8,128)(2,1)S(1)} %get-tuple-element.36), channel_id=1, source_target_pairs={{0,6},{2,4},{4,2},{6,0},{1,7},{3,5},{5,3},{7,1},{8,14},{10,12},{12... | collective-permute-start | bytes 294920 | tf_op jit(solution)/shard_map/ppermute | solution.py:532
  6.8 0.0 copy-start.4
  6.8 0.0 collective-permute-start.4
  6.8 0.6 %collective-permute-start.5 = (bf16[3,128,128]{2,1,0:T(8,128)(2,1)S(1)}, bf16[3,128,128]{2,1,0:T(8,128)(2,1)S(1)}, u32[]{:S(2)}, u32[]{:S(2)}) collective-permute-start(bf16[3,128,128]{2,1,0:T(8,128)(2,1)S(1)} %get-tuple-element.38), channel_id=1, source_target_pairs={{0,2},{2,0},{4,6},{6,4},{1,3},{3,1},{5,7},{7,5},{8,10},{10,8},{12,... | collective-permute-start | bytes 294920 | tf_op jit(solution)/shard_map/ppermute | solution.py:532
  7.5 0.0 copy-done.2
  7.5 0.0 copy-done.1
  7.5 0.0 copy-done
  7.5 0.0 copy-done.4
  7.5 0.0 copy-start.3
  7.5 0.9 %copy-done.3 = bf16[1,128,512]{2,1,0:T(8,128)(2,1)S(1)} copy-done((bf16[1,128,512]{2,1,0:T(8,128)(2,1)S(1)}, bf16[1,128,512]{2,1,0:T(8,128)(2,1)}, u32[]{:S(2)}) %copy-start.3) | copy-done | bytes 131096
  8.4 0.0 copy-start.5
  8.4 1.3 %masks.1 = (bf16[128,128]{1,0:T(8,128)(2,1)S(1)}, bf16[128,128]{1,0:T(8,128)(2,1)S(1)}, bf16[128,128]{1,0:T(8,128)(2,1)S(1)}, bf16[4,128,128]{2,1,0:T(8,128)(2,1...) custom-call(s32[1,16]{1,0:T(1,128)S(1)} %copy-done.4, ...), custom_call_target="tpu_custom_call" | custom-call | flops 4194304 | bytes 1048576 | tf_op jit(solution)/shard_map/masks/pallas_call | solution.py:537
  9.7 3.8 %collective-permute-start = (bf16[128,128]{1,0:T(8,128)(2,1)S(1)}, bf16[128,128]{1,0:T(8,128)(2,1)S(1)}, u32[]{:S(2)}, u32[]{:S(2)}) collective-permute-start(bf16[128,128]{1,0:T(8,128)(2,1)S(1)} %get-tuple-element.32), channel_id=1, source_target_pairs={{0,6},{2,4},{4,2},{6,0},{1,7},{3,5},{5,3},{7,1},{8,14},{10,12},{12... | collective-permute-start | bytes 98312 | tf_op jit(solution)/shard_map/ppermute | solution.py:532
  13.5 0.0 collective-permute-start.1
  13.5 0.0 collective-permute-done.3.refs_0_
  13.5 1.3 %collective-permute-start.2 = (bf16[128,128]{1,0:T(8,128)(2,1)S(1)}, bf16[128,128]{1,0:T(8,128)(2,1)S(1)}, u32[]{:S(2)}, u32[]{:S(2)}) collective-permute-start(bf16[128,128]{1,0:T(8,128)(2,1)S(1)} %get-tuple-element.34), channel_id=1, source_target_pairs={{0,2},{2,0},{4,6},{6,4},{1,3},{3,1},{5,7},{7,5},{8,10},{10,8},{12,... | collective-permute-start | bytes 98312 | tf_op jit(solution)/shard_map/ppermute | solution.py:532
  14.9 2.3 %collective-permute-done.4.refs_1_ = bf16[3,128,128]{2,1,0:T(8,128)(2,1)S(1)} collective-permute-done((bf16[3,128,128]{2,1,0:T(8,128)(2,1)S(1)}, bf16[3,128,128]{2,1,0:T(8,128)(2,1)S(1)}, u32[]{:S(2)}, u32[]{:S(2)}) %collective-permute-start.4) | collective-permute-done | bytes 98336 | tf_op jit(solution)/shard_map/ppermute | solution.py:532
  17.2 0.0 collective-permute-done.5.refs_2_
  17.2 0.0 copy-done.5
  17.2 2.6 %forward.1 = (bf16[2,512,512]{2,1,0:T(8,128)(2,1)S(1)}, f32[544,128]{1,0:T(8,128)S(1)}, f32[512,128]{1,0:T(8,128)S(1)}, bf16[2,512,128]{2,1,0:T(8,128)(2,1)S(1)}...) custom-call(bf16[3,128,128]{2,1,0:T(8,128)(2,1)S(1)} %collective-permute-done.3.refs_0_, ...), custom_call_target="tpu_custom_call" | custom-call | flops 419430400 | bytes 3145728 | tf_op jit(solution)/shard_map/forward/pallas_call | solution.py:556
  19.8 0.0 collective-permute-done.refs_0_
  19.8 0.0 collective-permute-done.1.refs_1_
  19.8 0.0 collective-permute-done.2.refs_2_
  19.8 1.2 %taps.1 = (bf16[512,128]{1,0:T(8,128)(2,1)S(1)}, f32[544,128]{1,0:T(8,128)S(1)}, f32[32,128]{1,0:T(8,128)S(1)}) custom-call(bf16[128,128]{1,0:T(8,128)(2,1)S(1)} %collective-permute-done.refs_0_, bf16[128,128]{1,0:T(8,128)(2,1)S(1)} %collective-permute-done.1.refs_1_, bf16[128,128]{1,0:T(8,128)(2,1)S(1)} %collective-permute-done.2.refs_2_, ...), custom_call_target="tpu_custom_call" | custom-call | flops 419430400 | bytes 3145728 | tf_op jit(solution)/shard_map/taps/pallas_call | solution.py:580
  21.1 1.6 %collective-permute-start.6 = (f32[32,128]{1,0:T(8,128)S(1)}, f32[32,128]{1,0:T(8,128)S(1)}, u32[]{:S(2)}, u32[]{:S(2)}) collective-permute-start(f32[32,128]{1,0:T(8,128)S(1)} %get-tuple-element.54.refs_4_), channel_id=1, source_target_pairs={{0,8},{8,0},{1,9},{9,1},{2,10},{10,2},{3,11},{11,3},{4,12},{12,4},... | collective-permute-start | bytes 49160 | tf_op jit(solution)/shard_map/ppermute | solution.py:597
  22.7 2.4 %backward.1 = (bf16[512,128]{1,0:T(8,128)(2,1)S(1)}, bf16[512,128]{1,0:T(8,128)(2,1)S(1)}, bf16[512,128]{1,0:T(8,128)(2,1)S(1)}) custom-call(bf16[2,512,512]{2,1,0:T(8,128)(2,1)S(1)} %get-tuple-element.46.soft_ref, f32[544,128]{1,0:T(8,128)S(1)} %get-tuple-element.43.refs_4_.att_ref, f32[544,128]{1,0:T(8,128)S(1)} %get-tuple-element.47.grad_pad, ...), custom_call_target="tpu_custom_call" | custom-call | flops 838860800 | bytes 3145728 | tf_op jit(solution)/shard_map/backward/pallas_call | solution.py:601
  25.1 0.0 collective-permute-done.6.refs_5_
  25.1 0.1 collective-permute-start.9
  25.2 3.1 %collective-permute-start.7 = (bf16[544,128]{1,0:T(8,128)(2,1)S(1)}, bf16[544,128]{1,0:T(8,128)(2,1)S(1)}, u32[]{:S(2)}, u32[]{:S(2)}) collective-permute-start(bf16[544,128]{1,0:T(8,128)(2,1)S(1)} %get-tuple-element.55), channel_id=1, source_target_pairs={{0,4},{1,7},{2,6},{3,5},{4,0},{5,3},{6,2},{7,1},{8,12},{9,15},{10,... | collective-permute-start | bytes 417800 | tf_op jit(solution)/shard_map/ppermute | solution.py:636
  28.4 1.3 %collective-permute-start.8 = (bf16[544,128]{1,0:T(8,128)(2,1)S(1)}, bf16[544,128]{1,0:T(8,128)(2,1)S(1)}, u32[]{:S(2)}, u32[]{:S(2)}) collective-permute-start(bf16[544,128]{1,0:T(8,128)(2,1)S(1)} %get-tuple-element.56), channel_id=1, source_target_pairs={{0,6},{1,3},{2,4},{3,1},{4,2},{5,7},{6,0},{7,5},{8,14},{9,11},{10,... | collective-permute-start | bytes 417800 | tf_op jit(solution)/shard_map/ppermute | solution.py:636
  29.7 4.1 %collective-permute-done.9.refs_2_ = bf16[544,128]{1,0:T(8,128)(2,1)S(1)} collective-permute-done((bf16[544,128]{1,0:T(8,128)(2,1)S(1)}, bf16[544,128]{1,0:T(8,128)(2,1)S(1)}, u32[]{:S(2)}, u32[]{:S(2)}) %collective-permute-start.9) | collective-permute-done | bytes 139296 | tf_op jit(solution)/shard_map/ppermute | solution.py:636
  33.8 1.9 %collective-permute-done.7.refs_0_ = bf16[544,128]{1,0:T(8,128)(2,1)S(1)} collective-permute-done((bf16[544,128]{1,0:T(8,128)(2,1)S(1)}, bf16[544,128]{1,0:T(8,128)(2,1)S(1)}, u32[]{:S(2)}, u32[]{:S(2)}) %collective-permute-start.7) | collective-permute-done | bytes 139296 | tf_op jit(solution)/shard_map/ppermute | solution.py:636
  35.7 0.0 collective-permute-done.8.refs_1_
  35.7 0.9 %spread.1 = (bf16[1,128,512]{2,1,0:T(8,128)(2,1)}, bf16[1,128,512]{2,1,0:T(8,128)(2,1)}, bf16[1,128,512]{2,1,0:T(8,128)(2,1)}, bf16[1,128,512]{2,1,0:T(8,128)(2,1)}, f32[31,512]{1,0:T(8,128)}) custom-call(bf16[544,128]{1,0:T(8,128)(2,1)S(1)} %collective-permute-done.7.refs_0_, bf16[544,128]{1,0:T(8,128)(2,1)S(1)} %collective-permute-done.8.refs_1_, ...), custom_call_target="tpu_custom_call" | custom-call | tf_op jit(solution)/shard_map/spread/pallas_call | solution.py:644
  (2 shorter events, 0.1 us)
Async XLA Ops:
  0.6 6.8 %copy-start.2 = (bf16[1,128,512]{2,1,0:T(8,128)(2,1)S(1)}, bf16[1,128,512]{2,1,0:T(8,128)(2,1)}, u32[]{:S(2)}) copy-start(bf16[1,128,512]{2,1,0:T(8,128)(2,1)} %v_ref.3) | copy-start | bytes 393220
  0.6 6.8 %copy-start.1 = (bf16[1,128,512]{2,1,0:T(8,128)(2,1)S(1)}, bf16[1,128,512]{2,1,0:T(8,128)(2,1)}, u32[]{:S(2)}) copy-start(bf16[1,128,512]{2,1,0:T(8,128)(2,1)} %k_ref.3) | copy-start | bytes 393220
  0.7 6.8 %copy-start = (bf16[1,128,512]{2,1,0:T(8,128)(2,1)S(1)}, bf16[1,128,512]{2,1,0:T(8,128)(2,1)}, u32[]{:S(2)}) copy-start(bf16[1,128,512]{2,1,0:T(8,128)(2,1)} %q_ref.3) | copy-start | bytes 393220
  1.7 11.8 %collective-permute-start.3 = (bf16[3,128,128]{2,1,0:T(8,128)(2,1)S(1)}, bf16[3,128,128]{2,1,0:T(8,128)(2,1)S(1)}, u32[]{:S(2)}, u32[]{:S(2)}) collective-permute-start(bf16[3,128,128]{2,1,0:T(8,128)(2,1)S(1)} %get-tuple-element.36), channel_id=1, source_target_pairs={{0,6},{2,4},{4,2},{6,0},{1,7},{3,5},{5,3},{7,1},{8,14},{10,12},{12... | collective-permute-start | bytes 294920 | tf_op jit(solution)/shard_map/ppermute | solution.py:532
  6.8 0.7 %copy-start.4 = (s32[1,16]{1,0:T(1,128)S(1)}, s32[1,16]{1,0:T(1,128)}, u32[]{:S(2)}) copy-start(s32[1,16]{1,0:T(1,128)} %lens_ref.1) | copy-start | bytes 196
  6.8 10.4 %collective-permute-start.4 = (bf16[3,128,128]{2,1,0:T(8,128)(2,1)S(1)}, bf16[3,128,128]{2,1,0:T(8,128)(2,1)S(1)}, u32[]{:S(2)}, u32[]{:S(2)}) collective-permute-start(bf16[3,128,128]{2,1,0:T(8,128)(2,1)S(1)} %get-tuple-element.37), channel_id=1, source_target_pairs={{0,4},{2,6},{4,0},{6,2},{1,5},{3,7},{5,1},{7,3},{8,12},{10,14},{12... | collective-permute-start | bytes 294920 | tf_op jit(solution)/shard_map/ppermute | solution.py:532
  6.8 10.4 %collective-permute-start.5 = (bf16[3,128,128]{2,1,0:T(8,128)(2,1)S(1)}, bf16[3,128,128]{2,1,0:T(8,128)(2,1)S(1)}, u32[]{:S(2)}, u32[]{:S(2)}) collective-permute-start(bf16[3,128,128]{2,1,0:T(8,128)(2,1)S(1)} %get-tuple-element.38), channel_id=1, source_target_pairs={{0,2},{2,0},{4,6},{6,4},{1,3},{3,1},{5,7},{7,5},{8,10},{10,8},{12,... | collective-permute-start | bytes 294920 | tf_op jit(solution)/shard_map/ppermute | solution.py:532
  7.5 0.9 %copy-start.3 = (bf16[1,128,512]{2,1,0:T(8,128)(2,1)S(1)}, bf16[1,128,512]{2,1,0:T(8,128)(2,1)}, u32[]{:S(2)}) copy-start(bf16[1,128,512]{2,1,0:T(8,128)(2,1)} %c_ref.1) | copy-start | bytes 393220
  8.4 8.8 %copy-start.5 = (f32[31,512]{1,0:T(8,128)S(1)}, f32[31,512]{1,0:T(8,128)}, u32[]{:S(2)}) copy-start(f32[31,512]{1,0:T(8,128)} %w_ref.1) | copy-start | bytes 190468
  9.7 10.1 %collective-permute-start = (bf16[128,128]{1,0:T(8,128)(2,1)S(1)}, bf16[128,128]{1,0:T(8,128)(2,1)S(1)}, u32[]{:S(2)}, u32[]{:S(2)}) collective-permute-start(bf16[128,128]{1,0:T(8,128)(2,1)S(1)} %get-tuple-element.32), channel_id=1, source_target_pairs={{0,6},{2,4},{4,2},{6,0},{1,7},{3,5},{5,3},{7,1},{8,14},{10,12},{12... | collective-permute-start | bytes 98312 | tf_op jit(solution)/shard_map/ppermute | solution.py:532
  13.5 6.3 %collective-permute-start.1 = (bf16[128,128]{1,0:T(8,128)(2,1)S(1)}, bf16[128,128]{1,0:T(8,128)(2,1)S(1)}, u32[]{:S(2)}, u32[]{:S(2)}) collective-permute-start(bf16[128,128]{1,0:T(8,128)(2,1)S(1)} %get-tuple-element.33), channel_id=1, source_target_pairs={{0,4},{2,6},{4,0},{6,2},{1,5},{3,7},{5,1},{7,3},{8,12},{10,14},{12... | collective-permute-start | bytes 98312 | tf_op jit(solution)/shard_map/ppermute | solution.py:532
  13.5 6.3 %collective-permute-start.2 = (bf16[128,128]{1,0:T(8,128)(2,1)S(1)}, bf16[128,128]{1,0:T(8,128)(2,1)S(1)}, u32[]{:S(2)}, u32[]{:S(2)}) collective-permute-start(bf16[128,128]{1,0:T(8,128)(2,1)S(1)} %get-tuple-element.34), channel_id=1, source_target_pairs={{0,2},{2,0},{4,6},{6,4},{1,3},{3,1},{5,7},{7,5},{8,10},{10,8},{12,... | collective-permute-start | bytes 98312 | tf_op jit(solution)/shard_map/ppermute | solution.py:532
  21.1 4.0 %collective-permute-start.6 = (f32[32,128]{1,0:T(8,128)S(1)}, f32[32,128]{1,0:T(8,128)S(1)}, u32[]{:S(2)}, u32[]{:S(2)}) collective-permute-start(f32[32,128]{1,0:T(8,128)S(1)} %get-tuple-element.54.refs_4_), channel_id=1, source_target_pairs={{0,8},{8,0},{1,9},{9,1},{2,10},{10,2},{3,11},{11,3},{4,12},{12,4},... | collective-permute-start | bytes 49160 | tf_op jit(solution)/shard_map/ppermute | solution.py:597
  25.1 8.7 %collective-permute-start.9 = (bf16[544,128]{1,0:T(8,128)(2,1)S(1)}, bf16[544,128]{1,0:T(8,128)(2,1)S(1)}, u32[]{:S(2)}, u32[]{:S(2)}) collective-permute-start(bf16[544,128]{1,0:T(8,128)(2,1)S(1)} %get-tuple-element.57), channel_id=1, source_target_pairs={{0,2},{1,5},{2,0},{3,7},{4,6},{5,1},{6,4},{7,3},{8,10},{9,13},{10,... | collective-permute-start | bytes 417800 | tf_op jit(solution)/shard_map/ppermute | solution.py:636
  25.2 10.5 %collective-permute-start.7 = (bf16[544,128]{1,0:T(8,128)(2,1)S(1)}, bf16[544,128]{1,0:T(8,128)(2,1)S(1)}, u32[]{:S(2)}, u32[]{:S(2)}) collective-permute-start(bf16[544,128]{1,0:T(8,128)(2,1)S(1)} %get-tuple-element.55), channel_id=1, source_target_pairs={{0,4},{1,7},{2,6},{3,5},{4,0},{5,3},{6,2},{7,1},{8,12},{9,15},{10,... | collective-permute-start | bytes 417800 | tf_op jit(solution)/shard_map/ppermute | solution.py:636
  28.4 7.4 %collective-permute-start.8 = (bf16[544,128]{1,0:T(8,128)(2,1)S(1)}, bf16[544,128]{1,0:T(8,128)(2,1)S(1)}, u32[]{:S(2)}, u32[]{:S(2)}) collective-permute-start(bf16[544,128]{1,0:T(8,128)(2,1)S(1)} %get-tuple-element.56), channel_id=1, source_target_pairs={{0,6},{1,3},{2,4},{3,1},{4,2},{5,7},{6,0},{7,5},{8,14},{9,11},{10,... | collective-permute-start | bytes 417800 | tf_op jit(solution)/shard_map/ppermute | solution.py:636

commit v13 on v12

--- a/solution.py
+++ b/solution.py
@@ -636,10 +636,8 @@
         return lax.ppermute(array, ("seq", "mp"), pairs)
 
     order = turns(ranks)
-    first, last = order[: ranks // 2], order[ranks // 2 :]
-    far = blocks_of(first)
-    *near, kept = blocks_of(last + [(0, 0)])
-    back = [exchange(block, turn) for block, turn in zip([*far, *near], order)]
+    *sent, kept = blocks_of(order + [(0, 0)])
+    back = [exchange(block, turn) for block, turn in zip(sent, order)]
 
     return pl.pallas_call(
         functools.partial(spread_kernel, order + [(0, 0)], frames),

time: 36.8 us -> 36.9 us (level)
  waiting for transfers between devices: 8.43 us -> 9.45 us
  starting transfers between devices: 16.9 us -> 16 us
    ppermute x3, waiting for transfers between devices: 6.08 us -> 7.09 us  [exchange(): return lax.ppermute(array, ('seq', 'mp'), pairs)]
    ppermute x3, starting transfers between devices: 4.49 us -> 3.55 us  [exchange(): return lax.ppermute(array, ('seq', 'mp'), pairs)]
  transfers between devices with their start and end apart: 10 -> 10, of which waited for: 3 -> 2; matrix products, arithmetic and copies ran while one was open for 0% -> 0% of each run, Pallas kernels for 17% -> 17%
where the time goes in v13:
time: 36.9 us; the launch traced here: 36.7 us
  starting transfers between devices  16 us (43%)
  Pallas kernels  9.57 us (26%)
  waiting for transfers between devices  9.45 us (26%)
  local copies, waits for them, and re-layouts  0.92 us (2%)
  between operations  0.76 us (2%)
    ppermute x6, starting transfers between devices, swap(): lax.ppermute(array, 'seq', [(rank, rank ^ step) for rank in range(ranks)])  10.9 us
    ppermute x3, waiting for transfers between devices, exchange(): return lax.ppermute(array, ('seq', 'mp'), pairs)  7.09 us
    ppermute x3, starting transfers between devices, exchange(): return lax.ppermute(array, ('seq', 'mp'), pairs)  3.55 us
    pallas_call x1, Pallas kernels, on_device_heads(): pl.pallas_call(functools.partial(forward_kernel, ranks, frames), out_shap...  2.6 us
    pallas_call x1, Pallas kernels, on_device_heads(): pl.pallas_call(backward_kernel, out_shape=[struct((length, LANES), bf16)]...  2.41 us
    ppermute x6, waiting for transfers between devices, swap(): lax.ppermute(array, 'seq', [(rank, rank ^ step) for rank in range(ranks)])  2.36 us
    ppermute x1, starting transfers between devices, on_device_heads(): lax.ppermute(own_taps, 'dp', [(one, (one + shift) % copies) for one in ra...  1.56 us
    pallas_call x1, Pallas kernels, on_device_heads(): pl.pallas_call(functools.partial(mask_kernel, ranks, length), out_shape=[...  1.32 us
  transfers between devices with their start and end apart: 10, of which 2 were waited for; matrix products, arithmetic and copies ran while one was open for 0% of the time, Pallas kernels for 17%

profile of v13, /device:TPU:0, one launch (start us, length us, event | category | flops | bytes accessed | tf_op | source)
XLA Modules:
  0.0 36.7 jit_solution(884274567750340478)
XLA Ops:
  0.6 0.0 copy-start.2
  0.6 0.0 copy-start.1
  0.7 0.0 copy-start
  0.7 1.0 %pack.1 = (bf16[3,128,128]{2,1,0:T(8,128)(2,1)S(1)}, bf16[3,128,128]{2,1,0:T(8,128)(2,1)S(1)}, bf16[3,128,128]{2,1,0:T(8,128)(2,1)S(1)}) custom-call(bf16[1,128,512]{2,1,0:T(8,128)(2,1)} %q_ref.3, bf16[1,128,512]{2,1,0:T(8,128)(2,1)} %k_ref.3, bf16[1,128,512]{2,1,0:T(8,128)(2,1)} %v_ref.3), custom_call_target="tpu_custom_call" | custom-call | tf_op jit(solution)/shard_map/pack/pallas_call | solution.py:521
  1.7 5.1 %collective-permute-start.3 = (bf16[3,128,128]{2,1,0:T(8,128)(2,1)S(1)}, bf16[3,128,128]{2,1,0:T(8,128)(2,1)S(1)}, u32[]{:S(2)}, u32[]{:S(2)}) collective-permute-start(bf16[3,128,128]{2,1,0:T(8,128)(2,1)S(1)} %get-tuple-element.36), channel_id=1, source_target_pairs={{0,6},{2,4},{4,2},{6,0},{1,7},{3,5},{5,3},{7,1},{8,14},{10,12},{12... | collective-permute-start | bytes 294920 | tf_op jit(solution)/shard_map/ppermute | solution.py:532
  6.8 0.0 copy-start.4
  6.8 0.0 collective-permute-start.4
  6.8 0.6 %collective-permute-start.5 = (bf16[3,128,128]{2,1,0:T(8,128)(2,1)S(1)}, bf16[3,128,128]{2,1,0:T(8,128)(2,1)S(1)}, u32[]{:S(2)}, u32[]{:S(2)}) collective-permute-start(bf16[3,128,128]{2,1,0:T(8,128)(2,1)S(1)} %get-tuple-element.38), channel_id=1, source_target_pairs={{0,2},{2,0},{4,6},{6,4},{1,3},{3,1},{5,7},{7,5},{8,10},{10,8},{12,... | collective-permute-start | bytes 294920 | tf_op jit(solution)/shard_map/ppermute | solution.py:532
  7.5 0.0 copy-done.2
  7.5 0.0 copy-done.1
  7.5 0.0 copy-done
  7.5 0.0 copy-done.4
  7.5 0.0 copy-start.3
  7.5 0.9 %copy-done.3 = bf16[1,128,512]{2,1,0:T(8,128)(2,1)S(1)} copy-done((bf16[1,128,512]{2,1,0:T(8,128)(2,1)S(1)}, bf16[1,128,512]{2,1,0:T(8,128)(2,1)}, u32[]{:S(2)}) %copy-start.3) | copy-done | bytes 131096
  8.4 0.0 copy-start.5
  8.4 1.3 %masks.1 = (bf16[128,128]{1,0:T(8,128)(2,1)S(1)}, bf16[128,128]{1,0:T(8,128)(2,1)S(1)}, bf16[128,128]{1,0:T(8,128)(2,1)S(1)}, bf16[4,128,128]{2,1,0:T(8,128)(2,1...) custom-call(s32[1,16]{1,0:T(1,128)S(1)} %copy-done.4, ...), custom_call_target="tpu_custom_call" | custom-call | flops 4194304 | bytes 1048576 | tf_op jit(solution)/shard_map/masks/pallas_call | solution.py:537
  9.7 3.8 %collective-permute-start = (bf16[128,128]{1,0:T(8,128)(2,1)S(1)}, bf16[128,128]{1,0:T(8,128)(2,1)S(1)}, u32[]{:S(2)}, u32[]{:S(2)}) collective-permute-start(bf16[128,128]{1,0:T(8,128)(2,1)S(1)} %get-tuple-element.32), channel_id=1, source_target_pairs={{0,6},{2,4},{4,2},{6,0},{1,7},{3,5},{5,3},{7,1},{8,14},{10,12},{12... | collective-permute-start | bytes 98312 | tf_op jit(solution)/shard_map/ppermute | solution.py:532
  13.5 0.0 collective-permute-start.1
  13.5 0.0 collective-permute-done.3.refs_0_
  13.5 1.3 %collective-permute-start.2 = (bf16[128,128]{1,0:T(8,128)(2,1)S(1)}, bf16[128,128]{1,0:T(8,128)(2,1)S(1)}, u32[]{:S(2)}, u32[]{:S(2)}) collective-permute-start(bf16[128,128]{1,0:T(8,128)(2,1)S(1)} %get-tuple-element.34), channel_id=1, source_target_pairs={{0,2},{2,0},{4,6},{6,4},{1,3},{3,1},{5,7},{7,5},{8,10},{10,8},{12,... | collective-permute-start | bytes 98312 | tf_op jit(solution)/shard_map/ppermute | solution.py:532
  14.9 2.3 %collective-permute-done.4.refs_1_ = bf16[3,128,128]{2,1,0:T(8,128)(2,1)S(1)} collective-permute-done((bf16[3,128,128]{2,1,0:T(8,128)(2,1)S(1)}, bf16[3,128,128]{2,1,0:T(8,128)(2,1)S(1)}, u32[]{:S(2)}, u32[]{:S(2)}) %collective-permute-start.4) | collective-permute-done | bytes 98336 | tf_op jit(solution)/shard_map/ppermute | solution.py:532
  17.2 0.0 collective-permute-done.5.refs_2_
  17.2 0.0 copy-done.5
  17.2 2.6 %forward.1 = (bf16[2,512,512]{2,1,0:T(8,128)(2,1)S(1)}, f32[544,128]{1,0:T(8,128)S(1)}, f32[512,128]{1,0:T(8,128)S(1)}, bf16[2,512,128]{2,1,0:T(8,128)(2,1)S(1)}...) custom-call(bf16[3,128,128]{2,1,0:T(8,128)(2,1)S(1)} %collective-permute-done.3.refs_0_, ...), custom_call_target="tpu_custom_call" | custom-call | flops 419430400 | bytes 3145728 | tf_op jit(solution)/shard_map/forward/pallas_call | solution.py:556
  19.8 0.0 collective-permute-done.refs_0_
  19.8 0.0 collective-permute-done.1.refs_1_
  19.8 0.0 collective-permute-done.2.refs_2_
  19.8 1.2 %taps.1 = (bf16[512,128]{1,0:T(8,128)(2,1)S(1)}, f32[544,128]{1,0:T(8,128)S(1)}, f32[32,128]{1,0:T(8,128)S(1)}) custom-call(bf16[128,128]{1,0:T(8,128)(2,1)S(1)} %collective-permute-done.refs_0_, bf16[128,128]{1,0:T(8,128)(2,1)S(1)} %collective-permute-done.1.refs_1_, bf16[128,128]{1,0:T(8,128)(2,1)S(1)} %collective-permute-done.2.refs_2_, ...), custom_call_target="tpu_custom_call" | custom-call | flops 419430400 | bytes 3145728 | tf_op jit(solution)/shard_map/taps/pallas_call | solution.py:580
  21.1 1.6 %collective-permute-start.6 = (f32[32,128]{1,0:T(8,128)S(1)}, f32[32,128]{1,0:T(8,128)S(1)}, u32[]{:S(2)}, u32[]{:S(2)}) collective-permute-start(f32[32,128]{1,0:T(8,128)S(1)} %get-tuple-element.54.refs_4_), channel_id=1, source_target_pairs={{0,8},{8,0},{1,9},{9,1},{2,10},{10,2},{3,11},{11,3},{4,12},{12,4},... | collective-permute-start | bytes 49160 | tf_op jit(solution)/shard_map/ppermute | solution.py:597
  22.7 2.4 %backward.1 = (bf16[512,128]{1,0:T(8,128)(2,1)S(1)}, bf16[512,128]{1,0:T(8,128)(2,1)S(1)}, bf16[512,128]{1,0:T(8,128)(2,1)S(1)}) custom-call(bf16[2,512,512]{2,1,0:T(8,128)(2,1)S(1)} %get-tuple-element.46.soft_ref, f32[544,128]{1,0:T(8,128)S(1)} %get-tuple-element.43.refs_4_.att_ref, f32[544,128]{1,0:T(8,128)S(1)} %get-tuple-element.47.grad_pad, ...), custom_call_target="tpu_custom_call" | custom-call | flops 838860800 | bytes 3145728 | tf_op jit(solution)/shard_map/backward/pallas_call | solution.py:601
  25.1 0.0 collective-permute-done.6.refs_5_
  25.1 0.1 blocks.1
  25.1 0.6 %collective-permute-start.7 = (bf16[544,128]{1,0:T(8,128)(2,1)S(1)}, bf16[544,128]{1,0:T(8,128)(2,1)S(1)}, u32[]{:S(2)}, u32[]{:S(2)}) collective-permute-start(bf16[544,128]{1,0:T(8,128)(2,1)S(1)} %get-tuple-element.55), channel_id=1, source_target_pairs={{0,4},{1,7},{2,6},{3,5},{4,0},{5,3},{6,2},{7,1},{8,12},{9,15},{10,... | collective-permute-start | bytes 417800 | tf_op jit(solution)/shard_map/ppermute | solution.py:636
  25.7 2.1 %collective-permute-start.8 = (bf16[544,128]{1,0:T(8,128)(2,1)S(1)}, bf16[544,128]{1,0:T(8,128)(2,1)S(1)}, u32[]{:S(2)}, u32[]{:S(2)}) collective-permute-start(bf16[544,128]{1,0:T(8,128)(2,1)S(1)} %get-tuple-element.56), channel_id=1, source_target_pairs={{0,6},{1,3},{2,4},{3,1},{4,2},{5,7},{6,0},{7,5},{8,14},{9,11},{10,... | collective-permute-start | bytes 417800 | tf_op jit(solution)/shard_map/ppermute | solution.py:636
  27.8 0.9 %collective-permute-start.9 = (bf16[544,128]{1,0:T(8,128)(2,1)S(1)}, bf16[544,128]{1,0:T(8,128)(2,1)S(1)}, u32[]{:S(2)}, u32[]{:S(2)}) collective-permute-start(bf16[544,128]{1,0:T(8,128)(2,1)S(1)} %get-tuple-element.57), channel_id=1, source_target_pairs={{0,2},{1,5},{2,0},{3,7},{4,6},{5,1},{6,4},{7,3},{8,10},{9,13},{10,... | collective-permute-start | bytes 417800 | tf_op jit(solution)/shard_map/ppermute | solution.py:636
  28.7 7.1 %collective-permute-done.7.refs_0_ = bf16[544,128]{1,0:T(8,128)(2,1)S(1)} collective-permute-done((bf16[544,128]{1,0:T(8,128)(2,1)S(1)}, bf16[544,128]{1,0:T(8,128)(2,1)S(1)}, u32[]{:S(2)}, u32[]{:S(2)}) %collective-permute-start.7) | collective-permute-done | bytes 139296 | tf_op jit(solution)/shard_map/ppermute | solution.py:636
  35.8 0.0 collective-permute-done.8.refs_1_
  35.8 0.0 collective-permute-done.9.refs_2_
  35.8 0.9 %spread.1 = (bf16[1,128,512]{2,1,0:T(8,128)(2,1)}, bf16[1,128,512]{2,1,0:T(8,128)(2,1)}, bf16[1,128,512]{2,1,0:T(8,128)(2,1)}, bf16[1,128,512]{2,1,0:T(8,128)(2,1)}, f32[31,512]{1,0:T(8,128)}) custom-call(bf16[544,128]{1,0:T(8,128)(2,1)S(1)} %collective-permute-done.7.refs_0_, bf16[544,128]{1,0:T(8,128)(2,1)S(1)} %collective-permute-done.8.refs_1_, ...), custom_call_target="tpu_custom_call" | custom-call | tf_op jit(solution)/shard_map/spread/pallas_call | solution.py:642
Async XLA Ops:
  0.6 6.8 %copy-start.2 = (bf16[1,128,512]{2,1,0:T(8,128)(2,1)S(1)}, bf16[1,128,512]{2,1,0:T(8,128)(2,1)}, u32[]{:S(2)}) copy-start(bf16[1,128,512]{2,1,0:T(8,128)(2,1)} %v_ref.3) | copy-start | bytes 393220
  0.6 6.8 %copy-start.1 = (bf16[1,128,512]{2,1,0:T(8,128)(2,1)S(1)}, bf16[1,128,512]{2,1,0:T(8,128)(2,1)}, u32[]{:S(2)}) copy-start(bf16[1,128,512]{2,1,0:T(8,128)(2,1)} %k_ref.3) | copy-start | bytes 393220
  0.7 6.8 %copy-start = (bf16[1,128,512]{2,1,0:T(8,128)(2,1)S(1)}, bf16[1,128,512]{2,1,0:T(8,128)(2,1)}, u32[]{:S(2)}) copy-start(bf16[1,128,512]{2,1,0:T(8,128)(2,1)} %q_ref.3) | copy-start | bytes 393220
  1.7 11.8 %collective-permute-start.3 = (bf16[3,128,128]{2,1,0:T(8,128)(2,1)S(1)}, bf16[3,128,128]{2,1,0:T(8,128)(2,1)S(1)}, u32[]{:S(2)}, u32[]{:S(2)}) collective-permute-start(bf16[3,128,128]{2,1,0:T(8,128)(2,1)S(1)} %get-tuple-element.36), channel_id=1, source_target_pairs={{0,6},{2,4},{4,2},{6,0},{1,7},{3,5},{5,3},{7,1},{8,14},{10,12},{12... | collective-permute-start | bytes 294920 | tf_op jit(solution)/shard_map/ppermute | solution.py:532
  6.8 0.7 %copy-start.4 = (s32[1,16]{1,0:T(1,128)S(1)}, s32[1,16]{1,0:T(1,128)}, u32[]{:S(2)}) copy-start(s32[1,16]{1,0:T(1,128)} %lens_ref.1) | copy-start | bytes 196
  6.8 10.4 %collective-permute-start.4 = (bf16[3,128,128]{2,1,0:T(8,128)(2,1)S(1)}, bf16[3,128,128]{2,1,0:T(8,128)(2,1)S(1)}, u32[]{:S(2)}, u32[]{:S(2)}) collective-permute-start(bf16[3,128,128]{2,1,0:T(8,128)(2,1)S(1)} %get-tuple-element.37), channel_id=1, source_target_pairs={{0,4},{2,6},{4,0},{6,2},{1,5},{3,7},{5,1},{7,3},{8,12},{10,14},{12... | collective-permute-start | bytes 294920 | tf_op jit(solution)/shard_map/ppermute | solution.py:532
  6.8 10.4 %collective-permute-start.5 = (bf16[3,128,128]{2,1,0:T(8,128)(2,1)S(1)}, bf16[3,128,128]{2,1,0:T(8,128)(2,1)S(1)}, u32[]{:S(2)}, u32[]{:S(2)}) collective-permute-start(bf16[3,128,128]{2,1,0:T(8,128)(2,1)S(1)} %get-tuple-element.38), channel_id=1, source_target_pairs={{0,2},{2,0},{4,6},{6,4},{1,3},{3,1},{5,7},{7,5},{8,10},{10,8},{12,... | collective-permute-start | bytes 294920 | tf_op jit(solution)/shard_map/ppermute | solution.py:532
  7.5 0.9 %copy-start.3 = (bf16[1,128,512]{2,1,0:T(8,128)(2,1)S(1)}, bf16[1,128,512]{2,1,0:T(8,128)(2,1)}, u32[]{:S(2)}) copy-start(bf16[1,128,512]{2,1,0:T(8,128)(2,1)} %c_ref.1) | copy-start | bytes 393220
  8.4 8.8 %copy-start.5 = (f32[31,512]{1,0:T(8,128)S(1)}, f32[31,512]{1,0:T(8,128)}, u32[]{:S(2)}) copy-start(f32[31,512]{1,0:T(8,128)} %w_ref.1) | copy-start | bytes 190468
  9.7 10.1 %collective-permute-start = (bf16[128,128]{1,0:T(8,128)(2,1)S(1)}, bf16[128,128]{1,0:T(8,128)(2,1)S(1)}, u32[]{:S(2)}, u32[]{:S(2)}) collective-permute-start(bf16[128,128]{1,0:T(8,128)(2,1)S(1)} %get-tuple-element.32), channel_id=1, source_target_pairs={{0,6},{2,4},{4,2},{6,0},{1,7},{3,5},{5,3},{7,1},{8,14},{10,12},{12... | collective-permute-start | bytes 98312 | tf_op jit(solution)/shard_map/ppermute | solution.py:532
  13.5 6.3 %collective-permute-start.1 = (bf16[128,128]{1,0:T(8,128)(2,1)S(1)}, bf16[128,128]{1,0:T(8,128)(2,1)S(1)}, u32[]{:S(2)}, u32[]{:S(2)}) collective-permute-start(bf16[128,128]{1,0:T(8,128)(2,1)S(1)} %get-tuple-element.33), channel_id=1, source_target_pairs={{0,4},{2,6},{4,0},{6,2},{1,5},{3,7},{5,1},{7,3},{8,12},{10,14},{12... | collective-permute-start | bytes 98312 | tf_op jit(solution)/shard_map/ppermute | solution.py:532
  13.5 6.3 %collective-permute-start.2 = (bf16[128,128]{1,0:T(8,128)(2,1)S(1)}, bf16[128,128]{1,0:T(8,128)(2,1)S(1)}, u32[]{:S(2)}, u32[]{:S(2)}) collective-permute-start(bf16[128,128]{1,0:T(8,128)(2,1)S(1)} %get-tuple-element.34), channel_id=1, source_target_pairs={{0,2},{2,0},{4,6},{6,4},{1,3},{3,1},{5,7},{7,5},{8,10},{10,8},{12,... | collective-permute-start | bytes 98312 | tf_op jit(solution)/shard_map/ppermute | solution.py:532
  21.1 4.0 %collective-permute-start.6 = (f32[32,128]{1,0:T(8,128)S(1)}, f32[32,128]{1,0:T(8,128)S(1)}, u32[]{:S(2)}, u32[]{:S(2)}) collective-permute-start(f32[32,128]{1,0:T(8,128)S(1)} %get-tuple-element.54.refs_4_), channel_id=1, source_target_pairs={{0,8},{8,0},{1,9},{9,1},{2,10},{10,2},{3,11},{11,3},{4,12},{12,4},... | collective-permute-start | bytes 49160 | tf_op jit(solution)/shard_map/ppermute | solution.py:597
  25.1 10.6 %collective-permute-start.7 = (bf16[544,128]{1,0:T(8,128)(2,1)S(1)}, bf16[544,128]{1,0:T(8,128)(2,1)S(1)}, u32[]{:S(2)}, u32[]{:S(2)}) collective-permute-start(bf16[544,128]{1,0:T(8,128)(2,1)S(1)} %get-tuple-element.55), channel_id=1, source_target_pairs={{0,4},{1,7},{2,6},{3,5},{4,0},{5,3},{6,2},{7,1},{8,12},{9,15},{10,... | collective-permute-start | bytes 417800 | tf_op jit(solution)/shard_map/ppermute | solution.py:636
  25.7 10.1 %collective-permute-start.8 = (bf16[544,128]{1,0:T(8,128)(2,1)S(1)}, bf16[544,128]{1,0:T(8,128)(2,1)S(1)}, u32[]{:S(2)}, u32[]{:S(2)}) collective-permute-start(bf16[544,128]{1,0:T(8,128)(2,1)S(1)} %get-tuple-element.56), channel_id=1, source_target_pairs={{0,6},{1,3},{2,4},{3,1},{4,2},{5,7},{6,0},{7,5},{8,14},{9,11},{10,... | collective-permute-start | bytes 417800 | tf_op jit(solution)/shard_map/ppermute | solution.py:636
  27.8 8.0 %collective-permute-start.9 = (bf16[544,128]{1,0:T(8,128)(2,1)S(1)}, bf16[544,128]{1,0:T(8,128)(2,1)S(1)}, u32[]{:S(2)}, u32[]{:S(2)}) collective-permute-start(bf16[544,128]{1,0:T(8,128)(2,1)S(1)} %get-tuple-element.57), channel_id=1, source_target_pairs={{0,2},{1,5},{2,0},{3,7},{4,6},{5,1},{6,4},{7,3},{8,10},{9,13},{10,... | collective-permute-start | bytes 417800 | tf_op jit(solution)/shard_map/ppermute | solution.py:636

commit v14 on v10

--- a/solution.py
+++ b/solution.py
@@ -321,9 +321,9 @@
 
 def forward_kernel(ranks, frames, *refs):
     recvs = refs[: ranks - 1]
-    own_ref, col_ref, row_ref, after_ref, before_ref, w_ref = refs[ranks - 1 : ranks + 5]
-    soft_ref, att_ref, pre_ref, q_ref, k_t_ref, v_ref = refs[ranks + 5 : ranks + 11]
-    att_t_ref, k_full, q_full, w_own, w_sem = refs[ranks + 11 :]
+    own_ref, col_ref, row_ref, span_ref, w_ref = refs[ranks - 1 : ranks + 4]
+    soft_ref, att_ref, pre_ref, q_ref, k_t_ref, v_ref = refs[ranks + 4 : ranks + 10]
+    att_t_ref, k_full, q_full, w_own, w_sem = refs[ranks + 10 :]
     me = lax.axis_index("seq")
     length = ranks * frames
     copy = pltpu.make_async_copy(w_ref.at[:, lanes_at(me)], w_own, w_sem)
@@ -364,35 +364,39 @@
     def some_rows(number, carry):
         base = pl.multiple_of(number * chunk, chunk)
         rows = pl.ds(base, chunk)
-        after, before = after_ref[rows, :], before_ref[rows, :]
         total = jnp.zeros((chunk, LANES), jnp.float32)
         for tap in range(KERNEL):
-            off = tap - HALF
-            piece = att_ref[pl.ds(base + (PAD + off), chunk), :]
-            if off > 0:
-                piece = jnp.where(after >= off, piece, 0.0)
-            if off < 0:
-                piece = jnp.where(before >= -off, piece, 0.0)
-            total = total + w_own[tap : tap + 1, :] * piece
+            total = total + w_own[tap : tap + 1, :] * masked(att_ref, base, chunk, tap - HALF, span_ref)
         pre_ref[rows, :] = total
         return carry
 
     lax.fori_loop(0, length // chunk, some_rows, 0)
 
 
-def masked(source, base, chunk, off, before, after):
+def span_kernel(after_ref, before_ref, span_ref):
+    chunk = 64
+
+    def some_rows(number, carry):
+        rows = pl.ds(pl.multiple_of(number * chunk, chunk), chunk)
+        after, before = after_ref[rows, :], before_ref[rows, :]
+        for tap in range(KERNEL):
+            off = tap - HALF
+            inside = after >= off if off > 0 else before >= -off
+            span_ref[tap, rows, :] = jnp.where(inside, 1.0, 0.0)
+        return carry
+
+    lax.fori_loop(0, after_ref.shape[0] // chunk, some_rows, 0)
+
+
+def masked(source, base, chunk, off, span_ref):
     piece = source[pl.ds(base + (PAD + off), chunk), :]
-    if off > 0:
-        piece = jnp.where(after >= off, piece, 0.0)
-    if off < 0:
-        piece = jnp.where(before >= -off, piece, 0.0)
-    return piece
+    return piece * span_ref[HALF + off, pl.ds(base, chunk), :] if off else piece
 
 
 def taps_kernel(ranks, frames, *refs):
     cots = refs[: ranks - 1]
-    own_ref, att_ref, pre_ref, after_ref, before_ref = refs[ranks - 1 : ranks + 4]
-    mixed_ref, grad_pad, taps_ref, cot, tap_sum = refs[ranks + 4 :]
+    own_ref, att_ref, pre_ref, span_ref = refs[ranks - 1 : ranks + 3]
+    mixed_ref, grad_pad, taps_ref, cot, tap_sum = refs[ranks + 3 :]
     me = lax.axis_index("seq")
     length = ranks * frames
     cot[rows_at(me, frames), :] = own_ref[3]
@@ -413,9 +417,8 @@
         conv_grad = cot[rows, :].astype(jnp.float32) * gate * (1.0 + pre * (1.0 - gate))
         conv_grad = conv_grad.astype(jnp.bfloat16).astype(jnp.float32)
         grad_pad[pl.ds(base + PAD, chunk), :] = conv_grad
-        after, before = after_ref[rows, :], before_ref[rows, :]
         for tap in range(KERNEL):
-            part = conv_grad * masked(att_ref, base, chunk, tap - HALF, before, after)
+            part = conv_grad * masked(att_ref, base, chunk, tap - HALF, span_ref)
             tap_sum[tap] = tap_sum[tap] + jnp.sum(part.reshape(chunk // 8, 8, LANES), axis=0)
         return carry
 
@@ -423,7 +426,7 @@
     taps_ref[...] = jnp.sum(tap_sum[...], axis=1)
 
 
-def backward_kernel(soft_ref, att_ref, grad_pad, after_ref, before_ref, q_ref, k_t_ref, v_ref, w_ref, *refs):
+def backward_kernel(soft_ref, att_ref, grad_pad, span_ref, q_ref, k_t_ref, v_ref, w_ref, *refs):
     res_q, res_k, res_v, g_att, grad_t, w_own, w_sem = refs
     length = v_ref.shape[0]
     copy = pltpu.make_async_copy(w_ref.at[:, lanes_at(lax.axis_index("seq"))], w_own, w_sem)
@@ -434,10 +437,9 @@
     def some_rows(number, carry):
         base = pl.multiple_of(number * chunk, chunk)
         rows = pl.ds(base, chunk)
-        after, before = after_ref[rows, :], before_ref[rows, :]
         total = jnp.zeros((chunk, LANES), jnp.float32)
         for tap in range(KERNEL):
-            total = total + w_own[tap : tap + 1, :] * masked(grad_pad, base, chunk, HALF - tap, before, after)
+            total = total + w_own[tap : tap + 1, :] * masked(grad_pad, base, chunk, HALF - tap, span_ref)
         g_att[rows, :] = total.astype(jnp.bfloat16)
         return carry
 
@@ -541,6 +543,16 @@
     )(rec_lengths, queries, keys, values, cotangent)
     cots = {step: swap(cot_sends[step - 1], step) for step in order}
 
+    span = pl.pallas_call(
+        span_kernel,
+        out_shape=struct((KERNEL, length, LANES), f32),
+        in_specs=[vmem] * 2,
+        out_specs=vmem,
+        compiler_params=params,
+        cost_estimate=cost(400 * MIB, 3 * MIB),
+        name="spans",
+    )(after, before)
+
     soft, att, pre, q_heads, k_t, v_full = pl.pallas_call(
         functools.partial(forward_kernel, ranks, frames),
         out_shape=[
@@ -551,7 +563,7 @@
             struct((LANES, length), bf16),
             struct((length, LANES), bf16),
         ],
-        in_specs=[vmem] * (ranks + 4) + [anywhere],
+        in_specs=[vmem] * (ranks + 3) + [anywhere],
         out_specs=[vmem] * 6,
         scratch_shapes=[
             VMEM((LANES, length), f32),
@@ -563,7 +575,7 @@
         compiler_params=params,
         cost_estimate=cost(400 * MIB, 3 * MIB),
         name="forward",
-    )(*[received[step] for step in order], own, col, row, after, before, conv_weight)
+    )(*[received[step] for step in order], own, col, row, span, conv_weight)
 
     mixed, grad_pad, own_taps = pl.pallas_call(
         functools.partial(taps_kernel, ranks, frames),
@@ -572,13 +584,13 @@
             struct((length + 2 * PAD, LANES), f32),
             struct((taps, LANES), f32),
         ],
-        in_specs=[vmem] * (ranks + 4),
+        in_specs=[vmem] * (ranks + 3),
         out_specs=[vmem] * 3,
         scratch_shapes=[VMEM((length, LANES), bf16), VMEM((taps, 8, LANES), f32)],
         compiler_params=params,
         cost_estimate=cost(400 * MIB, 3 * MIB),
         name="taps",
-    )(*[cots[step] for step in order], own, att, pre, after, before)
+    )(*[cots[step] for step in order], own, att, pre, span)
 
     copies = lax.axis_size("dp")
     part_taps = [own_taps] + [
@@ -589,7 +601,7 @@
     results = pl.pallas_call(
         backward_kernel,
         out_shape=[struct((length, LANES), bf16)] * 3,
-        in_specs=[vmem] * 8 + [anywhere],
+        in_specs=[vmem] * 7 + [anywhere],
         out_specs=[vmem] * 3,
         scratch_shapes=[
             VMEM((length, LANES), bf16),
@@ -600,7 +612,7 @@
         compiler_params=params,
         cost_estimate=cost(800 * MIB, 3 * MIB),
         name="backward",
-    )(soft, att, grad_pad, after, before, q_heads, k_t, v_full, conv_weight)
+    )(soft, att, grad_pad, span, q_heads, k_t, v_full, conv_weight)
 
     def blocks_of(steps):
         return pl.pallas_call(

time: 36.8 us -> 39.3 us (1.068)
  local copies, waits for them, and re-layouts: 0.92 us -> 4.27 us
  starting transfers between devices: 16.1 us -> 15.4 us
    unnamed x12, local copies, waits for them, and re-layouts: 0.92 us -> 4.27 us
    ppermute x9, starting transfers between devices: 14.5 us -> 13.9 us  [swap(): lax.ppermute(array, 'seq', [(rank, rank ^ step) for rank in range(ranks)])]
    pallas_call x0 -> x1, Pallas kernels: none -> 0.56 us  [on_device_heads(): pl.pallas_call(span_kernel, out_shape=struct((KERNEL, length, LANES), f32...]
  transfers between devices with their start and end apart: 10 -> 10, of which waited for: 3 -> 2; matrix products, arithmetic and copies ran while one was open for 0% -> 0% of each run, Pallas kernels for 17% -> 17%
where the time goes in v14:
time: 39.3 us; the launch traced here: 39 us
  starting transfers between devices  15.4 us (39%)
  Pallas kernels  9.62 us (24%)
  waiting for transfers between devices  8.94 us (23%)
  local copies, waits for them, and re-layouts  4.27 us (11%)
  between operations  0.74 us (2%)
    ppermute x9, starting transfers between devices, swap(): lax.ppermute(array, 'seq', [(rank, rank ^ step) for rank in range(ranks)])  13.9 us
    ppermute x9, waiting for transfers between devices, swap(): lax.ppermute(array, 'seq', [(rank, rank ^ step) for rank in range(ranks)])  8.94 us
    unnamed x12, local copies, waits for them, and re-layouts  4.27 us
    pallas_call x1, Pallas kernels, on_device_heads(): pl.pallas_call(functools.partial(forward_kernel, ranks, frames), out_shap...  2.47 us
    pallas_call x1, Pallas kernels, on_device_heads(): pl.pallas_call(backward_kernel, out_shape=[struct((length, LANES), bf16)]...  2.28 us
    ppermute x1, starting transfers between devices, on_device_heads(): lax.ppermute(own_taps, 'dp', [(one, (one + shift) % copies) for one in ra...  1.56 us
    pallas_call x1, Pallas kernels, on_device_heads(): pl.pallas_call(functools.partial(mask_kernel, ranks, length), out_shape=[...  1.32 us
    pallas_call x1, Pallas kernels, on_device_heads(): pl.pallas_call(functools.partial(taps_kernel, ranks, frames), out_shape=[...  1.01 us
  transfers between devices with their start and end apart: 10, of which 2 were waited for; matrix products, arithmetic and copies ran while one was open for 0% of the time, Pallas kernels for 17%

profile of v14, /device:TPU:0, one launch (start us, length us, event | category | flops | bytes accessed | tf_op | source)
XLA Modules:
  0.0 39.0 jit_solution(11611435794199056011)
XLA Ops:
  0.6 0.0 copy-start.3
  0.6 1.0 %pack.1 = (bf16[3,128,128]{2,1,0:T(8,128)(2,1)S(1)}, bf16[3,128,128]{2,1,0:T(8,128)(2,1)S(1)}, bf16[3,128,128]{2,1,0:T(8,128)(2,1)S(1)}) custom-call(bf16[1,128,512]{2,1,0:T(8,128)(2,1)} %q_ref.3, bf16[1,128,512]{2,1,0:T(8,128)(2,1)} %k_ref.3, bf16[1,128,512]{2,1,0:T(8,128)(2,1)} %v_ref.3), custom_call_target="tpu_custom_call" | custom-call | tf_op jit(solution)/shard_map/pack/pallas_call | solution.py:511
  1.7 5.1 %collective-permute-start.3 = (bf16[3,128,128]{2,1,0:T(8,128)(2,1)S(1)}, bf16[3,128,128]{2,1,0:T(8,128)(2,1)S(1)}, u32[]{:S(2)}, u32[]{:S(2)}) collective-permute-start(bf16[3,128,128]{2,1,0:T(8,128)(2,1)S(1)} %get-tuple-element.36), channel_id=1, source_target_pairs={{0,6},{2,4},{4,2},{6,0},{1,7},{3,5},{5,3},{7,1},{8,14},{10,12},{12... | collective-permute-start | bytes 294920 | tf_op jit(solution)/shard_map/ppermute | solution.py:522
  6.8 0.0 collective-permute-start.4
  6.8 0.6 %collective-permute-start.5 = (bf16[3,128,128]{2,1,0:T(8,128)(2,1)S(1)}, bf16[3,128,128]{2,1,0:T(8,128)(2,1)S(1)}, u32[]{:S(2)}, u32[]{:S(2)}) collective-permute-start(bf16[3,128,128]{2,1,0:T(8,128)(2,1)S(1)} %get-tuple-element.38), channel_id=1, source_target_pairs={{0,2},{2,0},{4,6},{6,4},{1,3},{3,1},{5,7},{7,5},{8,10},{10,8},{12,... | collective-permute-start | bytes 294920 | tf_op jit(solution)/shard_map/ppermute | solution.py:522
  7.4 0.0 copy-start
  7.4 0.9 %copy-done = bf16[1,128,512]{2,1,0:T(8,128)(2,1)S(1)} copy-done((bf16[1,128,512]{2,1,0:T(8,128)(2,1)S(1)}, bf16[1,128,512]{2,1,0:T(8,128)(2,1)}, u32[]{:S(2)}) %copy-start) | copy-done | bytes 131096
  8.3 0.0 copy-start.1
  8.3 0.9 %copy-done.1 = bf16[1,128,512]{2,1,0:T(8,128)(2,1)S(1)} copy-done((bf16[1,128,512]{2,1,0:T(8,128)(2,1)S(1)}, bf16[1,128,512]{2,1,0:T(8,128)(2,1)}, u32[]{:S(2)}) %copy-start.1) | copy-done | bytes 131096
  9.2 0.0 copy-start.2
  9.2 0.9 %copy-done.2 = bf16[1,128,512]{2,1,0:T(8,128)(2,1)S(1)} copy-done((bf16[1,128,512]{2,1,0:T(8,128)(2,1)S(1)}, bf16[1,128,512]{2,1,0:T(8,128)(2,1)}, u32[]{:S(2)}) %copy-start.2) | copy-done | bytes 131096
  10.1 0.0 copy-start.4
  10.1 0.9 %copy-done.4 = bf16[1,128,512]{2,1,0:T(8,128)(2,1)S(1)} copy-done((bf16[1,128,512]{2,1,0:T(8,128)(2,1)S(1)}, bf16[1,128,512]{2,1,0:T(8,128)(2,1)}, u32[]{:S(2)}) %copy-start.4) | copy-done | bytes 131096
  11.0 0.0 copy-start.5
  11.0 0.7 %copy-done.5 = s32[1,16]{1,0:T(1,128)S(1)} copy-done((s32[1,16]{1,0:T(1,128)S(1)}, s32[1,16]{1,0:T(1,128)}, u32[]{:S(2)}) %copy-start.5) | copy-done | bytes 88
  11.7 1.3 %masks.1 = (bf16[128,128]{1,0:T(8,128)(2,1)S(1)}, bf16[128,128]{1,0:T(8,128)(2,1)S(1)}, bf16[128,128]{1,0:T(8,128)(2,1)S(1)}, bf16[4,128,128]{2,1,0:T(8,128)(2,1...) custom-call(s32[1,16]{1,0:T(1,128)S(1)} %copy-done.5, ...), custom_call_target="tpu_custom_call" | custom-call | flops 4194304 | bytes 1048576 | tf_op jit(solution)/shard_map/masks/pallas_call | solution.py:527
  13.0 3.8 %collective-permute-start = (bf16[128,128]{1,0:T(8,128)(2,1)S(1)}, bf16[128,128]{1,0:T(8,128)(2,1)S(1)}, u32[]{:S(2)}, u32[]{:S(2)}) collective-permute-start(bf16[128,128]{1,0:T(8,128)(2,1)S(1)} %get-tuple-element.32), channel_id=1, source_target_pairs={{0,6},{2,4},{4,2},{6,0},{1,7},{3,5},{5,3},{7,1},{8,14},{10,12},{12... | collective-permute-start | bytes 98312 | tf_op jit(solution)/shard_map/ppermute | solution.py:522
  16.8 0.0 collective-permute-start.1
  16.8 0.6 %spans.1.refs_6_.span_ref = f32[31,512,128]{2,1,0:T(8,128)S(1)} custom-call(s32[512,128]{1,0:T(8,128)S(1)} %get-tuple-element.41.after_ref, s32[512,128]{1,0:T(8,128)S(1)} %get-tuple-element.42.before_ref), custom_call_target="tpu_custom_call" | custom-call | flops 419430400 | bytes 3145728 | tf_op jit(solution)/shard_map/spans/pallas_call | solution.py:546
  17.4 0.0 collective-permute-done.3.refs_0_
  17.4 0.7 %collective-permute-start.2 = (bf16[128,128]{1,0:T(8,128)(2,1)S(1)}, bf16[128,128]{1,0:T(8,128)(2,1)S(1)}, u32[]{:S(2)}, u32[]{:S(2)}) collective-permute-start(bf16[128,128]{1,0:T(8,128)(2,1)S(1)} %get-tuple-element.34), channel_id=1, source_target_pairs={{0,2},{2,0},{4,6},{6,4},{1,3},{3,1},{5,7},{7,5},{8,10},{10,8},{12,... | collective-permute-start | bytes 98312 | tf_op jit(solution)/shard_map/ppermute | solution.py:522
  18.1 0.0 collective-permute-done.4.refs_1_
  18.1 0.0 collective-permute-done.5.refs_2_
  18.1 0.0 copy-done.3
  18.1 2.5 %forward.1 = (bf16[2,512,512]{2,1,0:T(8,128)(2,1)S(1)}, f32[544,128]{1,0:T(8,128)S(1)}, f32[512,128]{1,0:T(8,128)S(1)}, bf16[2,512,128]{2,1,0:T(8,128)(2,1)S(1)}...) custom-call(bf16[3,128,128]{2,1,0:T(8,128)(2,1)S(1)} %collective-permute-done.3.refs_0_, ...), custom_call_target="tpu_custom_call" | custom-call | flops 419430400 | bytes 3145728 | tf_op jit(solution)/shard_map/forward/pallas_call | solution.py:556
  20.6 0.0 collective-permute-done.refs_0_
  20.6 1.1 %collective-permute-done.1.refs_1_ = bf16[128,128]{1,0:T(8,128)(2,1)S(1)} collective-permute-done((bf16[128,128]{1,0:T(8,128)(2,1)S(1)}, bf16[128,128]{1,0:T(8,128)(2,1)S(1)}, u32[]{:S(2)}, u32[]{:S(2)}) %collective-permute-start.1) | collective-permute-done | bytes 32800 | tf_op jit(solution)/shard_map/ppermute | solution.py:522
  21.8 0.0 collective-permute-done.2.refs_2_
  21.8 1.0 %taps.1 = (bf16[512,128]{1,0:T(8,128)(2,1)S(1)}, f32[544,128]{1,0:T(8,128)S(1)}, f32[32,128]{1,0:T(8,128)S(1)}) custom-call(bf16[128,128]{1,0:T(8,128)(2,1)S(1)} %collective-permute-done.refs_0_, bf16[128,128]{1,0:T(8,128)(2,1)S(1)} %collective-permute-done.1.refs_1_, bf16[128,128]{1,0:T(8,128)(2,1)S(1)} %collective-permute-done.2.refs_2_, ...), custom_call_target="tpu_custom_call" | custom-call | flops 419430400 | bytes 3145728 | tf_op jit(solution)/shard_map/taps/pallas_call | solution.py:580
  22.8 1.6 %collective-permute-start.6 = (f32[32,128]{1,0:T(8,128)S(1)}, f32[32,128]{1,0:T(8,128)S(1)}, u32[]{:S(2)}, u32[]{:S(2)}) collective-permute-start(f32[32,128]{1,0:T(8,128)S(1)} %get-tuple-element.54.refs_4_), channel_id=1, source_target_pairs={{0,8},{8,0},{1,9},{9,1},{2,10},{10,2},{3,11},{11,3},{4,12},{12,4},... | collective-permute-start | bytes 49160 | tf_op jit(solution)/shard_map/ppermute | solution.py:597
  24.3 2.3 %backward.1 = (bf16[512,128]{1,0:T(8,128)(2,1)S(1)}, bf16[512,128]{1,0:T(8,128)(2,1)S(1)}, bf16[512,128]{1,0:T(8,128)(2,1)S(1)}) custom-call(bf16[2,512,512]{2,1,0:T(8,128)(2,1)S(1)} %get-tuple-element.46.soft_ref, f32[544,128]{1,0:T(8,128)S(1)} %get-tuple-element.43.refs_4_.att_ref, f32[544,128]{1,0:T(8,128)S(1)} %get-tuple-element.47.grad_pad, ...), custom_call_target="tpu_custom_call" | custom-call | flops 838860800 | bytes 3145728 | tf_op jit(solution)/shard_map/backward/pallas_call | solution.py:601
  26.6 0.0 collective-permute-done.6.refs_5_
  26.7 2.6 %collective-permute-start.8 = (bf16[544,128]{1,0:T(8,128)(2,1)S(1)}, bf16[544,128]{1,0:T(8,128)(2,1)S(1)}, u32[]{:S(2)}, u32[]{:S(2)}) collective-permute-start(bf16[544,128]{1,0:T(8,128)(2,1)S(1)} %get-tuple-element.57), channel_id=1, source_target_pairs={{0,4},{2,6},{4,0},{6,2},{1,5},{3,7},{5,1},{7,3},{8,12},{10,14},{12... | collective-permute-start | bytes 417800 | tf_op jit(solution)/shard_map/ppermute | solution.py:522
  29.3 0.2 collective-permute-start.9
  29.6 0.8 %collective-permute-start.7 = (bf16[544,128]{1,0:T(8,128)(2,1)S(1)}, bf16[544,128]{1,0:T(8,128)(2,1)S(1)}, u32[]{:S(2)}, u32[]{:S(2)}) collective-permute-start(bf16[544,128]{1,0:T(8,128)(2,1)S(1)} %get-tuple-element.56), channel_id=1, source_target_pairs={{0,2},{2,0},{4,6},{6,4},{1,3},{3,1},{5,7},{7,5},{8,10},{10,8},{12,... | collective-permute-start | bytes 417800 | tf_op jit(solution)/shard_map/ppermute | solution.py:522
  30.3 7.8 %collective-permute-done.8.refs_2_ = bf16[544,128]{1,0:T(8,128)(2,1)S(1)} collective-permute-done((bf16[544,128]{1,0:T(8,128)(2,1)S(1)}, bf16[544,128]{1,0:T(8,128)(2,1)S(1)}, u32[]{:S(2)}, u32[]{:S(2)}) %collective-permute-start.8) | collective-permute-done | bytes 139296 | tf_op jit(solution)/shard_map/ppermute | solution.py:522
  38.1 0.0 collective-permute-done.9.refs_3_
  38.1 0.0 collective-permute-done.7.refs_1_
  38.1 0.9 %spread.1 = (bf16[1,128,512]{2,1,0:T(8,128)(2,1)}, bf16[1,128,512]{2,1,0:T(8,128)(2,1)}, bf16[1,128,512]{2,1,0:T(8,128)(2,1)}, bf16[1,128,512]{2,1,0:T(8,128)(2,1)}, f32[31,512]{1,0:T(8,128)}) custom-call(bf16[544,128]{1,0:T(8,128)(2,1)S(1)} %get-tuple-element.55.refs_0_, bf16[544,128]{1,0:T(8,128)(2,1)S(1)} %collective-permute-done.7.refs_1_, ...), custom_call_target="tpu_custom_call" | custom-call | tf_op jit(solution)/shard_map/spread/pallas_call | solution.py:635
  (2 shorter events, 0.1 us)
Async XLA Ops:
  0.6 17.5 %copy-start.3 = (f32[31,512]{1,0:T(8,128)S(1)}, f32[31,512]{1,0:T(8,128)}, u32[]{:S(2)}) copy-start(f32[31,512]{1,0:T(8,128)} %w_ref.1) | copy-start | bytes 190468
  1.7 15.8 %collective-permute-start.3 = (bf16[3,128,128]{2,1,0:T(8,128)(2,1)S(1)}, bf16[3,128,128]{2,1,0:T(8,128)(2,1)S(1)}, u32[]{:S(2)}, u32[]{:S(2)}) collective-permute-start(bf16[3,128,128]{2,1,0:T(8,128)(2,1)S(1)} %get-tuple-element.36), channel_id=1, source_target_pairs={{0,6},{2,4},{4,2},{6,0},{1,7},{3,5},{5,3},{7,1},{8,14},{10,12},{12... | collective-permute-start | bytes 294920 | tf_op jit(solution)/shard_map/ppermute | solution.py:522
  6.8 11.4 %collective-permute-start.4 = (bf16[3,128,128]{2,1,0:T(8,128)(2,1)S(1)}, bf16[3,128,128]{2,1,0:T(8,128)(2,1)S(1)}, u32[]{:S(2)}, u32[]{:S(2)}) collective-permute-start(bf16[3,128,128]{2,1,0:T(8,128)(2,1)S(1)} %get-tuple-element.37), channel_id=1, source_target_pairs={{0,4},{2,6},{4,0},{6,2},{1,5},{3,7},{5,1},{7,3},{8,12},{10,14},{12... | collective-permute-start | bytes 294920 | tf_op jit(solution)/shard_map/ppermute | solution.py:522
  6.8 11.4 %collective-permute-start.5 = (bf16[3,128,128]{2,1,0:T(8,128)(2,1)S(1)}, bf16[3,128,128]{2,1,0:T(8,128)(2,1)S(1)}, u32[]{:S(2)}, u32[]{:S(2)}) collective-permute-start(bf16[3,128,128]{2,1,0:T(8,128)(2,1)S(1)} %get-tuple-element.38), channel_id=1, source_target_pairs={{0,2},{2,0},{4,6},{6,4},{1,3},{3,1},{5,7},{7,5},{8,10},{10,8},{12,... | collective-permute-start | bytes 294920 | tf_op jit(solution)/shard_map/ppermute | solution.py:522
  7.4 0.9 %copy-start = (bf16[1,128,512]{2,1,0:T(8,128)(2,1)S(1)}, bf16[1,128,512]{2,1,0:T(8,128)(2,1)}, u32[]{:S(2)}) copy-start(bf16[1,128,512]{2,1,0:T(8,128)(2,1)} %q_ref.3) | copy-start | bytes 393220
  8.3 0.9 %copy-start.1 = (bf16[1,128,512]{2,1,0:T(8,128)(2,1)S(1)}, bf16[1,128,512]{2,1,0:T(8,128)(2,1)}, u32[]{:S(2)}) copy-start(bf16[1,128,512]{2,1,0:T(8,128)(2,1)} %k_ref.3) | copy-start | bytes 393220
  9.2 0.9 %copy-start.2 = (bf16[1,128,512]{2,1,0:T(8,128)(2,1)S(1)}, bf16[1,128,512]{2,1,0:T(8,128)(2,1)}, u32[]{:S(2)}) copy-start(bf16[1,128,512]{2,1,0:T(8,128)(2,1)} %v_ref.3) | copy-start | bytes 393220
  10.1 0.9 %copy-start.4 = (bf16[1,128,512]{2,1,0:T(8,128)(2,1)S(1)}, bf16[1,128,512]{2,1,0:T(8,128)(2,1)}, u32[]{:S(2)}) copy-start(bf16[1,128,512]{2,1,0:T(8,128)(2,1)} %c_ref.1) | copy-start | bytes 393220
  11.0 0.7 %copy-start.5 = (s32[1,16]{1,0:T(1,128)S(1)}, s32[1,16]{1,0:T(1,128)}, u32[]{:S(2)}) copy-start(s32[1,16]{1,0:T(1,128)} %lens_ref.1) | copy-start | bytes 196
  13.0 7.6 %collective-permute-start = (bf16[128,128]{1,0:T(8,128)(2,1)S(1)}, bf16[128,128]{1,0:T(8,128)(2,1)S(1)}, u32[]{:S(2)}, u32[]{:S(2)}) collective-permute-start(bf16[128,128]{1,0:T(8,128)(2,1)S(1)} %get-tuple-element.32), channel_id=1, source_target_pairs={{0,6},{2,4},{4,2},{6,0},{1,7},{3,5},{5,3},{7,1},{8,14},{10,12},{12... | collective-permute-start | bytes 98312 | tf_op jit(solution)/shard_map/ppermute | solution.py:522
  16.8 4.9 %collective-permute-start.1 = (bf16[128,128]{1,0:T(8,128)(2,1)S(1)}, bf16[128,128]{1,0:T(8,128)(2,1)S(1)}, u32[]{:S(2)}, u32[]{:S(2)}) collective-permute-start(bf16[128,128]{1,0:T(8,128)(2,1)S(1)} %get-tuple-element.33), channel_id=1, source_target_pairs={{0,4},{2,6},{4,0},{6,2},{1,5},{3,7},{5,1},{7,3},{8,12},{10,14},{12... | collective-permute-start | bytes 98312 | tf_op jit(solution)/shard_map/ppermute | solution.py:522
  17.4 4.3 %collective-permute-start.2 = (bf16[128,128]{1,0:T(8,128)(2,1)S(1)}, bf16[128,128]{1,0:T(8,128)(2,1)S(1)}, u32[]{:S(2)}, u32[]{:S(2)}) collective-permute-start(bf16[128,128]{1,0:T(8,128)(2,1)S(1)} %get-tuple-element.34), channel_id=1, source_target_pairs={{0,2},{2,0},{4,6},{6,4},{1,3},{3,1},{5,7},{7,5},{8,10},{10,8},{12,... | collective-permute-start | bytes 98312 | tf_op jit(solution)/shard_map/ppermute | solution.py:522
  22.8 3.8 %collective-permute-start.6 = (f32[32,128]{1,0:T(8,128)S(1)}, f32[32,128]{1,0:T(8,128)S(1)}, u32[]{:S(2)}, u32[]{:S(2)}) collective-permute-start(f32[32,128]{1,0:T(8,128)S(1)} %get-tuple-element.54.refs_4_), channel_id=1, source_target_pairs={{0,8},{8,0},{1,9},{9,1},{2,10},{10,2},{3,11},{11,3},{4,12},{12,4},... | collective-permute-start | bytes 49160 | tf_op jit(solution)/shard_map/ppermute | solution.py:597
  26.7 11.4 %collective-permute-start.8 = (bf16[544,128]{1,0:T(8,128)(2,1)S(1)}, bf16[544,128]{1,0:T(8,128)(2,1)S(1)}, u32[]{:S(2)}, u32[]{:S(2)}) collective-permute-start(bf16[544,128]{1,0:T(8,128)(2,1)S(1)} %get-tuple-element.57), channel_id=1, source_target_pairs={{0,4},{2,6},{4,0},{6,2},{1,5},{3,7},{5,1},{7,3},{8,12},{10,14},{12... | collective-permute-start | bytes 417800 | tf_op jit(solution)/shard_map/ppermute | solution.py:522
  29.3 8.8 %collective-permute-start.9 = (bf16[544,128]{1,0:T(8,128)(2,1)S(1)}, bf16[544,128]{1,0:T(8,128)(2,1)S(1)}, u32[]{:S(2)}, u32[]{:S(2)}) collective-permute-start(bf16[544,128]{1,0:T(8,128)(2,1)S(1)} %get-tuple-element.58), channel_id=1, source_target_pairs={{0,6},{2,4},{4,2},{6,0},{1,7},{3,5},{5,3},{7,1},{8,14},{10,12},{12... | collective-permute-start | bytes 417800 | tf_op jit(solution)/shard_map/ppermute | solution.py:522
  29.6 8.6 %collective-permute-start.7 = (bf16[544,128]{1,0:T(8,128)(2,1)S(1)}, bf16[544,128]{1,0:T(8,128)(2,1)S(1)}, u32[]{:S(2)}, u32[]{:S(2)}) collective-permute-start(bf16[544,128]{1,0:T(8,128)(2,1)S(1)} %get-tuple-element.56), channel_id=1, source_target_pairs={{0,2},{2,0},{4,6},{6,4},{1,3},{3,1},{5,7},{7,5},{8,10},{10,8},{12,... | collective-permute-start | bytes 417800 | tf_op jit(solution)/shard_map/ppermute | solution.py:522

commit v15 on v14

--- a/solution.py
+++ b/solution.py
@@ -255,13 +255,16 @@
     return pl.ds(pl.multiple_of(block * LANES, LANES), LANES)
 
 
-def pack_kernel(ranks, q_ref, k_ref, v_ref, *rest):
+def pack_kernel(ranks, q_ref, k_ref, v_ref, c_ref, *rest):
     outs, sems = rest[:-1], rest[-1]
     me = lax.axis_index("seq")
     pairs = []
     for step in range(ranks - 1, 0, -1):
         for place, source in enumerate((q_ref, k_ref, v_ref)):
             pairs.append((source.at[0, :, lanes_at(me ^ step)], outs[step - 1].at[place]))
+        pairs.append((c_ref.at[0, :, lanes_at(me ^ step)], outs[ranks + step - 2]))
+    for place, source in enumerate((q_ref, k_ref, v_ref, c_ref)):
+        pairs.append((source.at[0, :, lanes_at(me)], outs[-1].at[place]))
     run_copies(pairs, sems)
 
 
@@ -278,45 +281,39 @@
         copy.wait()
 
 
-def mask_kernel(ranks, length, lens_ref, q_ref, k_ref, v_ref, c_ref, *refs):
-    cot_refs = refs[: ranks - 1]
-    own_ref, col_ref, row_ref, after_ref, before_ref, sems = refs[ranks - 1 :]
-    me = lax.axis_index("seq")
-    pairs = [(c_ref.at[0, :, lanes_at(me ^ step)], cot_refs[step - 1]) for step in range(1, ranks)]
-    for place, source in enumerate((q_ref, k_ref, v_ref, c_ref)):
-        pairs.append((source.at[0, :, lanes_at(me)], own_ref.at[place]))
-
-    def extents():
-        ends = []
-        running = jnp.int32(0)
-        for number in range(lens_ref.shape[1]):
-            running = running + lens_ref[0, number]
-            ends.append(running)
-        row_time = lax.broadcasted_iota(jnp.int32, row_ref.shape, 1)
-        row_first = jnp.zeros(row_ref.shape, jnp.int32)
+def mask_kernel(length, lens_ref, *refs):
+    col_ref, row_ref, after_ref, before_ref = refs[-4:]
+    count = (len(refs) - 4) // 2
+    for source, target in zip(refs[:count], refs[count:]):
+        target[...] = source[...]
+    ends = []
+    running = jnp.int32(0)
+    for number in range(lens_ref.shape[1]):
+        running = running + lens_ref[0, number]
+        ends.append(running)
+    row_time = lax.broadcasted_iota(jnp.int32, row_ref.shape, 1)
+    row_first = jnp.zeros(row_ref.shape, jnp.int32)
+    for end in ends:
+        row_first = jnp.where(row_time >= end, end, row_first)
+    row_ref[...] = row_first
+    chunk = 64
+
+    def some_rows(number, carry):
+        base = pl.multiple_of(number * chunk, chunk)
+        time = base + lax.broadcasted_iota(jnp.int32, (chunk, LANES), 0)
+        first = jnp.zeros((chunk, LANES), jnp.int32)
+        last = jnp.full((chunk, LANES), length, jnp.int32)
         for end in ends:
-            row_first = jnp.where(row_time >= end, end, row_first)
-        row_ref[...] = row_first
-        chunk = 64
-
-        def some_rows(number, carry):
-            base = pl.multiple_of(number * chunk, chunk)
-            time = base + lax.broadcasted_iota(jnp.int32, (chunk, LANES), 0)
-            first = jnp.zeros((chunk, LANES), jnp.int32)
-            last = jnp.full((chunk, LANES), length, jnp.int32)
-            for end in ends:
-                first = jnp.where(time >= end, end, first)
-            for end in reversed(ends):
-                last = jnp.where(time < end, end, last)
-            rows = pl.ds(base, chunk)
-            col_ref[rows, :] = first
-            after_ref[rows, :] = last - 1 - time
-            before_ref[rows, :] = time - first
-            return carry
-
-        lax.fori_loop(0, length // chunk, some_rows, 0)
-
-    run_copies(pairs, sems, extents)
+            first = jnp.where(time >= end, end, first)
+        for end in reversed(ends):
+            last = jnp.where(time < end, end, last)
+        rows = pl.ds(base, chunk)
+        col_ref[rows, :] = first
+        after_ref[rows, :] = last - 1 - time
+        before_ref[rows, :] = time - first
+        return carry
+
+    lax.fori_loop(0, length // chunk, some_rows, 0)
 
 
 def forward_kernel(ranks, frames, *refs):
@@ -508,15 +505,17 @@
     params = pltpu.CompilerParams(vmem_limit_bytes=24 * MIB)
     taps = KERNEL + 1
 
-    sends = pl.pallas_call(
+    *sends, own = pl.pallas_call(
         functools.partial(pack_kernel, ranks),
-        out_shape=[struct((3, frames, LANES), bf16)] * (ranks - 1),
-        in_specs=[hbm] * 3,
-        out_specs=[vmem] * (ranks - 1),
-        scratch_shapes=[pltpu.SemaphoreType.DMA((3 * (ranks - 1),))],
-        compiler_params=pltpu.CompilerParams(vmem_limit_bytes=54912 * 1024),
+        out_shape=[struct((3, frames, LANES), bf16)] * (ranks - 1)
+        + [struct((frames, LANES), bf16)] * (ranks - 1)
+        + [struct((4, frames, LANES), bf16)],
+        in_specs=[hbm] * 4,
+        out_specs=[vmem] * (2 * ranks - 1),
+        scratch_shapes=[pltpu.SemaphoreType.DMA((4 * ranks,))],
+        compiler_params=pltpu.CompilerParams(vmem_limit_bytes=54672 * 1024),
         name="pack",
-    )(queries, keys, values)
+    )(queries, keys, values, cotangent)
 
     def swap(array, step):
         return lax.ppermute(array, "seq", [(rank, rank ^ step) for rank in range(ranks)])
@@ -524,23 +523,21 @@
     order = list(range(ranks - 1, 0, -1))
     received = {step: swap(sends[step - 1], step) for step in order}
 
-    *cot_sends, own, col, row, after, before = pl.pallas_call(
-        functools.partial(mask_kernel, ranks, length),
+    *cot_sends, col, row, after, before = pl.pallas_call(
+        functools.partial(mask_kernel, length),
         out_shape=[struct((frames, LANES), bf16)] * (ranks - 1)
         + [
-            struct((4, frames, LANES), bf16),
             struct((length, LANES), i32),
             struct((8, length), i32),
             struct((length, LANES), i32),
             struct((length, LANES), i32),
         ],
-        in_specs=[smem] + [hbm] * 4,
-        out_specs=[vmem] * (ranks + 4),
-        scratch_shapes=[pltpu.SemaphoreType.DMA((ranks + 3,))],
+        in_specs=[smem] + [vmem] * (ranks - 1),
+        out_specs=[vmem] * (ranks + 3),
         compiler_params=params,
         cost_estimate=cost(4 * MIB, MIB),
         name="masks",
-    )(rec_lengths, queries, keys, values, cotangent)
+    )(rec_lengths, *sends[ranks - 1 :])
     cots = {step: swap(cot_sends[step - 1], step) for step in order}
 
     span = pl.pallas_call(

time: 39.3 us -> 36.7 us (0.934)
  local copies, waits for them, and re-layouts: 4.27 us -> 0.66 us
  waiting for transfers between devices: 8.94 us -> 9.51 us
  starting transfers between devices: 15.4 us -> 15.9 us
    unnamed x12 -> x4, local copies, waits for them, and re-layouts: 4.27 us -> 0.66 us
    ppermute x9, waiting for transfers between devices: 8.94 us -> 9.51 us  [swap(): lax.ppermute(array, 'seq', [(rank, rank ^ step) for rank in range(ranks)])]
    ppermute x9, starting transfers between devices: 13.9 us -> 14.3 us  [swap(): lax.ppermute(array, 'seq', [(rank, rank ^ step) for rank in range(ranks)])]
  transfers between devices with their start and end apart: 10 -> 10, of which waited for: 2 -> 3; matrix products, arithmetic and copies ran while one was open for 0% -> 0% of each run, Pallas kernels for 17% -> 18%
where the time goes in v15:
time: 36.7 us; the launch traced here: 36.5 us
  starting transfers between devices  15.9 us (43%)
  Pallas kernels  9.65 us (26%)
  waiting for transfers between devices  9.51 us (26%)
  between operations  0.75 us (2%)
  local copies, waits for them, and re-layouts  0.66 us (2%)
    ppermute x9, starting transfers between devices, swap(): lax.ppermute(array, 'seq', [(rank, rank ^ step) for rank in range(ranks)])  14.3 us
    ppermute x9, waiting for transfers between devices, swap(): lax.ppermute(array, 'seq', [(rank, rank ^ step) for rank in range(ranks)])  9.51 us
    pallas_call x1, Pallas kernels, on_device_heads(): pl.pallas_call(functools.partial(forward_kernel, ranks, frames), out_shap...  2.45 us
    pallas_call x1, Pallas kernels, on_device_heads(): pl.pallas_call(backward_kernel, out_shape=[struct((length, LANES), bf16)]...  2.28 us
    ppermute x1, starting transfers between devices, on_device_heads(): lax.ppermute(own_taps, 'dp', [(one, (one + shift) % copies) for one in ra...  1.55 us
    pallas_call x1, Pallas kernels, on_device_heads(): pl.pallas_call(functools.partial(mask_kernel, length), out_shape=[struct(...  1.19 us
    pallas_call x1, Pallas kernels, on_device_heads(): pl.pallas_call(functools.partial(pack_kernel, ranks), out_shape=[struct((...  1.19 us
    pallas_call x1, Pallas kernels, on_device_heads(): pl.pallas_call(functools.partial(taps_kernel, ranks, frames), out_shape=[...  1.02 us
  transfers between devices with their start and end apart: 10, of which 3 were waited for; matrix products, arithmetic and copies ran while one was open for 0% of the time, Pallas kernels for 18%

profile of v15, /device:TPU:0, one launch (start us, length us, event | category | flops | bytes accessed | tf_op | source)
XLA Modules:
  0.0 36.5 jit_solution(12060938338762245635)
XLA Ops:
  0.6 0.0 copy-start
  0.6 1.2 %pack.1 = (bf16[3,128,128]{2,1,0:T(8,128)(2,1)S(1)}, bf16[3,128,128]{2,1,0:T(8,128)(2,1)S(1)}, bf16[3,128,128]{2,1,0:T(8,128)(2,1)S(1)}, bf16[128,128]{1,0:T(8,1...) custom-call(bf16[1,128,512]{2,1,0:T(8,128)(2,1)} %q_ref.1, ...), custom_call_target="tpu_custom_call" | custom-call | tf_op jit(solution)/shard_map/pack/pallas_call | solution.py:508
  1.8 5.1 %collective-permute-start.3 = (bf16[3,128,128]{2,1,0:T(8,128)(2,1)S(1)}, bf16[3,128,128]{2,1,0:T(8,128)(2,1)S(1)}, u32[]{:S(2)}, u32[]{:S(2)}) collective-permute-start(bf16[3,128,128]{2,1,0:T(8,128)(2,1)S(1)} %get-tuple-element.42), channel_id=1, source_target_pairs={{0,6},{2,4},{4,2},{6,0},{1,7},{3,5},{5,3},{7,1},{8,14},{10,12},{12... | collective-permute-start | bytes 294920 | tf_op jit(solution)/shard_map/ppermute | solution.py:521
  7.0 0.0 collective-permute-start.4
  7.0 0.6 %collective-permute-start.5 = (bf16[3,128,128]{2,1,0:T(8,128)(2,1)S(1)}, bf16[3,128,128]{2,1,0:T(8,128)(2,1)S(1)}, u32[]{:S(2)}, u32[]{:S(2)}) collective-permute-start(bf16[3,128,128]{2,1,0:T(8,128)(2,1)S(1)} %get-tuple-element.44), channel_id=1, source_target_pairs={{0,2},{2,0},{4,6},{6,4},{1,3},{3,1},{5,7},{7,5},{8,10},{10,8},{12,... | collective-permute-start | bytes 294920 | tf_op jit(solution)/shard_map/ppermute | solution.py:521
  7.6 0.0 copy-start.1
  7.6 0.7 %copy-done.1 = s32[1,16]{1,0:T(1,128)S(1)} copy-done((s32[1,16]{1,0:T(1,128)S(1)}, s32[1,16]{1,0:T(1,128)}, u32[]{:S(2)}) %copy-start.1) | copy-done | bytes 88
  8.3 1.2 %masks.1 = (bf16[128,128]{1,0:T(8,128)(2,1)S(1)}, bf16[128,128]{1,0:T(8,128)(2,1)S(1)}, bf16[128,128]{1,0:T(8,128)(2,1)S(1)}, s32[512,128]{1,0:T(8,128)S(1)}, s3...) custom-call(s32[1,16]{1,0:T(1,128)S(1)} %copy-done.1, ...), custom_call_target="tpu_custom_call" | custom-call | flops 4194304 | bytes 1048576 | tf_op jit(solution)/shard_map/masks/pallas_call | solution.py:526
  9.5 3.8 %collective-permute-start = (bf16[128,128]{1,0:T(8,128)(2,1)S(1)}, bf16[128,128]{1,0:T(8,128)(2,1)S(1)}, u32[]{:S(2)}, u32[]{:S(2)}) collective-permute-start(bf16[128,128]{1,0:T(8,128)(2,1)S(1)} %get-tuple-element.38), channel_id=1, source_target_pairs={{0,6},{2,4},{4,2},{6,0},{1,7},{3,5},{5,3},{7,1},{8,14},{10,12},{12... | collective-permute-start | bytes 98312 | tf_op jit(solution)/shard_map/ppermute | solution.py:521
  13.3 0.0 collective-permute-start.1
  13.3 0.6 %spans.1.refs_6_.span_ref = f32[31,512,128]{2,1,0:T(8,128)S(1)} custom-call(s32[512,128]{1,0:T(8,128)S(1)} %get-tuple-element.47.after_ref, s32[512,128]{1,0:T(8,128)S(1)} %get-tuple-element.48.before_ref), custom_call_target="tpu_custom_call" | custom-call | flops 419430400 | bytes 3145728 | tf_op jit(solution)/shard_map/spans/pallas_call | solution.py:543
  13.8 0.0 collective-permute-done.3.refs_0_
  13.8 1.2 %collective-permute-start.2 = (bf16[128,128]{1,0:T(8,128)(2,1)S(1)}, bf16[128,128]{1,0:T(8,128)(2,1)S(1)}, u32[]{:S(2)}, u32[]{:S(2)}) collective-permute-start(bf16[128,128]{1,0:T(8,128)(2,1)S(1)} %get-tuple-element.40), channel_id=1, source_target_pairs={{0,2},{2,0},{4,6},{6,4},{1,3},{3,1},{5,7},{7,5},{8,10},{10,8},{12,... | collective-permute-start | bytes 98312 | tf_op jit(solution)/shard_map/ppermute | solution.py:521
  15.0 2.3 %collective-permute-done.4.refs_1_ = bf16[3,128,128]{2,1,0:T(8,128)(2,1)S(1)} collective-permute-done((bf16[3,128,128]{2,1,0:T(8,128)(2,1)S(1)}, bf16[3,128,128]{2,1,0:T(8,128)(2,1)S(1)}, u32[]{:S(2)}, u32[]{:S(2)}) %collective-permute-start.4) | collective-permute-done | bytes 98336 | tf_op jit(solution)/shard_map/ppermute | solution.py:521
  17.3 0.0 collective-permute-done.5.refs_2_
  17.3 0.0 copy-done
  17.3 2.4 %forward.1 = (bf16[2,512,512]{2,1,0:T(8,128)(2,1)S(1)}, f32[544,128]{1,0:T(8,128)S(1)}, f32[512,128]{1,0:T(8,128)S(1)}, bf16[2,512,128]{2,1,0:T(8,128)(2,1)S(1)}...) custom-call(bf16[3,128,128]{2,1,0:T(8,128)(2,1)S(1)} %collective-permute-done.3.refs_0_, ...), custom_call_target="tpu_custom_call" | custom-call | flops 419430400 | bytes 3145728 | tf_op jit(solution)/shard_map/forward/pallas_call | solution.py:553
  19.8 0.0 collective-permute-done.refs_0_
  19.8 0.0 collective-permute-done.1.refs_1_
  19.8 0.0 collective-permute-done.2.refs_2_
  19.8 1.0 %taps.1 = (bf16[512,128]{1,0:T(8,128)(2,1)S(1)}, f32[544,128]{1,0:T(8,128)S(1)}, f32[32,128]{1,0:T(8,128)S(1)}) custom-call(bf16[128,128]{1,0:T(8,128)(2,1)S(1)} %collective-permute-done.refs_0_, bf16[128,128]{1,0:T(8,128)(2,1)S(1)} %collective-permute-done.1.refs_1_, bf16[128,128]{1,0:T(8,128)(2,1)S(1)} %collective-permute-done.2.refs_2_, ...), custom_call_target="tpu_custom_call" | custom-call | flops 419430400 | bytes 3145728 | tf_op jit(solution)/shard_map/taps/pallas_call | solution.py:577
  20.8 1.6 %collective-permute-start.6 = (f32[32,128]{1,0:T(8,128)S(1)}, f32[32,128]{1,0:T(8,128)S(1)}, u32[]{:S(2)}, u32[]{:S(2)}) collective-permute-start(f32[32,128]{1,0:T(8,128)S(1)} %get-tuple-element.60.refs_4_), channel_id=1, source_target_pairs={{0,8},{8,0},{1,9},{9,1},{2,10},{10,2},{3,11},{11,3},{4,12},{12,4},... | collective-permute-start | bytes 49160 | tf_op jit(solution)/shard_map/ppermute | solution.py:594
  22.4 2.3 %backward.1 = (bf16[512,128]{1,0:T(8,128)(2,1)S(1)}, bf16[512,128]{1,0:T(8,128)(2,1)S(1)}, bf16[512,128]{1,0:T(8,128)(2,1)S(1)}) custom-call(bf16[2,512,512]{2,1,0:T(8,128)(2,1)S(1)} %get-tuple-element.52.soft_ref, f32[544,128]{1,0:T(8,128)S(1)} %get-tuple-element.49.refs_4_.att_ref, f32[544,128]{1,0:T(8,128)S(1)} %get-tuple-element.53.grad_pad, ...), custom_call_target="tpu_custom_call" | custom-call | flops 838860800 | bytes 3145728 | tf_op jit(solution)/shard_map/backward/pallas_call | solution.py:598
  24.7 0.0 collective-permute-done.6.refs_5_
  24.7 1.0 %collective-permute-start.8 = (bf16[544,128]{1,0:T(8,128)(2,1)S(1)}, bf16[544,128]{1,0:T(8,128)(2,1)S(1)}, u32[]{:S(2)}, u32[]{:S(2)}) collective-permute-start(bf16[544,128]{1,0:T(8,128)(2,1)S(1)} %get-tuple-element.63), channel_id=1, source_target_pairs={{0,4},{2,6},{4,0},{6,2},{1,5},{3,7},{5,1},{7,3},{8,12},{10,14},{12... | collective-permute-start | bytes 417800 | tf_op jit(solution)/shard_map/ppermute | solution.py:521
  25.7 1.7 %collective-permute-start.9 = (bf16[544,128]{1,0:T(8,128)(2,1)S(1)}, bf16[544,128]{1,0:T(8,128)(2,1)S(1)}, u32[]{:S(2)}, u32[]{:S(2)}) collective-permute-start(bf16[544,128]{1,0:T(8,128)(2,1)S(1)} %get-tuple-element.64), channel_id=1, source_target_pairs={{0,6},{2,4},{4,2},{6,0},{1,7},{3,5},{5,3},{7,1},{8,14},{10,12},{12... | collective-permute-start | bytes 417800 | tf_op jit(solution)/shard_map/ppermute | solution.py:521
  27.4 1.0 %collective-permute-start.7 = (bf16[544,128]{1,0:T(8,128)(2,1)S(1)}, bf16[544,128]{1,0:T(8,128)(2,1)S(1)}, u32[]{:S(2)}, u32[]{:S(2)}) collective-permute-start(bf16[544,128]{1,0:T(8,128)(2,1)S(1)} %get-tuple-element.62), channel_id=1, source_target_pairs={{0,2},{2,0},{4,6},{6,4},{1,3},{3,1},{5,7},{7,5},{8,10},{10,8},{12,... | collective-permute-start | bytes 417800 | tf_op jit(solution)/shard_map/ppermute | solution.py:521
  28.4 6.7 %collective-permute-done.8.refs_2_ = bf16[544,128]{1,0:T(8,128)(2,1)S(1)} collective-permute-done((bf16[544,128]{1,0:T(8,128)(2,1)S(1)}, bf16[544,128]{1,0:T(8,128)(2,1)S(1)}, u32[]{:S(2)}, u32[]{:S(2)}) %collective-permute-start.8) | collective-permute-done | bytes 139296 | tf_op jit(solution)/shard_map/ppermute | solution.py:521
  35.1 0.0 collective-permute-done.9.refs_3_
  35.1 0.4 %collective-permute-done.7.refs_1_ = bf16[544,128]{1,0:T(8,128)(2,1)S(1)} collective-permute-done((bf16[544,128]{1,0:T(8,128)(2,1)S(1)}, bf16[544,128]{1,0:T(8,128)(2,1)S(1)}, u32[]{:S(2)}, u32[]{:S(2)}) %collective-permute-start.7) | collective-permute-done | bytes 139296 | tf_op jit(solution)/shard_map/ppermute | solution.py:521
  35.6 0.9 %spread.1 = (bf16[1,128,512]{2,1,0:T(8,128)(2,1)}, bf16[1,128,512]{2,1,0:T(8,128)(2,1)}, bf16[1,128,512]{2,1,0:T(8,128)(2,1)}, bf16[1,128,512]{2,1,0:T(8,128)(2,1)}, f32[31,512]{1,0:T(8,128)}) custom-call(bf16[544,128]{1,0:T(8,128)(2,1)S(1)} %get-tuple-element.61.refs_0_, bf16[544,128]{1,0:T(8,128)(2,1)S(1)} %collective-permute-done.7.refs_1_, ...), custom_call_target="tpu_custom_call" | custom-call | tf_op jit(solution)/shard_map/spread/pallas_call | solution.py:632
  (2 shorter events, 0.1 us)
Async XLA Ops:
  0.6 16.7 %copy-start = (f32[31,512]{1,0:T(8,128)S(1)}, f32[31,512]{1,0:T(8,128)}, u32[]{:S(2)}) copy-start(f32[31,512]{1,0:T(8,128)} %w_ref.1) | copy-start | bytes 190468
  1.8 12.0 %collective-permute-start.3 = (bf16[3,128,128]{2,1,0:T(8,128)(2,1)S(1)}, bf16[3,128,128]{2,1,0:T(8,128)(2,1)S(1)}, u32[]{:S(2)}, u32[]{:S(2)}) collective-permute-start(bf16[3,128,128]{2,1,0:T(8,128)(2,1)S(1)} %get-tuple-element.42), channel_id=1, source_target_pairs={{0,6},{2,4},{4,2},{6,0},{1,7},{3,5},{5,3},{7,1},{8,14},{10,12},{12... | collective-permute-start | bytes 294920 | tf_op jit(solution)/shard_map/ppermute | solution.py:521
  7.0 10.4 %collective-permute-start.4 = (bf16[3,128,128]{2,1,0:T(8,128)(2,1)S(1)}, bf16[3,128,128]{2,1,0:T(8,128)(2,1)S(1)}, u32[]{:S(2)}, u32[]{:S(2)}) collective-permute-start(bf16[3,128,128]{2,1,0:T(8,128)(2,1)S(1)} %get-tuple-element.43), channel_id=1, source_target_pairs={{0,4},{2,6},{4,0},{6,2},{1,5},{3,7},{5,1},{7,3},{8,12},{10,14},{12... | collective-permute-start | bytes 294920 | tf_op jit(solution)/shard_map/ppermute | solution.py:521
  7.0 10.4 %collective-permute-start.5 = (bf16[3,128,128]{2,1,0:T(8,128)(2,1)S(1)}, bf16[3,128,128]{2,1,0:T(8,128)(2,1)S(1)}, u32[]{:S(2)}, u32[]{:S(2)}) collective-permute-start(bf16[3,128,128]{2,1,0:T(8,128)(2,1)S(1)} %get-tuple-element.44), channel_id=1, source_target_pairs={{0,2},{2,0},{4,6},{6,4},{1,3},{3,1},{5,7},{7,5},{8,10},{10,8},{12,... | collective-permute-start | bytes 294920 | tf_op jit(solution)/shard_map/ppermute | solution.py:521
  7.6 0.7 %copy-start.1 = (s32[1,16]{1,0:T(1,128)S(1)}, s32[1,16]{1,0:T(1,128)}, u32[]{:S(2)}) copy-start(s32[1,16]{1,0:T(1,128)} %lens_ref.1) | copy-start | bytes 196
  9.5 10.3 %collective-permute-start = (bf16[128,128]{1,0:T(8,128)(2,1)S(1)}, bf16[128,128]{1,0:T(8,128)(2,1)S(1)}, u32[]{:S(2)}, u32[]{:S(2)}) collective-permute-start(bf16[128,128]{1,0:T(8,128)(2,1)S(1)} %get-tuple-element.38), channel_id=1, source_target_pairs={{0,6},{2,4},{4,2},{6,0},{1,7},{3,5},{5,3},{7,1},{8,14},{10,12},{12... | collective-permute-start | bytes 98312 | tf_op jit(solution)/shard_map/ppermute | solution.py:521
  13.3 6.5 %collective-permute-start.1 = (bf16[128,128]{1,0:T(8,128)(2,1)S(1)}, bf16[128,128]{1,0:T(8,128)(2,1)S(1)}, u32[]{:S(2)}, u32[]{:S(2)}) collective-permute-start(bf16[128,128]{1,0:T(8,128)(2,1)S(1)} %get-tuple-element.39), channel_id=1, source_target_pairs={{0,4},{2,6},{4,0},{6,2},{1,5},{3,7},{5,1},{7,3},{8,12},{10,14},{12... | collective-permute-start | bytes 98312 | tf_op jit(solution)/shard_map/ppermute | solution.py:521
  13.8 6.0 %collective-permute-start.2 = (bf16[128,128]{1,0:T(8,128)(2,1)S(1)}, bf16[128,128]{1,0:T(8,128)(2,1)S(1)}, u32[]{:S(2)}, u32[]{:S(2)}) collective-permute-start(bf16[128,128]{1,0:T(8,128)(2,1)S(1)} %get-tuple-element.40), channel_id=1, source_target_pairs={{0,2},{2,0},{4,6},{6,4},{1,3},{3,1},{5,7},{7,5},{8,10},{10,8},{12,... | collective-permute-start | bytes 98312 | tf_op jit(solution)/shard_map/ppermute | solution.py:521
  20.8 3.8 %collective-permute-start.6 = (f32[32,128]{1,0:T(8,128)S(1)}, f32[32,128]{1,0:T(8,128)S(1)}, u32[]{:S(2)}, u32[]{:S(2)}) collective-permute-start(f32[32,128]{1,0:T(8,128)S(1)} %get-tuple-element.60.refs_4_), channel_id=1, source_target_pairs={{0,8},{8,0},{1,9},{9,1},{2,10},{10,2},{3,11},{11,3},{4,12},{12,4},... | collective-permute-start | bytes 49160 | tf_op jit(solution)/shard_map/ppermute | solution.py:594
  24.7 10.4 %collective-permute-start.8 = (bf16[544,128]{1,0:T(8,128)(2,1)S(1)}, bf16[544,128]{1,0:T(8,128)(2,1)S(1)}, u32[]{:S(2)}, u32[]{:S(2)}) collective-permute-start(bf16[544,128]{1,0:T(8,128)(2,1)S(1)} %get-tuple-element.63), channel_id=1, source_target_pairs={{0,4},{2,6},{4,0},{6,2},{1,5},{3,7},{5,1},{7,3},{8,12},{10,14},{12... | collective-permute-start | bytes 417800 | tf_op jit(solution)/shard_map/ppermute | solution.py:521
  25.7 9.4 %collective-permute-start.9 = (bf16[544,128]{1,0:T(8,128)(2,1)S(1)}, bf16[544,128]{1,0:T(8,128)(2,1)S(1)}, u32[]{:S(2)}, u32[]{:S(2)}) collective-permute-start(bf16[544,128]{1,0:T(8,128)(2,1)S(1)} %get-tuple-element.64), channel_id=1, source_target_pairs={{0,6},{2,4},{4,2},{6,0},{1,7},{3,5},{5,3},{7,1},{8,14},{10,12},{12... | collective-permute-start | bytes 417800 | tf_op jit(solution)/shard_map/ppermute | solution.py:521
  27.4 8.1 %collective-permute-start.7 = (bf16[544,128]{1,0:T(8,128)(2,1)S(1)}, bf16[544,128]{1,0:T(8,128)(2,1)S(1)}, u32[]{:S(2)}, u32[]{:S(2)}) collective-permute-start(bf16[544,128]{1,0:T(8,128)(2,1)S(1)} %get-tuple-element.62), channel_id=1, source_target_pairs={{0,2},{2,0},{4,6},{6,4},{1,3},{3,1},{5,7},{7,5},{8,10},{10,8},{12,... | collective-permute-start | bytes 417800 | tf_op jit(solution)/shard_map/ppermute | solution.py:521

commit v16 on v15

--- a/solution.py
+++ b/solution.py
@@ -313,7 +313,7 @@
         before_ref[rows, :] = time - first
         return carry
 
-    lax.fori_loop(0, length // chunk, some_rows, 0)
+    lax.fori_loop(0, length // chunk, some_rows, 0, unroll=True)
 
 
 def forward_kernel(ranks, frames, *refs):
@@ -367,7 +367,7 @@
         pre_ref[rows, :] = total
         return carry
 
-    lax.fori_loop(0, length // chunk, some_rows, 0)
+    lax.fori_loop(0, length // chunk, some_rows, 0, unroll=True)
 
 
 def span_kernel(after_ref, before_ref, span_ref):
@@ -419,7 +419,7 @@
             tap_sum[tap] = tap_sum[tap] + jnp.sum(part.reshape(chunk // 8, 8, LANES), axis=0)
         return carry
 
-    lax.fori_loop(0, length // chunk, some_rows, 0)
+    lax.fori_loop(0, length // chunk, some_rows, 0, unroll=True)
     taps_ref[...] = jnp.sum(tap_sum[...], axis=1)
 
 
@@ -440,7 +440,7 @@
         g_att[rows, :] = total.astype(jnp.bfloat16)
         return carry
 
-    lax.fori_loop(0, length // chunk, some_rows, 0)
+    lax.fori_loop(0, length // chunk, some_rows, 0, unroll=True)
     heads = LANES // HDIM
     lane_head = lax.broadcasted_iota(jnp.int32, (1, LANES), 1) // HDIM
     g_wide = g_att[...].astype(jnp.float32)

time: 36.7 us -> 36.5 us (level)
  transfers between devices with their start and end apart: 10 -> 10, of which waited for: 3 -> 3; matrix products, arithmetic and copies ran while one was open for 0% -> 0% of each run, Pallas kernels for 18% -> 17%
where the time goes in v16:
time: 36.5 us; the launch traced here: 36.3 us
  starting transfers between devices  16 us (44%)
  waiting for transfers between devices  9.65 us (26%)
  Pallas kernels  9.29 us (25%)
  between operations  0.74 us (2%)
  local copies, waits for them, and re-layouts  0.66 us (2%)
    ppermute x9, starting transfers between devices, swap(): lax.ppermute(array, 'seq', [(rank, rank ^ step) for rank in range(ranks)])  14.5 us
    ppermute x9, waiting for transfers between devices, swap(): lax.ppermute(array, 'seq', [(rank, rank ^ step) for rank in range(ranks)])  9.64 us
    pallas_call x1, Pallas kernels, on_device_heads(): pl.pallas_call(functools.partial(forward_kernel, ranks, frames), out_shap...  2.27 us
    pallas_call x1, Pallas kernels, on_device_heads(): pl.pallas_call(backward_kernel, out_shape=[struct((length, LANES), bf16)]...  2.23 us
    ppermute x1, starting transfers between devices, on_device_heads(): lax.ppermute(own_taps, 'dp', [(one, (one + shift) % copies) for one in ra...  1.55 us
    pallas_call x1, Pallas kernels, on_device_heads(): pl.pallas_call(functools.partial(pack_kernel, ranks), out_shape=[struct((...  1.19 us
    pallas_call x1, Pallas kernels, on_device_heads(): pl.pallas_call(functools.partial(mask_kernel, length), out_shape=[struct(...  1.14 us
    pallas_call x1, Pallas kernels, on_device_heads(): pl.pallas_call(functools.partial(taps_kernel, ranks, frames), out_shape=[...  0.94 us
  transfers between devices with their start and end apart: 10, of which 3 were waited for; matrix products, arithmetic and copies ran while one was open for 0% of the time, Pallas kernels for 17%

profile of v16, /device:TPU:0, one launch (start us, length us, event | category | flops | bytes accessed | tf_op | source)
XLA Modules:
  0.0 36.3 jit_solution(4582630618822936101)
XLA Ops:
  0.6 0.0 copy-start
  0.6 1.2 %pack.1 = (bf16[3,128,128]{2,1,0:T(8,128)(2,1)S(1)}, bf16[3,128,128]{2,1,0:T(8,128)(2,1)S(1)}, bf16[3,128,128]{2,1,0:T(8,128)(2,1)S(1)}, bf16[128,128]{1,0:T(8,1...) custom-call(bf16[1,128,512]{2,1,0:T(8,128)(2,1)} %q_ref.1, ...), custom_call_target="tpu_custom_call" | custom-call | tf_op jit(solution)/shard_map/pack/pallas_call | solution.py:508
  1.8 5.1 %collective-permute-start.3 = (bf16[3,128,128]{2,1,0:T(8,128)(2,1)S(1)}, bf16[3,128,128]{2,1,0:T(8,128)(2,1)S(1)}, u32[]{:S(2)}, u32[]{:S(2)}) collective-permute-start(bf16[3,128,128]{2,1,0:T(8,128)(2,1)S(1)} %get-tuple-element.42), channel_id=1, source_target_pairs={{0,6},{2,4},{4,2},{6,0},{1,7},{3,5},{5,3},{7,1},{8,14},{10,12},{12... | collective-permute-start | bytes 294920 | tf_op jit(solution)/shard_map/ppermute | solution.py:521
  7.0 0.0 collective-permute-start.4
  7.0 0.6 %collective-permute-start.5 = (bf16[3,128,128]{2,1,0:T(8,128)(2,1)S(1)}, bf16[3,128,128]{2,1,0:T(8,128)(2,1)S(1)}, u32[]{:S(2)}, u32[]{:S(2)}) collective-permute-start(bf16[3,128,128]{2,1,0:T(8,128)(2,1)S(1)} %get-tuple-element.44), channel_id=1, source_target_pairs={{0,2},{2,0},{4,6},{6,4},{1,3},{3,1},{5,7},{7,5},{8,10},{10,8},{12,... | collective-permute-start | bytes 294920 | tf_op jit(solution)/shard_map/ppermute | solution.py:521
  7.6 0.0 copy-start.1
  7.6 0.7 %copy-done.1 = s32[1,16]{1,0:T(1,128)S(1)} copy-done((s32[1,16]{1,0:T(1,128)S(1)}, s32[1,16]{1,0:T(1,128)}, u32[]{:S(2)}) %copy-start.1) | copy-done | bytes 88
  8.3 1.1 %masks.1 = (bf16[128,128]{1,0:T(8,128)(2,1)S(1)}, bf16[128,128]{1,0:T(8,128)(2,1)S(1)}, bf16[128,128]{1,0:T(8,128)(2,1)S(1)}, s32[512,128]{1,0:T(8,128)S(1)}, s3...) custom-call(s32[1,16]{1,0:T(1,128)S(1)} %copy-done.1, ...), custom_call_target="tpu_custom_call" | custom-call | flops 4194304 | bytes 1048576 | tf_op jit(solution)/shard_map/masks/pallas_call | solution.py:526
  9.4 3.8 %collective-permute-start = (bf16[128,128]{1,0:T(8,128)(2,1)S(1)}, bf16[128,128]{1,0:T(8,128)(2,1)S(1)}, u32[]{:S(2)}, u32[]{:S(2)}) collective-permute-start(bf16[128,128]{1,0:T(8,128)(2,1)S(1)} %get-tuple-element.38), channel_id=1, source_target_pairs={{0,6},{2,4},{4,2},{6,0},{1,7},{3,5},{5,3},{7,1},{8,14},{10,12},{12... | collective-permute-start | bytes 98312 | tf_op jit(solution)/shard_map/ppermute | solution.py:521
  13.2 0.0 collective-permute-start.1
  13.2 0.6 %spans.1.refs_6_.span_ref = f32[31,512,128]{2,1,0:T(8,128)S(1)} custom-call(s32[512,128]{1,0:T(8,128)S(1)} %get-tuple-element.47.after_ref, s32[512,128]{1,0:T(8,128)S(1)} %get-tuple-element.48.before_ref), custom_call_target="tpu_custom_call" | custom-call | flops 419430400 | bytes 3145728 | tf_op jit(solution)/shard_map/spans/pallas_call | solution.py:543
  13.8 0.0 collective-permute-done.3.refs_0_
  13.8 1.3 %collective-permute-start.2 = (bf16[128,128]{1,0:T(8,128)(2,1)S(1)}, bf16[128,128]{1,0:T(8,128)(2,1)S(1)}, u32[]{:S(2)}, u32[]{:S(2)}) collective-permute-start(bf16[128,128]{1,0:T(8,128)(2,1)S(1)} %get-tuple-element.40), channel_id=1, source_target_pairs={{0,2},{2,0},{4,6},{6,4},{1,3},{3,1},{5,7},{7,5},{8,10},{10,8},{12,... | collective-permute-start | bytes 98312 | tf_op jit(solution)/shard_map/ppermute | solution.py:521
  15.1 2.3 %collective-permute-done.4.refs_1_ = bf16[3,128,128]{2,1,0:T(8,128)(2,1)S(1)} collective-permute-done((bf16[3,128,128]{2,1,0:T(8,128)(2,1)S(1)}, bf16[3,128,128]{2,1,0:T(8,128)(2,1)S(1)}, u32[]{:S(2)}, u32[]{:S(2)}) %collective-permute-start.4) | collective-permute-done | bytes 98336 | tf_op jit(solution)/shard_map/ppermute | solution.py:521
  17.3 0.0 collective-permute-done.5.refs_2_
  17.3 0.0 copy-done
  17.3 2.3 %forward.1 = (bf16[2,512,512]{2,1,0:T(8,128)(2,1)S(1)}, f32[544,128]{1,0:T(8,128)S(1)}, f32[512,128]{1,0:T(8,128)S(1)}, bf16[2,512,128]{2,1,0:T(8,128)(2,1)S(1)}...) custom-call(bf16[3,128,128]{2,1,0:T(8,128)(2,1)S(1)} %collective-permute-done.3.refs_0_, ...), custom_call_target="tpu_custom_call" | custom-call | flops 419430400 | bytes 3145728 | tf_op jit(solution)/shard_map/forward/pallas_call | solution.py:553
  19.6 0.0 collective-permute-done.refs_0_
  19.6 0.0 collective-permute-done.1.refs_1_
  19.6 0.0 collective-permute-done.2.refs_2_
  19.6 0.9 %taps.1 = (bf16[512,128]{1,0:T(8,128)(2,1)S(1)}, f32[544,128]{1,0:T(8,128)S(1)}, f32[32,128]{1,0:T(8,128)S(1)}) custom-call(bf16[128,128]{1,0:T(8,128)(2,1)S(1)} %collective-permute-done.refs_0_, bf16[128,128]{1,0:T(8,128)(2,1)S(1)} %collective-permute-done.1.refs_1_, bf16[128,128]{1,0:T(8,128)(2,1)S(1)} %collective-permute-done.2.refs_2_, ...), custom_call_target="tpu_custom_call" | custom-call | flops 419430400 | bytes 3145728 | tf_op jit(solution)/shard_map/taps/pallas_call | solution.py:577
  20.6 1.6 %collective-permute-start.6 = (f32[32,128]{1,0:T(8,128)S(1)}, f32[32,128]{1,0:T(8,128)S(1)}, u32[]{:S(2)}, u32[]{:S(2)}) collective-permute-start(f32[32,128]{1,0:T(8,128)S(1)} %get-tuple-element.60.refs_4_), channel_id=1, source_target_pairs={{0,8},{8,0},{1,9},{9,1},{2,10},{10,2},{3,11},{11,3},{4,12},{12,4},... | collective-permute-start | bytes 49160 | tf_op jit(solution)/shard_map/ppermute | solution.py:594
  22.1 2.2 %backward.1 = (bf16[512,128]{1,0:T(8,128)(2,1)S(1)}, bf16[512,128]{1,0:T(8,128)(2,1)S(1)}, bf16[512,128]{1,0:T(8,128)(2,1)S(1)}) custom-call(bf16[2,512,512]{2,1,0:T(8,128)(2,1)S(1)} %get-tuple-element.52.soft_ref, f32[544,128]{1,0:T(8,128)S(1)} %get-tuple-element.49.refs_4_.att_ref, f32[544,128]{1,0:T(8,128)S(1)} %get-tuple-element.53.grad_pad, ...), custom_call_target="tpu_custom_call" | custom-call | flops 838860800 | bytes 3145728 | tf_op jit(solution)/shard_map/backward/pallas_call | solution.py:598
  24.4 0.0 collective-permute-done.6.refs_5_
  24.4 1.1 %collective-permute-start.8 = (bf16[544,128]{1,0:T(8,128)(2,1)S(1)}, bf16[544,128]{1,0:T(8,128)(2,1)S(1)}, u32[]{:S(2)}, u32[]{:S(2)}) collective-permute-start(bf16[544,128]{1,0:T(8,128)(2,1)S(1)} %get-tuple-element.63), channel_id=1, source_target_pairs={{0,4},{2,6},{4,0},{6,2},{1,5},{3,7},{5,1},{7,3},{8,12},{10,14},{12... | collective-permute-start | bytes 417800 | tf_op jit(solution)/shard_map/ppermute | solution.py:521
  25.6 1.5 %collective-permute-start.9 = (bf16[544,128]{1,0:T(8,128)(2,1)S(1)}, bf16[544,128]{1,0:T(8,128)(2,1)S(1)}, u32[]{:S(2)}, u32[]{:S(2)}) collective-permute-start(bf16[544,128]{1,0:T(8,128)(2,1)S(1)} %get-tuple-element.64), channel_id=1, source_target_pairs={{0,6},{2,4},{4,2},{6,0},{1,7},{3,5},{5,3},{7,1},{8,14},{10,12},{12... | collective-permute-start | bytes 417800 | tf_op jit(solution)/shard_map/ppermute | solution.py:521
  27.1 0.9 %collective-permute-start.7 = (bf16[544,128]{1,0:T(8,128)(2,1)S(1)}, bf16[544,128]{1,0:T(8,128)(2,1)S(1)}, u32[]{:S(2)}, u32[]{:S(2)}) collective-permute-start(bf16[544,128]{1,0:T(8,128)(2,1)S(1)} %get-tuple-element.62), channel_id=1, source_target_pairs={{0,2},{2,0},{4,6},{6,4},{1,3},{3,1},{5,7},{7,5},{8,10},{10,8},{12,... | collective-permute-start | bytes 417800 | tf_op jit(solution)/shard_map/ppermute | solution.py:521
  28.1 6.7 %collective-permute-done.8.refs_2_ = bf16[544,128]{1,0:T(8,128)(2,1)S(1)} collective-permute-done((bf16[544,128]{1,0:T(8,128)(2,1)S(1)}, bf16[544,128]{1,0:T(8,128)(2,1)S(1)}, u32[]{:S(2)}, u32[]{:S(2)}) %collective-permute-start.8) | collective-permute-done | bytes 139296 | tf_op jit(solution)/shard_map/ppermute | solution.py:521
  34.8 0.0 collective-permute-done.9.refs_3_
  34.8 0.6 %collective-permute-done.7.refs_1_ = bf16[544,128]{1,0:T(8,128)(2,1)S(1)} collective-permute-done((bf16[544,128]{1,0:T(8,128)(2,1)S(1)}, bf16[544,128]{1,0:T(8,128)(2,1)S(1)}, u32[]{:S(2)}, u32[]{:S(2)}) %collective-permute-start.7) | collective-permute-done | bytes 139296 | tf_op jit(solution)/shard_map/ppermute | solution.py:521
  35.4 0.9 %spread.1 = (bf16[1,128,512]{2,1,0:T(8,128)(2,1)}, bf16[1,128,512]{2,1,0:T(8,128)(2,1)}, bf16[1,128,512]{2,1,0:T(8,128)(2,1)}, bf16[1,128,512]{2,1,0:T(8,128)(2,1)}, f32[31,512]{1,0:T(8,128)}) custom-call(bf16[544,128]{1,0:T(8,128)(2,1)S(1)} %get-tuple-element.61.refs_0_, bf16[544,128]{1,0:T(8,128)(2,1)S(1)} %collective-permute-done.7.refs_1_, ...), custom_call_target="tpu_custom_call" | custom-call | tf_op jit(solution)/shard_map/spread/pallas_call | solution.py:632
  (2 shorter events, 0.0 us)
Async XLA Ops:
  0.6 16.7 %copy-start = (f32[31,512]{1,0:T(8,128)S(1)}, f32[31,512]{1,0:T(8,128)}, u32[]{:S(2)}) copy-start(f32[31,512]{1,0:T(8,128)} %w_ref.1) | copy-start | bytes 190468
  1.8 12.0 %collective-permute-start.3 = (bf16[3,128,128]{2,1,0:T(8,128)(2,1)S(1)}, bf16[3,128,128]{2,1,0:T(8,128)(2,1)S(1)}, u32[]{:S(2)}, u32[]{:S(2)}) collective-permute-start(bf16[3,128,128]{2,1,0:T(8,128)(2,1)S(1)} %get-tuple-element.42), channel_id=1, source_target_pairs={{0,6},{2,4},{4,2},{6,0},{1,7},{3,5},{5,3},{7,1},{8,14},{10,12},{12... | collective-permute-start | bytes 294920 | tf_op jit(solution)/shard_map/ppermute | solution.py:521
  7.0 10.4 %collective-permute-start.4 = (bf16[3,128,128]{2,1,0:T(8,128)(2,1)S(1)}, bf16[3,128,128]{2,1,0:T(8,128)(2,1)S(1)}, u32[]{:S(2)}, u32[]{:S(2)}) collective-permute-start(bf16[3,128,128]{2,1,0:T(8,128)(2,1)S(1)} %get-tuple-element.43), channel_id=1, source_target_pairs={{0,4},{2,6},{4,0},{6,2},{1,5},{3,7},{5,1},{7,3},{8,12},{10,14},{12... | collective-permute-start | bytes 294920 | tf_op jit(solution)/shard_map/ppermute | solution.py:521
  7.0 10.4 %collective-permute-start.5 = (bf16[3,128,128]{2,1,0:T(8,128)(2,1)S(1)}, bf16[3,128,128]{2,1,0:T(8,128)(2,1)S(1)}, u32[]{:S(2)}, u32[]{:S(2)}) collective-permute-start(bf16[3,128,128]{2,1,0:T(8,128)(2,1)S(1)} %get-tuple-element.44), channel_id=1, source_target_pairs={{0,2},{2,0},{4,6},{6,4},{1,3},{3,1},{5,7},{7,5},{8,10},{10,8},{12,... | collective-permute-start | bytes 294920 | tf_op jit(solution)/shard_map/ppermute | solution.py:521
  7.6 0.7 %copy-start.1 = (s32[1,16]{1,0:T(1,128)S(1)}, s32[1,16]{1,0:T(1,128)}, u32[]{:S(2)}) copy-start(s32[1,16]{1,0:T(1,128)} %lens_ref.1) | copy-start | bytes 196
  9.4 10.2 %collective-permute-start = (bf16[128,128]{1,0:T(8,128)(2,1)S(1)}, bf16[128,128]{1,0:T(8,128)(2,1)S(1)}, u32[]{:S(2)}, u32[]{:S(2)}) collective-permute-start(bf16[128,128]{1,0:T(8,128)(2,1)S(1)} %get-tuple-element.38), channel_id=1, source_target_pairs={{0,6},{2,4},{4,2},{6,0},{1,7},{3,5},{5,3},{7,1},{8,14},{10,12},{12... | collective-permute-start | bytes 98312 | tf_op jit(solution)/shard_map/ppermute | solution.py:521
  13.2 6.4 %collective-permute-start.1 = (bf16[128,128]{1,0:T(8,128)(2,1)S(1)}, bf16[128,128]{1,0:T(8,128)(2,1)S(1)}, u32[]{:S(2)}, u32[]{:S(2)}) collective-permute-start(bf16[128,128]{1,0:T(8,128)(2,1)S(1)} %get-tuple-element.39), channel_id=1, source_target_pairs={{0,4},{2,6},{4,0},{6,2},{1,5},{3,7},{5,1},{7,3},{8,12},{10,14},{12... | collective-permute-start | bytes 98312 | tf_op jit(solution)/shard_map/ppermute | solution.py:521
  13.8 5.8 %collective-permute-start.2 = (bf16[128,128]{1,0:T(8,128)(2,1)S(1)}, bf16[128,128]{1,0:T(8,128)(2,1)S(1)}, u32[]{:S(2)}, u32[]{:S(2)}) collective-permute-start(bf16[128,128]{1,0:T(8,128)(2,1)S(1)} %get-tuple-element.40), channel_id=1, source_target_pairs={{0,2},{2,0},{4,6},{6,4},{1,3},{3,1},{5,7},{7,5},{8,10},{10,8},{12,... | collective-permute-start | bytes 98312 | tf_op jit(solution)/shard_map/ppermute | solution.py:521
  20.6 3.8 %collective-permute-start.6 = (f32[32,128]{1,0:T(8,128)S(1)}, f32[32,128]{1,0:T(8,128)S(1)}, u32[]{:S(2)}, u32[]{:S(2)}) collective-permute-start(f32[32,128]{1,0:T(8,128)S(1)} %get-tuple-element.60.refs_4_), channel_id=1, source_target_pairs={{0,8},{8,0},{1,9},{9,1},{2,10},{10,2},{3,11},{11,3},{4,12},{12,4},... | collective-permute-start | bytes 49160 | tf_op jit(solution)/shard_map/ppermute | solution.py:594
  24.4 10.4 %collective-permute-start.8 = (bf16[544,128]{1,0:T(8,128)(2,1)S(1)}, bf16[544,128]{1,0:T(8,128)(2,1)S(1)}, u32[]{:S(2)}, u32[]{:S(2)}) collective-permute-start(bf16[544,128]{1,0:T(8,128)(2,1)S(1)} %get-tuple-element.63), channel_id=1, source_target_pairs={{0,4},{2,6},{4,0},{6,2},{1,5},{3,7},{5,1},{7,3},{8,12},{10,14},{12... | collective-permute-start | bytes 417800 | tf_op jit(solution)/shard_map/ppermute | solution.py:521
  25.6 9.3 %collective-permute-start.9 = (bf16[544,128]{1,0:T(8,128)(2,1)S(1)}, bf16[544,128]{1,0:T(8,128)(2,1)S(1)}, u32[]{:S(2)}, u32[]{:S(2)}) collective-permute-start(bf16[544,128]{1,0:T(8,128)(2,1)S(1)} %get-tuple-element.64), channel_id=1, source_target_pairs={{0,6},{2,4},{4,2},{6,0},{1,7},{3,5},{5,3},{7,1},{8,14},{10,12},{12... | collective-permute-start | bytes 417800 | tf_op jit(solution)/shard_map/ppermute | solution.py:521
  27.1 8.3 %collective-permute-start.7 = (bf16[544,128]{1,0:T(8,128)(2,1)S(1)}, bf16[544,128]{1,0:T(8,128)(2,1)S(1)}, u32[]{:S(2)}, u32[]{:S(2)}) collective-permute-start(bf16[544,128]{1,0:T(8,128)(2,1)S(1)} %get-tuple-element.62), channel_id=1, source_target_pairs={{0,2},{2,0},{4,6},{6,4},{1,3},{3,1},{5,7},{7,5},{8,10},{10,8},{12,... | collective-permute-start | bytes 417800 | tf_op jit(solution)/shard_map/ppermute | solution.py:521

commit v17 on v16

--- a/solution.py
+++ b/solution.py
@@ -253,6 +253,11 @@
 
 def lanes_at(block):
     return pl.ds(pl.multiple_of(block * LANES, LANES), LANES)
+
+
+def late_order(ranks):
+    middle = ranks // 2
+    return [step for step in range(ranks - 1, 0, -1) if step != middle] + [middle]
 
 
 def pack_kernel(ranks, q_ref, k_ref, v_ref, c_ref, *rest):
@@ -391,14 +396,14 @@
 
 
 def taps_kernel(ranks, frames, *refs):
-    cots = refs[: ranks - 1]
+    cots = dict(zip(late_order(ranks), refs))
     own_ref, att_ref, pre_ref, span_ref = refs[ranks - 1 : ranks + 3]
     mixed_ref, grad_pad, taps_ref, cot, tap_sum = refs[ranks + 3 :]
     me = lax.axis_index("seq")
     length = ranks * frames
     cot[rows_at(me, frames), :] = own_ref[3]
     for step in range(1, ranks):
-        cot[rows_at(me ^ step, frames), :] = cots[ranks - 1 - step][...]
+        cot[rows_at(me ^ step, frames), :] = cots[step][...]
     zeros = jnp.zeros((PAD, LANES), jnp.float32)
     grad_pad[0:PAD, :] = zeros
     grad_pad[PAD + length :, :] = zeros
@@ -587,7 +592,7 @@
         compiler_params=params,
         cost_estimate=cost(400 * MIB, 3 * MIB),
         name="taps",
-    )(*[cots[step] for step in order], own, att, pre, span)
+    )(*[cots[step] for step in late_order(ranks)], own, att, pre, span)
 
     copies = lax.axis_size("dp")
     part_taps = [own_taps] + [

time: 36.5 us -> 36.7 us (level)
  starting transfers between devices: 16 us -> 17.7 us
  waiting for transfers between devices: 9.65 us -> 8.1 us
    ppermute x9, starting transfers between devices: 14.5 us -> 16.1 us  [swap(): lax.ppermute(array, 'seq', [(rank, rank ^ step) for rank in range(ranks)])]
    ppermute x9, waiting for transfers between devices: 9.64 us -> 8.09 us  [swap(): lax.ppermute(array, 'seq', [(rank, rank ^ step) for rank in range(ranks)])]
where the time goes in v17:
time: 36.7 us; the launch traced here: 36.5 us
  starting transfers between devices  17.7 us (48%)
  Pallas kernels  9.3 us (25%)
  waiting for transfers between devices  8.1 us (22%)
  between operations  0.75 us (2%)
  local copies, waits for them, and re-layouts  0.66 us (2%)
    ppermute x9, starting transfers between devices, swap(): lax.ppermute(array, 'seq', [(rank, rank ^ step) for rank in range(ranks)])  16.1 us
    ppermute x9, waiting for transfers between devices, swap(): lax.ppermute(array, 'seq', [(rank, rank ^ step) for rank in range(ranks)])  8.09 us
    pallas_call x1, Pallas kernels, on_device_heads(): pl.pallas_call(functools.partial(forward_kernel, ranks, frames), out_shap...  2.27 us
    pallas_call x1, Pallas kernels, on_device_heads(): pl.pallas_call(backward_kernel, out_shape=[struct((length, LANES), bf16)]...  2.23 us
    ppermute x1, starting transfers between devices, on_device_heads(): lax.ppermute(own_taps, 'dp', [(one, (one + shift) % copies) for one in ra...  1.56 us
    pallas_call x1, Pallas kernels, on_device_heads(): pl.pallas_call(functools.partial(pack_kernel, ranks), out_shape=[struct((...  1.19 us
    pallas_call x1, Pallas kernels, on_device_heads(): pl.pallas_call(functools.partial(mask_kernel, length), out_shape=[struct(...  1.14 us
    pallas_call x1, Pallas kernels, on_device_heads(): pl.pallas_call(functools.partial(taps_kernel, ranks, frames), out_shape=[...  0.94 us
  transfers between devices with their start and end apart: 10, of which 3 were waited for; matrix products, arithmetic and copies ran while one was open for 0% of the time, Pallas kernels for 17%

profile of v17, /device:TPU:0, one launch (start us, length us, event | category | flops | bytes accessed | tf_op | source)
XLA Modules:
  0.0 36.5 jit_solution(2516347803184251084)
XLA Ops:
  0.6 0.0 copy-start
  0.6 1.2 %pack.1 = (bf16[3,128,128]{2,1,0:T(8,128)(2,1)S(1)}, bf16[3,128,128]{2,1,0:T(8,128)(2,1)S(1)}, bf16[3,128,128]{2,1,0:T(8,128)(2,1)S(1)}, bf16[128,128]{1,0:T(8,1...) custom-call(bf16[1,128,512]{2,1,0:T(8,128)(2,1)} %q_ref.1, ...), custom_call_target="tpu_custom_call" | custom-call | tf_op jit(solution)/shard_map/pack/pallas_call | solution.py:513
  1.8 5.1 %collective-permute-start.3 = (bf16[3,128,128]{2,1,0:T(8,128)(2,1)S(1)}, bf16[3,128,128]{2,1,0:T(8,128)(2,1)S(1)}, u32[]{:S(2)}, u32[]{:S(2)}) collective-permute-start(bf16[3,128,128]{2,1,0:T(8,128)(2,1)S(1)} %get-tuple-element.42), channel_id=1, source_target_pairs={{0,6},{2,4},{4,2},{6,0},{1,7},{3,5},{5,3},{7,1},{8,14},{10,12},{12... | collective-permute-start | bytes 294920 | tf_op jit(solution)/shard_map/ppermute | solution.py:526
  7.0 0.0 collective-permute-start.4
  7.0 0.6 %collective-permute-start.5 = (bf16[3,128,128]{2,1,0:T(8,128)(2,1)S(1)}, bf16[3,128,128]{2,1,0:T(8,128)(2,1)S(1)}, u32[]{:S(2)}, u32[]{:S(2)}) collective-permute-start(bf16[3,128,128]{2,1,0:T(8,128)(2,1)S(1)} %get-tuple-element.44), channel_id=1, source_target_pairs={{0,2},{2,0},{4,6},{6,4},{1,3},{3,1},{5,7},{7,5},{8,10},{10,8},{12,... | collective-permute-start | bytes 294920 | tf_op jit(solution)/shard_map/ppermute | solution.py:526
  7.6 0.0 copy-start.1
  7.6 0.7 %copy-done.1 = s32[1,16]{1,0:T(1,128)S(1)} copy-done((s32[1,16]{1,0:T(1,128)S(1)}, s32[1,16]{1,0:T(1,128)}, u32[]{:S(2)}) %copy-start.1) | copy-done | bytes 88
  8.3 1.1 %masks.1 = (bf16[128,128]{1,0:T(8,128)(2,1)S(1)}, bf16[128,128]{1,0:T(8,128)(2,1)S(1)}, bf16[128,128]{1,0:T(8,128)(2,1)S(1)}, s32[512,128]{1,0:T(8,128)S(1)}, s3...) custom-call(s32[1,16]{1,0:T(1,128)S(1)} %copy-done.1, ...), custom_call_target="tpu_custom_call" | custom-call | flops 4194304 | bytes 1048576 | tf_op jit(solution)/shard_map/masks/pallas_call | solution.py:531
  9.4 3.8 %collective-permute-start = (bf16[128,128]{1,0:T(8,128)(2,1)S(1)}, bf16[128,128]{1,0:T(8,128)(2,1)S(1)}, u32[]{:S(2)}, u32[]{:S(2)}) collective-permute-start(bf16[128,128]{1,0:T(8,128)(2,1)S(1)} %get-tuple-element.38), channel_id=1, source_target_pairs={{0,6},{2,4},{4,2},{6,0},{1,7},{3,5},{5,3},{7,1},{8,14},{10,12},{12... | collective-permute-start | bytes 98312 | tf_op jit(solution)/shard_map/ppermute | solution.py:526
  13.2 0.0 collective-permute-start.1
  13.2 0.6 %spans.1.refs_6_.span_ref = f32[31,512,128]{2,1,0:T(8,128)S(1)} custom-call(s32[512,128]{1,0:T(8,128)S(1)} %get-tuple-element.47.after_ref, s32[512,128]{1,0:T(8,128)S(1)} %get-tuple-element.48.before_ref), custom_call_target="tpu_custom_call" | custom-call | flops 419430400 | bytes 3145728 | tf_op jit(solution)/shard_map/spans/pallas_call | solution.py:548
  13.8 0.0 collective-permute-done.3.refs_0_
  13.8 2.1 %collective-permute-start.2 = (bf16[128,128]{1,0:T(8,128)(2,1)S(1)}, bf16[128,128]{1,0:T(8,128)(2,1)S(1)}, u32[]{:S(2)}, u32[]{:S(2)}) collective-permute-start(bf16[128,128]{1,0:T(8,128)(2,1)S(1)} %get-tuple-element.40), channel_id=1, source_target_pairs={{0,4},{2,6},{4,0},{6,2},{1,5},{3,7},{5,1},{7,3},{8,12},{10,14},{12... | collective-permute-start | bytes 98312 | tf_op jit(solution)/shard_map/ppermute | solution.py:526
  15.9 0.5 %collective-permute-done.4.refs_1_ = bf16[3,128,128]{2,1,0:T(8,128)(2,1)S(1)} collective-permute-done((bf16[3,128,128]{2,1,0:T(8,128)(2,1)S(1)}, bf16[3,128,128]{2,1,0:T(8,128)(2,1)S(1)}, u32[]{:S(2)}, u32[]{:S(2)}) %collective-permute-start.4) | collective-permute-done | bytes 98336 | tf_op jit(solution)/shard_map/ppermute | solution.py:526
  16.4 0.0 collective-permute-done.5.refs_2_
  16.4 0.0 copy-done
  16.4 2.3 %forward.1 = (bf16[2,512,512]{2,1,0:T(8,128)(2,1)S(1)}, f32[544,128]{1,0:T(8,128)S(1)}, f32[512,128]{1,0:T(8,128)S(1)}, bf16[2,512,128]{2,1,0:T(8,128)(2,1)S(1)}...) custom-call(bf16[3,128,128]{2,1,0:T(8,128)(2,1)S(1)} %collective-permute-done.3.refs_0_, ...), custom_call_target="tpu_custom_call" | custom-call | flops 419430400 | bytes 3145728 | tf_op jit(solution)/shard_map/forward/pallas_call | solution.py:558
  18.7 0.0 collective-permute-done.refs_0_
  18.7 0.0 collective-permute-done.1.refs_1_
  18.7 0.0 collective-permute-done.2.refs_2_
  18.7 0.9 %taps.1 = (bf16[512,128]{1,0:T(8,128)(2,1)S(1)}, f32[544,128]{1,0:T(8,128)S(1)}, f32[32,128]{1,0:T(8,128)S(1)}) custom-call(bf16[128,128]{1,0:T(8,128)(2,1)S(1)} %collective-permute-done.refs_0_, bf16[128,128]{1,0:T(8,128)(2,1)S(1)} %collective-permute-done.1.refs_1_, bf16[128,128]{1,0:T(8,128)(2,1)S(1)} %collective-permute-done.2.refs_2_, ...), custom_call_target="tpu_custom_call" | custom-call | flops 419430400 | bytes 3145728 | tf_op jit(solution)/shard_map/taps/pallas_call | solution.py:582
  19.7 1.6 %collective-permute-start.6 = (f32[32,128]{1,0:T(8,128)S(1)}, f32[32,128]{1,0:T(8,128)S(1)}, u32[]{:S(2)}, u32[]{:S(2)}) collective-permute-start(f32[32,128]{1,0:T(8,128)S(1)} %get-tuple-element.60.refs_4_), channel_id=1, source_target_pairs={{0,8},{8,0},{1,9},{9,1},{2,10},{10,2},{3,11},{11,3},{4,12},{12,4},... | collective-permute-start | bytes 49160 | tf_op jit(solution)/shard_map/ppermute | solution.py:599
  21.2 2.2 %backward.1 = (bf16[512,128]{1,0:T(8,128)(2,1)S(1)}, bf16[512,128]{1,0:T(8,128)(2,1)S(1)}, bf16[512,128]{1,0:T(8,128)(2,1)S(1)}) custom-call(bf16[2,512,512]{2,1,0:T(8,128)(2,1)S(1)} %get-tuple-element.52.soft_ref, f32[544,128]{1,0:T(8,128)S(1)} %get-tuple-element.49.refs_4_.att_ref, f32[544,128]{1,0:T(8,128)S(1)} %get-tuple-element.53.grad_pad, ...), custom_call_target="tpu_custom_call" | custom-call | flops 838860800 | bytes 3145728 | tf_op jit(solution)/shard_map/backward/pallas_call | solution.py:603
  23.5 0.0 collective-permute-done.6.refs_5_
  23.5 2.0 %collective-permute-start.8 = (bf16[544,128]{1,0:T(8,128)(2,1)S(1)}, bf16[544,128]{1,0:T(8,128)(2,1)S(1)}, u32[]{:S(2)}, u32[]{:S(2)}) collective-permute-start(bf16[544,128]{1,0:T(8,128)(2,1)S(1)} %get-tuple-element.63), channel_id=1, source_target_pairs={{0,4},{2,6},{4,0},{6,2},{1,5},{3,7},{5,1},{7,3},{8,12},{10,14},{12... | collective-permute-start | bytes 417800 | tf_op jit(solution)/shard_map/ppermute | solution.py:526
  25.5 2.4 %collective-permute-start.9 = (bf16[544,128]{1,0:T(8,128)(2,1)S(1)}, bf16[544,128]{1,0:T(8,128)(2,1)S(1)}, u32[]{:S(2)}, u32[]{:S(2)}) collective-permute-start(bf16[544,128]{1,0:T(8,128)(2,1)S(1)} %get-tuple-element.64), channel_id=1, source_target_pairs={{0,6},{2,4},{4,2},{6,0},{1,7},{3,5},{5,3},{7,1},{8,14},{10,12},{12... | collective-permute-start | bytes 417800 | tf_op jit(solution)/shard_map/ppermute | solution.py:526
  27.9 0.1 collective-permute-start.7
  28.0 6.7 %collective-permute-done.8.refs_2_ = bf16[544,128]{1,0:T(8,128)(2,1)S(1)} collective-permute-done((bf16[544,128]{1,0:T(8,128)(2,1)S(1)}, bf16[544,128]{1,0:T(8,128)(2,1)S(1)}, u32[]{:S(2)}, u32[]{:S(2)}) %collective-permute-start.8) | collective-permute-done | bytes 139296 | tf_op jit(solution)/shard_map/ppermute | solution.py:526
  34.7 0.0 collective-permute-done.9.refs_3_
  34.7 0.9 %collective-permute-done.7.refs_1_ = bf16[544,128]{1,0:T(8,128)(2,1)S(1)} collective-permute-done((bf16[544,128]{1,0:T(8,128)(2,1)S(1)}, bf16[544,128]{1,0:T(8,128)(2,1)S(1)}, u32[]{:S(2)}, u32[]{:S(2)}) %collective-permute-start.7) | collective-permute-done | bytes 139296 | tf_op jit(solution)/shard_map/ppermute | solution.py:526
  35.6 0.9 %spread.1 = (bf16[1,128,512]{2,1,0:T(8,128)(2,1)}, bf16[1,128,512]{2,1,0:T(8,128)(2,1)}, bf16[1,128,512]{2,1,0:T(8,128)(2,1)}, bf16[1,128,512]{2,1,0:T(8,128)(2,1)}, f32[31,512]{1,0:T(8,128)}) custom-call(bf16[544,128]{1,0:T(8,128)(2,1)S(1)} %get-tuple-element.61.refs_0_, bf16[544,128]{1,0:T(8,128)(2,1)S(1)} %collective-permute-done.7.refs_1_, ...), custom_call_target="tpu_custom_call" | custom-call | tf_op jit(solution)/shard_map/spread/pallas_call | solution.py:637
  (2 shorter events, 0.1 us)
Async XLA Ops:
  0.6 15.8 %copy-start = (f32[31,512]{1,0:T(8,128)S(1)}, f32[31,512]{1,0:T(8,128)}, u32[]{:S(2)}) copy-start(f32[31,512]{1,0:T(8,128)} %w_ref.1) | copy-start | bytes 190468
  1.8 12.0 %collective-permute-start.3 = (bf16[3,128,128]{2,1,0:T(8,128)(2,1)S(1)}, bf16[3,128,128]{2,1,0:T(8,128)(2,1)S(1)}, u32[]{:S(2)}, u32[]{:S(2)}) collective-permute-start(bf16[3,128,128]{2,1,0:T(8,128)(2,1)S(1)} %get-tuple-element.42), channel_id=1, source_target_pairs={{0,6},{2,4},{4,2},{6,0},{1,7},{3,5},{5,3},{7,1},{8,14},{10,12},{12... | collective-permute-start | bytes 294920 | tf_op jit(solution)/shard_map/ppermute | solution.py:526
  7.0 9.4 %collective-permute-start.4 = (bf16[3,128,128]{2,1,0:T(8,128)(2,1)S(1)}, bf16[3,128,128]{2,1,0:T(8,128)(2,1)S(1)}, u32[]{:S(2)}, u32[]{:S(2)}) collective-permute-start(bf16[3,128,128]{2,1,0:T(8,128)(2,1)S(1)} %get-tuple-element.43), channel_id=1, source_target_pairs={{0,4},{2,6},{4,0},{6,2},{1,5},{3,7},{5,1},{7,3},{8,12},{10,14},{12... | collective-permute-start | bytes 294920 | tf_op jit(solution)/shard_map/ppermute | solution.py:526
  7.0 9.4 %collective-permute-start.5 = (bf16[3,128,128]{2,1,0:T(8,128)(2,1)S(1)}, bf16[3,128,128]{2,1,0:T(8,128)(2,1)S(1)}, u32[]{:S(2)}, u32[]{:S(2)}) collective-permute-start(bf16[3,128,128]{2,1,0:T(8,128)(2,1)S(1)} %get-tuple-element.44), channel_id=1, source_target_pairs={{0,2},{2,0},{4,6},{6,4},{1,3},{3,1},{5,7},{7,5},{8,10},{10,8},{12,... | collective-permute-start | bytes 294920 | tf_op jit(solution)/shard_map/ppermute | solution.py:526
  7.6 0.7 %copy-start.1 = (s32[1,16]{1,0:T(1,128)S(1)}, s32[1,16]{1,0:T(1,128)}, u32[]{:S(2)}) copy-start(s32[1,16]{1,0:T(1,128)} %lens_ref.1) | copy-start | bytes 196
  9.4 9.3 %collective-permute-start = (bf16[128,128]{1,0:T(8,128)(2,1)S(1)}, bf16[128,128]{1,0:T(8,128)(2,1)S(1)}, u32[]{:S(2)}, u32[]{:S(2)}) collective-permute-start(bf16[128,128]{1,0:T(8,128)(2,1)S(1)} %get-tuple-element.38), channel_id=1, source_target_pairs={{0,6},{2,4},{4,2},{6,0},{1,7},{3,5},{5,3},{7,1},{8,14},{10,12},{12... | collective-permute-start | bytes 98312 | tf_op jit(solution)/shard_map/ppermute | solution.py:526
  13.2 5.5 %collective-permute-start.1 = (bf16[128,128]{1,0:T(8,128)(2,1)S(1)}, bf16[128,128]{1,0:T(8,128)(2,1)S(1)}, u32[]{:S(2)}, u32[]{:S(2)}) collective-permute-start(bf16[128,128]{1,0:T(8,128)(2,1)S(1)} %get-tuple-element.39), channel_id=1, source_target_pairs={{0,2},{2,0},{4,6},{6,4},{1,3},{3,1},{5,7},{7,5},{8,10},{10,8},{12,... | collective-permute-start | bytes 98312 | tf_op jit(solution)/shard_map/ppermute | solution.py:526
  13.8 4.9 %collective-permute-start.2 = (bf16[128,128]{1,0:T(8,128)(2,1)S(1)}, bf16[128,128]{1,0:T(8,128)(2,1)S(1)}, u32[]{:S(2)}, u32[]{:S(2)}) collective-permute-start(bf16[128,128]{1,0:T(8,128)(2,1)S(1)} %get-tuple-element.40), channel_id=1, source_target_pairs={{0,4},{2,6},{4,0},{6,2},{1,5},{3,7},{5,1},{7,3},{8,12},{10,14},{12... | collective-permute-start | bytes 98312 | tf_op jit(solution)/shard_map/ppermute | solution.py:526
  19.7 3.8 %collective-permute-start.6 = (f32[32,128]{1,0:T(8,128)S(1)}, f32[32,128]{1,0:T(8,128)S(1)}, u32[]{:S(2)}, u32[]{:S(2)}) collective-permute-start(f32[32,128]{1,0:T(8,128)S(1)} %get-tuple-element.60.refs_4_), channel_id=1, source_target_pairs={{0,8},{8,0},{1,9},{9,1},{2,10},{10,2},{3,11},{11,3},{4,12},{12,4},... | collective-permute-start | bytes 49160 | tf_op jit(solution)/shard_map/ppermute | solution.py:599
  23.5 11.2 %collective-permute-start.8 = (bf16[544,128]{1,0:T(8,128)(2,1)S(1)}, bf16[544,128]{1,0:T(8,128)(2,1)S(1)}, u32[]{:S(2)}, u32[]{:S(2)}) collective-permute-start(bf16[544,128]{1,0:T(8,128)(2,1)S(1)} %get-tuple-element.63), channel_id=1, source_target_pairs={{0,4},{2,6},{4,0},{6,2},{1,5},{3,7},{5,1},{7,3},{8,12},{10,14},{12... | collective-permute-start | bytes 417800 | tf_op jit(solution)/shard_map/ppermute | solution.py:526
  25.5 9.2 %collective-permute-start.9 = (bf16[544,128]{1,0:T(8,128)(2,1)S(1)}, bf16[544,128]{1,0:T(8,128)(2,1)S(1)}, u32[]{:S(2)}, u32[]{:S(2)}) collective-permute-start(bf16[544,128]{1,0:T(8,128)(2,1)S(1)} %get-tuple-element.64), channel_id=1, source_target_pairs={{0,6},{2,4},{4,2},{6,0},{1,7},{3,5},{5,3},{7,1},{8,14},{10,12},{12... | collective-permute-start | bytes 417800 | tf_op jit(solution)/shard_map/ppermute | solution.py:526
  27.9 7.6 %collective-permute-start.7 = (bf16[544,128]{1,0:T(8,128)(2,1)S(1)}, bf16[544,128]{1,0:T(8,128)(2,1)S(1)}, u32[]{:S(2)}, u32[]{:S(2)}) collective-permute-start(bf16[544,128]{1,0:T(8,128)(2,1)S(1)} %get-tuple-element.62), channel_id=1, source_target_pairs={{0,2},{2,0},{4,6},{6,4},{1,3},{3,1},{5,7},{7,5},{8,10},{10,8},{12,... | collective-permute-start | bytes 417800 | tf_op jit(solution)/shard_map/ppermute | solution.py:526
